TPU v7x, 32 devices: a whole 2x2x4 slice. The times are simulated.
32 devices in a mesh: tok: 8 (over y, x, core), fac: 4 (over z).
Axes of the slice: x: 2, y: 2, z: 4, core: 2. Of those that a mesh axis runs over, the one named last changes fastest.
Arguments:
- grad_rows: bfloat16 [4096, 6144], P('tok', 'fac'), may hold values from -6 to 6
- routes: int32 [4096, 1], P('tok'), may hold values from 0 to 1; in each aligned block of 512 rows (0 to 511, 512 to 1023, ...) at most 320 rows name the same one
- counts: int32 [8], P('tok'), may hold values from 64 to 512, as said below
- factor_old: float32 [12288, 6144], P('tok', 'fac'), as said below
- damping: float32 [2], replicated, may hold values from 0.1 to 1
- weight_grad: bfloat16 [12288, 8192], P('tok', 'fac'), may hold values from -6 to 6
Outputs:
- running: float32 [12288, 6144], P('tok', 'fac')
- factored: float32 [12288, 6144], P('tok', 'fac')
- preconditioned: float32 [12288, 8192], P('tok', 'fac')
Inputs may be any that keep to these rules, and one draw needn't show every extreme that they name: `routes`: in the rows of one device, at most 320 rows name the same expert. The first counts[j] rows of index j of tok are live; the others take no part. `factor_old`: symmetric and positive definite.
All inputs are finite; a program needn't handle non-finite values.
Results may differ from a plain program's by a relative error of at most 0.0015.
Values may be sent and summed in bfloat16 or wider, within the bound.
No kernel may reach another device: no remote copies, remote signals or barrier semaphores. Data moves between devices by JAX's collectives and lax.ppermute only.
A program may use at most 192 MiB of HBM per device.

v0:
```python
import jax
import jax.numpy as jnp
from jax import lax
from jax.sharding import PartitionSpec as P

D = 6144
PB = 256
CAP = 320


DECAY = 0.8


def swapped(value, axis, bit):
    mask = 2**bit
    pairs = [(source, source ^ mask) for source in range(lax.axis_size(axis))]
    return lax.ppermute(value, axis, pairs)


def broadcast(array, axis, root):
    mine = lax.axis_index(axis) == root
    return lax.psum(jnp.where(mine, array, jnp.zeros_like(array)), axis)


def lower_solve(factor, values):
    return jax.scipy.linalg.solve_triangular(factor, values, lower=True)


def highest(left_side, right_side):
    return jnp.dot(left_side, right_side, precision=lax.Precision.HIGHEST)


def apply_inverse(diag_factor, values):
    return lower_solve(diag_factor, values)


def compact_rows(row_flags, values, capacity):
    slot_ranks = jnp.cumsum(row_flags.astype(jnp.int32)) - 1
    picker = (slot_ranks[None, :] == jnp.arange(capacity)[:, None]) & row_flags[None, :]
    return jnp.dot(picker.astype(values.dtype), values, preferred_element_type=jnp.float32).astype(
        jnp.bfloat16
    )


def stack_pairs(gathered, position, depth_bits, swapper):
    for bit_level in range(depth_bits):
        partner = swapper(gathered, bit_level)
        upper_side = position >> bit_level & 1 == 1
        gathered = jnp.where(
            upper_side,
            jnp.concatenate([partner, gathered], 0),
            jnp.concatenate([gathered, partner], 0),
        )
    return gathered


def stack_carry(gathered, carried, position, depth_bits, swapper):
    for bit_level in range(depth_bits):
        row_count = gathered.shape[0]
        message = jnp.concatenate([gathered, carried], 0)
        partner = swapper(message, bit_level)
        partner_rows = partner[:row_count]
        partner_carry = partner[row_count:]
        upper_side = position >> bit_level & 1 == 1
        gathered = jnp.where(
            upper_side,
            jnp.concatenate([partner_rows, gathered], 0),
            jnp.concatenate([gathered, partner_rows], 0),
        )
        carried = carried + partner_carry
    return (gathered, carried)


def local(grad_rows, routes, counts, factor_old, damping, weight_grad):
    group_size = lax.axis_size("tok") // 2
    depth_bits = group_size.bit_length() - 1
    position = lax.axis_index("tok")
    expert_id = position // group_size
    member = position % group_size
    column = lax.axis_index("fac")
    tok_rows, block_width = grad_rows.shape
    grad_cols = weight_grad.shape[1]
    capacity = CAP
    live_rows = jnp.arange(tok_rows) < counts[0]
    route_ids = routes[:, 0]
    own_flags = live_rows & (route_ids == expert_id)
    away_flags = live_rows & (route_ids != expert_id)
    outgoing = compact_rows(away_flags, grad_rows, capacity)
    incoming = swapped(outgoing, "tok", depth_bits)
    arrived = jnp.concatenate([compact_rows(own_flags, grad_rows, capacity), incoming], 0)
    tallies = jnp.stack(
        [jnp.sum(live_rows & (route_ids == 0)), jnp.sum(live_rows & (route_ids == 1))]
    ).astype(jnp.float32)
    totals = lax.psum(tallies, "tok")
    total_mine = jnp.where(expert_id == 0, totals[0], totals[1])
    collected = stack_pairs(
        arrived, member, depth_bits, lambda operand, bit_level: swapped(operand, "tok", bit_level)
    )
    features = broadcast(collected, "fac", member)
    gram_block = lax.dot_general(
        features, collected, (((0,), (0,)), ((), ())), preferred_element_type=jnp.float32
    )
    running = DECAY * factor_old + (1.0 - DECAY) * (gram_block / total_mine)
    row_index = member * block_width + jnp.arange(block_width)[:, None]
    col_index = column * block_width + jnp.arange(block_width)[None, :]
    damp_value = jnp.where(expert_id == 0, damping[0], damping[1])
    matrix = running + jnp.where(row_index == col_index, damp_value, 0.0)
    global_rows = jnp.arange(D)[:, None]
    lead_seed = jnp.where(member == 0, weight_grad[0 : 2 * PB].astype(jnp.float32), 0.0).reshape(
        2 * grad_cols, PB
    )
    lead_rows = lead_seed
    lowers = []
    inverses = []
    full_panels = []
    own_panels = []
    for panel_step in range(2):
        begin_col = panel_step * PB
        end_col = begin_col + PB
        shared = broadcast(matrix[:, begin_col:end_col], "fac", 0)
        carried_in = lead_seed if panel_step == 0 else jnp.zeros((0, PB), jnp.float32)
        stacked, carried_out = stack_carry(
            shared,
            carried_in,
            member,
            depth_bits,
            lambda operand, bit_level: swapped(
                operand.astype(jnp.bfloat16), "tok", bit_level
            ).astype(operand.dtype),
        )
        if panel_step == 0:
            lead_rows = carried_out
        diag_factor = jnp.linalg.cholesky(stacked[begin_col:end_col])
        solved = lower_solve(diag_factor, stacked.T).T
        lower_panel = jnp.where(global_rows >= end_col, solved, 0.0)
        lower_panel = lower_panel.at[begin_col:end_col].set(diag_factor)
        own_rows = lax.dynamic_slice_in_dim(lower_panel, member * block_width, block_width, 0)
        col_rows = lax.dynamic_slice_in_dim(lower_panel, column * block_width, block_width, 0)
        trailing = (row_index >= end_col) & (col_index >= end_col)
        matrix = jnp.where(trailing, matrix - highest(own_rows, col_rows.T), matrix)
        placed = (
            jnp.zeros((block_width, block_width), jnp.float32)
            .at[:, begin_col:end_col]
            .set(own_rows)
        )
        matrix = jnp.where((col_index >= begin_col) & (col_index < end_col), placed, matrix)
        matrix = jnp.where(
            (row_index >= begin_col) & (row_index < end_col) & (col_index >= end_col), 0.0, matrix
        )
        lowers.append(diag_factor)
        inverses.append(diag_factor)
        full_panels.append(lower_panel)
        own_panels.append(own_rows)
    leading_float = lead_rows.reshape(2 * PB, grad_cols)
    first_solve = apply_inverse(lowers[0], leading_float[0:PB])
    second_in = leading_float[PB : 2 * PB] - highest(full_panels[0][PB : 2 * PB], first_solve)
    second_solve = apply_inverse(lowers[1], second_in)
    gradient = weight_grad.astype(jnp.float32)
    remainder = (
        gradient - highest(own_panels[0], first_solve) - highest(own_panels[1], second_solve)
    )
    head_rows = jnp.concatenate(
        [first_solve, second_solve, jnp.zeros((block_width - 2 * PB, grad_cols), jnp.float32)], 0
    )
    local_rows = jnp.arange(block_width)[:, None]
    precond = jnp.where((member == 0) & (local_rows < 2 * PB), head_rows, remainder)
    return (running, matrix, precond)


def solution(mesh):
    placed = (P("tok", "fac"), P("tok", None), P("tok"), P("tok", "fac"), P(), P("tok", "fac"))
    return jax.shard_map(
        local,
        mesh=mesh,
        in_specs=placed,
        out_specs=(P("tok", "fac"), P("tok", "fac"), P("tok", "fac")),
        check_vma=False,
    )
```

profile of v0, /device:TPU:2, one launch (start us, length us, event | category | flops | bytes accessed | tf_op | source)
XLA Modules:
  0.0 975.8 jit_solution(3789293834391190537)
XLA Ops:
  13.8 20.9 %collective-permute-done = bf16[320,1536]{1,0:T(8,128)(2,1)S(1)} collective-permute-done((bf16[320,1536]{1,0:T(8,128)(2,1)}, bf16[320,1536]{1,0:T(8,128)(2,1)S(1)}, u32[]{:S(2)}, u32[]{:S(2)}) %collective-permute-start) | collective-permute-done | bytes 983072 | tf_op jit(solution)/shard_map/ppermute | solution.py:17
  44.7 87.0 %collective-permute-done.2 = bf16[1280,1536]{1,0:T(8,128)(2,1)} collective-permute-done((bf16[1280,1536]{1,0:T(8,128)(2,1)}, bf16[1280,1536]{1,0:T(8,128)(2,1)}, u32[]{:S(2)}, u32[]{:S(2)}) %collective-permute-start.2) | collective-permute-done | bytes 3932192 | tf_op jit(solution)/shard_map/ppermute | solution.py:17
  131.8 9.6 broadcast_select_fusion
  143.4 10.5 %psum.29 = f32[2]{0:T(128)S(1)} all-reduce(f32[2]{0:T(128)S(1)} %add_convert_fusion), channel_id=1, replica_groups=mesh['tok'=8,'fac'=4] {'tok'}, use_global_device_ids=true, to_apply=%region_7.8 | all-reduce | flops 2 | bytes 16 | tf_op jit(solution)/shard_map/psum | solution.py:94
  153.9 9.6 copy.27
  167.3 249.2 %all-reduce.7.cloned.1.call-done = bf16[2560,1536]{1,0:T(8,128)(2,1)} async-done(((bf16[2560,1536]{1,0:T(8,128)(2,1)}), bf16[2560,1536]{1,0:T(8,128)(2,1)}) %all-reduce.7.cloned.1.call-update) | async-done | bytes 7864336 | tf_op jit(solution)/shard_map/psum | solution.py:22
  416.5 24.0 %select_add_fusion = (f32[1536,1536]{0,1:T(8,128)}, f32[1536,1536]{0,1:T(8,128)}) fusion(f32[]{:T(128)S(6)} %select_n.149, s32[1536]{0:T(1024)S(1)} %get-tuple-element.175, s32[1536]{0:T(1024)S(1)} %get-tuple-element.174, f32[]{:T(128)S(6)} %select_n.145, bf16[2560,1536]{1,0:T(8,128)(2,1)} %all-reduce.7.cloned.1.call-done, ...), kind=kOutput, calls=%fused_computation.9 | convolution fusion | flops 12131500032 | bytes 44052488 | tf_op jit(solution)/shard_map/dot_general | solution.py:100
  462.2 49.1 %all-reduce.9.cloned.1.call-done = f32[1536,256]{0,1:T(8,128)} async-done(((f32[1536,256]{0,1:T(8,128)}), f32[1536,256]{0,1:T(8,128)}) %all-reduce.9.cloned.1.call-update) | async-done | bytes 1572880 | tf_op jit(solution)/shard_map/psum | solution.py:22
  530.0 80.4 %collective-permute-done.4 = bf16[7168,256]{0,1:T(8,128)(2,1)} collective-permute-done((bf16[7168,256]{0,1:T(8,128)(2,1)}, bf16[7168,256]{0,1:T(8,128)(2,1)}, u32[]{:S(2)}, u32[]{:S(2)}) %collective-permute-start.4) | collective-permute-done | bytes 3670048 | tf_op jit(solution)/shard_map/ppermute | solution.py:17
  619.8 11.7 %cholesky.130 = f32[128,128]{1,0:T(8,128)S(1)} custom-call(f32[128,128]{1,0:T(8,128)S(1)} %cholesky.194), custom_call_target="Cholesky" | custom-call | tf_op jit(solution)/shard_map/jit(cholesky)/cholesky | solution.py:133
  631.6 9.8 %custom-call.17 = f32[1,128,128]{1,2,0:T(8,128)S(1)} custom-call(f32[1,128,128]{2,1,0:T(8,128)S(1)} %get-tuple-element.157), custom_call_target="InvertDiagBlocksLowerTriangular" | custom-call | tf_op jit(solution)/shard_map/jit(cholesky)/cholesky | solution.py:133
  641.9 11.7 %cholesky.147 = f32[128,128]{1,0:T(8,128)S(1)} custom-call(f32[128,128]{1,0:T(8,128)S(1)} %convolution_subtract_fusion.5), custom_call_target="Cholesky" | custom-call | tf_op jit(solution)/shard_map/jit(cholesky)/cholesky | solution.py:133
  660.9 19.8 %custom-call.18 = f32[2,128,128]{1,2,0:T(8,128)S(1)} custom-call(f32[2,128,128]{2,1,0:T(8,128)S(1)} %get-tuple-element.82), custom_call_target="InvertDiagBlocksLowerTriangular" | custom-call | tf_op jit(solution)/shard_map/jit(_solve_triangular)/triangular_solve | solution.py:26
  693.0 14.4 %select_select_fusion.1 = f32[1536,1536]{0,1:T(8,128)S(1)} fusion(f32[1536,256]{0,1:T(8,128)S(1)} %dynamic-slice_select_fusion.1, f32[1536,1536]{0,1:T(8,128)} %get-tuple-element.162, pred[1536]{0:T(1024)(128)(4,1)S(1)} %get-tuple-element.171, pred[1536]{0:T(1024)(128)(4,1)S(1)} %get-tuple-element.168, pred[1536]{0:T(1024)(128)(4,1)S(1)} %get-tuple-element.169, ...), kind=kOutput, calls=%fused_computation.8 | convolution fusion | flops 7261913088 | bytes 23601160 | tf_op jit(solution)/shard_map/dot_general | solution.py:30
  713.2 9.7 copy.47
  728.8 52.0 %all-reduce.11.cloned.1.call-done = f32[1536,256]{0,1:T(8,128)} async-done(((f32[1536,256]{0,1:T(8,128)}), f32[1536,256]{0,1:T(8,128)}) %all-reduce.11.cloned.1.call-update) | async-done | bytes 1572880 | tf_op jit(solution)/shard_map/psum | solution.py:22
  812.4 13.7 %fusion.9 = f32[1536,2048]{1,0:T(8,128)} fusion(f32[128,2048]{1,0:T(8,128)S(1)} %fusion.49, f32[128,2048]{1,0:T(8,128)S(1)} %fusion.20, f32[6144,256]{0,1:T(8,128)} %copy-done.8, s32[]{:T(128)S(6)} %select_n.158), kind=kOutput, calls=%fused_computation.42 | convolution fusion | flops 9664200704 | bytes 16252932 | tf_op jit(solution)/shard_map/dot_general | solution.py:30
  826.1 14.5 %collective-permute-done.6 = bf16[3072,256]{0,1:T(8,128)(2,1)S(1)} collective-permute-done((bf16[3072,256]{0,1:T(8,128)(2,1)S(1)}, bf16[3072,256]{0,1:T(8,128)(2,1)S(1)}, u32[]{:S(2)}, u32[]{:S(2)}) %collective-permute-start.6) | collective-permute-done | bytes 1572896 | tf_op jit(solution)/shard_map/ppermute | solution.py:17
  845.8 11.7 %cholesky.164 = f32[128,128]{1,0:T(8,128)S(1)} custom-call(f32[128,128]{1,0:T(8,128)S(1)} %cholesky.197), custom_call_target="Cholesky" | custom-call | tf_op jit(solution)/shard_map/jit(cholesky)/cholesky | solution.py:133
  857.6 9.8 %custom-call.19 = f32[1,128,128]{1,2,0:T(8,128)S(1)} custom-call(f32[1,128,128]{2,1,0:T(8,128)S(1)} %get-tuple-element.155), custom_call_target="InvertDiagBlocksLowerTriangular" | custom-call | tf_op jit(solution)/shard_map/jit(cholesky)/cholesky | solution.py:133
  867.9 11.7 %cholesky.181 = f32[128,128]{1,0:T(8,128)S(1)} custom-call(f32[128,128]{1,0:T(8,128)S(1)} %convolution_subtract_fusion.4), custom_call_target="Cholesky" | custom-call | tf_op jit(solution)/shard_map/jit(cholesky)/cholesky | solution.py:133
  886.8 19.9 %custom-call.20 = f32[2,128,128]{1,2,0:T(8,128)S(1)} custom-call(f32[2,128,128]{2,1,0:T(8,128)S(1)} %get-tuple-element.83), custom_call_target="InvertDiagBlocksLowerTriangular" | custom-call | tf_op jit(solution)/shard_map/jit(_solve_triangular)/triangular_solve | solution.py:26
  926.5 12.8 %select_select_fusion = f32[1536,1536]{0,1:T(8,128)} fusion(f32[1536,256]{0,1:T(8,128)S(1)} %dynamic-slice_select_fusion, f32[1536,1536]{0,1:T(8,128)S(1)} %bitcast.114, pred[1536]{0:T(1024)(128)(4,1)S(1)} %get-tuple-element.173, pred[1536]{0:T(1024)(128)(4,1)S(1)} %get-tuple-element.166, pred[1536]{0:T(1024)(128)(4,1)S(1)} %get-tuple-element.167, ...), kind=kOutput, calls=%fused_computation.7 | convolution fusion | flops 7261913088 | bytes 23601160 | tf_op jit(solution)/shard_map/dot_general | solution.py:30
  948.9 19.9 %maximum_select_fusion = f32[1536,2048]{1,0:T(8,128)} fusion(f32[128,2048]{1,0:T(8,128)} %fusion.51, f32[128,2048]{1,0:T(8,128)} %copy-done.15, f32[128,2048]{1,0:T(8,128)} %copy-done.10, f32[128,2048]{1,0:T(8,128)S(1)} %fusion.20, f32[1536,2048]{1,0:T(8,128)} %fusion.9, bf16[1536,2048]{1,0:T(8,128)(2,1)} %param.24, f32[1536]{0:T(1024)S(1)} %pad.19.clone, ...), kind=kOutput, calls=%fused_computation.6 | convolution fusion | flops 9689366528 | bytes 39329284 | tf_op jit(solution)/shard_map/dot_general | solution.py:30
  (201 shorter events, 179.7 us)
Async XLA Ops:
  7.2 409.3 %all-reduce.7.cloned.1.call-start = ((), (), s32[]{:S(2)}) async-start(), calls=%async_computation | async-start | bytes 15728640 | tf_op jit(solution)/shard_map/psum | solution.py:22
  11.0 23.7 %collective-permute-start = (bf16[320,1536]{1,0:T(8,128)(2,1)}, bf16[320,1536]{1,0:T(8,128)(2,1)S(1)}, u32[]{:S(2)}, u32[]{:S(2)}) collective-permute-start(bf16[320,1536]{1,0:T(8,128)(2,1)} %convolution_convert_fusion), channel_id=1, source_target_pairs={{0,16},{4,20},{8,24},{12,28},{16,0},{20,4},{24,8},{28,12},{1,17},{... | collective-permute-start | bytes 2949128 | tf_op jit(solution)/shard_map/ppermute | solution.py:17
  36.1 4.3 collective-permute-start.1
  44.4 87.3 %collective-permute-start.2 = (bf16[1280,1536]{1,0:T(8,128)(2,1)}, bf16[1280,1536]{1,0:T(8,128)(2,1)}, u32[]{:S(2)}, u32[]{:S(2)}) collective-permute-start(bf16[1280,1536]{1,0:T(8,128)(2,1)} %maximum_select_fusion.6), channel_id=1, source_target_pairs={{0,8},{4,12},{8,0},{12,4},{16,24},{20,28},{24,16},{28,20},{1,9},{5... | collective-permute-start | bytes 11796488 | tf_op jit(solution)/shard_map/ppermute | solution.py:17
  141.4 370.0 %all-reduce.9.cloned.1.call-start = ((), (), s32[]{:S(2)}) async-start(), calls=%async_computation.1 | async-start | bytes 3145728 | tf_op jit(solution)/shard_map/psum | solution.py:22
  153.9 11.5 %copy-start.17 = (f32[2]{0:T(128)S(1)}, f32[2]{0:T(128)}, u32[]{:S(2)}) copy-start(f32[2]{0:T(128)} %param.23) | copy-start | bytes 28
  443.2 337.6 %all-reduce.11.cloned.1.call-start = ((), (), s32[]{:S(2)}) async-start(), calls=%async_computation.2 | async-start | bytes 3145728 | tf_op jit(solution)/shard_map/psum | solution.py:22
  514.6 6.0 copy-start.2
  514.6 5.3 collective-permute-start.3
  528.8 81.7 %collective-permute-start.4 = (bf16[7168,256]{0,1:T(8,128)(2,1)}, bf16[7168,256]{0,1:T(8,128)(2,1)}, u32[]{:S(2)}, u32[]{:S(2)}) collective-permute-start(bf16[7168,256]{0,1:T(8,128)(2,1)} %pad_maximum_fusion), channel_id=1, source_target_pairs={{0,8},{4,12},{8,0},{12,4},{16,24},{20,28},{24,16},{28,20},{1,9},{5... | collective-permute-start | bytes 11010056 | tf_op jit(solution)/shard_map/ppermute | solution.py:17
  680.8 4.9 copy-start.7
  692.2 15.2 %copy-start.8 = (f32[6144,256]{0,1:T(8,128)}, f32[6144,256]{0,1:T(8,128)S(1)}, u32[]{:S(2)}) copy-start(f32[6144,256]{0,1:T(8,128)S(1)} %fusion.38) | copy-start | bytes 18874372
  707.4 3.7 copy-start.16
  783.2 19.8 %collective-permute-start.5 = (bf16[1536,256]{0,1:T(8,128)(2,1)}, bf16[1536,256]{0,1:T(8,128)(2,1)S(1)}, u32[]{:S(2)}, u32[]{:S(2)}) collective-permute-start(bf16[1536,256]{0,1:T(8,128)(2,1)} %convert_element_type.61), channel_id=1, source_target_pairs={{0,4},{4,0},{8,12},{12,8},{16,20},{20,16},{24,28},{28,24},{1,5},{5... | collective-permute-start | bytes 2359304 | tf_op jit(solution)/shard_map/ppermute | solution.py:17
  799.7 3.5 copy-start.13
  803.7 4.2 copy-start.11
  803.8 36.9 %collective-permute-start.6 = (bf16[3072,256]{0,1:T(8,128)(2,1)S(1)}, bf16[3072,256]{0,1:T(8,128)(2,1)S(1)}, u32[]{:S(2)}, u32[]{:S(2)}) collective-permute-start(bf16[3072,256]{0,1:T(8,128)(2,1)S(1)} %get-tuple-element.144), channel_id=1, source_target_pairs={{0,8},{4,12},{8,0},{12,4},{16,24},{20,28},{24,16},{28,20},{1,9},{5... | collective-permute-start | bytes 4718600 | tf_op jit(solution)/shard_map/ppermute | solution.py:17
  807.9 18.2 %copy-start.10 = (f32[128,2048]{1,0:T(8,128)}, f32[128,2048]{1,0:T(8,128)S(1)}, u32[]{:S(2)}) copy-start(f32[128,2048]{1,0:T(8,128)S(1)} %fusion.49) | copy-start | bytes 3145732
  906.7 7.2 copy-start.5
  909.1 7.6 copy-start.15
  919.8 6.7 slice-start
  922.7 3.8 slice-start.1
  922.7 3.8 slice-start.2
  948.9 19.9 %copy-start.1 = (bf16[512,1536]{1,0:T(8,128)(2,1)S(1)}, bf16[512,1536]{1,0:T(8,128)(2,1)}, u32[]{:S(2)}) copy-start(bf16[512,1536]{1,0:T(8,128)(2,1)} %param.19) | copy-start | bytes 4718596
  (7 other events, 15.8 us)
Sparse Core Ops, SparseCore 0:
  141.5 274.9 all-reduce.6
  443.3 67.9 all-reduce.8
  712.6 68.1 all-reduce.10
where the time goes:
time: 985 us; the launch traced here: 976 us
  waiting for transfers between devices  563 us (57%)
  other arithmetic  176 us (18%)
  matrix products  122 us (12%)
  local copies, waits for them, and re-layouts  79.2 us (8%)
  between operations  20.8 us (2%)
  blocking collectives  10.5 us (1%)
    psum x3, waiting for transfers between devices, broadcast(): return lax.psum(jnp.where(mine, array, jnp.zeros_like(array)), axis)  350 us
    ppermute x7, waiting for transfers between devices, swapped(): return lax.ppermute(value, axis, pairs)  212 us
    another operation x14, other arithmetic, local(): diag_factor = jnp.linalg.cholesky(stacked[begin_col:end_col])  69.3 us
    dot_general x5, matrix products, highest(): return jnp.dot(left_side, right_side, precision=lax.Precision.HIGHEST)  65.3 us
    unnamed x45, local copies, waits for them, and re-layouts  41.9 us
    another operation x5, other arithmetic, lower_solve(): return jax.scipy.linalg.solve_triangular(factor, values, lower=True)  39.8 us
    another operation x12, matrix products, lower_solve(): return jax.scipy.linalg.solve_triangular(factor, values, lower=True)  29.7 us
    dot_general x1, matrix products, local(): lax.dot_general(features, collected, (((0,), (0,)), ((), ())), preferred_...  24 us
  transfers between devices with their start and end apart: 10, of which 9 were waited for; matrix products, arithmetic and copies ran while one was open for 9% of the time, Pallas kernels for 0%

commit v1 on v0

v1 whole, which is shorter than its diff:
```python
import jax
import jax.numpy as jnp
from jax import lax
from jax.experimental import pallas as pl
from jax.experimental.pallas import tpu as pltpu
from jax.sharding import PartitionSpec as P

CAP = 320
LEAD = 512
TILE = 128
GROUP = 8
DECAY = 0.8

HIGHEST = lax.Precision.HIGHEST
BF16 = jnp.bfloat16
F32 = jnp.float32


def dot_t(left, right, precision=None):
    return lax.dot_general(
        left, right, (((0,), (0,)), ((), ())), precision=precision, preferred_element_type=F32
    )


def splat(rows, lane):
    return jnp.broadcast_to(rows[:, lane : lane + 1], rows.shape)


def eliminate_tile(rows):
    lanes = lax.broadcasted_iota(jnp.int32, (GROUP, TILE), 1)
    subs = lax.broadcasted_iota(jnp.int32, (GROUP, TILE), 0)
    upper, inverse = [], []
    for step in range(TILE // GROUP):
        base = step * GROUP
        inside = (lanes >= base) & (lanes < base + GROUP)
        block = rows[step]
        first = [jnp.broadcast_to(block[t : t + 1, :], (GROUP, TILE)) for t in range(GROUP)]
        second = [
            jnp.where(inside, jnp.where(lanes == base + t, 1.0, 0.0), first[t])
            for t in range(GROUP)
        ]
        pivot = [
            [splat(first[t], base + u) if u >= t else None for u in range(GROUP)]
            for t in range(GROUP)
        ]
        scale = [None] * GROUP
        for t in range(GROUP):
            scale[t] = lax.rsqrt(pivot[t][t])
            for u in range(t + 1, GROUP):
                pivot[t][u] = pivot[t][u] * scale[t]
            for u in range(t + 1, GROUP):
                for w in range(u, GROUP):
                    pivot[u][w] = pivot[u][w] - pivot[t][u] * pivot[t][w]
            first[t] = first[t] * scale[t]
            second[t] = second[t] * scale[t]
            for u in range(t + 1, GROUP):
                first[u] = first[u] - pivot[t][u] * first[t]
                second[u] = second[u] - pivot[t][u] * second[t]
        solved = [None] * GROUP
        for t in reversed(range(GROUP)):
            value = second[t]
            for u in range(t + 1, GROUP):
                value = value - pivot[t][u] * solved[u]
            solved[t] = value * scale[t]
        for later in range(step + 1, TILE // GROUP):
            value = jnp.where(inside, 0.0, rows[later])
            for t in range(GROUP):
                value = value - splat(rows[later], base + t) * solved[t]
            rows[later] = value
        upper_rows, inverse_rows = first[0], second[0]
        for t in range(1, GROUP):
            upper_rows = jnp.where(subs == t, first[t], upper_rows)
            inverse_rows = jnp.where(subs == t, second[t], inverse_rows)
        upper.append(upper_rows)
        inverse.append(inverse_rows)
    return upper, inverse


def factor_kernel(matrix_ref, upper_ref, inverse_ref, work_ref):
    steps = LEAD // TILE
    work_ref[...] = matrix_ref[...]
    upper_ref[...] = jnp.zeros_like(upper_ref)
    inverse_ref[...] = jnp.zeros_like(inverse_ref)
    lanes = lax.broadcasted_iota(jnp.int32, (GROUP, TILE), 1)
    subs = lax.broadcasted_iota(jnp.int32, (GROUP, TILE), 0)

    def tile_step(k, carry):
        begin = pl.multiple_of(k * TILE, TILE)
        rows = [
            work_ref[pl.ds(begin + g * GROUP, GROUP), pl.ds(begin, TILE)]
            for g in range(TILE // GROUP)
        ]
        upper, inverse = eliminate_tile(rows)
        upper_tile = jnp.concatenate(
            [jnp.where(lanes >= subs + g * GROUP, part, 0.0) for g, part in enumerate(upper)], 0
        )
        inverse_tile = jnp.concatenate(
            [jnp.where(lanes <= subs + g * GROUP, part, 0.0) for g, part in enumerate(inverse)], 0
        )
        band = jnp.dot(
            inverse_tile,
            work_ref[pl.ds(begin, TILE), :],
            precision=HIGHEST,
            preferred_element_type=F32,
        )
        work_ref[pl.ds(begin, TILE), :] = band
        work_ref[pl.ds(begin, TILE), pl.ds(begin, TILE)] = inverse_tile
        upper_ref[pl.ds(begin, TILE), pl.ds(begin, TILE)] = upper_tile
        inverse_ref[pl.ds(begin, TILE), pl.ds(begin, TILE)] = inverse_tile
        for other in range(steps):

            @pl.when(other < k)
            def _():
                inverse_ref[pl.ds(begin, TILE), other * TILE : (other + 1) * TILE] = work_ref[
                    pl.ds(begin, TILE), other * TILE : (other + 1) * TILE
                ]

            @pl.when(other > k)
            def _():
                span = slice(other * TILE, (other + 1) * TILE)
                part = work_ref[pl.ds(begin, TILE), span]
                upper_ref[pl.ds(begin, TILE), span] = part
                work_ref[span, pl.ds(begin, TILE)] = jnp.zeros((TILE, TILE), F32)
                work_ref[span, :] = work_ref[span, :] - dot_t(
                    part, work_ref[pl.ds(begin, TILE), :], HIGHEST
                )

        return carry

    lax.fori_loop(0, steps, tile_step, 0)


def factor_lead(matrix):
    shape = jax.ShapeDtypeStruct((LEAD, LEAD), F32)
    return pl.pallas_call(
        factor_kernel,
        out_shape=(shape, shape),
        in_specs=[pl.BlockSpec(memory_space=pltpu.VMEM)],
        out_specs=(pl.BlockSpec(memory_space=pltpu.VMEM), pl.BlockSpec(memory_space=pltpu.VMEM)),
        scratch_shapes=[pltpu.VMEM((LEAD, LEAD), F32)],
        compiler_params=pltpu.CompilerParams(vmem_limit_bytes=32 * 1024 * 1024),
        cost_estimate=pl.CostEstimate(
            flops=20_000_000_000, bytes_accessed=3 * LEAD * LEAD * 4, transcendentals=LEAD
        ),
    )(matrix)


def swapped(value, mask):
    size = lax.axis_size("tok")
    return lax.ppermute(value, "tok", [(source, source ^ mask) for source in range(size)])


def gather_members(value, bits):
    for bit in reversed(range(bits)):
        value = jnp.concatenate([value, swapped(value, 1 << bit)], 0)
    return value


def exchange_members(blocks, member, bits):
    for bit in reversed(range(bits)):
        half = blocks.shape[0] // 2
        mine = member >> bit & 1
        keep = lax.dynamic_slice_in_dim(blocks, mine * half, half, 0)
        send = lax.dynamic_slice_in_dim(blocks, (1 - mine) * half, half, 0)
        blocks = jnp.concatenate([keep, swapped(send, 1 << bit)], 1)
    return blocks[0]


def from_first_member(value, member, group, bits):
    value = jnp.where(member == 0, value, jnp.zeros_like(value))
    for bit in reversed(range(bits)):
        mask = 1 << bit
        pairs = [
            (source, source + mask)
            for source in range(lax.axis_size("tok"))
            if source % group % (2 * mask) == 0
        ]
        value = value + lax.ppermute(value, "tok", pairs)
    return value


def lines(hops, group):
    toks, facs = lax.axis_size("tok"), lax.axis_size("fac")
    pairs = []
    for tok in range(toks):
        root = tok % group
        for before, after in hops:
            if 0 <= root + before < facs and 0 <= root + after < facs:
                pairs.append((tok * facs + root + before, tok * facs + root + after))
    return pairs


def from_own_column(value, member, column, group):
    axes = ("tok", "fac")
    facs = lax.axis_size("fac")
    upward = lax.ppermute(value, axes, lines([(0, 1)], group))
    downward = lax.ppermute(value, axes, lines([(0, -1)], group))
    moving = upward + downward
    total = jnp.where(member == column, value, moving)
    for distance in range(1, facs - 1):
        pairs = lines([(distance, distance + 1), (-distance, -distance - 1)], group)
        moving = lax.ppermute(moving, axes, pairs)
        total = total + moving
    return total


def local(grad_rows, routes, counts, factor_old, damping, weight_grad):
    group = lax.axis_size("tok") // 2
    facs = lax.axis_size("fac")
    bits = group.bit_length() - 1
    position = lax.axis_index("tok")
    expert = position // group
    member = position % group
    column = lax.axis_index("fac")
    tok_rows, width = grad_rows.shape
    grad_cols = weight_grad.shape[1]
    damp = jnp.where(expert == 0, damping[0], damping[1])

    near = from_first_member(
        jnp.concatenate([factor_old[:LEAD].astype(BF16), weight_grad[:LEAD]], 1),
        member,
        group,
        bits,
    )
    near_factor, near_grad = near[:, :width], near[:, width:]
    corner = jnp.where(column == 0, factor_old[:LEAD, :LEAD], 0.0)
    moving = corner
    for place in range(facs - 1):
        moving = lax.ppermute(moving, "fac", [(place, place + 1)])
        corner = corner + moving
    corner = from_first_member(corner, member, group, bits)

    live = jnp.arange(tok_rows) < counts[0]
    named = routes[:, 0]
    own = live & (named == expert)
    away = live & (named != expert)
    flags = jnp.stack([own, away])
    ranks = jnp.cumsum(flags.astype(jnp.int32), 1) - 1
    picker = (ranks[:, None, :] == jnp.arange(CAP)[None, :, None]) & flags[:, None, :]
    packed = jnp.dot(
        picker.reshape(2 * CAP, tok_rows).astype(BF16), grad_rows, preferred_element_type=F32
    ).astype(BF16)
    tally = jnp.sum(flags.astype(F32), 1)
    tally = jnp.broadcast_to(tally[:, None], (2, 128))
    other = swapped(tally, group)
    total = tally[0] + other[1]
    for bit in range(bits):
        total = total + swapped(total, 1 << bit)
    share = (1.0 - DECAY) / total[0]

    chunks = [(begin, min(begin + LEAD, width)) for begin in range(0, width, LEAD)]
    quarters = []
    for begin, end in chunks:
        incoming = swapped(packed[CAP:, begin:end], group)
        quarters.append(jnp.concatenate([packed[:CAP, begin:end], incoming], 0))
    spread = [lax.all_gather(quarter, "fac") for quarter in quarters]
    lead = gather_members(spread[0][0][:, :LEAD], bits)
    across = gather_members(jnp.concatenate(quarters, 1), bits)
    down = [exchange_members(part, member, bits) for part in spread]

    eye = jnp.eye(LEAD, dtype=F32)
    top = DECAY * corner + share * dot_t(lead, lead) + damp * eye
    upper, inverse = factor_lead(top)
    lower = upper.T
    beside = DECAY * near_factor.astype(F32) + share * dot_t(lead, across)
    panel_cols = jnp.dot(inverse, beside, precision=lax.Precision.HIGH).astype(BF16)
    panel_rows = from_own_column(panel_cols, member, column, group)
    solution_rows = jnp.dot(inverse, near_grad.astype(F32), precision=lax.Precision.HIGH)

    gram = jnp.concatenate([dot_t(part, across) for part in down], 0)
    running = DECAY * factor_old + share * gram

    row_index = jnp.arange(width)[:, None]
    col_index = jnp.arange(width)[None, :]
    diagonal = member * width + row_index == column * width + col_index
    matrix = running + jnp.where(diagonal, damp, 0.0)
    head = (member == 0) & (row_index < LEAD)
    updated = jnp.where(head, 0.0, matrix - dot_t(panel_rows, panel_cols))
    first = lax.dot_general(
        matrix[:, :LEAD],
        inverse,
        (((1,), (1,)), ((), ())),
        precision=lax.Precision.HIGH,
        preferred_element_type=F32,
    )
    first = jnp.where(head, jnp.pad(lower, ((0, width - LEAD), (0, 0))), first)
    factored = lax.dynamic_update_slice(
        updated, jnp.where(column == 0, first, updated[:, :LEAD]), (0, 0)
    )

    minus = jnp.pad(-jnp.eye(LEAD, dtype=BF16), ((0, 0), (0, width - LEAD)))
    weights = jnp.where(head.T, minus, panel_rows)
    high = solution_rows.astype(BF16)
    low = (solution_rows - high.astype(F32)).astype(BF16)
    product = dot_t(jnp.concatenate([weights, weights], 0), jnp.concatenate([high, low], 0))
    precond = jnp.where(head, 0.0, weight_grad.astype(F32)) - product
    return (running, factored, precond)


def solution(mesh):
    placed = (P("tok", "fac"), P("tok", None), P("tok"), P("tok", "fac"), P(), P("tok", "fac"))
    return jax.shard_map(
        local,
        mesh=mesh,
        in_specs=placed,
        out_specs=(P("tok", "fac"), P("tok", "fac"), P("tok", "fac")),
        check_vma=False,
    )
```

time: 985 us -> 478 us (0.49)
  waiting for transfers between devices: 563 us -> 196 us
  other arithmetic: 176 us -> 75 us
  matrix products: 122 us -> 72.1 us
  starting transfers between devices: 3.68 us -> 37.7 us
  local copies, waits for them, and re-layouts: 79.2 us -> 45.3 us
  Pallas kernels: 0 us -> 26.6 us
  blocking collectives: 10.5 us -> 0 us
    psum x3 -> x0, waiting for transfers between devices: 350 us -> none  [broadcast(): return lax.psum(jnp.where(mine, array, jnp.zeros_like(array)), axis)]
    another operation x31 -> x2, other arithmetic: 122 us -> 0.81 us  [the longest x14 69.3 us: local(): diag_factor = jnp.linalg.cholesky(stacked[begin_col:end_col])]
    ppermute x7 -> x27, waiting for transfers between devices: 212 us -> 126 us  [the longest x16 61.8 us: swapped(): lax.ppermute(value, 'tok', [(source, source ^ mask) for source in range(s...]
    all_gather x0 -> x3, waiting for transfers between devices: none -> 69.7 us  [local(): spread = [lax.all_gather(quarter, 'fac') for quarter in quarters]]
    concatenate x3 -> x10, other arithmetic: 5.25 us -> 42 us  [the longest x3 18.4 us: gather_members(): value = jnp.concatenate([value, swapped(value, 1 << bit)], 0)]
    ppermute x7 -> x27, starting transfers between devices: 3.09 us -> 37.6 us  [the longest x16 18.1 us: swapped(): lax.ppermute(value, 'tok', [(source, source ^ mask) for source in range(s...]
    another operation x16 -> x0, matrix products: 30.6 us -> none  [the longest x12 29.7 us: lower_solve(): return jax.scipy.linalg.solve_triangular(factor, values, lower=True)]
    pallas_call x0 -> x1, Pallas kernels: none -> 26.6 us  [factor_lead(): pl.pallas_call(factor_kernel, out_shape=(shape, shape), in_specs=[pl.Bloc...]
  transfers between devices with their start and end apart: 10 -> 30, of which waited for: 9 -> 10; matrix products, arithmetic and copies ran while one was open for 9% -> 31% of each run, Pallas kernels for 0% -> 6%
where the time goes in v1:
time: 478 us; the launch traced here: 469 us
  waiting for transfers between devices  196 us (41%)
  other arithmetic  75 us (16%)
  matrix products  72.1 us (15%)
  local copies, waits for them, and re-layouts  45.3 us (9%)
  starting transfers between devices  37.7 us (8%)
  Pallas kernels  26.6 us (6%)
  between operations  16.8 us (4%)
    all_gather x3, waiting for transfers between devices, local(): spread = [lax.all_gather(quarter, 'fac') for quarter in quarters]  69.7 us
    ppermute x16, waiting for transfers between devices, swapped(): lax.ppermute(value, 'tok', [(source, source ^ mask) for source in range(s...  61.8 us
    dot_general x7, matrix products, dot_t(): lax.dot_general(left, right, (((0,), (0,)), ((), ())), precision=precisio...  53.2 us
    ppermute x3, waiting for transfers between devices, local(): moving = lax.ppermute(moving, 'fac', [(place, place + 1)])  44.9 us
    unnamed x64, local copies, waits for them, and re-layouts  30.1 us
    pallas_call x1, Pallas kernels, factor_lead(): pl.pallas_call(factor_kernel, out_shape=(shape, shape), in_specs=[pl.Bloc...  26.6 us
    ppermute x2, waiting for transfers between devices, from_own_column(): moving = lax.ppermute(moving, axes, pairs)  19.1 us
    concatenate x3, other arithmetic, gather_members(): value = jnp.concatenate([value, swapped(value, 1 << bit)], 0)  18.4 us
  transfers between devices with their start and end apart: 30, of which 10 were waited for; matrix products, arithmetic and copies ran while one was open for 31% of the time, Pallas kernels for 6%

profile of v1, /device:TPU:2, one launch (start us, length us, event | category | flops | bytes accessed | tf_op | source)
XLA Modules:
  0.0 469.1 jit_solution(4349089939502503299)
XLA Ops:
  14.7 7.9 %collective-permute-done.7 = bf16[320,512]{1,0:T(8,128)(2,1)S(1)} collective-permute-done((bf16[320,512]{1,0:T(8,128)(2,1)S(1)}, bf16[320,512]{1,0:T(8,128)(2,1)S(1)}, u32[]{:S(2)}, u32[]{:S(2)}) %collective-permute-start.7) | collective-permute-done | bytes 327712 | tf_op jit(solution)/shard_map/ppermute | solution.py:150
  25.2 7.1 %collective-permute-done.3 = bf16[320,512]{1,0:T(8,128)(2,1)S(1)} collective-permute-done((bf16[320,512]{1,0:T(8,128)(2,1)S(1)}, bf16[320,512]{1,0:T(8,128)(2,1)S(1)}, u32[]{:S(2)}, u32[]{:S(2)}) %collective-permute-start.3) | collective-permute-done | bytes 327712 | tf_op jit(solution)/shard_map/ppermute | solution.py:150
  38.2 44.9 %collective-permute-done.14 = f32[512,512]{1,0:T(8,128)S(1)} collective-permute-done((f32[512,512]{1,0:T(8,128)S(1)}, f32[512,512]{1,0:T(8,128)S(1)}, u32[]{:S(2)}, u32[]{:S(2)}) %collective-permute-start.14) | collective-permute-done | bytes 1048608 | tf_op jit(solution)/shard_map/ppermute | solution.py:229
  86.3 5.8 %collective-permute-done.6 = bf16[320,512]{1,0:T(8,128)(2,1)S(1)} collective-permute-done((bf16[320,512]{1,0:T(8,128)(2,1)}, bf16[320,512]{1,0:T(8,128)(2,1)S(1)}, u32[]{:S(2)}, u32[]{:S(2)}) %collective-permute-start.6) | collective-permute-done | bytes 327712 | tf_op jit(solution)/shard_map/ppermute | solution.py:150
  96.3 12.3 %maximum_maximum_fusion = bf16[640,1536]{1,0:T(8,128)(2,1)} fusion(bf16[320,512]{1,0:T(8,128)(2,1)S(1)} %collective-permute-done.7, bf16[320,512]{1,0:T(8,128)(2,1)S(1)} %get-tuple-element.40, bf16[320,512]{1,0:T(8,128)(2,1)S(1)} %collective-permute-done.6, bf16[320,512]{1,0:T(8,128)(2,1)S(1)} %get-tuple-element.42, ...), kind=kLoop, calls=%fused_computation.54 | loop fusion | flops 11796480 | bytes 3932160 | tf_op jit(solution)/shard_map/concatenate | solution.py:258
  135.3 19.9 %all-gather.7.cloned.1.call-done = bf16[2560,512]{1,0:T(8,128)(2,1)} async-done(((bf16[640,512]{1,0:T(8,128)(2,1)}), bf16[2560,512]{1,0:T(8,128)(2,1)}) %all-gather.7.cloned.1.call-update) | async-done | bytes 2621456 | tf_op jit(solution)/shard_map/all_gather | solution.py:256
  157.8 8.0 %pad_maximum_fusion.1 = bf16[1280,1536]{1,0:T(8,128)(2,1)} fusion(bf16[640,1536]{1,0:T(8,128)(2,1)} %collective-permute-done.8, bf16[320,512]{1,0:T(8,128)(2,1)S(1)} %collective-permute-done.7, bf16[320,512]{1,0:T(8,128)(2,1)S(1)} %get-tuple-element.40, bf16[320,512]{1,0:T(8,128)(2,1)S(1)} %collective-permute-done.6, ...), kind=kLoop, calls=%fused_computation.10 | loop fusion | flops 27525120 | bytes 7864320 | tf_op jit(solution)/shard_map/concatenate | solution.py:155
  165.8 49.7 %all-gather.9.cloned.1.call-done = bf16[2560,512]{1,0:T(8,128)(2,1)} async-done(((bf16[640,512]{1,0:T(8,128)(2,1)}), bf16[2560,512]{1,0:T(8,128)(2,1)}) %all-gather.9.cloned.1.call-update) | async-done | bytes 2621456 | tf_op jit(solution)/shard_map/all_gather | solution.py:256
  218.9 37.9 %collective-permute-done.19 = bf16[640,512]{1,0:T(8,128)(2,1)} collective-permute-done((bf16[640,512]{1,0:T(8,128)(2,1)}, bf16[640,512]{1,0:T(8,128)(2,1)}, u32[]{:S(2)}, u32[]{:S(2)}) %collective-permute-start.19) | collective-permute-done | bytes 655392 | tf_op jit(solution)/shard_map/ppermute | solution.py:150
  259.8 9.6 %copy.25 = f32[1536,1536]{0,1:T(8,128)} copy(f32[1536,1536]{1,0:T(8,128)} %param.9) | data formatting | bytes 18874368 | tf_op args[3]
  295.7 26.6 %shard_map.85 = (f32[512,512]{1,0:T(8,128)S(1)}, f32[512,512]{1,0:T(8,128)S(1)}) custom-call(f32[512,512]{1,0:T(8,128)S(1)} %select_add_fusion.1.matrix_ref), custom_call_target="tpu_custom_call" | custom-call | flops 20000000000 | bytes 3145728 | tf_op jit(solution)/shard_map/pallas_call | solution.py:135
  322.3 8.0 %pad_maximum_fusion = bf16[2560,1536]{1,0:T(8,128)(2,1)S(1)} fusion(bf16[1280,1536]{1,0:T(8,128)(2,1)} %collective-permute-done.9, bf16[640,1536]{1,0:T(8,128)(2,1)} %collective-permute-done.8, bf16[320,512]{1,0:T(8,128)(2,1)S(1)} %copy-done.10, bf16[320,512]{1,0:T(8,128)(2,1)S(1)} %get-tuple-element.40, bf16[320,512]{1,0:T(8,128)(2,1)S(1)} %copy-done.14, ...), kind=kLoop, calls=%fused_computation.5 | loop fusion | flops 62914560 | bytes 15728640 | tf_op jit(solution)/shard_map/concatenate | solution.py:155
  330.3 7.8 %fusion.40 = f32[512,1536]{1,0:T(8,128)} fusion(bf16[2560,1536]{1,0:T(8,128)(2,1)S(1)} %pad_maximum_fusion, bf16[1280,512]{1,0:T(8,128)(2,1)} %collective-permute-done.20, bf16[640,512]{1,0:T(8,128)(2,1)} %collective-permute-done.19, bf16[640,512]{1,0:T(8,128)(2,1)} %slice.95), kind=kOutput, calls=%fused_computation.69 | convolution fusion | flops 4034396160 | bytes 13631488 | tf_op jit(solution)/shard_map/dot_general | solution.py:20
  339.0 6.0 %fusion.14 = bf16[512,1536]{1,0:T(8,128)(2,1)S(1)} fusion(f32[512,512]{1,0:T(8,128)S(1)} %get-tuple-element.5, f32[512,1536]{1,0:T(8,128)} %fusion.40, bf16[512,3584]{1,0:T(8,128)(2,1)S(1)} %add.146, f32[]{:T(128)} %bitcast.5), kind=kOutput, calls=%fused_computation.26 | convolution fusion | flops 2419851264 | bytes 7340036 | tf_op jit(solution)/shard_map/dot_general | solution.py:266
  349.4 7.4 %fusion.25 = f32[512,1536]{0,1:T(8,128)} fusion(bf16[2560,1536]{1,0:T(8,128)(2,1)S(1)} %pad_maximum_fusion, bf16[1,1280,512]{2,1,0:T(8,128)(2,1)} %collective-permute-done.13, bf16[1,1280,512]{2,1,0:T(8,128)(2,1)S(1)} %copy-done.19), kind=kOutput, calls=%fused_computation.48 | convolution fusion | flops 4031774720 | bytes 13631488 | tf_op jit(solution)/shard_map/dot_general | solution.py:20
  358.8 7.5 %fusion.22 = f32[512,1536]{0,1:T(8,128)} fusion(bf16[2560,1536]{1,0:T(8,128)(2,1)S(1)} %pad_maximum_fusion, bf16[1,1280,512]{2,1,0:T(8,128)(2,1)} %collective-permute-done.11, bf16[1,1280,512]{2,1,0:T(8,128)(2,1)S(1)} %copy-done.18), kind=kOutput, calls=%fused_computation.44 | convolution fusion | flops 4031774720 | bytes 13631488 | tf_op jit(solution)/shard_map/dot_general | solution.py:20
  367.4 7.7 %fusion.19 = f32[512,1536]{0,1:T(8,128)} fusion(bf16[2560,1536]{1,0:T(8,128)(2,1)S(1)} %pad_maximum_fusion, bf16[1,1280,512]{2,1,0:T(8,128)(2,1)} %copy-done.23, bf16[1,1280,512]{2,1,0:T(8,128)(2,1)S(1)} %copy-done.20), kind=kOutput, calls=%fused_computation.40 | convolution fusion | flops 4031774720 | bytes 13631488 | tf_op jit(solution)/shard_map/dot_general | solution.py:20
  375.0 19.1 %collective-permute-done.25 = bf16[512,1536]{1,0:T(8,128)(2,1)} collective-permute-done((bf16[512,1536]{1,0:T(8,128)(2,1)S(1)}, bf16[512,1536]{1,0:T(8,128)(2,1)}, u32[]{:S(2)}, u32[]{:S(2)}) %collective-permute-start.25) | collective-permute-done | bytes 1572896 | tf_op jit(solution)/shard_map/ppermute | solution.py:202
  396.3 11.2 %select_add_fusion = (f32[1536,1536]{0,1:T(8,128)}, f32[1536,1536]{0,1:T(8,128)}) fusion(f32[]{:T(128)S(6)} %select_n.101, s32[1536]{0:T(1024)S(1)} %iota_add_fusion.1, s32[1536]{0:T(1024)S(1)} %iota_add_fusion, f32[512,1536]{0,1:T(8,128)} %fusion.25, f32[512,1536]{0,1:T(8,128)} %fusion.22, f32[512,1536]{0,1:T(8,128)} %fusion.19, f32[]{:T(128)} %bitcast.5, ...), kind=kLoop, calls=%fused_computation.4 | loop fusion | flops 18874368 | bytes 37761032 | tf_op jit(solution)/shard_map/add | solution.py:276
  407.4 9.6 %copy.31 = f32[1536,1536]{1,0:T(8,128)} copy(f32[1536,1536]{0,1:T(8,128)} %get-tuple-element.23) | data formatting | bytes 18874368
  417.1 6.1 %subtract_convert_fusion = (bf16[512,2048]{1,0:T(8,128)(2,1)}, bf16[512,2048]{1,0:T(8,128)(2,1)}) fusion(f32[512,512]{1,0:T(8,128)S(1)} %get-tuple-element.5, bf16[512,3584]{1,0:T(8,128)(2,1)} %copy-done.4), kind=kOutput, calls=%fused_computation.9 | convolution fusion | flops 3225419776 | bytes 7340032 | tf_op jit(solution)/shard_map/dot_general | solution.py:268
  433.3 5.6 %fusion.4 = f32[1536,1536]{0,1:T(8,128)} fusion(f32[1536,1536]{0,1:T(8,128)} %subtract_select_fusion, f32[512,512]{1,0:T(8,128)S(1)} %get-tuple-element.5, f32[1536,1536]{0,1:T(8,128)S(1)} %bitcast.59, f32[512,512]{0,1:T(8,128)S(1)} %bitcast.57, pred[1536]{0:T(1024)(128)(4,1)S(1)} %fusion.44, pred[]{:T(512)S(6)} %eq.96), kind=kOutput, calls=%fused_computation.15 | convolution fusion | flops 2417491968 | bytes 11536385 | tf_op jit(solution)/shard_map/dot_general | solution.py:279
  438.9 9.7 %copy.32 = f32[1536,1536]{1,0:T(8,128)} copy(f32[1536,1536]{0,1:T(8,128)} %fusion.4) | data formatting | bytes 18874368
  448.6 13.5 %select_subtract_fusion = f32[1536,2048]{1,0:T(8,128)} fusion(bf16[1536,2048]{1,0:T(8,128)(2,1)} %param.11, pred[1536]{0:T(1024)(128)(4,1)S(1)} %fusion.44, bf16[512,2048]{1,0:T(8,128)(2,1)} %get-tuple-element.20, bf16[512,2048]{1,0:T(8,128)(2,1)} %get-tuple-element.21, bf16[512,1536]{1,0:T(8,128)(2,1)S(1)} %copy-done.17), kind=kOutput, calls=%fused_computation | convolution fusion | flops 6466568192 | bytes 24643072 | tf_op jit(solution)/shard_map/dot_general | solution.py:20
  (165 shorter events, 103.5 us)
Async XLA Ops:
  7.2 121.1 %all-gather.11.cloned.1.call-start = ((), (), s32[]{:S(2)}) async-start(), calls=%async_computation.2 | async-start | bytes 3276800 | tf_op jit(solution)/shard_map/all_gather | solution.py:256
  23.6 131.6 %all-gather.7.cloned.1.call-start = ((), (), s32[]{:S(2)}) async-start(), calls=%async_computation | async-start | bytes 3276800 | tf_op jit(solution)/shard_map/all_gather | solution.py:256
  33.2 182.3 %all-gather.9.cloned.1.call-start = ((), (), s32[]{:S(2)}) async-start(), calls=%async_computation.1 | async-start | bytes 3276800 | tf_op jit(solution)/shard_map/all_gather | solution.py:256
  34.6 48.5 %collective-permute-start.14 = (f32[512,512]{1,0:T(8,128)S(1)}, f32[512,512]{1,0:T(8,128)S(1)}, u32[]{:S(2)}, u32[]{:S(2)}) collective-permute-start(f32[512,512]{1,0:T(8,128)S(1)} %slice_select_fusion.1), channel_id=1, source_target_pairs={{0,1},{4,5},{8,9},{12,13},{16,17},{20,21},{24,25},{28,29}} | collective-permute-start | bytes 3145736 | tf_op jit(solution)/shard_map/ppermute | solution.py:229
  83.1 26.0 %collective-permute-start.15 = (f32[512,512]{1,0:T(8,128)S(1)}, f32[512,512]{1,0:T(8,128)}, u32[]{:S(2)}, u32[]{:S(2)}) collective-permute-start(f32[512,512]{1,0:T(8,128)S(1)} %collective-permute-done.14), channel_id=1, source_target_pairs={{1,2},{5,6},{9,10},{13,14},{17,18},{21,22},{25,26},{29,30}} | collective-permute-start | bytes 3145736 | tf_op jit(solution)/shard_map/ppermute | solution.py:229
  108.6 48.6 %collective-permute-start.8 = (bf16[640,1536]{1,0:T(8,128)(2,1)}, bf16[640,1536]{1,0:T(8,128)(2,1)}, u32[]{:S(2)}, u32[]{:S(2)}) collective-permute-start(bf16[640,1536]{1,0:T(8,128)(2,1)} %maximum_maximum_fusion), channel_id=1, source_target_pairs={{0,8},{4,12},{8,0},{12,4},{16,24},{20,28},{24,16},{28,20},{1,9},{5... | collective-permute-start | bytes 5898248 | tf_op jit(solution)/shard_map/ppermute | solution.py:150
  109.1 14.9 %collective-permute-start.16 = (f32[512,512]{1,0:T(8,128)}, f32[512,512]{1,0:T(8,128)}, u32[]{:S(2)}, u32[]{:S(2)}) collective-permute-start(f32[512,512]{1,0:T(8,128)} %collective-permute-done.15), channel_id=1, source_target_pairs={{2,3},{6,7},{10,11},{14,15},{18,19},{22,23},{26,27},{30,31}} | collective-permute-start | bytes 3145736 | tf_op jit(solution)/shard_map/ppermute | solution.py:229
  113.2 158.9 %collective-permute-start.21 = (bf16[512,3584]{1,0:T(8,128)(2,1)}, bf16[512,3584]{1,0:T(8,128)(2,1)}, u32[]{:S(2)}, u32[]{:S(2)}) collective-permute-start(bf16[512,3584]{1,0:T(8,128)(2,1)} %maximum_select_fusion), channel_id=1, source_target_pairs={{0,8},{16,24},{1,9},{17,25},{2,10},{18,26},{3,11},{19,27}} | collective-permute-start | bytes 11010056 | tf_op jit(solution)/shard_map/ppermute | solution.py:178
  119.4 99.5 %collective-permute-start.2 = (f32[128]{0:T(128)S(1)}, f32[128]{0:T(128)S(1)}, u32[]{:S(2)}, u32[]{:S(2)}) collective-permute-start(f32[128]{0:T(128)S(1)} %fusion.66), channel_id=1, source_target_pairs={{0,8},{4,12},{8,0},{12,4},{16,24},{20,28},{24,16},{28,20},{1,9},{5... | collective-permute-start | bytes 1544 | tf_op jit(solution)/shard_map/ppermute | solution.py:150
  126.7 132.5 %collective-permute-start.17 = (f32[512,512]{1,0:T(8,128)S(1)}, f32[512,512]{1,0:T(8,128)}, u32[]{:S(2)}, u32[]{:S(2)}) collective-permute-start(f32[512,512]{1,0:T(8,128)S(1)} %add_select_fusion), channel_id=1, source_target_pairs={{0,8},{16,24},{1,9},{17,25},{2,10},{18,26},{3,11},{19,27}} | collective-permute-start | bytes 3145736 | tf_op jit(solution)/shard_map/ppermute | solution.py:178
  131.7 149.3 %collective-permute-start.12 = (bf16[2,640,512]{2,1,0:T(8,128)(2,1)}, bf16[2,640,512]{2,1,0:T(8,128)(2,1)}, u32[]{:S(2)}, u32[]{:S(2)}) collective-permute-start(bf16[2,640,512]{2,1,0:T(8,128)(2,1)} %get-tuple-element.36), channel_id=1, source_target_pairs={{0,8},{4,12},{8,0},{12,4},{16,24},{20,28},{24,16},{28,20},{1,9},{5... | collective-permute-start | bytes 3932168 | tf_op jit(solution)/shard_map/ppermute | solution.py:150
  157.2 99.6 %collective-permute-start.19 = (bf16[640,512]{1,0:T(8,128)(2,1)}, bf16[640,512]{1,0:T(8,128)(2,1)}, u32[]{:S(2)}, u32[]{:S(2)}) collective-permute-start(bf16[640,512]{1,0:T(8,128)(2,1)} %slice.95), channel_id=1, source_target_pairs={{0,8},{4,12},{8,0},{12,4},{16,24},{20,28},{24,16},{28,20},{1,9},{5... | collective-permute-start | bytes 1966088 | tf_op jit(solution)/shard_map/ppermute | solution.py:150
  218.9 103.3 %collective-permute-start.9 = (bf16[1280,1536]{1,0:T(8,128)(2,1)}, bf16[1280,1536]{1,0:T(8,128)(2,1)}, u32[]{:S(2)}, u32[]{:S(2)}) collective-permute-start(bf16[1280,1536]{1,0:T(8,128)(2,1)} %pad_maximum_fusion.1), channel_id=1, source_target_pairs={{0,4},{4,0},{8,12},{12,8},{16,20},{20,16},{24,28},{28,24},{1,5},{5... | collective-permute-start | bytes 11796488 | tf_op jit(solution)/shard_map/ppermute | solution.py:150
  256.8 29.3 %collective-permute-start.10 = (bf16[2,640,512]{2,1,0:T(8,128)(2,1)}, bf16[2,640,512]{2,1,0:T(8,128)(2,1)}, u32[]{:S(2)}, u32[]{:S(2)}) collective-permute-start(bf16[2,640,512]{2,1,0:T(8,128)(2,1)} %get-tuple-element.32), channel_id=1, source_target_pairs={{0,8},{4,12},{8,0},{12,4},{16,24},{20,28},{24,16},{28,20},{1,9},{5... | collective-permute-start | bytes 3932168 | tf_op jit(solution)/shard_map/ppermute | solution.py:150
  259.2 31.9 %collective-permute-start.20 = (bf16[1280,512]{1,0:T(8,128)(2,1)}, bf16[1280,512]{1,0:T(8,128)(2,1)}, u32[]{:S(2)}, u32[]{:S(2)}) collective-permute-start(bf16[1280,512]{1,0:T(8,128)(2,1)} %pad_maximum_fusion.3), channel_id=1, source_target_pairs={{0,4},{4,0},{8,12},{12,8},{16,20},{20,16},{24,28},{28,24},{1,5},{5... | collective-permute-start | bytes 3932168 | tf_op jit(solution)/shard_map/ppermute | solution.py:150
  272.1 19.0 %collective-permute-start.18 = (f32[512,512]{1,0:T(8,128)S(1)}, f32[512,512]{1,0:T(8,128)S(1)}, u32[]{:S(2)}, u32[]{:S(2)}) collective-permute-start(f32[512,512]{1,0:T(8,128)S(1)} %add.141), channel_id=1, source_target_pairs={{0,4},{8,12},{16,20},{24,28},{1,5},{9,13},{17,21},{25,29},{2,6},{1... | collective-permute-start | bytes 3145736 | tf_op jit(solution)/shard_map/ppermute | solution.py:178
  281.0 57.1 %collective-permute-start.22 = (bf16[512,3584]{1,0:T(8,128)(2,1)S(1)}, bf16[512,3584]{1,0:T(8,128)(2,1)S(1)}, u32[]{:S(2)}, u32[]{:S(2)}) collective-permute-start(bf16[512,3584]{1,0:T(8,128)(2,1)S(1)} %add.145), channel_id=1, source_target_pairs={{0,4},{8,12},{16,20},{24,28},{1,5},{9,13},{17,21},{25,29},{2,6},{1... | collective-permute-start | bytes 11010056 | tf_op jit(solution)/shard_map/ppermute | solution.py:178
  286.1 60.8 %collective-permute-start.4 = (bf16[2,640,512]{2,1,0:T(8,128)(2,1)}, bf16[2,640,512]{2,1,0:T(8,128)(2,1)}, u32[]{:S(2)}, u32[]{:S(2)}) collective-permute-start(bf16[2,640,512]{2,1,0:T(8,128)(2,1)} %get-tuple-element.28), channel_id=1, source_target_pairs={{0,8},{4,12},{8,0},{12,4},{16,24},{20,28},{24,16},{28,20},{1,9},{5... | collective-permute-start | bytes 3932168 | tf_op jit(solution)/shard_map/ppermute | solution.py:150
  291.1 58.4 %collective-permute-start.13 = (bf16[1,1280,512]{2,1,0:T(8,128)(2,1)}, bf16[1,1280,512]{2,1,0:T(8,128)(2,1)}, u32[]{:S(2)}, u32[]{:S(2)}) collective-permute-start(bf16[1,1280,512]{2,1,0:T(8,128)(2,1)} %get-tuple-element.35), channel_id=1, source_target_pairs={{0,4},{4,0},{8,12},{12,8},{16,20},{20,16},{24,28},{28,24},{1,5},{5... | collective-permute-start | bytes 3932168 | tf_op jit(solution)/shard_map/ppermute | solution.py:150
  291.1 67.7 %collective-permute-start.11 = (bf16[1,1280,512]{2,1,0:T(8,128)(2,1)}, bf16[1,1280,512]{2,1,0:T(8,128)(2,1)}, u32[]{:S(2)}, u32[]{:S(2)}) collective-permute-start(bf16[1,1280,512]{2,1,0:T(8,128)(2,1)} %get-tuple-element.31), channel_id=1, source_target_pairs={{0,4},{4,0},{8,12},{12,8},{16,20},{20,16},{24,28},{28,24},{1,5},{5... | collective-permute-start | bytes 3932168 | tf_op jit(solution)/shard_map/ppermute | solution.py:150
  345.0 11.8 %collective-permute-start.23 = (bf16[512,1536]{1,0:T(8,128)(2,1)S(1)}, bf16[512,1536]{1,0:T(8,128)(2,1)S(1)}, u32[]{:S(2)}, u32[]{:S(2)}) collective-permute-start(bf16[512,1536]{1,0:T(8,128)(2,1)S(1)} %fusion.14), channel_id=1, source_target_pairs={{0,1},{5,6},{10,11},{16,17},{21,22},{26,27}} | collective-permute-start | bytes 4718600 | tf_op jit(solution)/shard_map/ppermute | solution.py:196
  349.4 17.0 %collective-permute-start.5 = (bf16[1,1280,512]{2,1,0:T(8,128)(2,1)S(1)}, bf16[1,1280,512]{2,1,0:T(8,128)(2,1)S(1)}, u32[]{:S(2)}, u32[]{:S(2)}) collective-permute-start(bf16[1,1280,512]{2,1,0:T(8,128)(2,1)S(1)} %get-tuple-element.27), channel_id=1, source_target_pairs={{0,4},{4,0},{8,12},{12,8},{16,20},{20,16},{24,28},{28,24},{1,5},{5... | collective-permute-start | bytes 3932168 | tf_op jit(solution)/shard_map/ppermute | solution.py:150
  357.3 36.9 %collective-permute-start.25 = (bf16[512,1536]{1,0:T(8,128)(2,1)S(1)}, bf16[512,1536]{1,0:T(8,128)(2,1)}, u32[]{:S(2)}, u32[]{:S(2)}) collective-permute-start(bf16[512,1536]{1,0:T(8,128)(2,1)S(1)} %add.148), channel_id=1, source_target_pairs={{1,2},{6,7},{9,8},{14,13},{17,18},{22,23},{25,24},{30,29}} | collective-permute-start | bytes 4718600 | tf_op jit(solution)/shard_map/ppermute | solution.py:202
  394.2 29.0 %collective-permute-start.26 = (bf16[512,1536]{1,0:T(8,128)(2,1)}, bf16[512,1536]{1,0:T(8,128)(2,1)}, u32[]{:S(2)}, u32[]{:S(2)}) collective-permute-start(bf16[512,1536]{1,0:T(8,128)(2,1)} %collective-permute-done.25), channel_id=1, source_target_pairs={{2,3},{13,12},{18,19},{29,28}} | collective-permute-start | bytes 4718600 | tf_op jit(solution)/shard_map/ppermute | solution.py:202
  (37 other events, 751.2 us)
Sparse Core Ops, SparseCore 0:
  23.7 74.7 all-gather.10
  100.0 55.1 all-gather.6
  156.8 58.7 all-gather.8

commit v2 on v1

--- a/solution.py
+++ b/solution.py
@@ -9,6 +9,8 @@
 LEAD = 512
 TILE = 128
 GROUP = 8
+ROWS = 256
+COLS = 512
 DECAY = 0.8
 
 HIGHEST = lax.Precision.HIGHEST
@@ -76,9 +78,17 @@
     return upper, inverse
 
 
-def factor_kernel(matrix_ref, upper_ref, inverse_ref, work_ref):
+def factor_kernel(scalars_ref, corner_ref, *refs):
+    *lead_refs, upper_ref, inverse_ref, work_ref = refs
     steps = LEAD // TILE
-    work_ref[...] = matrix_ref[...]
+    gram = sum(dot_t(lead[...], lead[...]) for lead in lead_refs)
+    rows = lax.broadcasted_iota(jnp.int32, (LEAD, LEAD), 0)
+    cols = lax.broadcasted_iota(jnp.int32, (LEAD, LEAD), 1)
+    work_ref[...] = (
+        DECAY * corner_ref[...]
+        + scalars_ref[0] * gram
+        + jnp.where(rows == cols, scalars_ref[1], 0.0)
+    )
     upper_ref[...] = jnp.zeros_like(upper_ref)
     inverse_ref[...] = jnp.zeros_like(inverse_ref)
     lanes = lax.broadcasted_iota(jnp.int32, (GROUP, TILE), 1)
@@ -130,19 +140,218 @@
     lax.fori_loop(0, steps, tile_step, 0)
 
 
-def factor_lead(matrix):
+def factor_lead(scalars, corner, lead):
     shape = jax.ShapeDtypeStruct((LEAD, LEAD), F32)
+    vmem = pl.BlockSpec(memory_space=pltpu.VMEM)
     return pl.pallas_call(
         factor_kernel,
         out_shape=(shape, shape),
-        in_specs=[pl.BlockSpec(memory_space=pltpu.VMEM)],
-        out_specs=(pl.BlockSpec(memory_space=pltpu.VMEM), pl.BlockSpec(memory_space=pltpu.VMEM)),
+        in_specs=[pl.BlockSpec(memory_space=pltpu.SMEM)] + [vmem] * (1 + len(lead)),
+        out_specs=(vmem, vmem),
         scratch_shapes=[pltpu.VMEM((LEAD, LEAD), F32)],
         compiler_params=pltpu.CompilerParams(vmem_limit_bytes=32 * 1024 * 1024),
         cost_estimate=pl.CostEstimate(
-            flops=20_000_000_000, bytes_accessed=3 * LEAD * LEAD * 4, transcendentals=LEAD
+            flops=25_000_000_000, bytes_accessed=6 * LEAD * LEAD * 4, transcendentals=LEAD
         ),
-    )(matrix)
+    )(scalars, corner, *lead)
+
+
+def panel_kernel(scalars_ref, inverse_ref, factor_ref, *refs):
+    *pieces, out_ref = refs
+    half = len(pieces) // 2
+    gram = sum(dot_t(pieces[q][...], pieces[half + q][...]) for q in range(half))
+    beside = DECAY * factor_ref[...].astype(F32) + scalars_ref[0] * gram
+    out_ref[...] = jnp.dot(
+        inverse_ref[...], beside, precision=HIGHEST, preferred_element_type=F32
+    ).astype(BF16)
+
+
+def panel_columns(scalars, inverse, near_factor, lead, across):
+    width = near_factor.shape[1]
+    cols = COLS if width % COLS == 0 else ROWS
+    rows = lead[0].shape[0]
+    whole = lambda height: pl.BlockSpec((height, LEAD), lambda j: (0, 0))
+    tiled = lambda height: pl.BlockSpec((height, cols), lambda j: (0, j))
+    return pl.pallas_call(
+        panel_kernel,
+        grid=(width // cols,),
+        out_shape=jax.ShapeDtypeStruct((LEAD, width), BF16),
+        in_specs=[pl.BlockSpec(memory_space=pltpu.SMEM), whole(LEAD), tiled(LEAD)]
+        + [whole(rows)] * len(lead)
+        + [tiled(rows)] * len(across),
+        out_specs=tiled(LEAD),
+        compiler_params=pltpu.CompilerParams(vmem_limit_bytes=48 * 1024 * 1024),
+        cost_estimate=pl.CostEstimate(
+            flops=2 * width * LEAD * (rows * len(lead) + 6 * LEAD),
+            bytes_accessed=2 * rows * len(lead) * (width + LEAD) + 4 * LEAD * width,
+            transcendentals=0,
+        ),
+    )(scalars, inverse, near_factor, *lead, *across)
+
+
+def finish_kernel(
+    count,
+    gram_steps,
+    first_chunk,
+    aliased,
+    places_ref,
+    scalars_ref,
+    factor_ref,
+    first_ref,
+    grad_ref,
+    panel_ref,
+    inverse_ref,
+    lower_ref,
+    high_ref,
+    low_ref,
+    *refs,
+):
+    mine, lead, across = refs[:count], refs[count : 2 * count], refs[2 * count : 3 * count]
+    running_ref, factored_ref, precond_ref, mine_ref, rows_ref = refs[3 * count + aliased :]
+    j, i = pl.program_id(0), pl.program_id(1)
+    member, column, base = places_ref[0], places_ref[1], places_ref[2]
+    share, damp = scalars_ref[0], scalars_ref[1]
+    height = ROWS
+    depth = mine[0].shape[1]
+    cols = running_ref.shape[1]
+    span = pl.ds(pl.multiple_of(i * height, height), height)
+    head = (member == 0) & first_chunk
+
+    @pl.when(j == 0)
+    def _():
+        for q in range(count):
+            mine_ref[span, q * depth : (q + 1) * depth] = mine[q][0].T
+        source = first_ref[...].astype(F32)
+        if cols == LEAD:
+            source = jnp.where(column == 0, factor_ref[...], source)
+        stacked = jnp.concatenate([part[...] for part in lead], 0)
+        gram = jnp.dot(mine_ref[span, :], stacked, preferred_element_type=F32)
+        row = base + i * height + lax.broadcasted_iota(jnp.int32, (height, LEAD), 0)
+        col = lax.broadcasted_iota(jnp.int32, (height, LEAD), 1)
+        source = DECAY * source + share * gram
+        source = source + jnp.where(row == col, damp, 0.0)
+        rows_ref[span, :] = lax.dot_general(
+            source,
+            inverse_ref[...],
+            (((1,), (1,)), ((), ())),
+            precision=HIGHEST,
+            preferred_element_type=F32,
+        )
+
+    panel = rows_ref[span, :].astype(BF16)
+
+    @pl.when(j < gram_steps)
+    def _():
+        stacked = jnp.concatenate([part[...] for part in across], 0)
+        gram = jnp.dot(mine_ref[span, :], stacked, preferred_element_type=F32)
+        running = DECAY * factor_ref[...] + share * gram
+        running_ref[...] = running
+        row = base + i * height + lax.broadcasted_iota(jnp.int32, (height, cols), 0)
+        col = (column * gram_steps + j) * cols + lax.broadcasted_iota(jnp.int32, (height, cols), 1)
+        matrix = running + jnp.where(row == col, damp, 0.0)
+        factored = matrix - jnp.dot(panel, panel_ref[...], preferred_element_type=F32)
+        factored_ref[...] = jnp.where(head, 0.0, factored)
+
+        for part in range(LEAD // cols):
+            side = slice(part * cols, (part + 1) * cols)
+
+            @pl.when((column == 0) & (j == part))
+            def _():
+                factored_ref[...] = rows_ref[span, side]
+
+                @pl.when(head)
+                def _():
+                    factored_ref[...] = lower_ref[span, side]
+
+    high, low = high_ref[...], low_ref[...]
+    product = jnp.dot(panel, high, preferred_element_type=F32)
+    product = product + jnp.dot(panel, low, preferred_element_type=F32)
+    precond_ref[...] = grad_ref[...].astype(F32) - product
+
+    @pl.when(head)
+    def _():
+        precond_ref[...] = high_ref[span, :].astype(F32) + low_ref[span, :].astype(F32)
+
+
+def finish_rows(
+    begin, places, scalars, factor, first, grad, panel, inverse, lower, high, low,
+    mine, lead, across, earlier,
+):
+    count = len(mine)
+    depth, rows = mine[0].shape[1:]
+    width, grad_cols = factor.shape[0], grad.shape[1]
+    tiles = rows // ROWS
+    start = begin // ROWS
+    cols = COLS if width % COLS == 0 else ROWS
+    gram_steps = width // cols
+    grad_tile = cols
+    steps = max(gram_steps, grad_cols // grad_tile)
+    grad_steps = grad_cols // grad_tile
+    assert steps == grad_steps and rows % ROWS == 0
+
+    def once(j, i):
+        return jnp.where(j == 0, i, tiles - 1)
+
+    def mine_spec(q):
+        return pl.BlockSpec((1, depth, ROWS), lambda j, i, p: (p[3 + q], 0, once(j, i)))
+
+    def gram_col(j):
+        return jnp.minimum(j, gram_steps - 1)
+
+    def gram_tile(j, i, p):
+        return (start + jnp.where(j < gram_steps, i, tiles - 1), gram_col(j))
+
+    grad_spec = pl.BlockSpec((ROWS, grad_tile), lambda j, i, p: (start + i, j))
+    factor_spec = pl.BlockSpec((ROWS, cols), gram_tile)
+    lead_whole = pl.BlockSpec((LEAD, LEAD), lambda j, i, p: (0, 0))
+    in_specs = [
+        pl.BlockSpec(memory_space=pltpu.SMEM),
+        factor_spec,
+        pl.BlockSpec((ROWS, LEAD), lambda j, i, p: (start + once(j, i), 0)),
+        grad_spec,
+        pl.BlockSpec((LEAD, cols), lambda j, i, p: (0, gram_col(j))),
+        lead_whole,
+        lead_whole,
+        pl.BlockSpec((LEAD, grad_tile), lambda j, i, p: (0, j)),
+        pl.BlockSpec((LEAD, grad_tile), lambda j, i, p: (0, j)),
+    ]
+    in_specs += [mine_spec(q) for q in range(count)]
+    in_specs += [pl.BlockSpec((depth, LEAD), lambda j, i, p: (0, 0))] * count
+    in_specs += [pl.BlockSpec((depth, cols), lambda j, i, p: (0, gram_col(j)))] * count
+    in_specs += [pl.BlockSpec(memory_space=pl.ANY)] * len(earlier)
+    operands = [scalars, factor, first, grad, panel, inverse, lower, high, low]
+    operands += [*mine, *lead, *across, *earlier]
+    aliases = {1 + len(operands) - len(earlier) + k: k for k in range(len(earlier))}
+    tall = depth * count
+    return pl.pallas_call(
+        lambda *refs: finish_kernel(count, gram_steps, begin == 0, len(earlier), *refs),
+        grid_spec=pltpu.PrefetchScalarGridSpec(
+            num_scalar_prefetch=1,
+            grid=(steps, tiles),
+            in_specs=in_specs,
+            out_specs=(factor_spec, factor_spec, grad_spec),
+            scratch_shapes=[pltpu.VMEM((rows, tall), BF16), pltpu.VMEM((rows, LEAD), F32)],
+        ),
+        out_shape=(
+            jax.ShapeDtypeStruct(factor.shape, F32),
+            jax.ShapeDtypeStruct(factor.shape, F32),
+            jax.ShapeDtypeStruct(grad.shape, F32),
+        ),
+        input_output_aliases=aliases,
+        compiler_params=pltpu.CompilerParams(vmem_limit_bytes=56 * 1024 * 1024),
+        cost_estimate=pl.CostEstimate(
+            flops=2 * rows * (tall * (width + LEAD) + LEAD * (6 * LEAD + width + 2 * grad_cols)),
+            bytes_accessed=2 * tall * (width + LEAD + rows)
+            + rows * (12 * width + 6 * grad_cols)
+            + LEAD * (4 * grad_cols + 8 * LEAD + 2 * width),
+            transcendentals=0,
+        ),
+    )(places, *operands)
+
+
+def after(value, earlier):
+    mark = earlier[(0,) * earlier.ndim]
+    return jnp.where(mark == mark, value, jnp.zeros_like(value))
 
 
 def swapped(value, mask):
@@ -151,19 +360,25 @@
 
 
 def gather_members(value, bits):
+    pieces = [value]
     for bit in reversed(range(bits)):
-        value = jnp.concatenate([value, swapped(value, 1 << bit)], 0)
-    return value
-
-
-def exchange_members(blocks, member, bits):
+        pieces = pieces + [swapped(piece, 1 << bit) for piece in pieces]
+    return pieces
+
+
+def exchange_members(blocks, member, bits, earlier):
+    views = [(blocks, 0)]
+    count = blocks.shape[0]
     for bit in reversed(range(bits)):
-        half = blocks.shape[0] // 2
+        count = count // 2
         mine = member >> bit & 1
-        keep = lax.dynamic_slice_in_dim(blocks, mine * half, half, 0)
-        send = lax.dynamic_slice_in_dim(blocks, (1 - mine) * half, half, 0)
-        blocks = jnp.concatenate([keep, swapped(send, 1 << bit)], 1)
-    return blocks[0]
+        sent = [
+            after(lax.dynamic_slice_in_dim(array, at + (1 - mine) * count, count, 0), earlier)
+            for array, at in views
+        ]
+        kept = [(array, at + mine * count) for array, at in views]
+        views = kept + [(swapped(part, 1 << bit), 0) for part in sent]
+    return views
 
 
 def from_first_member(value, member, group, bits):
@@ -179,56 +394,32 @@
     return value
 
 
-def lines(hops, group):
-    toks, facs = lax.axis_size("tok"), lax.axis_size("fac")
-    pairs = []
-    for tok in range(toks):
-        root = tok % group
-        for before, after in hops:
-            if 0 <= root + before < facs and 0 <= root + after < facs:
-                pairs.append((tok * facs + root + before, tok * facs + root + after))
-    return pairs
-
-
-def from_own_column(value, member, column, group):
-    axes = ("tok", "fac")
+def up_columns(value, column, toks):
     facs = lax.axis_size("fac")
-    upward = lax.ppermute(value, axes, lines([(0, 1)], group))
-    downward = lax.ppermute(value, axes, lines([(0, -1)], group))
-    moving = upward + downward
-    total = jnp.where(member == column, value, moving)
-    for distance in range(1, facs - 1):
-        pairs = lines([(distance, distance + 1), (-distance, -distance - 1)], group)
-        moving = lax.ppermute(moving, axes, pairs)
+    total = jnp.where(column == 0, value, jnp.zeros_like(value))
+    moving = total
+    for place in range(facs - 1):
+        pairs = [(tok * facs + place, tok * facs + place + 1) for tok in toks]
+        moving = lax.ppermute(moving, ("tok", "fac"), pairs)
         total = total + moving
     return total
 
 
 def local(grad_rows, routes, counts, factor_old, damping, weight_grad):
-    group = lax.axis_size("tok") // 2
-    facs = lax.axis_size("fac")
+    toks = lax.axis_size("tok")
+    group = toks // 2
     bits = group.bit_length() - 1
     position = lax.axis_index("tok")
     expert = position // group
     member = position % group
     column = lax.axis_index("fac")
     tok_rows, width = grad_rows.shape
-    grad_cols = weight_grad.shape[1]
     damp = jnp.where(expert == 0, damping[0], damping[1])
 
-    near = from_first_member(
-        jnp.concatenate([factor_old[:LEAD].astype(BF16), weight_grad[:LEAD]], 1),
-        member,
-        group,
-        bits,
-    )
-    near_factor, near_grad = near[:, :width], near[:, width:]
-    corner = jnp.where(column == 0, factor_old[:LEAD, :LEAD], 0.0)
-    moving = corner
-    for place in range(facs - 1):
-        moving = lax.ppermute(moving, "fac", [(place, place + 1)])
-        corner = corner + moving
+    corner = up_columns(factor_old[:LEAD, :LEAD], column, [0, group])
     corner = from_first_member(corner, member, group, bits)
+    first_cols = up_columns(factor_old[:, :LEAD].astype(BF16), column, range(toks))
+    near_factor = from_first_member(factor_old[:LEAD].astype(BF16), member, group, bits)
 
     live = jnp.arange(tok_rows) < counts[0]
     named = routes[:, 0]
@@ -246,55 +437,54 @@
     total = tally[0] + other[1]
     for bit in range(bits):
         total = total + swapped(total, 1 << bit)
-    share = (1.0 - DECAY) / total[0]
-
-    chunks = [(begin, min(begin + LEAD, width)) for begin in range(0, width, LEAD)]
-    quarters = []
+    scalars = jnp.stack([(1.0 - DECAY) / total[0], damp])
+
+    ends = [LEAD, width - ROWS, width] if width > LEAD + ROWS else [LEAD, width]
+    chunks = list(zip([0, *ends], ends))
+    spread, parts = [], []
     for begin, end in chunks:
-        incoming = swapped(packed[CAP:, begin:end], group)
-        quarters.append(jnp.concatenate([packed[:CAP, begin:end], incoming], 0))
-    spread = [lax.all_gather(quarter, "fac") for quarter in quarters]
-    lead = gather_members(spread[0][0][:, :LEAD], bits)
-    across = gather_members(jnp.concatenate(quarters, 1), bits)
-    down = [exchange_members(part, member, bits) for part in spread]
-
-    eye = jnp.eye(LEAD, dtype=F32)
-    top = DECAY * corner + share * dot_t(lead, lead) + damp * eye
-    upper, inverse = factor_lead(top)
-    lower = upper.T
-    beside = DECAY * near_factor.astype(F32) + share * dot_t(lead, across)
-    panel_cols = jnp.dot(inverse, beside, precision=lax.Precision.HIGH).astype(BF16)
-    panel_rows = from_own_column(panel_cols, member, column, group)
-    solution_rows = jnp.dot(inverse, near_grad.astype(F32), precision=lax.Precision.HIGH)
-
-    gram = jnp.concatenate([dot_t(part, across) for part in down], 0)
-    running = DECAY * factor_old + share * gram
-
-    row_index = jnp.arange(width)[:, None]
-    col_index = jnp.arange(width)[None, :]
-    diagonal = member * width + row_index == column * width + col_index
-    matrix = running + jnp.where(diagonal, damp, 0.0)
-    head = (member == 0) & (row_index < LEAD)
-    updated = jnp.where(head, 0.0, matrix - dot_t(panel_rows, panel_cols))
-    first = lax.dot_general(
-        matrix[:, :LEAD],
-        inverse,
-        (((1,), (1,)), ((), ())),
-        precision=lax.Precision.HIGH,
-        preferred_element_type=F32,
-    )
-    first = jnp.where(head, jnp.pad(lower, ((0, width - LEAD), (0, 0))), first)
-    factored = lax.dynamic_update_slice(
-        updated, jnp.where(column == 0, first, updated[:, :LEAD]), (0, 0)
-    )
-
-    minus = jnp.pad(-jnp.eye(LEAD, dtype=BF16), ((0, 0), (0, width - LEAD)))
-    weights = jnp.where(head.T, minus, panel_rows)
-    high = solution_rows.astype(BF16)
-    low = (solution_rows - high.astype(F32)).astype(BF16)
-    product = dot_t(jnp.concatenate([weights, weights], 0), jnp.concatenate([high, low], 0))
-    precond = jnp.where(head, 0.0, weight_grad.astype(F32)) - product
-    return (running, factored, precond)
+        sent = packed[CAP:, begin:end]
+        if parts:
+            sent = after(sent, incoming)
+        incoming = swapped(sent, group)
+        part = jnp.concatenate([packed[:CAP, begin:end], incoming], 0)
+        parts.append(part)
+        if spread:
+            part = after(part, spread[-1])
+        spread.append(lax.all_gather(part, "fac"))
+    across = gather_members(jnp.concatenate(parts, 1), bits)
+    lead = gather_members(after(spread[0][0], across[1]), bits)
+    near_grad = from_first_member(after(weight_grad[:LEAD], lead[1]), member, group, bits)
+
+    upper, inverse = factor_lead(scalars, corner, lead)
+    panel = panel_columns(scalars, inverse, near_factor, lead, across)
+    solved = jnp.dot(inverse, near_grad.astype(F32), precision=lax.Precision.HIGH)
+    high = solved.astype(BF16)
+    low = (solved - high.astype(F32)).astype(BF16)
+
+    results = ()
+    gates = [lead[1], inverse, panel]
+    for (begin, _), part, gate in zip(chunks, spread, gates):
+        views = exchange_members(part, member, bits, gate)
+        places = jnp.stack([member, column, member * width + begin] + [at for _, at in views])
+        results = finish_rows(
+            begin,
+            places.astype(jnp.int32),
+            scalars,
+            factor_old,
+            first_cols,
+            weight_grad,
+            panel,
+            inverse,
+            upper.T,
+            high,
+            low,
+            [array for array, _ in views],
+            lead,
+            across,
+            results,
+        )
+    return results
 
 
 def solution(mesh):

time: 478 us -> 402 us (0.84)
  the two profiles are of different devices: /device:TPU:2 before, /device:TPU:23 now
where the time goes in v2:
time: 402 us; the launch traced here: 401 us
  Pallas kernels  111 us (28%)
  waiting for transfers between devices  106 us (26%)
  other arithmetic  67.3 us (17%)
  starting transfers between devices  65.4 us (16%)
  between operations  26.7 us (7%)
  local copies, waits for them, and re-layouts  17 us (4%)
  matrix products  7.79 us (2%)
    pallas_call x3, Pallas kernels, finish_rows(): pl.pallas_call(lambda *refs: finish_kernel(count, gram_steps, begin == 0,...  68.9 us
    ppermute x21, waiting for transfers between devices, swapped(): lax.ppermute(value, 'tok', [(source, source ^ mask) for source in range(s...  57.7 us
    ppermute x6, waiting for transfers between devices, up_columns(): moving = lax.ppermute(moving, ('tok', 'fac'), pairs)  48 us
    ppermute x21, starting transfers between devices, swapped(): lax.ppermute(value, 'tok', [(source, source ^ mask) for source in range(s...  46.1 us
    pallas_call x1, Pallas kernels, factor_lead(): pl.pallas_call(factor_kernel, out_shape=(shape, shape), in_specs=[pl.Bloc...  28.8 us
    select_n x12, other arithmetic, after(): return jnp.where(mark == mark, value, jnp.zeros_like(value))  16.9 us
    pallas_call x1, Pallas kernels, panel_columns(): pl.pallas_call(panel_kernel, grid=(width // cols,), out_shape=jax.ShapeDt...  13 us
    add x5, other arithmetic, from_first_member(): value = value + lax.ppermute(value, 'tok', pairs)  12 us
  transfers between devices with their start and end apart: 36, of which 8 were waited for; matrix products, arithmetic and copies ran while one was open for 20% of the time, Pallas kernels for 24%

profile of v2, /device:TPU:23, one launch (start us, length us, event | category | flops | bytes accessed | tf_op | source)
XLA Modules:
  0.0 400.9 jit_solution(17901500001916504561)
XLA Ops:
  12.6 8.3 %collective-permute-done.11 = bf16[320,512]{1,0:T(8,128)(2,1)S(1)} collective-permute-done((bf16[320,512]{1,0:T(8,128)(2,1)S(1)}, bf16[320,512]{1,0:T(8,128)(2,1)S(1)}, u32[]{:S(2)}, u32[]{:S(2)}) %collective-permute-start.11) | collective-permute-done | bytes 327712 | tf_op jit(solution)/shard_map/ppermute | solution.py:359
  28.1 8.1 %collective-permute-done.12 = bf16[320,768]{1,0:T(8,128)(2,1)S(1)} collective-permute-done((bf16[320,768]{1,0:T(8,128)(2,1)}, bf16[320,768]{1,0:T(8,128)(2,1)S(1)}, u32[]{:S(2)}, u32[]{:S(2)}) %collective-permute-start.12) | collective-permute-done | bytes 491552 | tf_op jit(solution)/shard_map/ppermute | solution.py:359
  38.4 4.3 %collective-permute-done.13 = bf16[320,256]{1,0:T(8,128)(2,1)S(1)} collective-permute-done((bf16[320,256]{1,0:T(8,128)(2,1)S(1)}, bf16[320,256]{1,0:T(8,128)(2,1)S(1)}, u32[]{:S(2)}, u32[]{:S(2)}) %collective-permute-start.13) | collective-permute-done | bytes 163872 | tf_op jit(solution)/shard_map/ppermute | solution.py:359
  42.7 11.3 %maximum_maximum_fusion.refs_4_.refs_18_ = bf16[640,1536]{1,0:T(8,128)(2,1)} fusion(bf16[320,256]{1,0:T(8,128)(2,1)S(1)} %collective-permute-done.13, bf16[320,256]{1,0:T(8,128)(2,1)S(1)} %get-tuple-element.30, bf16[320,768]{1,0:T(8,128)(2,1)S(1)} %collective-permute-done.12, bf16[320,768]{1,0:T(8,128)(2,1)S(1)} %get-tuple-element.27, ...), kind=kLoop, calls=%fused_computation.5 | loop fusion | flops 11796480 | bytes 3932160 | tf_op jit(solution)/shard_map/concatenate | solution.py:455
  55.7 6.5 %convert.4 = bf16[1536,1536]{1,0:T(8,128)(2,1)} convert(f32[1536,1536]{1,0:T(8,128)} %refs_2_.5) | non-fusion elementwise | flops 2359296 | bytes 14155776 | tf_op jit(solution)/shard_map/convert.1
  67.3 28.1 %collective-permute-done.14.refs_5_.refs_19_ = bf16[640,1536]{1,0:T(8,128)(2,1)} collective-permute-done((bf16[640,1536]{1,0:T(8,128)(2,1)}, bf16[640,1536]{1,0:T(8,128)(2,1)}, u32[]{:S(2)}, u32[]{:S(2)}) %collective-permute-start.14) | collective-permute-done | bytes 1966112 | tf_op jit(solution)/shard_map/ppermute | solution.py:359
  111.0 5.1 %collective-permute-done.15.refs_1_.refs_15_ = bf16[640,512]{1,0:T(8,128)(2,1)S(1)} collective-permute-done((bf16[640,512]{1,0:T(8,128)(2,1)S(1)}, bf16[640,512]{1,0:T(8,128)(2,1)S(1)}, u32[]{:S(2)}, u32[]{:S(2)}) %collective-permute-start.15) | collective-permute-done | bytes 655392 | tf_op jit(solution)/shard_map/ppermute | solution.py:359
  118.0 3.1 select_select_fusion
  133.5 17.0 %collective-permute-start.1 = (f32[128]{0:T(128)S(1)}, f32[128]{0:T(128)S(1)}, u32[]{:S(2)}, u32[]{:S(2)}) collective-permute-start(f32[128]{0:T(128)S(1)} %add_bitcast_fusion.1), channel_id=1, source_target_pairs={{0,4},{4,0},{8,12},{12,8},{16,20},{20,16},{24,28},{28,24},{1,5},{5... | collective-permute-start | bytes 1544 | tf_op jit(solution)/shard_map/ppermute | solution.py:359
  151.7 3.8 collective-permute-start.2
  157.6 3.1 add.115.factor_ref
  160.7 7.6 %collective-permute-start.16 = (bf16[640,512]{1,0:T(8,128)(2,1)S(1)}, bf16[640,512]{1,0:T(8,128)(2,1)S(1)}, u32[]{:S(2)}, u32[]{:S(2)}) collective-permute-start(bf16[640,512]{1,0:T(8,128)(2,1)S(1)} %slice_select_fusion.3.refs_0_.refs_14_), channel_id=1, source_target_pairs={{0,4},{4,0},{8,12},{12,8},{16,20},{20,16},{24,28},{28,24},{1,5},{5... | collective-permute-start | bytes 1966088 | tf_op jit(solution)/shard_map/ppermute | solution.py:359
  171.8 48.0 %collective-permute-done.4 = bf16[1536,512]{1,0:T(8,128)(2,1)} collective-permute-done((bf16[1536,512]{1,0:T(8,128)(2,1)}, bf16[1536,512]{1,0:T(8,128)(2,1)}, u32[]{:S(2)}, u32[]{:S(2)}) %collective-permute-start.4) | collective-permute-done | bytes 1572896 | tf_op jit(solution)/shard_map/ppermute | solution.py:403
  219.8 5.8 %collective-permute-start.21 = (bf16[640,1536]{1,0:T(8,128)(2,1)}, bf16[640,1536]{1,0:T(8,128)(2,1)}, u32[]{:S(2)}, u32[]{:S(2)}) collective-permute-start(bf16[640,1536]{1,0:T(8,128)(2,1)} %collective-permute-done.14.refs_5_.refs_19_), channel_id=1, source_target_pairs={{0,4},{4,0},{8,12},{12,8},{16,20},{20,16},{24,28},{28,24},{1,5},{5... | collective-permute-start | bytes 5898248 | tf_op jit(solution)/shard_map/ppermute | solution.py:359
  228.1 3.8 fusion.8
  233.2 28.8 %shard_map.85 = (f32[512,512]{1,0:T(8,128)S(1)}, f32[512,512]{1,0:T(8,128)S(1)}) custom-call(f32[2]{0:T(128)S(1)} %pad_maximum_fusion.1.scalars_ref.refs_1_, f32[512,512]{1,0:T(8,128)S(1)} %add.113.corner_ref, bf16[640,512]{1,0:T(8,128)(2,1)S(1)} %slice_select_fusion.3.refs_0_.refs_14_, bf16[640,512]{1,0:T(8,128)(2,1)S(1)} %collective-permute-done.15.refs_1_.refs_15_, ...), custom_call_target="tpu_custom_call" | custom-call | flops 24999999488 | bytes 6291456 | tf_op jit(solution)/shard_map/pallas_call | solution.py:146
  268.2 3.0 dynamic-slice_select_fusion
  272.6 4.3 %add_add_fusion.refs_3_ = bf16[1536,512]{1,0:T(8,128)(2,1)} fusion(bf16[1536,512]{1,0:T(8,128)(2,1)} %collective-permute-done.5, bf16[1536,512]{1,0:T(8,128)(2,1)} %collective-permute-done.4, bf16[1536,512]{1,0:T(8,128)(2,1)} %collective-permute-done.3, bf16[1536,1536]{1,0:T(8,128)(2,1)} %convert.4, pred[]{:T(512)S(6)} %eq.117), kind=kLoop, calls=%fused_computation.9 | loop fusion | flops 3145728 | bytes 7864321 | tf_op jit(solution)/shard_map/add | solution.py:404
  286.4 13.0 %shard_map.86.refs_5_ = bf16[512,1536]{1,0:T(8,128)(2,1)S(1)} custom-call(f32[2]{0:T(128)S(1)} %pad_maximum_fusion.1.scalars_ref.refs_1_, f32[512,512]{1,0:T(8,128)S(1)} %copy-done.5, bf16[512,1536]{1,0:T(8,128)(2,1)} %add.115.factor_ref, bf16[640,512]{1,0:T(8,128)(2,1)S(1)} %slice_select_fusion.3.refs_0_.refs_14_, ...), custom_call_target="tpu_custom_call" | custom-call | flops 8858370048 | bytes 13631488 | tf_op jit(solution)/shard_map/pallas_call | solution.py:175
  303.3 6.6 %subtract_convert_fusion = (bf16[512,2048]{1,0:T(8,128)(2,1)}, bf16[512,2048]{1,0:T(8,128)(2,1)}) fusion(f32[512,512]{1,0:T(8,128)S(1)} %copy-done.5, bf16[512,2048]{1,0:T(8,128)(2,1)} %fusion.8, bf16[512,2048]{1,0:T(8,128)(2,1)} %collective-permute-done.23), kind=kOutput, calls=%fused_computation | convolution fusion | flops 3226468352 | bytes 9437184 | tf_op jit(solution)/shard_map/dot_general | solution.py:461
  315.6 3.3 collective-permute-start.29
  321.6 23.6 %shard_map.87 = (f32[1536,1536]{1,0:T(8,128)}, f32[1536,1536]{1,0:T(8,128)}, f32[1536,2048]{1,0:T(8,128)}) custom-call(s32[7]{0:T(128)} %stack.65.refs_0_, f32[2]{0:T(128)} %copy-done.11, f32[1536,1536]{1,0:T(8,128)} %refs_2_.5, bf16[1536,512]{1,0:T(8,128)(2,1)} %add_add_fusion.refs_3_, bf16[1536,2048]{1,0:T(8,128)(2,1)} %refs_4_.5, ...), custom_call_target="tpu_custom_call" | custom-call | flops 9932111872 | bytes 36700160 | tf_op jit(solution)/shard_map/pallas_call | solution.py:326
  348.1 30.5 %shard_map.88 = (f32[1536,1536]{1,0:T(8,128)}, f32[1536,1536]{1,0:T(8,128)}, f32[1536,2048]{1,0:T(8,128)}) custom-call(s32[7]{0:T(128)} %stack.63.refs_0_, f32[2]{0:T(128)} %copy-done.11, f32[1536,1536]{1,0:T(8,128)} %refs_2_.5, bf16[1536,512]{1,0:T(8,128)(2,1)} %add_add_fusion.refs_3_, ...), custom_call_target="tpu_custom_call", output_to_operand_aliasing={{0}: (22, {}), {1}: (23, {}), {2}: (24, {})} | custom-call | flops 14898167808 | bytes 45875200 | tf_op jit(solution)/shard_map/pallas_call | solution.py:326
  379.5 14.8 %shard_map.89 = (f32[1536,1536]{1,0:T(8,128)}, f32[1536,1536]{1,0:T(8,128)}, f32[1536,2048]{1,0:T(8,128)}) custom-call(s32[7]{0:T(128)} %stack.57.refs_0_, f32[2]{0:T(128)} %copy-done.11, f32[1536,1536]{1,0:T(8,128)} %refs_2_.5, bf16[1536,512]{1,0:T(8,128)(2,1)} %add_add_fusion.refs_3_, ...), custom_call_target="tpu_custom_call", output_to_operand_aliasing={{0}: (22, {}), {1}: (23, {}), {2}: (24, {})} | custom-call | flops 4966055936 | bytes 27525120 | tf_op jit(solution)/shard_map/pallas_call | solution.py:326
  (167 shorter events, 82.1 us)
Async XLA Ops:
  7.2 90.7 %all-gather.9.cloned.1.call-start = ((), (), s32[]{:S(2)}) async-start(), calls=%async_computation.2 | async-start | bytes 3276800 | tf_op jit(solution)/shard_map/all_gather | solution.py:454
  21.9 243.0 %all-gather.5.cloned.1.call-start = ((), (), s32[]{:S(2)}) async-start(), calls=%async_computation | async-start | bytes 4915200 | tf_op jit(solution)/shard_map/all_gather | solution.py:454
  26.4 27.6 %collective-permute-start.6 = (f32[512,512]{1,0:T(8,128)S(1)}, f32[512,512]{1,0:T(8,128)}, u32[]{:S(2)}, u32[]{:S(2)}) collective-permute-start(f32[512,512]{1,0:T(8,128)S(1)} %slice_select_fusion.2), channel_id=1, source_target_pairs={{0,1},{16,17}} | collective-permute-start | bytes 3145736 | tf_op jit(solution)/shard_map/ppermute | solution.py:403
  54.0 41.4 %collective-permute-start.14 = (bf16[640,1536]{1,0:T(8,128)(2,1)}, bf16[640,1536]{1,0:T(8,128)(2,1)}, u32[]{:S(2)}, u32[]{:S(2)}) collective-permute-start(bf16[640,1536]{1,0:T(8,128)(2,1)} %maximum_maximum_fusion.refs_4_.refs_18_), channel_id=1, source_target_pairs={{0,8},{4,12},{8,0},{12,4},{16,24},{20,28},{24,16},{28,20},{1,9},{5... | collective-permute-start | bytes 5898248 | tf_op jit(solution)/shard_map/ppermute | solution.py:359
  62.2 45.4 %collective-permute-start.8 = (f32[512,512]{1,0:T(8,128)}, f32[512,512]{1,0:T(8,128)}, u32[]{:S(2)}, u32[]{:S(2)}) collective-permute-start(f32[512,512]{1,0:T(8,128)} %collective-permute-done.7), channel_id=1, source_target_pairs={{2,3},{18,19}} | collective-permute-start | bytes 3145736 | tf_op jit(solution)/shard_map/ppermute | solution.py:403
  65.5 57.7 %collective-permute-start.18 = (bf16[512,1536]{1,0:T(8,128)(2,1)S(1)}, bf16[512,1536]{1,0:T(8,128)(2,1)}, u32[]{:S(2)}, u32[]{:S(2)}) collective-permute-start(bf16[512,1536]{1,0:T(8,128)(2,1)S(1)} %slice_select_fusion), channel_id=1, source_target_pairs={{0,8},{16,24},{1,9},{17,25},{2,10},{18,26},{3,11},{19,27}} | collective-permute-start | bytes 4718600 | tf_op jit(solution)/shard_map/ppermute | solution.py:393
  107.5 211.4 %all-gather.7.cloned.1.call-start = ((), (), s32[]{:S(2)}) async-start(), calls=%async_computation.1 | async-start | bytes 1638400 | tf_op jit(solution)/shard_map/all_gather | solution.py:454
  121.1 104.5 %collective-permute-start.22 = (bf16[512,2048]{1,0:T(8,128)(2,1)}, bf16[512,2048]{1,0:T(8,128)(2,1)}, u32[]{:S(2)}, u32[]{:S(2)}) collective-permute-start(bf16[512,2048]{1,0:T(8,128)(2,1)} %select_select_fusion), channel_id=1, source_target_pairs={{0,8},{16,24},{1,9},{17,25},{2,10},{18,26},{3,11},{19,27}} | collective-permute-start | bytes 6291464 | tf_op jit(solution)/shard_map/ppermute | solution.py:393
  125.2 32.3 %collective-permute-start.19 = (bf16[512,1536]{1,0:T(8,128)(2,1)S(1)}, bf16[512,1536]{1,0:T(8,128)(2,1)}, u32[]{:S(2)}, u32[]{:S(2)}) collective-permute-start(bf16[512,1536]{1,0:T(8,128)(2,1)S(1)} %fusion.9), channel_id=1, source_target_pairs={{0,4},{8,12},{16,20},{24,28},{1,5},{9,13},{17,21},{25,29},{2,6},{1... | collective-permute-start | bytes 4718600 | tf_op jit(solution)/shard_map/ppermute | solution.py:393
  126.6 93.2 %collective-permute-start.4 = (bf16[1536,512]{1,0:T(8,128)(2,1)}, bf16[1536,512]{1,0:T(8,128)(2,1)}, u32[]{:S(2)}, u32[]{:S(2)}) collective-permute-start(bf16[1536,512]{1,0:T(8,128)(2,1)} %collective-permute-done.3), channel_id=1, source_target_pairs={{1,2},{5,6},{9,10},{13,14},{17,18},{21,22},{25,26},{29,30}} | collective-permute-start | bytes 4718600 | tf_op jit(solution)/shard_map/ppermute | solution.py:403
  129.0 40.4 %collective-permute-start.10 = (f32[512,512]{1,0:T(8,128)}, f32[512,512]{1,0:T(8,128)}, u32[]{:S(2)}, u32[]{:S(2)}) collective-permute-start(f32[512,512]{1,0:T(8,128)} %add.112), channel_id=1, source_target_pairs={{0,4},{8,12},{16,20},{24,28},{1,5},{9,13},{17,21},{25,29},{2,6},{1... | collective-permute-start | bytes 3145736 | tf_op jit(solution)/shard_map/ppermute | solution.py:393
  160.7 71.2 %collective-permute-start.16 = (bf16[640,512]{1,0:T(8,128)(2,1)S(1)}, bf16[640,512]{1,0:T(8,128)(2,1)S(1)}, u32[]{:S(2)}, u32[]{:S(2)}) collective-permute-start(bf16[640,512]{1,0:T(8,128)(2,1)S(1)} %slice_select_fusion.3.refs_0_.refs_14_), channel_id=1, source_target_pairs={{0,4},{4,0},{8,12},{12,8},{16,20},{20,16},{24,28},{28,24},{1,5},{5... | collective-permute-start | bytes 1966088 | tf_op jit(solution)/shard_map/ppermute | solution.py:359
  168.3 63.6 %collective-permute-start.17 = (bf16[640,512]{1,0:T(8,128)(2,1)S(1)}, bf16[640,512]{1,0:T(8,128)(2,1)S(1)}, u32[]{:S(2)}, u32[]{:S(2)}) collective-permute-start(bf16[640,512]{1,0:T(8,128)(2,1)S(1)} %collective-permute-done.15.refs_1_.refs_15_), channel_id=1, source_target_pairs={{0,4},{4,0},{8,12},{12,8},{16,20},{20,16},{24,28},{28,24},{1,5},{5... | collective-permute-start | bytes 1966088 | tf_op jit(solution)/shard_map/ppermute | solution.py:359
  169.5 110.7 %collective-permute-start.20 = (bf16[640,1536]{1,0:T(8,128)(2,1)}, bf16[640,1536]{1,0:T(8,128)(2,1)}, u32[]{:S(2)}, u32[]{:S(2)}) collective-permute-start(bf16[640,1536]{1,0:T(8,128)(2,1)} %maximum_maximum_fusion.refs_4_.refs_18_), channel_id=1, source_target_pairs={{0,4},{4,0},{8,12},{12,8},{16,20},{20,16},{24,28},{28,24},{1,5},{5... | collective-permute-start | bytes 5898248 | tf_op jit(solution)/shard_map/ppermute | solution.py:359
  219.8 63.2 %collective-permute-start.21 = (bf16[640,1536]{1,0:T(8,128)(2,1)}, bf16[640,1536]{1,0:T(8,128)(2,1)}, u32[]{:S(2)}, u32[]{:S(2)}) collective-permute-start(bf16[640,1536]{1,0:T(8,128)(2,1)} %collective-permute-done.14.refs_5_.refs_19_), channel_id=1, source_target_pairs={{0,4},{4,0},{8,12},{12,8},{16,20},{20,16},{24,28},{28,24},{1,5},{5... | collective-permute-start | bytes 5898248 | tf_op jit(solution)/shard_map/ppermute | solution.py:359
  225.6 45.5 %collective-permute-start.5 = (bf16[1536,512]{1,0:T(8,128)(2,1)}, bf16[1536,512]{1,0:T(8,128)(2,1)}, u32[]{:S(2)}, u32[]{:S(2)}) collective-permute-start(bf16[1536,512]{1,0:T(8,128)(2,1)} %collective-permute-done.4), channel_id=1, source_target_pairs={{2,3},{6,7},{10,11},{14,15},{18,19},{22,23},{26,27},{30,31}} | collective-permute-start | bytes 4718600 | tf_op jit(solution)/shard_map/ppermute | solution.py:403
  231.9 69.4 %collective-permute-start.30 = (bf16[2,640,512]{2,1,0:T(8,128)(2,1)}, bf16[2,640,512]{2,1,0:T(8,128)(2,1)}, u32[]{:S(2)}, u32[]{:S(2)}) collective-permute-start(bf16[2,640,512]{2,1,0:T(8,128)(2,1)} %dynamic-slice_select_fusion.1), channel_id=1, source_target_pairs={{0,8},{4,12},{8,0},{12,4},{16,24},{20,28},{24,16},{28,20},{1,9},{5... | collective-permute-start | bytes 3932168 | tf_op jit(solution)/shard_map/ppermute | solution.py:359
  231.9 71.4 %collective-permute-start.23 = (bf16[512,2048]{1,0:T(8,128)(2,1)}, bf16[512,2048]{1,0:T(8,128)(2,1)}, u32[]{:S(2)}, u32[]{:S(2)}) collective-permute-start(bf16[512,2048]{1,0:T(8,128)(2,1)} %fusion.8), channel_id=1, source_target_pairs={{0,4},{8,12},{16,20},{24,28},{1,5},{9,13},{17,21},{25,29},{2,6},{1... | collective-permute-start | bytes 6291464 | tf_op jit(solution)/shard_map/ppermute | solution.py:393
  271.1 42.2 %collective-permute-start.27 = (bf16[2,640,768]{2,1,0:T(8,128)(2,1)}, bf16[2,640,768]{2,1,0:T(8,128)(2,1)}, u32[]{:S(2)}, u32[]{:S(2)}) collective-permute-start(bf16[2,640,768]{2,1,0:T(8,128)(2,1)} %dynamic-slice_select_fusion), channel_id=1, source_target_pairs={{0,8},{4,12},{8,0},{12,4},{16,24},{20,28},{24,16},{28,20},{1,9},{5... | collective-permute-start | bytes 5898248 | tf_op jit(solution)/shard_map/ppermute | solution.py:359
  280.2 41.4 %collective-permute-start.31 = (bf16[1,640,512]{2,1,0:T(8,128)(2,1)}, bf16[1,640,512]{2,1,0:T(8,128)(2,1)}, u32[]{:S(2)}, u32[]{:S(2)}) collective-permute-start(bf16[1,640,512]{2,1,0:T(8,128)(2,1)} %dynamic-slice_select_fusion.5), channel_id=1, source_target_pairs={{0,4},{4,0},{8,12},{12,8},{16,20},{20,16},{24,28},{28,24},{1,5},{5... | collective-permute-start | bytes 1966088 | tf_op jit(solution)/shard_map/ppermute | solution.py:359
  311.2 35.7 %collective-permute-start.28 = (bf16[1,640,768]{2,1,0:T(8,128)(2,1)S(1)}, bf16[1,640,768]{2,1,0:T(8,128)(2,1)S(1)}, u32[]{:S(2)}, u32[]{:S(2)}) collective-permute-start(bf16[1,640,768]{2,1,0:T(8,128)(2,1)S(1)} %dynamic-slice_select_fusion.3), channel_id=1, source_target_pairs={{0,4},{4,0},{8,12},{12,8},{16,20},{20,16},{24,28},{28,24},{1,5},{5... | collective-permute-start | bytes 2949128 | tf_op jit(solution)/shard_map/ppermute | solution.py:359
  315.6 31.3 %collective-permute-start.29 = (bf16[1,640,768]{2,1,0:T(8,128)(2,1)}, bf16[1,640,768]{2,1,0:T(8,128)(2,1)S(1)}, u32[]{:S(2)}, u32[]{:S(2)}) collective-permute-start(bf16[1,640,768]{2,1,0:T(8,128)(2,1)} %dynamic-slice_select_fusion.2), channel_id=1, source_target_pairs={{0,4},{4,0},{8,12},{12,8},{16,20},{20,16},{24,28},{28,24},{1,5},{5... | collective-permute-start | bytes 2949128 | tf_op jit(solution)/shard_map/ppermute | solution.py:359
  346.2 32.4 %collective-permute-start.25 = (bf16[1,640,256]{2,1,0:T(8,128)(2,1)S(1)}, bf16[1,640,256]{2,1,0:T(8,128)(2,1)S(1)}, u32[]{:S(2)}, u32[]{:S(2)}) collective-permute-start(bf16[1,640,256]{2,1,0:T(8,128)(2,1)S(1)} %dynamic-slice_select_fusion.8), channel_id=1, source_target_pairs={{0,4},{4,0},{8,12},{12,8},{16,20},{20,16},{24,28},{28,24},{1,5},{5... | collective-permute-start | bytes 983048 | tf_op jit(solution)/shard_map/ppermute | solution.py:359
  346.4 32.2 %collective-permute-start.26 = (bf16[1,640,256]{2,1,0:T(8,128)(2,1)S(1)}, bf16[1,640,256]{2,1,0:T(8,128)(2,1)S(1)}, u32[]{:S(2)}, u32[]{:S(2)}) collective-permute-start(bf16[1,640,256]{2,1,0:T(8,128)(2,1)S(1)} %dynamic-slice_select_fusion.7), channel_id=1, source_target_pairs={{0,4},{4,0},{8,12},{12,8},{16,20},{20,16},{24,28},{28,24},{1,5},{5... | collective-permute-start | bytes 983048 | tf_op jit(solution)/shard_map/ppermute | solution.py:359
  (36 other events, 841.7 us)
Sparse Core Ops, SparseCore 0:
  22.0 55.4 all-gather.8
  107.7 94.2 all-gather.4
  268.3 33.6 all-gather.6

commit v3 on v2

v3 whole, which is shorter than its diff:
```python
import jax
import jax.numpy as jnp
from jax import lax
from jax.experimental import pallas as pl
from jax.experimental.pallas import tpu as pltpu
from jax.sharding import PartitionSpec as P

CAP = 320
LEAD = 512
TILE = 128
GROUP = 8
ROWS = 256
COLS = 512
PLACES = 3
DECAY = 0.8

HIGHEST = lax.Precision.HIGHEST
BF16 = jnp.bfloat16
F32 = jnp.float32


def dot_t(left, right, precision=None):
    return lax.dot_general(
        left, right, (((0,), (0,)), ((), ())), precision=precision, preferred_element_type=F32
    )


def splat(rows, lane):
    return jnp.broadcast_to(rows[:, lane : lane + 1], rows.shape)


def eliminate_tile(rows):
    lanes = lax.broadcasted_iota(jnp.int32, (GROUP, TILE), 1)
    subs = lax.broadcasted_iota(jnp.int32, (GROUP, TILE), 0)
    upper, inverse = [], []
    for step in range(TILE // GROUP):
        base = step * GROUP
        inside = (lanes >= base) & (lanes < base + GROUP)
        block = rows[step]
        first = [jnp.broadcast_to(block[t : t + 1, :], (GROUP, TILE)) for t in range(GROUP)]
        second = [
            jnp.where(inside, jnp.where(lanes == base + t, 1.0, 0.0), first[t])
            for t in range(GROUP)
        ]
        pivot = [
            [splat(first[t], base + u) if u >= t else None for u in range(GROUP)]
            for t in range(GROUP)
        ]
        scale = [None] * GROUP
        for t in range(GROUP):
            scale[t] = lax.rsqrt(pivot[t][t])
            for u in range(t + 1, GROUP):
                pivot[t][u] = pivot[t][u] * scale[t]
            for u in range(t + 1, GROUP):
                for w in range(u, GROUP):
                    pivot[u][w] = pivot[u][w] - pivot[t][u] * pivot[t][w]
            first[t] = first[t] * scale[t]
            second[t] = second[t] * scale[t]
            for u in range(t + 1, GROUP):
                first[u] = first[u] - pivot[t][u] * first[t]
                second[u] = second[u] - pivot[t][u] * second[t]
        solved = [None] * GROUP
        for t in reversed(range(GROUP)):
            value = second[t]
            for u in range(t + 1, GROUP):
                value = value - pivot[t][u] * solved[u]
            solved[t] = value * scale[t]
        for later in range(step + 1, TILE // GROUP):
            value = jnp.where(inside, 0.0, rows[later])
            for t in range(GROUP):
                value = value - splat(rows[later], base + t) * solved[t]
            rows[later] = value
        upper_rows, inverse_rows = first[0], second[0]
        for t in range(1, GROUP):
            upper_rows = jnp.where(subs == t, first[t], upper_rows)
            inverse_rows = jnp.where(subs == t, second[t], inverse_rows)
        upper.append(upper_rows)
        inverse.append(inverse_rows)
    return upper, inverse


def factor_kernel(count, places_ref, damp_ref, exact_ref, *refs):
    lead_refs = refs[:count]
    upper_ref, inverse_ref, share_ref, work_ref = refs[-4:]
    steps = LEAD // TILE
    side = LEAD // count
    marks = sum(lead[2 * CAP + side :, :].astype(F32) for lead in lead_refs)
    row = lax.broadcasted_iota(jnp.int32, marks.shape, 0)
    weight = jnp.where(row < 4, jnp.where(row % 2 == 0, 256.0, 1.0), 0.0)
    total = jnp.sum(marks * weight, axis=0, keepdims=True)[:, :1]
    share = (1.0 - DECAY) / total
    share_ref[...] = jnp.broadcast_to(share, share_ref.shape)
    for q, lead in enumerate(lead_refs):
        begin = pl.multiple_of(places_ref[PLACES + q] * side, side)
        work_ref[pl.ds(begin, side), :] = lead[2 * CAP : 2 * CAP + side, :].astype(F32)

    @pl.when((places_ref[0] == 0) & (places_ref[1] == 0))
    def _():
        work_ref[...] = exact_ref[...]

    gram = sum(dot_t(lead[: 2 * CAP, :], lead[: 2 * CAP, :]) for lead in lead_refs)
    rows = lax.broadcasted_iota(jnp.int32, (LEAD, LEAD), 0)
    cols = lax.broadcasted_iota(jnp.int32, (LEAD, LEAD), 1)
    work_ref[...] = (
        DECAY * work_ref[...] + share * gram + jnp.where(rows == cols, damp_ref[0], 0.0)
    )
    upper_ref[...] = jnp.zeros_like(upper_ref)
    inverse_ref[...] = jnp.zeros_like(inverse_ref)
    lanes = lax.broadcasted_iota(jnp.int32, (GROUP, TILE), 1)
    subs = lax.broadcasted_iota(jnp.int32, (GROUP, TILE), 0)

    def tile_step(k, carry):
        begin = pl.multiple_of(k * TILE, TILE)
        rows = [
            work_ref[pl.ds(begin + g * GROUP, GROUP), pl.ds(begin, TILE)]
            for g in range(TILE // GROUP)
        ]
        upper, inverse = eliminate_tile(rows)
        upper_tile = jnp.concatenate(
            [jnp.where(lanes >= subs + g * GROUP, part, 0.0) for g, part in enumerate(upper)], 0
        )
        inverse_tile = jnp.concatenate(
            [jnp.where(lanes <= subs + g * GROUP, part, 0.0) for g, part in enumerate(inverse)], 0
        )
        band = jnp.dot(
            inverse_tile,
            work_ref[pl.ds(begin, TILE), :],
            precision=HIGHEST,
            preferred_element_type=F32,
        )
        work_ref[pl.ds(begin, TILE), :] = band
        work_ref[pl.ds(begin, TILE), pl.ds(begin, TILE)] = inverse_tile
        upper_ref[pl.ds(begin, TILE), pl.ds(begin, TILE)] = upper_tile
        inverse_ref[pl.ds(begin, TILE), pl.ds(begin, TILE)] = inverse_tile
        for other in range(steps):

            @pl.when(other < k)
            def _():
                inverse_ref[pl.ds(begin, TILE), other * TILE : (other + 1) * TILE] = work_ref[
                    pl.ds(begin, TILE), other * TILE : (other + 1) * TILE
                ]

            @pl.when(other > k)
            def _():
                span = slice(other * TILE, (other + 1) * TILE)
                part = work_ref[pl.ds(begin, TILE), span]
                upper_ref[pl.ds(begin, TILE), span] = part
                work_ref[span, pl.ds(begin, TILE)] = jnp.zeros((TILE, TILE), F32)
                work_ref[span, :] = work_ref[span, :] - dot_t(
                    part, work_ref[pl.ds(begin, TILE), :], HIGHEST
                )

        return carry

    lax.fori_loop(0, steps, tile_step, 0)


def factor_lead(places, damp, exact, lead, earlier):
    shape = jax.ShapeDtypeStruct((LEAD, LEAD), F32)
    vmem = pl.BlockSpec(memory_space=pltpu.VMEM)
    smem = pl.BlockSpec(memory_space=pltpu.SMEM)
    return pl.pallas_call(
        lambda *refs: factor_kernel(len(lead), *refs),
        out_shape=(shape, shape, jax.ShapeDtypeStruct((GROUP, TILE), F32)),
        in_specs=[smem, smem]
        + [vmem] * (1 + len(lead))
        + [pl.BlockSpec(memory_space=pl.ANY)] * len(earlier),
        out_specs=(vmem, vmem, vmem),
        scratch_shapes=[pltpu.VMEM((LEAD, LEAD), F32)],
        compiler_params=pltpu.CompilerParams(vmem_limit_bytes=32 * 1024 * 1024),
        cost_estimate=pl.CostEstimate(
            flops=25_000_000_000, bytes_accessed=6 * LEAD * LEAD * 4, transcendentals=LEAD
        ),
    )(places, damp, exact, *lead, *earlier)


def panel_kernel(count, places_ref, share_ref, inverse_ref, *refs):
    lead, across = refs[:count], refs[count : 2 * count]
    out_ref, lead_ref, across_ref, near_ref = refs[-4:]
    side = LEAD // count
    depth = 2 * CAP
    for q in range(count):
        span = slice(q * depth, (q + 1) * depth)
        across_ref[span, :] = across[q][:depth, :]
        begin = pl.multiple_of(places_ref[PLACES + q] * side, side)
        near_ref[pl.ds(begin, side), :] = across[q][depth : depth + side, :].astype(F32)

    @pl.when(pl.program_id(0) == 0)
    def _():
        for q in range(count):
            lead_ref[q * depth : (q + 1) * depth, :] = lead[q][:depth, :]

    gram = dot_t(lead_ref[...], across_ref[...])
    beside = DECAY * near_ref[...] + share_ref[:1, :1] * gram
    out_ref[...] = jnp.dot(
        inverse_ref[...], beside, precision=HIGHEST, preferred_element_type=F32
    ).astype(BF16)


def panel_columns(places, share, inverse, lead, across, earlier):
    count = len(lead)
    width = across[0].shape[1]
    cols = COLS if width % COLS == 0 else ROWS
    tall = 2 * CAP * count
    whole = lambda height: pl.BlockSpec((height, LEAD), lambda j: (0, 0))
    tiled = lambda height: pl.BlockSpec((height, cols), lambda j: (0, j))
    return pl.pallas_call(
        lambda *refs: panel_kernel(count, *refs),
        grid=(width // cols,),
        out_shape=(
            jax.ShapeDtypeStruct((LEAD, width), BF16),
            jax.ShapeDtypeStruct((tall, LEAD), BF16),
            jax.ShapeDtypeStruct((tall, width), BF16),
        ),
        in_specs=[
            pl.BlockSpec(memory_space=pltpu.SMEM),
            pl.BlockSpec((GROUP, TILE), lambda j: (0, 0)),
            whole(LEAD),
        ]
        + [whole(lead[0].shape[0])] * count
        + [tiled(across[0].shape[0])] * count
        + [pl.BlockSpec(memory_space=pl.ANY)] * len(earlier),
        out_specs=(tiled(LEAD), whole(tall), tiled(tall)),
        scratch_shapes=[pltpu.VMEM((LEAD, cols), F32)],
        compiler_params=pltpu.CompilerParams(vmem_limit_bytes=56 * 1024 * 1024),
        cost_estimate=pl.CostEstimate(
            flops=2 * width * LEAD * (tall + 6 * LEAD),
            bytes_accessed=4 * tall * (width + LEAD) + 4 * LEAD * width,
            transcendentals=0,
        ),
    )(places, share, inverse, *lead, *across, *earlier)


def finish_kernel(
    count,
    gram_steps,
    first_chunk,
    aliased,
    places_ref,
    damp_ref,
    share_ref,
    factor_ref,
    grad_ref,
    panel_ref,
    inverse_ref,
    high_ref,
    low_ref,
    lead_ref,
    across_ref,
    *refs,
):
    if first_chunk:
        lower_ref, *refs = refs
    mine = refs[:count]
    outs = refs[count + aliased :]
    running_ref, factored_ref, precond_ref, token_ref, mine_ref, rows_ref, first_ref = outs
    j, i = pl.program_id(0), pl.program_id(1)
    member, column, base = places_ref[0], places_ref[1], places_ref[2]
    share, damp = share_ref[:1, :1], damp_ref[0]
    height = ROWS
    depth = 2 * CAP
    side = LEAD // count
    cols = running_ref.shape[1]
    span = pl.ds(pl.multiple_of(i * height, height), height)
    head = (member == 0) & first_chunk

    @pl.when(j == 0)
    def _():
        token_ref[...] = jnp.zeros_like(token_ref)
        for q in range(count):
            mine_ref[span, q * depth : (q + 1) * depth] = mine[q][0, :depth, :].T
            begin = pl.multiple_of(places_ref[PLACES + q] * side, side)
            first_ref[pl.ds(begin, side), :] = mine[q][0, depth : depth + side, :].astype(F32)
        source = first_ref[...].T
        if cols == LEAD:
            source = jnp.where(column == 0, factor_ref[...], source)
        gram = jnp.dot(mine_ref[span, :], lead_ref[...], preferred_element_type=F32)
        row = base + i * height + lax.broadcasted_iota(jnp.int32, (height, LEAD), 0)
        col = lax.broadcasted_iota(jnp.int32, (height, LEAD), 1)
        source = DECAY * source + share * gram
        source = source + jnp.where(row == col, damp, 0.0)
        rows_ref[span, :] = lax.dot_general(
            source,
            inverse_ref[...],
            (((1,), (1,)), ((), ())),
            precision=HIGHEST,
            preferred_element_type=F32,
        )

    panel = rows_ref[span, :].astype(BF16)

    @pl.when(j < gram_steps)
    def _():
        gram = jnp.dot(mine_ref[span, :], across_ref[...], preferred_element_type=F32)
        running = DECAY * factor_ref[...] + share * gram
        running_ref[...] = running
        row = base + i * height + lax.broadcasted_iota(jnp.int32, (height, cols), 0)
        col = (column * gram_steps + j) * cols + lax.broadcasted_iota(jnp.int32, (height, cols), 1)
        matrix = running + jnp.where(row == col, damp, 0.0)
        factored = matrix - jnp.dot(panel, panel_ref[...], preferred_element_type=F32)
        factored_ref[...] = jnp.where(head, 0.0, factored)

        for part in range(LEAD // cols):
            edge = slice(part * cols, (part + 1) * cols)

            @pl.when((column == 0) & (j == part))
            def _():
                factored_ref[...] = rows_ref[span, edge]

                if first_chunk:

                    @pl.when(head)
                    def _():
                        factored_ref[...] = lower_ref[span, edge]

    high, low = high_ref[...], low_ref[...]
    product = jnp.dot(panel, high, preferred_element_type=F32)
    product = product + jnp.dot(panel, low, preferred_element_type=F32)
    precond_ref[...] = grad_ref[...].astype(F32) - product

    if first_chunk:

        @pl.when(head)
        def _():
            precond_ref[...] = high_ref[span, :].astype(F32) + low_ref[span, :].astype(F32)


def finish_rows(
    begin, places, damp, share, factor, grad, panel, inverse, lower, high, low,
    lead, across, mine, earlier,
):
    count = len(mine)
    deep, rows = mine[0].shape[1:]
    width, grad_cols = factor.shape[0], grad.shape[1]
    tall = lead.shape[0]
    tiles = rows // ROWS
    start = begin // ROWS
    cols = COLS if width % COLS == 0 else ROWS
    gram_steps, steps = width // cols, grad_cols // cols
    assert steps >= gram_steps and rows % ROWS == 0

    def mine_spec(q):
        return pl.BlockSpec(
            (1, deep, ROWS),
            lambda j, i, p: (p[PLACES + count + q], 0, jnp.where(j == 0, i, tiles - 1)),
        )

    def gram_col(j):
        return jnp.minimum(j, gram_steps - 1)

    def gram_tile(j, i, p):
        return (start + jnp.where(j < gram_steps, i, tiles - 1), gram_col(j))

    grad_spec = pl.BlockSpec((ROWS, cols), lambda j, i, p: (start + i, j))
    factor_spec = pl.BlockSpec((ROWS, cols), gram_tile)
    lead_whole = pl.BlockSpec((LEAD, LEAD), lambda j, i, p: (0, 0))
    small = pl.BlockSpec((GROUP, TILE), lambda j, i, p: (0, 0))
    in_specs = [
        pl.BlockSpec(memory_space=pltpu.SMEM),
        small,
        factor_spec,
        grad_spec,
        pl.BlockSpec((LEAD, cols), lambda j, i, p: (0, gram_col(j))),
        lead_whole,
        pl.BlockSpec((LEAD, cols), lambda j, i, p: (0, j)),
        pl.BlockSpec((LEAD, cols), lambda j, i, p: (0, j)),
        pl.BlockSpec((tall, LEAD), lambda j, i, p: (0, 0)),
        pl.BlockSpec((tall, cols), lambda j, i, p: (0, gram_col(j))),
    ]
    operands = [damp, share, factor, grad, panel, inverse, high, low, lead, across]
    if begin == 0:
        in_specs += [lead_whole]
        operands += [lower]
    in_specs += [mine_spec(q) for q in range(count)]
    operands += mine
    in_specs += [pl.BlockSpec(memory_space=pl.ANY)] * len(earlier)
    aliases = {1 + len(operands) + k: k for k in range(len(earlier))}
    operands += earlier
    return pl.pallas_call(
        lambda *refs: finish_kernel(count, gram_steps, begin == 0, len(earlier), *refs),
        grid_spec=pltpu.PrefetchScalarGridSpec(
            num_scalar_prefetch=1,
            grid=(steps, tiles),
            in_specs=in_specs,
            out_specs=(factor_spec, factor_spec, grad_spec, small),
            scratch_shapes=[
                pltpu.VMEM((rows, tall), BF16),
                pltpu.VMEM((rows, LEAD), F32),
                pltpu.VMEM((LEAD, ROWS), F32),
            ],
        ),
        out_shape=(
            jax.ShapeDtypeStruct(factor.shape, F32),
            jax.ShapeDtypeStruct(factor.shape, F32),
            jax.ShapeDtypeStruct(grad.shape, F32),
            jax.ShapeDtypeStruct((GROUP, TILE), F32),
        ),
        input_output_aliases=aliases,
        compiler_params=pltpu.CompilerParams(vmem_limit_bytes=56 * 1024 * 1024),
        cost_estimate=pl.CostEstimate(
            flops=2 * rows * (tall * (width + LEAD) + LEAD * (6 * LEAD + width + 2 * grad_cols)),
            bytes_accessed=2 * tall * (width + LEAD + rows)
            + rows * (12 * width + 6 * grad_cols)
            + LEAD * (4 * grad_cols + 8 * LEAD + 2 * width),
            transcendentals=0,
        ),
    )(places, *operands)


def after(value, earlier):
    mark = earlier[(0,) * earlier.ndim]
    return jnp.where(mark == mark, value, jnp.zeros_like(value))


def swapped(value, mask):
    size = lax.axis_size("tok")
    return lax.ppermute(value, "tok", [(source, source ^ mask) for source in range(size)])


def gather_members(value, bits):
    pieces = [value]
    for bit in reversed(range(bits)):
        pieces = pieces + [swapped(piece, 1 << bit) for piece in pieces]
    return pieces


def exchange_members(blocks, member, bits, earlier):
    views = [(blocks, 0)]
    count = blocks.shape[0]
    for bit in reversed(range(bits)):
        count = count // 2
        mine = member >> bit & 1
        sent = [
            after(lax.dynamic_slice_in_dim(array, at + (1 - mine) * count, count, 0), earlier)
            for array, at in views
        ]
        kept = [(array, at + mine * count) for array, at in views]
        views = kept + [(swapped(part, 1 << bit), 0) for part in sent]
    return views


def member_order(bits):
    order = [0]
    for bit in reversed(range(bits)):
        order = order + [other ^ (1 << bit) for other in order]
    return order


def down_pairs(bit, group):
    mask = 1 << bit
    return [
        (source, source + mask)
        for source in range(lax.axis_size("tok"))
        if source % group % (2 * mask) == 0
    ]


def from_first_member(value, member, group, bits):
    value = jnp.where(member == 0, value, jnp.zeros_like(value))
    for bit in reversed(range(bits)):
        value = value + lax.ppermute(value, "tok", down_pairs(bit, group))
    return value


def share_of_first(blocks, member, group, bits):
    for bit in reversed(range(bits)):
        half = blocks.shape[0] // 2
        moved = lax.ppermute(blocks[half:], "tok", down_pairs(bit, group))
        blocks = jnp.where(member >> bit & 1 == 1, moved, blocks[:half])
    return blocks[0]


def count_rows(number, row, width):
    index = lax.broadcasted_iota(jnp.int32, (16, width), 0)
    rest = jnp.where(index == row + 1, number % 256, 0)
    return jnp.where(index == row, number // 256, rest).astype(BF16)


def local(grad_rows, routes, counts, factor_old, damping, weight_grad):
    group = lax.axis_size("tok") // 2
    bits = group.bit_length() - 1
    position = lax.axis_index("tok")
    expert = position // group
    member = position % group
    column = lax.axis_index("fac")
    tok_rows, width = grad_rows.shape
    damp = jnp.where(expert == 0, damping[0], damping[1])[None]
    order = [member ^ other for other in member_order(bits)]

    lead_factor = factor_old[:LEAD].astype(BF16).reshape(group, LEAD // group, width)
    lead_factor = share_of_first(lead_factor, member, group, bits)

    live = jnp.arange(tok_rows) < counts[0]
    named = routes[:, 0]
    own = live & (named == expert)
    away = live & (named != expert)
    flags = jnp.stack([own, away])
    ranks = jnp.cumsum(flags.astype(jnp.int32), 1) - 1
    picker = (ranks[:, None, :] == jnp.arange(CAP)[None, :, None]) & flags[:, None, :]
    packed = jnp.dot(
        picker.reshape(2 * CAP, tok_rows).astype(BF16), grad_rows, preferred_element_type=F32
    ).astype(BF16)
    tally = jnp.sum(flags.astype(jnp.int32), 1)
    front = swapped(
        jnp.concatenate([packed[CAP:, :LEAD], count_rows(tally[1], 2, LEAD)], 0), group
    )
    first_part = jnp.concatenate(
        [
            packed[:CAP, :LEAD],
            front[:CAP],
            lead_factor[:, :LEAD],
            front[CAP:] + count_rows(tally[0], 0, LEAD),
        ],
        0,
    )
    incoming = swapped(after(packed[CAP:], front), group)
    quarter = jnp.concatenate([packed[:CAP], incoming, lead_factor], 0)

    ends = [end for end in (LEAD, 2 * LEAD, 2 * LEAD + ROWS) if end < width] + [width]
    chunks = list(zip([0, *ends], ends))
    spread = [lax.all_gather(first_part, "fac")]
    across = gather_members(quarter, bits)
    lead = gather_members(after(spread[0][0], across[1]), bits)
    near_grad = from_first_member(after(weight_grad[:LEAD], lead[1]), member, group, bits)

    places = [member, column, member * width]
    assert len(places) == PLACES
    slots = jnp.stack(places + order).astype(jnp.int32)
    parts = [first_part]
    for (begin, end), gate in zip(chunks[1:], [spread[0], lead[1], lead[1]]):
        parts.append(after(quarter[:, begin:end], gate))
        spread.append(lax.all_gather(parts[-1], "fac"))
    upper, inverse, share = factor_lead(
        slots, damp, factor_old[:LEAD, :LEAD], lead, parts[1:3]
    )
    panel, lead_stack, across_stack = panel_columns(
        slots, share, inverse, lead, across, parts[3:]
    )
    solved = jnp.dot(inverse, near_grad.astype(F32), precision=lax.Precision.HIGH)
    high = solved.astype(BF16)
    low = (solved - high.astype(F32)).astype(BF16)
    lower = upper.T

    results = ()
    gates = [lead[1], panel]
    for (begin, end), part in zip(chunks, spread):
        views = exchange_members(part, member, bits, gates.pop(0))
        places[2] = member * width + begin
        slots = jnp.stack(places + order + [jnp.int32(at) for _, at in views])
        *results, token = finish_rows(
            begin,
            slots.astype(jnp.int32),
            damp,
            share,
            factor_old,
            weight_grad,
            panel,
            inverse,
            lower,
            high,
            low,
            lead_stack,
            across_stack,
            [array for array, _ in views],
            list(results),
        )
        gates.append(token)
    return tuple(results)


def solution(mesh):
    placed = (P("tok", "fac"), P("tok", None), P("tok"), P("tok", "fac"), P(), P("tok", "fac"))
    return jax.shard_map(
        local,
        mesh=mesh,
        in_specs=placed,
        out_specs=(P("tok", "fac"), P("tok", "fac"), P("tok", "fac")),
        check_vma=False,
    )
```

time: 402 us -> 384 us (0.955)
  the two profiles are of different devices: /device:TPU:23 before, /device:TPU:2 now
where the time goes in v3:
time: 384 us; the launch traced here: 382 us
  waiting for transfers between devices  137 us (36%)
  Pallas kernels  123 us (32%)
  other arithmetic  42.5 us (11%)
  between operations  30.3 us (8%)
  local copies, waits for them, and re-layouts  23.8 us (6%)
  starting transfers between devices  17.1 us (4%)
  matrix products  7.81 us (2%)
    pallas_call x4, Pallas kernels, finish_rows(): pl.pallas_call(lambda *refs: finish_kernel(count, gram_steps, begin == 0,...  77.4 us
    ppermute x20, waiting for transfers between devices, swapped(): lax.ppermute(value, 'tok', [(source, source ^ mask) for source in range(s...  67.6 us
    all_gather x1, waiting for transfers between devices, local(): spread = [lax.all_gather(first_part, 'fac')]  38.8 us
    pallas_call x1, Pallas kernels, factor_lead(): pl.pallas_call(lambda *refs: factor_kernel(len(lead), *refs), out_shape=(...  30.2 us
    ppermute x2, waiting for transfers between devices, from_first_member(): value = value + lax.ppermute(value, 'tok', down_pairs(bit, group))  30.1 us
    select_n x15, other arithmetic, after(): return jnp.where(mark == mark, value, jnp.zeros_like(value))  24.2 us
    pallas_call x1, Pallas kernels, panel_columns(): pl.pallas_call(lambda *refs: panel_kernel(count, *refs), grid=(width // c...  15.4 us
    ppermute x20, starting transfers between devices, swapped(): lax.ppermute(value, 'tok', [(source, source ^ mask) for source in range(s...  10.3 us
  transfers between devices with their start and end apart: 28, of which 9 were waited for; matrix products, arithmetic and copies ran while one was open for 16% of the time, Pallas kernels for 28%

profile of v3, /device:TPU:2, one launch (start us, length us, event | category | flops | bytes accessed | tf_op | source)
XLA Modules:
  0.0 381.8 jit_solution(2134485556868866616)
XLA Ops:
  7.2 4.4 %convert.3 = bf16[1536,1536]{1,0:T(8,128)(2,1)S(1)} convert(f32[1536,1536]{1,0:T(8,128)} %refs_3_.7) | non-fusion elementwise | flops 2359296 | bytes 14155776 | tf_op jit(solution)/shard_map/convert
  29.7 3.2 collective-permute-done
  40.0 21.4 %collective-permute-done.1 = bf16[320,1536]{1,0:T(8,128)(2,1)S(1)} collective-permute-done((bf16[320,1536]{1,0:T(8,128)(2,1)S(1)}, bf16[320,1536]{1,0:T(8,128)(2,1)S(1)}, u32[]{:S(2)}, u32[]{:S(2)}) %collective-permute-start.1) | collective-permute-done | bytes 983072 | tf_op jit(solution)/shard_map/ppermute | solution.py:417
  63.0 38.8 %all-gather.9.cloned.1.call-done = bf16[3136,512]{1,0:T(8,128)(2,1)} async-done(((bf16[784,512]{1,0:T(8,128)(2,1)}), bf16[3136,512]{1,0:T(8,128)(2,1)}) %all-gather.9.cloned.1.call-update) | async-done | bytes 3211280 | tf_op jit(solution)/shard_map/all_gather | solution.py:521
  106.3 8.5 %collective-permute-done.4.refs_8_ = bf16[768,1536]{1,0:T(8,128)(2,1)} collective-permute-done((bf16[768,1536]{1,0:T(8,128)(2,1)}, bf16[768,1536]{1,0:T(8,128)(2,1)}, u32[]{:S(2)}, u32[]{:S(2)}) %collective-permute-start.4) | collective-permute-done | bytes 2359328 | tf_op jit(solution)/shard_map/ppermute | solution.py:417
  118.9 17.2 %collective-permute-done.5.refs_4_ = bf16[784,512]{1,0:T(8,128)(2,1)} collective-permute-done((bf16[784,512]{1,0:T(8,128)(2,1)S(1)}, bf16[784,512]{1,0:T(8,128)(2,1)}, u32[]{:S(2)}, u32[]{:S(2)}) %collective-permute-start.5) | collective-permute-done | bytes 802848 | tf_op jit(solution)/shard_map/ppermute | solution.py:417
  138.6 3.1 select_select_fusion
  149.7 2.7 dynamic-slice_select_fusion
  152.3 30.1 %collective-permute-done.10 = bf16[512,2048]{1,0:T(8,128)(2,1)} collective-permute-done((bf16[512,2048]{1,0:T(8,128)(2,1)}, bf16[512,2048]{1,0:T(8,128)(2,1)}, u32[]{:S(2)}, u32[]{:S(2)}) %collective-permute-start.10) | collective-permute-done | bytes 2097184 | tf_op jit(solution)/shard_map/ppermute | solution.py:461
  182.5 3.8 fusion.13
  186.3 2.7 collective-permute-start.11
  189.0 30.2 %shard_map.85 = (f32[512,512]{1,0:T(8,128)S(1)}, f32[512,512]{1,0:T(8,128)S(1)}, f32[8,128]{1,0:T(8,128)S(1)}) custom-call(s32[7]{0:T(128)S(1)} %stack.46.refs_0_, f32[1]{0:T(128)} %bitcast.10.refs_1_, f32[512,512]{1,0:T(8,128)S(1)} %slice.113.refs_2_, bf16[784,512]{1,0:T(8,128)(2,1)S(1)} %slice_select_fusion.1.refs_3_, ...), custom_call_target="tpu_custom_call" | custom-call | flops 24999999488 | bytes 6291456 | tf_op jit(solution)/shard_map/pallas_call | solution.py:162
  221.7 15.4 %shard_map.86 = (bf16[512,1536]{1,0:T(8,128)(2,1)}, bf16[2560,512]{1,0:T(8,128)(2,1)}, bf16[2560,1536]{1,0:T(8,128)(2,1)}) custom-call(s32[7]{0:T(128)} %copy-done.10, f32[8,128]{1,0:T(8,128)} %copy-done.9, f32[512,512]{1,0:T(8,128)} %copy-done.2, bf16[784,512]{1,0:T(8,128)(2,1)} %copy-done.8, bf16[784,512]{1,0:T(8,128)(2,1)} %collective-permute-done.5.refs_4_, ...), custom_call_target="tpu_custom_call" | custom-call | flops 8858370048 | bytes 24117248 | tf_op jit(solution)/shard_map/pallas_call | solution.py:207
  239.6 2.7 dynamic-slice_select_fusion.1
  250.8 2.1 dynamic-slice_select_fusion.7
  252.9 6.6 %subtract_convert_fusion = (bf16[512,2048]{1,0:T(8,128)(2,1)}, bf16[512,2048]{1,0:T(8,128)(2,1)}) fusion(f32[512,512]{1,0:T(8,128)S(1)} %copy-done.3, bf16[512,2048]{1,0:T(8,128)(2,1)} %fusion.13, bf16[512,2048]{1,0:T(8,128)(2,1)} %collective-permute-done.11), kind=kOutput, calls=%fused_computation | convolution fusion | flops 3226468352 | bytes 9437184 | tf_op jit(solution)/shard_map/dot_general | solution.py:539
  259.6 3.5 collective-permute-done.12.refs_12_
  263.1 2.2 dynamic-slice_select_fusion.6
  265.2 23.6 %shard_map.87 = (f32[1536,1536]{1,0:T(8,128)}, f32[1536,1536]{1,0:T(8,128)}, f32[1536,2048]{1,0:T(8,128)}, f32[8,128]{1,0:T(8,128)}) custom-call(s32[11]{0:T(128)} %stack.102.refs_0_, f32[1]{0:T(128)} %bitcast.10.refs_1_, f32[8,128]{1,0:T(8,128)} %copy-done.9, f32[1536,1536]{1,0:T(8,128)} %refs_3_.7, bf16[1536,2048]{1,0:T(8,128)(2,1)} %refs_4_.7, ...), custom_call_target="tpu_custom_call" | custom-call | flops 9932111872 | bytes 36700160 | tf_op jit(solution)/shard_map/pallas_call | solution.py:379
  292.5 2.4 collective-permute-start.21
  296.2 22.5 %shard_map.88 = (f32[1536,1536]{1,0:T(8,128)}, f32[1536,1536]{1,0:T(8,128)}, f32[1536,2048]{1,0:T(8,128)}, f32[8,128]{1,0:T(8,128)}) custom-call(s32[11]{0:T(128)} %stack.50.refs_0_, f32[1]{0:T(128)} %bitcast.10.refs_1_, f32[8,128]{1,0:T(8,128)} %copy-done.9, f32[1536,1536]{1,0:T(8,128)} %refs_3_.7, ...), custom_call_target="tpu_custom_call", output_to_operand_aliasing={{0}: (15, {}), {1}: (16, {}), {2}: (17, {})} | custom-call | flops 9932111872 | bytes 36700160 | tf_op jit(solution)/shard_map/pallas_call | solution.py:379
  328.0 13.8 %collective-permute-done.18.refs_12_ = bf16[2,768,256]{2,1,0:T(8,128)(2,1)S(1)} collective-permute-done((bf16[2,768,256]{2,1,0:T(8,128)(2,1)S(1)}, bf16[2,768,256]{2,1,0:T(8,128)(2,1)S(1)}, u32[]{:S(2)}, u32[]{:S(2)}) %collective-permute-start.18) | collective-permute-done | bytes 786464 | tf_op jit(solution)/shard_map/ppermute | solution.py:417
  342.9 15.5 %shard_map.89 = (f32[1536,1536]{1,0:T(8,128)}, f32[1536,1536]{1,0:T(8,128)}, f32[1536,2048]{1,0:T(8,128)}, f32[8,128]{1,0:T(8,128)}) custom-call(s32[11]{0:T(128)} %stack.104.refs_0_, f32[1]{0:T(128)} %bitcast.10.refs_1_, f32[8,128]{1,0:T(8,128)} %copy-done.9, f32[1536,1536]{1,0:T(8,128)} %refs_3_.7, ...), custom_call_target="tpu_custom_call", output_to_operand_aliasing={{0}: (15, {}), {1}: (16, {}), {2}: (17, {})} | custom-call | flops 4966055936 | bytes 27525120 | tf_op jit(solution)/shard_map/pallas_call | solution.py:379
  359.3 15.9 %shard_map.90 = (f32[1536,1536]{1,0:T(8,128)}, f32[1536,1536]{1,0:T(8,128)}, f32[1536,2048]{1,0:T(8,128)}, f32[8,128]{1,0:T(8,128)}) custom-call(s32[11]{0:T(128)} %stack.44.refs_0_, f32[1]{0:T(128)} %bitcast.10.refs_1_, f32[8,128]{1,0:T(8,128)} %copy-done.9, f32[1536,1536]{1,0:T(8,128)} %refs_3_.7, ...), custom_call_target="tpu_custom_call", output_to_operand_aliasing={{0}: (15, {}), {1}: (16, {}), {2}: (17, {})} | custom-call | flops 4966055936 | bytes 27525120 | tf_op jit(solution)/shard_map/pallas_call | solution.py:379
  (159 shorter events, 59.3 us)
Async XLA Ops:
  7.2 94.5 %all-gather.9.cloned.1.call-start = ((), (), s32[]{:S(2)}) async-start(), calls=%async_computation | async-start | bytes 4014080 | tf_op jit(solution)/shard_map/all_gather | solution.py:521
  35.8 203.9 %all-gather.13.cloned.1.call-start = ((), (), s32[]{:S(2)}) async-start(), calls=%async_computation.2 | async-start | bytes 3932160 | tf_op jit(solution)/shard_map/all_gather | solution.py:532
  38.4 23.0 %collective-permute-start.1 = (bf16[320,1536]{1,0:T(8,128)(2,1)S(1)}, bf16[320,1536]{1,0:T(8,128)(2,1)S(1)}, u32[]{:S(2)}, u32[]{:S(2)}) collective-permute-start(bf16[320,1536]{1,0:T(8,128)(2,1)S(1)} %get-tuple-element.54), channel_id=1, source_target_pairs={{0,16},{4,20},{8,24},{12,28},{16,0},{20,4},{24,8},{28,12},{1,17},{... | collective-permute-start | bytes 2949128 | tf_op jit(solution)/shard_map/ppermute | solution.py:417
  63.0 51.9 %collective-permute-start.4 = (bf16[768,1536]{1,0:T(8,128)(2,1)}, bf16[768,1536]{1,0:T(8,128)(2,1)}, u32[]{:S(2)}, u32[]{:S(2)}) collective-permute-start(bf16[768,1536]{1,0:T(8,128)(2,1)} %pad_maximum_fusion.refs_7_), channel_id=1, source_target_pairs={{0,8},{4,12},{8,0},{12,4},{16,24},{20,28},{24,16},{28,20},{1,9},{5... | collective-permute-start | bytes 7077896 | tf_op jit(solution)/shard_map/ppermute | solution.py:417
  106.3 185.0 %all-gather.15.cloned.1.call-start = ((), (), s32[]{:S(2)}) async-start(), calls=%async_computation.3 | async-start | bytes 1966080 | tf_op jit(solution)/shard_map/all_gather | solution.py:532
  118.6 17.5 %collective-permute-start.5 = (bf16[784,512]{1,0:T(8,128)(2,1)S(1)}, bf16[784,512]{1,0:T(8,128)(2,1)}, u32[]{:S(2)}, u32[]{:S(2)}) collective-permute-start(bf16[784,512]{1,0:T(8,128)(2,1)S(1)} %slice_select_fusion.1.refs_3_), channel_id=1, source_target_pairs={{0,8},{4,12},{8,0},{12,4},{16,24},{20,28},{24,16},{28,20},{1,9},{5... | collective-permute-start | bytes 2408456 | tf_op jit(solution)/shard_map/ppermute | solution.py:417
  141.7 40.8 %collective-permute-start.10 = (bf16[512,2048]{1,0:T(8,128)(2,1)}, bf16[512,2048]{1,0:T(8,128)(2,1)}, u32[]{:S(2)}, u32[]{:S(2)}) collective-permute-start(bf16[512,2048]{1,0:T(8,128)(2,1)} %select_select_fusion), channel_id=1, source_target_pairs={{0,8},{16,24},{1,9},{17,25},{2,10},{18,26},{3,11},{19,27}} | collective-permute-start | bytes 6291464 | tf_op jit(solution)/shard_map/ppermute | solution.py:461
  146.5 75.2 %collective-permute-start.8 = (bf16[768,1536]{1,0:T(8,128)(2,1)}, bf16[768,1536]{1,0:T(8,128)(2,1)}, u32[]{:S(2)}, u32[]{:S(2)}) collective-permute-start(bf16[768,1536]{1,0:T(8,128)(2,1)} %pad_maximum_fusion.refs_7_), channel_id=1, source_target_pairs={{0,4},{4,0},{8,12},{12,8},{16,20},{20,16},{24,28},{28,24},{1,5},{5... | collective-permute-start | bytes 7077896 | tf_op jit(solution)/shard_map/ppermute | solution.py:417
  146.5 75.2 %collective-permute-start.9 = (bf16[768,1536]{1,0:T(8,128)(2,1)}, bf16[768,1536]{1,0:T(8,128)(2,1)}, u32[]{:S(2)}, u32[]{:S(2)}) collective-permute-start(bf16[768,1536]{1,0:T(8,128)(2,1)} %collective-permute-done.4.refs_8_), channel_id=1, source_target_pairs={{0,4},{4,0},{8,12},{12,8},{16,20},{20,16},{24,28},{28,24},{1,5},{5... | collective-permute-start | bytes 7077896 | tf_op jit(solution)/shard_map/ppermute | solution.py:417
  147.0 39.2 %collective-permute-start.6 = (bf16[784,512]{1,0:T(8,128)(2,1)S(1)}, bf16[784,512]{1,0:T(8,128)(2,1)}, u32[]{:S(2)}, u32[]{:S(2)}) collective-permute-start(bf16[784,512]{1,0:T(8,128)(2,1)S(1)} %slice_select_fusion.1.refs_3_), channel_id=1, source_target_pairs={{0,4},{4,0},{8,12},{12,8},{16,20},{20,16},{24,28},{28,24},{1,5},{5... | collective-permute-start | bytes 2408456 | tf_op jit(solution)/shard_map/ppermute | solution.py:417
  147.1 41.8 %collective-permute-start.7 = (bf16[784,512]{1,0:T(8,128)(2,1)}, bf16[784,512]{1,0:T(8,128)(2,1)}, u32[]{:S(2)}, u32[]{:S(2)}) collective-permute-start(bf16[784,512]{1,0:T(8,128)(2,1)} %collective-permute-done.5.refs_4_), channel_id=1, source_target_pairs={{0,4},{4,0},{8,12},{12,8},{16,20},{20,16},{24,28},{28,24},{1,5},{5... | collective-permute-start | bytes 2408456 | tf_op jit(solution)/shard_map/ppermute | solution.py:417
  149.6 171.6 %all-gather.11.cloned.1.call-start = ((), (), s32[]{:S(2)}) async-start(), calls=%async_computation.1 | async-start | bytes 1966080 | tf_op jit(solution)/shard_map/all_gather | solution.py:532
  182.5 63.2 %collective-permute-start.15 = (bf16[2,784,512]{2,1,0:T(8,128)(2,1)}, bf16[2,784,512]{2,1,0:T(8,128)(2,1)}, u32[]{:S(2)}, u32[]{:S(2)}) collective-permute-start(bf16[2,784,512]{2,1,0:T(8,128)(2,1)} %dynamic-slice_select_fusion), channel_id=1, source_target_pairs={{0,8},{4,12},{8,0},{12,4},{16,24},{20,28},{24,16},{28,20},{1,9},{5... | collective-permute-start | bytes 4816904 | tf_op jit(solution)/shard_map/ppermute | solution.py:417
  186.3 66.7 %collective-permute-start.11 = (bf16[512,2048]{1,0:T(8,128)(2,1)}, bf16[512,2048]{1,0:T(8,128)(2,1)}, u32[]{:S(2)}, u32[]{:S(2)}) collective-permute-start(bf16[512,2048]{1,0:T(8,128)(2,1)} %fusion.13), channel_id=1, source_target_pairs={{0,4},{8,12},{16,20},{24,28},{1,5},{9,13},{17,21},{25,29},{2,6},{1... | collective-permute-start | bytes 6291464 | tf_op jit(solution)/shard_map/ppermute | solution.py:461
  242.3 20.8 %collective-permute-start.12 = (bf16[2,768,512]{2,1,0:T(8,128)(2,1)}, bf16[2,768,512]{2,1,0:T(8,128)(2,1)}, u32[]{:S(2)}, u32[]{:S(2)}) collective-permute-start(bf16[2,768,512]{2,1,0:T(8,128)(2,1)} %dynamic-slice_select_fusion.1), channel_id=1, source_target_pairs={{0,8},{4,12},{8,0},{12,4},{16,24},{20,28},{24,16},{28,20},{1,9},{5... | collective-permute-start | bytes 4718600 | tf_op jit(solution)/shard_map/ppermute | solution.py:417
  245.5 19.7 %collective-permute-start.16 = (bf16[1,784,512]{2,1,0:T(8,128)(2,1)S(1)}, bf16[1,784,512]{2,1,0:T(8,128)(2,1)}, u32[]{:S(2)}, u32[]{:S(2)}) collective-permute-start(bf16[1,784,512]{2,1,0:T(8,128)(2,1)S(1)} %dynamic-slice_select_fusion.3), channel_id=1, source_target_pairs={{0,4},{4,0},{8,12},{12,8},{16,20},{20,16},{24,28},{28,24},{1,5},{5... | collective-permute-start | bytes 2408456 | tf_op jit(solution)/shard_map/ppermute | solution.py:417
  247.7 17.5 %collective-permute-start.17 = (bf16[1,784,512]{2,1,0:T(8,128)(2,1)}, bf16[1,784,512]{2,1,0:T(8,128)(2,1)}, u32[]{:S(2)}, u32[]{:S(2)}) collective-permute-start(bf16[1,784,512]{2,1,0:T(8,128)(2,1)} %dynamic-slice_select_fusion.2), channel_id=1, source_target_pairs={{0,4},{4,0},{8,12},{12,8},{16,20},{20,16},{24,28},{28,24},{1,5},{5... | collective-permute-start | bytes 2408456 | tf_op jit(solution)/shard_map/ppermute | solution.py:417
  252.9 42.0 %collective-permute-start.13 = (bf16[1,768,512]{2,1,0:T(8,128)(2,1)}, bf16[1,768,512]{2,1,0:T(8,128)(2,1)S(1)}, u32[]{:S(2)}, u32[]{:S(2)}) collective-permute-start(bf16[1,768,512]{2,1,0:T(8,128)(2,1)} %dynamic-slice_select_fusion.7), channel_id=1, source_target_pairs={{0,4},{4,0},{8,12},{12,8},{16,20},{20,16},{24,28},{28,24},{1,5},{5... | collective-permute-start | bytes 2359304 | tf_op jit(solution)/shard_map/ppermute | solution.py:417
  265.2 29.7 %collective-permute-start.14 = (bf16[1,768,512]{2,1,0:T(8,128)(2,1)}, bf16[1,768,512]{2,1,0:T(8,128)(2,1)S(1)}, u32[]{:S(2)}, u32[]{:S(2)}) collective-permute-start(bf16[1,768,512]{2,1,0:T(8,128)(2,1)} %dynamic-slice_select_fusion.6), channel_id=1, source_target_pairs={{0,4},{4,0},{8,12},{12,8},{16,20},{20,16},{24,28},{28,24},{1,5},{5... | collective-permute-start | bytes 2359304 | tf_op jit(solution)/shard_map/ppermute | solution.py:417
  292.5 31.8 %collective-permute-start.21 = (bf16[2,768,256]{2,1,0:T(8,128)(2,1)S(1)}, bf16[2,768,256]{2,1,0:T(8,128)(2,1)S(1)}, u32[]{:S(2)}, u32[]{:S(2)}) collective-permute-start(bf16[2,768,256]{2,1,0:T(8,128)(2,1)S(1)} %dynamic-slice_select_fusion.4), channel_id=1, source_target_pairs={{0,8},{4,12},{8,0},{12,4},{16,24},{20,28},{24,16},{28,20},{1,9},{5... | collective-permute-start | bytes 2359304 | tf_op jit(solution)/shard_map/ppermute | solution.py:417
  322.4 19.4 %collective-permute-start.18 = (bf16[2,768,256]{2,1,0:T(8,128)(2,1)S(1)}, bf16[2,768,256]{2,1,0:T(8,128)(2,1)S(1)}, u32[]{:S(2)}, u32[]{:S(2)}) collective-permute-start(bf16[2,768,256]{2,1,0:T(8,128)(2,1)S(1)} %dynamic-slice_select_fusion.5), channel_id=1, source_target_pairs={{0,8},{4,12},{8,0},{12,4},{16,24},{20,28},{24,16},{28,20},{1,9},{5... | collective-permute-start | bytes 2359304 | tf_op jit(solution)/shard_map/ppermute | solution.py:417
  324.3 17.6 %collective-permute-start.22 = (bf16[1,768,256]{2,1,0:T(8,128)(2,1)}, bf16[1,768,256]{2,1,0:T(8,128)(2,1)S(1)}, u32[]{:S(2)}, u32[]{:S(2)}) collective-permute-start(bf16[1,768,256]{2,1,0:T(8,128)(2,1)} %dynamic-slice_select_fusion.9), channel_id=1, source_target_pairs={{0,4},{4,0},{8,12},{12,8},{16,20},{20,16},{24,28},{28,24},{1,5},{5... | collective-permute-start | bytes 1179656 | tf_op jit(solution)/shard_map/ppermute | solution.py:417
  325.1 16.8 %collective-permute-start.23 = (bf16[1,768,256]{2,1,0:T(8,128)(2,1)}, bf16[1,768,256]{2,1,0:T(8,128)(2,1)S(1)}, u32[]{:S(2)}, u32[]{:S(2)}) collective-permute-start(bf16[1,768,256]{2,1,0:T(8,128)(2,1)} %dynamic-slice_select_fusion.8), channel_id=1, source_target_pairs={{0,4},{4,0},{8,12},{12,8},{16,20},{20,16},{24,28},{28,24},{1,5},{5... | collective-permute-start | bytes 1179656 | tf_op jit(solution)/shard_map/ppermute | solution.py:417
  327.9 30.5 %collective-permute-start.19 = (bf16[1,768,256]{2,1,0:T(8,128)(2,1)S(1)}, bf16[1,768,256]{2,1,0:T(8,128)(2,1)S(1)}, u32[]{:S(2)}, u32[]{:S(2)}) collective-permute-start(bf16[1,768,256]{2,1,0:T(8,128)(2,1)S(1)} %dynamic-slice_select_fusion.11), channel_id=1, source_target_pairs={{0,4},{4,0},{8,12},{12,8},{16,20},{20,16},{24,28},{28,24},{1,5},{5... | collective-permute-start | bytes 1179656 | tf_op jit(solution)/shard_map/ppermute | solution.py:417
  (29 other events, 363.2 us)
Sparse Core Ops, SparseCore 0:
  35.9 65.8 all-gather.8
  106.4 62.1 all-gather.12
  170.2 35.7 all-gather.14
  249.6 38.2 all-gather.10

commit v4 on v3

--- a/solution.py
+++ b/solution.py
@@ -12,6 +12,7 @@
 ROWS = 256
 COLS = 512
 PLACES = 3
+NO_COST = pl.CostEstimate(flops=1, bytes_accessed=1, transcendentals=0)
 DECAY = 0.8
 
 HIGHEST = lax.Precision.HIGHEST
@@ -155,35 +156,31 @@
     lax.fori_loop(0, steps, tile_step, 0)
 
 
-def factor_lead(places, damp, exact, lead, earlier):
+def factor_lead(places, damp, exact, lead):
     shape = jax.ShapeDtypeStruct((LEAD, LEAD), F32)
     vmem = pl.BlockSpec(memory_space=pltpu.VMEM)
     smem = pl.BlockSpec(memory_space=pltpu.SMEM)
     return pl.pallas_call(
         lambda *refs: factor_kernel(len(lead), *refs),
         out_shape=(shape, shape, jax.ShapeDtypeStruct((GROUP, TILE), F32)),
-        in_specs=[smem, smem]
-        + [vmem] * (1 + len(lead))
-        + [pl.BlockSpec(memory_space=pl.ANY)] * len(earlier),
+        in_specs=[smem, smem] + [vmem] * (1 + len(lead)),
         out_specs=(vmem, vmem, vmem),
         scratch_shapes=[pltpu.VMEM((LEAD, LEAD), F32)],
         compiler_params=pltpu.CompilerParams(vmem_limit_bytes=32 * 1024 * 1024),
-        cost_estimate=pl.CostEstimate(
-            flops=25_000_000_000, bytes_accessed=6 * LEAD * LEAD * 4, transcendentals=LEAD
-        ),
-    )(places, damp, exact, *lead, *earlier)
+        cost_estimate=NO_COST,
+    )(places, damp, exact, *lead)
 
 
 def panel_kernel(count, places_ref, share_ref, inverse_ref, *refs):
-    lead, across = refs[:count], refs[count : 2 * count]
+    lead, own, other = refs[:count], refs[count : 2 * count], refs[2 * count : 3 * count]
     out_ref, lead_ref, across_ref, near_ref = refs[-4:]
     side = LEAD // count
     depth = 2 * CAP
     for q in range(count):
-        span = slice(q * depth, (q + 1) * depth)
-        across_ref[span, :] = across[q][:depth, :]
+        across_ref[q * depth : q * depth + CAP, :] = own[q][:CAP, :]
+        across_ref[q * depth + CAP : (q + 1) * depth, :] = other[q][...]
         begin = pl.multiple_of(places_ref[PLACES + q] * side, side)
-        near_ref[pl.ds(begin, side), :] = across[q][depth : depth + side, :].astype(F32)
+        near_ref[pl.ds(begin, side), :] = own[q][CAP:, :].astype(F32)
 
     @pl.when(pl.program_id(0) == 0)
     def _():
@@ -197,9 +194,9 @@
     ).astype(BF16)
 
 
-def panel_columns(places, share, inverse, lead, across, earlier):
+def panel_columns(places, share, inverse, lead, own, other):
     count = len(lead)
-    width = across[0].shape[1]
+    width = own[0].shape[1]
     cols = COLS if width % COLS == 0 else ROWS
     tall = 2 * CAP * count
     whole = lambda height: pl.BlockSpec((height, LEAD), lambda j: (0, 0))
@@ -218,24 +215,20 @@
             whole(LEAD),
         ]
         + [whole(lead[0].shape[0])] * count
-        + [tiled(across[0].shape[0])] * count
-        + [pl.BlockSpec(memory_space=pl.ANY)] * len(earlier),
+        + [tiled(own[0].shape[0])] * count
+        + [tiled(CAP)] * count,
         out_specs=(tiled(LEAD), whole(tall), tiled(tall)),
         scratch_shapes=[pltpu.VMEM((LEAD, cols), F32)],
         compiler_params=pltpu.CompilerParams(vmem_limit_bytes=56 * 1024 * 1024),
-        cost_estimate=pl.CostEstimate(
-            flops=2 * width * LEAD * (tall + 6 * LEAD),
-            bytes_accessed=4 * tall * (width + LEAD) + 4 * LEAD * width,
-            transcendentals=0,
-        ),
-    )(places, share, inverse, *lead, *across, *earlier)
+        cost_estimate=NO_COST,
+    )(places, share, inverse, *lead, *own, *other)
 
 
 def finish_kernel(
     count,
     gram_steps,
     first_chunk,
-    aliased,
+    unread,
     places_ref,
     damp_ref,
     share_ref,
@@ -252,15 +245,14 @@
     if first_chunk:
         lower_ref, *refs = refs
     mine = refs[:count]
-    outs = refs[count + aliased :]
+    outs = refs[count + unread :]
     running_ref, factored_ref, precond_ref, token_ref, mine_ref, rows_ref, first_ref = outs
     j, i = pl.program_id(0), pl.program_id(1)
     member, column, base = places_ref[0], places_ref[1], places_ref[2]
     share, damp = share_ref[:1, :1], damp_ref[0]
-    height = ROWS
+    height, cols = running_ref.shape
     depth = 2 * CAP
     side = LEAD // count
-    cols = running_ref.shape[1]
     span = pl.ds(pl.multiple_of(i * height, height), height)
     head = (member == 0) & first_chunk
 
@@ -327,21 +319,22 @@
 
 def finish_rows(
     begin, places, damp, share, factor, grad, panel, inverse, lower, high, low,
-    lead, across, mine, earlier,
+    lead, across, mine, results, earlier,
 ):
     count = len(mine)
     deep, rows = mine[0].shape[1:]
     width, grad_cols = factor.shape[0], grad.shape[1]
     tall = lead.shape[0]
-    tiles = rows // ROWS
-    start = begin // ROWS
+    height = min(rows, COLS)
+    tiles = rows // height
+    start = begin // height
     cols = COLS if width % COLS == 0 else ROWS
     gram_steps, steps = width // cols, grad_cols // cols
-    assert steps >= gram_steps and rows % ROWS == 0
+    assert steps >= gram_steps and rows % height == 0 and begin % height == 0
 
     def mine_spec(q):
         return pl.BlockSpec(
-            (1, deep, ROWS),
+            (1, deep, height),
             lambda j, i, p: (p[PLACES + count + q], 0, jnp.where(j == 0, i, tiles - 1)),
         )
 
@@ -351,8 +344,8 @@
     def gram_tile(j, i, p):
         return (start + jnp.where(j < gram_steps, i, tiles - 1), gram_col(j))
 
-    grad_spec = pl.BlockSpec((ROWS, cols), lambda j, i, p: (start + i, j))
-    factor_spec = pl.BlockSpec((ROWS, cols), gram_tile)
+    grad_spec = pl.BlockSpec((height, cols), lambda j, i, p: (start + i, j))
+    factor_spec = pl.BlockSpec((height, cols), gram_tile)
     lead_whole = pl.BlockSpec((LEAD, LEAD), lambda j, i, p: (0, 0))
     small = pl.BlockSpec((GROUP, TILE), lambda j, i, p: (0, 0))
     in_specs = [
@@ -373,11 +366,12 @@
         operands += [lower]
     in_specs += [mine_spec(q) for q in range(count)]
     operands += mine
-    in_specs += [pl.BlockSpec(memory_space=pl.ANY)] * len(earlier)
-    aliases = {1 + len(operands) + k: k for k in range(len(earlier))}
-    operands += earlier
+    aliases = {1 + len(operands) + k: k for k in range(len(results))}
+    operands += [*results, *earlier]
+    unread = len(results) + len(earlier)
+    in_specs += [pl.BlockSpec(memory_space=pl.ANY)] * unread
     return pl.pallas_call(
-        lambda *refs: finish_kernel(count, gram_steps, begin == 0, len(earlier), *refs),
+        lambda *refs: finish_kernel(count, gram_steps, begin == 0, unread, *refs),
         grid_spec=pltpu.PrefetchScalarGridSpec(
             num_scalar_prefetch=1,
             grid=(steps, tiles),
@@ -386,7 +380,7 @@
             scratch_shapes=[
                 pltpu.VMEM((rows, tall), BF16),
                 pltpu.VMEM((rows, LEAD), F32),
-                pltpu.VMEM((LEAD, ROWS), F32),
+                pltpu.VMEM((LEAD, height), F32),
             ],
         ),
         out_shape=(
@@ -397,13 +391,7 @@
         ),
         input_output_aliases=aliases,
         compiler_params=pltpu.CompilerParams(vmem_limit_bytes=56 * 1024 * 1024),
-        cost_estimate=pl.CostEstimate(
-            flops=2 * rows * (tall * (width + LEAD) + LEAD * (6 * LEAD + width + 2 * grad_cols)),
-            bytes_accessed=2 * tall * (width + LEAD + rows)
-            + rows * (12 * width + 6 * grad_cols)
-            + LEAD * (4 * grad_cols + 8 * LEAD + 2 * width),
-            transcendentals=0,
-        ),
+        cost_estimate=NO_COST,
     )(places, *operands)
 
 
@@ -424,16 +412,66 @@
     return pieces
 
 
+def copy_kernel(plans, starts_ref, *refs):
+    outs, sems = refs[-1 - len(plans) : -1], refs[-1]
+    copies = []
+    for number, (count, axis, begin) in enumerate(plans):
+        source, out = refs[number], outs[number]
+        rows = out.shape[-2] // 32 * 16
+        for part in (slice(0, rows), slice(rows, out.shape[-2])):
+            if axis is None:
+                pairs = [
+                    (source.at[starts_ref[number] + k, part], out.at[k, part])
+                    for k in range(count)
+                ]
+            else:
+                pairs = [(source.at[part, begin : begin + out.shape[1]], out.at[part])]
+            copies += [
+                pltpu.make_async_copy(before, after, sems.at[len(copies) + k])
+                for k, (before, after) in enumerate(pairs)
+            ]
+    for copy in copies:
+        copy.start()
+    for copy in copies:
+        copy.wait()
+
+
+def copied(requests, earlier):
+    plans, shapes, starts, total = [], [], [], 0
+    for array, begin, size in requests:
+        if array.ndim == 3:
+            plans.append((size, None, None))
+            shapes.append((size, *array.shape[1:]))
+            starts.append(begin)
+            total += 2 * size
+        else:
+            plans.append((1, 1, begin))
+            shapes.append((array.shape[0], size - begin))
+            starts.append(0)
+            total += 2
+    anywhere = pl.BlockSpec(memory_space=pl.ANY)
+    arrays = [array for array, _, _ in requests]
+    return pl.pallas_call(
+        lambda *refs: copy_kernel(plans, *refs),
+        in_specs=[pl.BlockSpec(memory_space=pltpu.SMEM)]
+        + [anywhere] * (len(arrays) + len(earlier)),
+        out_specs=[anywhere] * len(plans),
+        out_shape=[jax.ShapeDtypeStruct(shape, BF16) for shape in shapes],
+        scratch_shapes=[pltpu.SemaphoreType.DMA((total,))],
+        cost_estimate=NO_COST,
+    )(jnp.stack([jnp.int32(start) for start in starts]), *arrays, *earlier)
+
+
 def exchange_members(blocks, member, bits, earlier):
     views = [(blocks, 0)]
+    sent = []
     count = blocks.shape[0]
     for bit in reversed(range(bits)):
         count = count // 2
         mine = member >> bit & 1
-        sent = [
-            after(lax.dynamic_slice_in_dim(array, at + (1 - mine) * count, count, 0), earlier)
-            for array, at in views
-        ]
+        sent = copied(
+            [(array, at + (1 - mine) * count, count) for array, at in views], earlier
+        )
         kept = [(array, at + mine * count) for array, at in views]
         views = kept + [(swapped(part, 1 << bit), 0) for part in sent]
     return views
@@ -455,10 +493,12 @@
     ]
 
 
-def from_first_member(value, member, group, bits):
-    value = jnp.where(member == 0, value, jnp.zeros_like(value))
+def from_first_member(value, member, group, bits, earlier):
     for bit in reversed(range(bits)):
-        value = value + lax.ppermute(value, "tok", down_pairs(bit, group))
+        if 1 << bit < group // 2:
+            value = after(value, earlier)
+        moved = lax.ppermute(value, "tok", down_pairs(bit, group))
+        value = jnp.where(member >> bit & 1 == 1, moved, value)
     return value
 
 
@@ -514,37 +554,39 @@
         0,
     )
     incoming = swapped(after(packed[CAP:], front), group)
-    quarter = jnp.concatenate([packed[:CAP], incoming, lead_factor], 0)
+    outgoing = jnp.concatenate([packed[:CAP], lead_factor], 0)
 
     ends = [end for end in (LEAD, 2 * LEAD, 2 * LEAD + ROWS) if end < width] + [width]
     chunks = list(zip([0, *ends], ends))
-    spread = [lax.all_gather(first_part, "fac")]
-    across = gather_members(quarter, bits)
-    lead = gather_members(after(spread[0][0], across[1]), bits)
-    near_grad = from_first_member(after(weight_grad[:LEAD], lead[1]), member, group, bits)
+    parts = [first_part]
+    quarter = jnp.concatenate([packed[:CAP], incoming, lead_factor], 0)
+    for begin, end in chunks[1:]:
+        parts += copied([(quarter, begin, end)], [parts[-1]])
+    spread = [lax.all_gather(part, "fac") for part in parts]
+    across_own = gather_members(outgoing, bits)
+    across_other = gather_members(incoming, bits)
+    earlier = [across_own[1], across_other[1], *parts[1:]]
+    lead = gather_members(copied([(spread[0], 0, 1)], earlier)[0][0], bits)
 
     places = [member, column, member * width]
     assert len(places) == PLACES
     slots = jnp.stack(places + order).astype(jnp.int32)
-    parts = [first_part]
-    for (begin, end), gate in zip(chunks[1:], [spread[0], lead[1], lead[1]]):
-        parts.append(after(quarter[:, begin:end], gate))
-        spread.append(lax.all_gather(parts[-1], "fac"))
-    upper, inverse, share = factor_lead(
-        slots, damp, factor_old[:LEAD, :LEAD], lead, parts[1:3]
+    upper, inverse, share = factor_lead(slots, damp, factor_old[:LEAD, :LEAD], lead)
+    panel, lead_stack, across_stack = panel_columns(
+        slots, share, inverse, lead, across_own, across_other
     )
-    panel, lead_stack, across_stack = panel_columns(
-        slots, share, inverse, lead, across, parts[3:]
-    )
+    near_grad = weight_grad.reshape(-1, ROWS, weight_grad.shape[1])
+    near_grad = copied([(near_grad, 0, LEAD // ROWS)], [lead[1]])[0].reshape(LEAD, -1)
+    near_grad = from_first_member(near_grad, member, group, bits, inverse)
     solved = jnp.dot(inverse, near_grad.astype(F32), precision=lax.Precision.HIGH)
     high = solved.astype(BF16)
     low = (solved - high.astype(F32)).astype(BF16)
     lower = upper.T
 
     results = ()
-    gates = [lead[1], panel]
+    gates = [lead[1], inverse, panel]
     for (begin, end), part in zip(chunks, spread):
-        views = exchange_members(part, member, bits, gates.pop(0))
+        views = exchange_members(part, member, bits, [gates.pop(0)])
         places[2] = member * width + begin
         slots = jnp.stack(places + order + [jnp.int32(at) for _, at in views])
         *results, token = finish_rows(
@@ -563,8 +605,10 @@
             across_stack,
             [array for array, _ in views],
             list(results),
+            [] if begin else spread[2:3],
         )
-        gates.append(token)
+        if begin:
+            gates.append(token)
     return tuple(results)
 
 

time: 384 us -> 725 us (1.89)
  Pallas kernels: 123 us -> 560 us
  waiting for transfers between devices: 137 us -> 65.4 us
  other arithmetic: 42.5 us -> 15.2 us
  starting transfers between devices: 17.1 us -> 25.1 us
    pallas_call x0 -> x13, Pallas kernels: none -> 441 us  [copied(): pl.pallas_call(lambda *refs: copy_kernel(plans, *refs), in_specs=[pl.Bloc...]
    all_gather x4, waiting for transfers between devices: 38.8 us -> 0.05 us  [local(): spread = [lax.all_gather(part, 'fac') for part in parts]]
    ppermute x2, waiting for transfers between devices: 30.1 us -> 0.01 us  [from_first_member(): moved = lax.ppermute(value, 'tok', down_pairs(bit, group))]
    select_n x15 -> x2, other arithmetic: 24.2 us -> 4.76 us  [after(): return jnp.where(mark == mark, value, jnp.zeros_like(value))]
    ppermute x20 -> x23, starting transfers between devices: 10.3 us -> 17.3 us  [swapped(): lax.ppermute(value, 'tok', [(source, source ^ mask) for source in range(s...]
    ppermute x20 -> x23, waiting for transfers between devices: 67.6 us -> 65.3 us  [swapped(): lax.ppermute(value, 'tok', [(source, source ^ mask) for source in range(s...]
  transfers between devices with their start and end apart: 28 -> 31, of which waited for: 9 -> 4; matrix products, arithmetic and copies ran while one was open for 16% -> 4% of each run, Pallas kernels for 28% -> 75%
where the time goes in v4:
time: 725 us; the launch traced here: 722 us
  Pallas kernels  560 us (77%)
  waiting for transfers between devices  65.4 us (9%)
  starting transfers between devices  25.1 us (3%)
  between operations  24.2 us (3%)
  local copies, waits for them, and re-layouts  23.3 us (3%)
  other arithmetic  15.2 us (2%)
  matrix products  8.44 us (1%)
    pallas_call x13, Pallas kernels, copied(): pl.pallas_call(lambda *refs: copy_kernel(plans, *refs), in_specs=[pl.Bloc...  441 us
    pallas_call x4, Pallas kernels, finish_rows(): pl.pallas_call(lambda *refs: finish_kernel(count, gram_steps, begin == 0,...  74.9 us
    ppermute x23, waiting for transfers between devices, swapped(): lax.ppermute(value, 'tok', [(source, source ^ mask) for source in range(s...  65.3 us
    pallas_call x1, Pallas kernels, factor_lead(): pl.pallas_call(lambda *refs: factor_kernel(len(lead), *refs), out_shape=(...  28.9 us
    ppermute x23, starting transfers between devices, swapped(): lax.ppermute(value, 'tok', [(source, source ^ mask) for source in range(s...  17.3 us
    pallas_call x1, Pallas kernels, panel_columns(): pl.pallas_call(lambda *refs: panel_kernel(count, *refs), grid=(width // c...  15.6 us
  transfers between devices with their start and end apart: 31, of which 4 were waited for; matrix products, arithmetic and copies ran while one was open for 4% of the time, Pallas kernels for 75%

profile of v4, /device:TPU:2, one launch (start us, length us, event | category | flops | bytes accessed | tf_op | source)
XLA Modules:
  0.0 721.8 jit_solution(5121922968713433824)
XLA Ops:
  7.2 4.4 convert.3
  38.7 20.6 %collective-permute-done.4.refs_11_ = bf16[320,1536]{1,0:T(8,128)(2,1)} collective-permute-done((bf16[320,1536]{1,0:T(8,128)(2,1)S(1)}, bf16[320,1536]{1,0:T(8,128)(2,1)}, u32[]{:S(2)}, u32[]{:S(2)}) %collective-permute-start.4) | collective-permute-done | bytes 983072 | tf_op jit(solution)/shard_map/ppermute | solution.py:405
  62.0 24.9 %shard_map.85.refs_2_.refs_4_ = bf16[768,512]{1,0:T(8,128)(2,1)} custom-call(s32[1]{0:T(128)} %constant.87.clone.1.refs_0_, bf16[768,1536]{1,0:T(8,128)(2,1)} %pad_maximum_fusion.refs_1_, bf16[784,512]{1,0:T(8,128)(2,1)} %pad_maximum_fusion.2.refs_2_), custom_call_target="tpu_custom_call" | custom-call | flops 1 | bytes 1 | tf_op jit(solution)/shard_map/pallas_call | solution.py:454
  89.6 13.0 %shard_map.86.refs_2_.refs_5_ = bf16[768,256]{1,0:T(8,128)(2,1)} custom-call(s32[1]{0:T(128)} %constant.87.clone.1.refs_0_, bf16[768,1536]{1,0:T(8,128)(2,1)} %pad_maximum_fusion.refs_1_, bf16[768,512]{1,0:T(8,128)(2,1)} %shard_map.85.refs_2_.refs_4_), custom_call_target="tpu_custom_call" | custom-call | flops 1 | bytes 1 | tf_op jit(solution)/shard_map/pallas_call | solution.py:454
  102.6 13.0 %shard_map.87.refs_6_ = bf16[768,256]{1,0:T(8,128)(2,1)} custom-call(s32[1]{0:T(128)} %constant.87.clone.1.refs_0_, bf16[768,1536]{1,0:T(8,128)(2,1)} %pad_maximum_fusion.refs_1_, bf16[768,256]{1,0:T(8,128)(2,1)} %shard_map.86.refs_2_.refs_5_), custom_call_target="tpu_custom_call" | custom-call | flops 1 | bytes 1 | tf_op jit(solution)/shard_map/pallas_call | solution.py:454
  115.7 24.4 %collective-permute-done.5.refs_3_.refs_12_ = bf16[320,1536]{1,0:T(8,128)(2,1)} collective-permute-done((bf16[320,1536]{1,0:T(8,128)(2,1)}, bf16[320,1536]{1,0:T(8,128)(2,1)}, u32[]{:S(2)}, u32[]{:S(2)}) %collective-permute-start.5) | collective-permute-done | bytes 983072 | tf_op jit(solution)/shard_map/ppermute | solution.py:405
  140.1 25.4 %shard_map.88 = bf16[1,784,512]{2,1,0:T(8,128)(2,1)} custom-call(s32[1]{0:T(128)} %constant.87.clone.1.refs_0_, bf16[4,784,512]{2,1,0:T(8,128)(2,1)} %bitcast.65, bf16[448,1536]{1,0:T(8,128)(2,1)} %collective-permute-done.3.refs_2_.refs_8_, bf16[320,1536]{1,0:T(8,128)(2,1)} %collective-permute-done.5.refs_3_.refs_12_, ...), custom_call_target="tpu_custom_call" | custom-call | flops 1 | bytes 1 | tf_op jit(solution)/shard_map/pallas_call | solution.py:454
  167.3 16.7 %collective-permute-done.6.refs_4_.refs_2_.refs_3_ = bf16[784,512]{1,0:T(8,128)(2,1)S(1)} collective-permute-done((bf16[784,512]{1,0:T(8,128)(2,1)}, bf16[784,512]{1,0:T(8,128)(2,1)S(1)}, u32[]{:S(2)}, u32[]{:S(2)}) %collective-permute-start.6) | collective-permute-done | bytes 802848 | tf_op jit(solution)/shard_map/ppermute | solution.py:405
  184.9 64.7 %shard_map.91 = bf16[2,256,2048]{2,1,0:T(8,128)(2,1)} custom-call(s32[1]{0:T(128)} %constant.87.clone.1.refs_0_, bf16[6,256,2048]{2,1,0:T(8,128)(2,1)} %bitcast.64, bf16[784,512]{1,0:T(8,128)(2,1)} %copy-done.4), custom_call_target="tpu_custom_call" | custom-call | flops 1 | bytes 1 | tf_op jit(solution)/shard_map/pallas_call | solution.py:454
  251.5 49.8 %shard_map.94 = bf16[2,784,512]{2,1,0:T(8,128)(2,1)} custom-call(s32[1]{0:T(128)} %bitcast.29.refs_0_, bf16[4,784,512]{2,1,0:T(8,128)(2,1)} %bitcast.66, bf16[784,512]{1,0:T(8,128)(2,1)} %copy-done.4), custom_call_target="tpu_custom_call" | custom-call | flops 1 | bytes 1 | tf_op jit(solution)/shard_map/pallas_call | solution.py:454
  314.9 28.9 %shard_map.89 = (f32[512,512]{1,0:T(8,128)S(1)}, f32[512,512]{1,0:T(8,128)S(1)}, f32[8,128]{1,0:T(8,128)S(1)}) custom-call(s32[7]{0:T(128)S(1)} %stack.54.refs_0_, f32[1]{0:T(128)} %bitcast.10.refs_1_, f32[512,512]{1,0:T(8,128)S(1)} %copy-done.7, bf16[784,512]{1,0:T(8,128)(2,1)S(1)} %bitcast.63, bf16[784,512]{1,0:T(8,128)(2,1)S(1)} %copy-done.5, ...), custom_call_target="tpu_custom_call" | custom-call | flops 1 | bytes 1 | tf_op jit(solution)/shard_map/pallas_call | solution.py:163
  353.2 48.8 %shard_map.92 = bf16[2,768,512]{2,1,0:T(8,128)(2,1)} custom-call(s32[1]{0:T(128)} %bitcast.29.refs_0_, bf16[4,768,512]{2,1,0:T(8,128)(2,1)} %bitcast.69, f32[512,512]{1,0:T(8,128)} %copy-done.2), custom_call_target="tpu_custom_call" | custom-call | flops 1 | bytes 1 | tf_op jit(solution)/shard_map/pallas_call | solution.py:454
  403.4 50.4 %shard_map.95 = (bf16[1,784,512]{2,1,0:T(8,128)(2,1)}, bf16[1,784,512]{2,1,0:T(8,128)(2,1)}) custom-call(s32[2]{0:T(128)} %pad_add_fusion.1.refs_0_, bf16[4,784,512]{2,1,0:T(8,128)(2,1)} %bitcast.67, bf16[2,784,512]{2,1,0:T(8,128)(2,1)} %collective-permute-done.18.refs_2_.refs_13_, bf16[784,512]{1,0:T(8,128)(2,1)} %copy-done.4), custom_call_target="tpu_custom_call" | custom-call | flops 1 | bytes 1 | tf_op jit(solution)/shard_map/pallas_call | solution.py:454
  455.5 49.4 %shard_map.93 = (bf16[1,768,512]{2,1,0:T(8,128)(2,1)}, bf16[1,768,512]{2,1,0:T(8,128)(2,1)}) custom-call(s32[2]{0:T(128)} %pad_add_fusion.1.refs_0_, bf16[4,768,512]{2,1,0:T(8,128)(2,1)} %bitcast.70, bf16[2,768,512]{2,1,0:T(8,128)(2,1)} %copy-done.17, f32[512,512]{1,0:T(8,128)} %copy-done.2), custom_call_target="tpu_custom_call" | custom-call | flops 1 | bytes 1 | tf_op jit(solution)/shard_map/pallas_call | solution.py:454
  506.9 15.6 %shard_map.90 = (bf16[512,1536]{1,0:T(8,128)(2,1)}, bf16[2560,512]{1,0:T(8,128)(2,1)}, bf16[2560,1536]{1,0:T(8,128)(2,1)}) custom-call(s32[7]{0:T(128)} %copy-done.15, f32[8,128]{1,0:T(8,128)} %copy-done.14, f32[512,512]{1,0:T(8,128)} %copy-done.2, bf16[784,512]{1,0:T(8,128)(2,1)} %bitcast.61, bf16[784,512]{1,0:T(8,128)(2,1)} %copy-done.4, ...), custom_call_target="tpu_custom_call" | custom-call | flops 1 | bytes 1 | tf_op jit(solution)/shard_map/pallas_call | solution.py:204
  522.5 25.0 %shard_map.100 = bf16[2,768,256]{2,1,0:T(8,128)(2,1)} custom-call(s32[1]{0:T(128)} %bitcast.29.refs_0_, bf16[4,768,256]{2,1,0:T(8,128)(2,1)} %bitcast.72, bf16[512,1536]{1,0:T(8,128)(2,1)} %get-tuple-element.32.refs_5_.refs_2_.refs_3_), custom_call_target="tpu_custom_call" | custom-call | flops 1 | bytes 1 | tf_op jit(solution)/shard_map/pallas_call | solution.py:454
  550.9 6.0 subtract_convert_fusion
  557.8 22.3 %shard_map.96 = (f32[1536,1536]{1,0:T(8,128)}, f32[1536,1536]{1,0:T(8,128)}, f32[1536,2048]{1,0:T(8,128)}, f32[8,128]{1,0:T(8,128)}) custom-call(s32[11]{0:T(128)} %stack.63.refs_0_, f32[1]{0:T(128)} %bitcast.10.refs_1_, f32[8,128]{1,0:T(8,128)} %copy-done.14, f32[1536,1536]{1,0:T(8,128)} %refs_3_.7, bf16[1536,2048]{1,0:T(8,128)(2,1)} %refs_4_.7, ...), custom_call_target="tpu_custom_call" | custom-call | flops 1 | bytes 1 | tf_op jit(solution)/shard_map/pallas_call | solution.py:373
  580.1 21.6 %shard_map.97 = (f32[1536,1536]{1,0:T(8,128)}, f32[1536,1536]{1,0:T(8,128)}, f32[1536,2048]{1,0:T(8,128)}, f32[8,128]{1,0:T(8,128)}) custom-call(s32[11]{0:T(128)} %stack.59.refs_0_, f32[1]{0:T(128)} %bitcast.10.refs_1_, f32[8,128]{1,0:T(8,128)} %copy-done.14, f32[1536,1536]{1,0:T(8,128)} %refs_3_.7, ...), custom_call_target="tpu_custom_call", output_to_operand_aliasing={{0}: (15, {}), {1}: (16, {}), {2}: (17, {})} | custom-call | flops 1 | bytes 1 | tf_op jit(solution)/shard_map/pallas_call | solution.py:373
  601.7 25.0 %shard_map.98 = bf16[2,768,256]{2,1,0:T(8,128)(2,1)} custom-call(s32[1]{0:T(128)} %bitcast.29.refs_0_, bf16[4,768,256]{2,1,0:T(8,128)(2,1)} %bitcast.76, f32[8,128]{1,0:T(8,128)} %get-tuple-element.43.refs_2_.refs_3_), custom_call_target="tpu_custom_call" | custom-call | flops 1 | bytes 1 | tf_op jit(solution)/shard_map/pallas_call | solution.py:454
  627.8 25.6 %shard_map.101 = (bf16[1,768,256]{2,1,0:T(8,128)(2,1)}, bf16[1,768,256]{2,1,0:T(8,128)(2,1)}) custom-call(s32[2]{0:T(128)} %pad_add_fusion.1.refs_0_, bf16[4,768,256]{2,1,0:T(8,128)(2,1)} %bitcast.74, bf16[2,768,256]{2,1,0:T(8,128)(2,1)} %copy-done.20, bf16[512,1536]{1,0:T(8,128)(2,1)} %get-tuple-element.32.refs_5_.refs_2_.refs_3_), custom_call_target="tpu_custom_call" | custom-call | flops 1 | bytes 1 | tf_op jit(solution)/shard_map/pallas_call | solution.py:454
  654.9 25.6 %shard_map.99 = (bf16[1,768,256]{2,1,0:T(8,128)(2,1)}, bf16[1,768,256]{2,1,0:T(8,128)(2,1)}) custom-call(s32[2]{0:T(128)} %pad_add_fusion.1.refs_0_, bf16[4,768,256]{2,1,0:T(8,128)(2,1)} %bitcast.77, bf16[2,768,256]{2,1,0:T(8,128)(2,1)} %copy-done.21, f32[8,128]{1,0:T(8,128)} %get-tuple-element.43.refs_2_.refs_3_), custom_call_target="tpu_custom_call" | custom-call | flops 1 | bytes 1 | tf_op jit(solution)/shard_map/pallas_call | solution.py:454
  683.3 15.5 %shard_map.102 = (f32[1536,1536]{1,0:T(8,128)}, f32[1536,1536]{1,0:T(8,128)}, f32[1536,2048]{1,0:T(8,128)}, f32[8,128]{1,0:T(8,128)}) custom-call(s32[11]{0:T(128)} %stack.65.refs_0_, f32[1]{0:T(128)} %bitcast.10.refs_1_, f32[8,128]{1,0:T(8,128)} %copy-done.14, f32[1536,1536]{1,0:T(8,128)} %refs_3_.7, ...), custom_call_target="tpu_custom_call", output_to_operand_aliasing={{0}: (15, {}), {1}: (16, {}), {2}: (17, {})} | custom-call | flops 1 | bytes 1 | tf_op jit(solution)/shard_map/pallas_call | solution.py:373
  699.7 15.6 %shard_map.103 = (f32[1536,1536]{1,0:T(8,128)}, f32[1536,1536]{1,0:T(8,128)}, f32[1536,2048]{1,0:T(8,128)}, f32[8,128]{1,0:T(8,128)}) custom-call(s32[11]{0:T(128)} %stack.52.refs_0_, f32[1]{0:T(128)} %bitcast.10.refs_1_, f32[8,128]{1,0:T(8,128)} %copy-done.14, f32[1536,1536]{1,0:T(8,128)} %refs_3_.7, ...), custom_call_target="tpu_custom_call", output_to_operand_aliasing={{0}: (15, {}), {1}: (16, {}), {2}: (17, {})} | custom-call | flops 1 | bytes 1 | tf_op jit(solution)/shard_map/pallas_call | solution.py:373
  (167 shorter events, 65.5 us)
Async XLA Ops:
  7.2 132.9 %all-gather.9.cloned.1.call-start = ((), (), s32[]{:S(2)}) async-start(), calls=%async_computation | async-start | bytes 4014080 | tf_op jit(solution)/shard_map/all_gather | solution.py:565
  33.6 319.6 %all-gather.13.cloned.1.call-start = ((), (), s32[]{:S(2)}) async-start(), calls=%async_computation.2 | async-start | bytes 3932160 | tf_op jit(solution)/shard_map/all_gather | solution.py:565
  87.0 435.5 %all-gather.15.cloned.1.call-start = ((), (), s32[]{:S(2)}) async-start(), calls=%async_computation.3 | async-start | bytes 1966080 | tf_op jit(solution)/shard_map/all_gather | solution.py:565
  87.1 52.9 %collective-permute-start.3 = (bf16[448,1536]{1,0:T(8,128)(2,1)S(1)}, bf16[448,1536]{1,0:T(8,128)(2,1)}, u32[]{:S(2)}, u32[]{:S(2)}) collective-permute-start(bf16[448,1536]{1,0:T(8,128)(2,1)S(1)} %pad_maximum_fusion.1.refs_7_), channel_id=1, source_target_pairs={{0,8},{4,12},{8,0},{12,4},{16,24},{20,28},{24,16},{28,20},{1,9},{5... | collective-permute-start | bytes 4128776 | tf_op jit(solution)/shard_map/ppermute | solution.py:405
  89.5 50.5 %collective-permute-start.5 = (bf16[320,1536]{1,0:T(8,128)(2,1)}, bf16[320,1536]{1,0:T(8,128)(2,1)}, u32[]{:S(2)}, u32[]{:S(2)}) collective-permute-start(bf16[320,1536]{1,0:T(8,128)(2,1)} %collective-permute-done.4.refs_11_), channel_id=1, source_target_pairs={{0,8},{4,12},{8,0},{12,4},{16,24},{20,28},{24,16},{28,20},{1,9},{5... | collective-permute-start | bytes 2949128 | tf_op jit(solution)/shard_map/ppermute | solution.py:405
  249.5 96.7 %collective-permute-start.13 = (bf16[512,2048]{1,0:T(8,128)(2,1)}, bf16[512,2048]{1,0:T(8,128)(2,1)}, u32[]{:S(2)}, u32[]{:S(2)}) collective-permute-start(bf16[512,2048]{1,0:T(8,128)(2,1)} %bitcast.79), channel_id=1, source_target_pairs={{0,8},{16,24},{1,9},{17,25},{2,10},{18,26},{3,11},{19,27}} | collective-permute-start | bytes 6291464 | tf_op jit(solution)/shard_map/ppermute | solution.py:500
  250.9 350.8 %all-gather.11.cloned.1.call-start = ((), (), s32[]{:S(2)}) async-start(), calls=%async_computation.1 | async-start | bytes 1966080 | tf_op jit(solution)/shard_map/all_gather | solution.py:565
  250.9 58.7 %collective-permute-start.7 = (bf16[784,512]{1,0:T(8,128)(2,1)S(1)}, bf16[784,512]{1,0:T(8,128)(2,1)S(1)}, u32[]{:S(2)}, u32[]{:S(2)}) collective-permute-start(bf16[784,512]{1,0:T(8,128)(2,1)S(1)} %bitcast.62), channel_id=1, source_target_pairs={{0,4},{4,0},{8,12},{12,8},{16,20},{20,16},{24,28},{28,24},{1,5},{5... | collective-permute-start | bytes 2408456 | tf_op jit(solution)/shard_map/ppermute | solution.py:405
  251.0 59.5 %collective-permute-start.8 = (bf16[784,512]{1,0:T(8,128)(2,1)}, bf16[784,512]{1,0:T(8,128)(2,1)S(1)}, u32[]{:S(2)}, u32[]{:S(2)}) collective-permute-start(bf16[784,512]{1,0:T(8,128)(2,1)} %copy-done.4), channel_id=1, source_target_pairs={{0,4},{4,0},{8,12},{12,8},{16,20},{20,16},{24,28},{28,24},{1,5},{5... | collective-permute-start | bytes 2408456 | tf_op jit(solution)/shard_map/ppermute | solution.py:405
  301.3 101.4 %collective-permute-start.18 = (bf16[2,784,512]{2,1,0:T(8,128)(2,1)}, bf16[2,784,512]{2,1,0:T(8,128)(2,1)}, u32[]{:S(2)}, u32[]{:S(2)}) collective-permute-start(bf16[2,784,512]{2,1,0:T(8,128)(2,1)} %shard_map.94), channel_id=1, source_target_pairs={{0,8},{4,12},{8,0},{12,4},{16,24},{20,28},{24,16},{28,20},{1,9},{5... | collective-permute-start | bytes 4816904 | tf_op jit(solution)/shard_map/ppermute | solution.py:405
  309.6 92.6 %collective-permute-start.11 = (bf16[320,1536]{1,0:T(8,128)(2,1)}, bf16[320,1536]{1,0:T(8,128)(2,1)}, u32[]{:S(2)}, u32[]{:S(2)}) collective-permute-start(bf16[320,1536]{1,0:T(8,128)(2,1)} %collective-permute-done.4.refs_11_), channel_id=1, source_target_pairs={{0,4},{4,0},{8,12},{12,8},{16,20},{20,16},{24,28},{28,24},{1,5},{5... | collective-permute-start | bytes 2949128 | tf_op jit(solution)/shard_map/ppermute | solution.py:405
  349.4 199.4 %collective-permute-start.14 = (bf16[512,2048]{1,0:T(8,128)(2,1)}, bf16[512,2048]{1,0:T(8,128)(2,1)}, u32[]{:S(2)}, u32[]{:S(2)}) collective-permute-start(bf16[512,2048]{1,0:T(8,128)(2,1)} %select_select_fusion), channel_id=1, source_target_pairs={{0,4},{8,12},{16,20},{24,28},{1,5},{9,13},{17,21},{25,29},{2,6},{1... | collective-permute-start | bytes 6291464 | tf_op jit(solution)/shard_map/ppermute | solution.py:500
  402.0 52.4 %collective-permute-start.15 = (bf16[2,768,512]{2,1,0:T(8,128)(2,1)}, bf16[2,768,512]{2,1,0:T(8,128)(2,1)S(1)}, u32[]{:S(2)}, u32[]{:S(2)}) collective-permute-start(bf16[2,768,512]{2,1,0:T(8,128)(2,1)} %shard_map.92), channel_id=1, source_target_pairs={{0,8},{4,12},{8,0},{12,4},{16,24},{20,28},{24,16},{28,20},{1,9},{5... | collective-permute-start | bytes 4718600 | tf_op jit(solution)/shard_map/ppermute | solution.py:405
  402.1 51.8 %collective-permute-start.9 = (bf16[448,1536]{1,0:T(8,128)(2,1)S(1)}, bf16[448,1536]{1,0:T(8,128)(2,1)}, u32[]{:S(2)}, u32[]{:S(2)}) collective-permute-start(bf16[448,1536]{1,0:T(8,128)(2,1)S(1)} %copy-done.19), channel_id=1, source_target_pairs={{0,4},{4,0},{8,12},{12,8},{16,20},{20,16},{24,28},{28,24},{1,5},{5... | collective-permute-start | bytes 4128776 | tf_op jit(solution)/shard_map/ppermute | solution.py:405
  402.2 102.9 %collective-permute-start.10 = (bf16[448,1536]{1,0:T(8,128)(2,1)}, bf16[448,1536]{1,0:T(8,128)(2,1)}, u32[]{:S(2)}, u32[]{:S(2)}) collective-permute-start(bf16[448,1536]{1,0:T(8,128)(2,1)} %collective-permute-done.3.refs_2_.refs_8_), channel_id=1, source_target_pairs={{0,4},{4,0},{8,12},{12,8},{16,20},{20,16},{24,28},{28,24},{1,5},{5... | collective-permute-start | bytes 4128776 | tf_op jit(solution)/shard_map/ppermute | solution.py:405
  402.7 102.3 %collective-permute-start.12 = (bf16[320,1536]{1,0:T(8,128)(2,1)}, bf16[320,1536]{1,0:T(8,128)(2,1)}, u32[]{:S(2)}, u32[]{:S(2)}) collective-permute-start(bf16[320,1536]{1,0:T(8,128)(2,1)} %collective-permute-done.5.refs_3_.refs_12_), channel_id=1, source_target_pairs={{0,4},{4,0},{8,12},{12,8},{16,20},{20,16},{24,28},{28,24},{1,5},{5... | collective-permute-start | bytes 2949128 | tf_op jit(solution)/shard_map/ppermute | solution.py:405
  453.9 103.0 %collective-permute-start.19 = (bf16[1,784,512]{2,1,0:T(8,128)(2,1)}, bf16[1,784,512]{2,1,0:T(8,128)(2,1)S(1)}, u32[]{:S(2)}, u32[]{:S(2)}) collective-permute-start(bf16[1,784,512]{2,1,0:T(8,128)(2,1)} %get-tuple-element.38), channel_id=1, source_target_pairs={{0,4},{4,0},{8,12},{12,8},{16,20},{20,16},{24,28},{28,24},{1,5},{5... | collective-permute-start | bytes 2408456 | tf_op jit(solution)/shard_map/ppermute | solution.py:405
  454.3 102.5 %collective-permute-start.20 = (bf16[1,784,512]{2,1,0:T(8,128)(2,1)}, bf16[1,784,512]{2,1,0:T(8,128)(2,1)}, u32[]{:S(2)}, u32[]{:S(2)}) collective-permute-start(bf16[1,784,512]{2,1,0:T(8,128)(2,1)} %get-tuple-element.39), channel_id=1, source_target_pairs={{0,4},{4,0},{8,12},{12,8},{16,20},{20,16},{24,28},{28,24},{1,5},{5... | collective-permute-start | bytes 2408456 | tf_op jit(solution)/shard_map/ppermute | solution.py:405
  505.0 75.1 %collective-permute-start.16 = (bf16[1,768,512]{2,1,0:T(8,128)(2,1)}, bf16[1,768,512]{2,1,0:T(8,128)(2,1)}, u32[]{:S(2)}, u32[]{:S(2)}) collective-permute-start(bf16[1,768,512]{2,1,0:T(8,128)(2,1)} %get-tuple-element.35), channel_id=1, source_target_pairs={{0,4},{4,0},{8,12},{12,8},{16,20},{20,16},{24,28},{28,24},{1,5},{5... | collective-permute-start | bytes 2359304 | tf_op jit(solution)/shard_map/ppermute | solution.py:405
  505.1 75.0 %collective-permute-start.17 = (bf16[1,768,512]{2,1,0:T(8,128)(2,1)}, bf16[1,768,512]{2,1,0:T(8,128)(2,1)}, u32[]{:S(2)}, u32[]{:S(2)}) collective-permute-start(bf16[1,768,512]{2,1,0:T(8,128)(2,1)} %get-tuple-element.36), channel_id=1, source_target_pairs={{0,4},{4,0},{8,12},{12,8},{16,20},{20,16},{24,28},{28,24},{1,5},{5... | collective-permute-start | bytes 2359304 | tf_op jit(solution)/shard_map/ppermute | solution.py:405
  548.8 78.1 %collective-permute-start.24 = (bf16[2,768,256]{2,1,0:T(8,128)(2,1)}, bf16[2,768,256]{2,1,0:T(8,128)(2,1)S(1)}, u32[]{:S(2)}, u32[]{:S(2)}) collective-permute-start(bf16[2,768,256]{2,1,0:T(8,128)(2,1)} %shard_map.100), channel_id=1, source_target_pairs={{0,8},{4,12},{8,0},{12,4},{16,24},{20,28},{24,16},{28,20},{1,9},{5... | collective-permute-start | bytes 2359304 | tf_op jit(solution)/shard_map/ppermute | solution.py:405
  626.7 27.3 %collective-permute-start.21 = (bf16[2,768,256]{2,1,0:T(8,128)(2,1)}, bf16[2,768,256]{2,1,0:T(8,128)(2,1)S(1)}, u32[]{:S(2)}, u32[]{:S(2)}) collective-permute-start(bf16[2,768,256]{2,1,0:T(8,128)(2,1)} %shard_map.98), channel_id=1, source_target_pairs={{0,8},{4,12},{8,0},{12,4},{16,24},{20,28},{24,16},{28,20},{1,9},{5... | collective-permute-start | bytes 2359304 | tf_op jit(solution)/shard_map/ppermute | solution.py:405
  653.4 29.0 %collective-permute-start.25 = (bf16[1,768,256]{2,1,0:T(8,128)(2,1)}, bf16[1,768,256]{2,1,0:T(8,128)(2,1)S(1)}, u32[]{:S(2)}, u32[]{:S(2)}) collective-permute-start(bf16[1,768,256]{2,1,0:T(8,128)(2,1)} %get-tuple-element.46), channel_id=1, source_target_pairs={{0,4},{4,0},{8,12},{12,8},{16,20},{20,16},{24,28},{28,24},{1,5},{5... | collective-permute-start | bytes 1179656 | tf_op jit(solution)/shard_map/ppermute | solution.py:405
  653.5 28.9 %collective-permute-start.26 = (bf16[1,768,256]{2,1,0:T(8,128)(2,1)}, bf16[1,768,256]{2,1,0:T(8,128)(2,1)S(1)}, u32[]{:S(2)}, u32[]{:S(2)}) collective-permute-start(bf16[1,768,256]{2,1,0:T(8,128)(2,1)} %get-tuple-element.47), channel_id=1, source_target_pairs={{0,4},{4,0},{8,12},{12,8},{16,20},{20,16},{24,28},{28,24},{1,5},{5... | collective-permute-start | bytes 1179656 | tf_op jit(solution)/shard_map/ppermute | solution.py:405
  (36 other events, 410.8 us)
Sparse Core Ops, SparseCore 0:
  33.7 65.8 all-gather.8
  101.1 62.1 all-gather.12
  251.0 39.9 all-gather.14
  402.2 37.9 all-gather.10

commit v5 on v4

--- a/solution.py
+++ b/solution.py
@@ -412,52 +412,40 @@
     return pieces
 
 
-def copy_kernel(plans, starts_ref, *refs):
-    outs, sems = refs[-1 - len(plans) : -1], refs[-1]
-    copies = []
-    for number, (count, axis, begin) in enumerate(plans):
-        source, out = refs[number], outs[number]
-        rows = out.shape[-2] // 32 * 16
-        for part in (slice(0, rows), slice(rows, out.shape[-2])):
-            if axis is None:
-                pairs = [
-                    (source.at[starts_ref[number] + k, part], out.at[k, part])
-                    for k in range(count)
-                ]
-            else:
-                pairs = [(source.at[part, begin : begin + out.shape[1]], out.at[part])]
-            copies += [
-                pltpu.make_async_copy(before, after, sems.at[len(copies) + k])
-                for k, (before, after) in enumerate(pairs)
-            ]
-    for copy in copies:
-        copy.start()
-    for copy in copies:
-        copy.wait()
+def copy_kernel(count, starts_ref, *refs):
+    for source, out in zip(refs[:count], refs[-count:]):
+        out[...] = source[...].astype(BF16)
 
 
 def copied(requests, earlier):
-    plans, shapes, starts, total = [], [], [], 0
-    for array, begin, size in requests:
+    in_specs, out_specs, shapes, starts = [], [], [], []
+    for number, (array, begin, size) in enumerate(requests):
+        rows = array.shape[-2]
+        split = next(parts for parts in (4, 7, 1) if rows % (16 * parts) == 0)
         if array.ndim == 3:
-            plans.append((size, None, None))
-            shapes.append((size, *array.shape[1:]))
+            count, width = size, array.shape[2]
+            shapes.append((count, rows, width))
             starts.append(begin)
-            total += 2 * size
+            block = (1, rows // split, width)
+            in_specs.append(pl.BlockSpec(block, lambda k, r, p, n=number: (p[n] + k, r, 0)))
+            out_specs.append(pl.BlockSpec(block, lambda k, r, p: (k, r, 0)))
         else:
-            plans.append((1, 1, begin))
-            shapes.append((array.shape[0], size - begin))
-            starts.append(0)
-            total += 2
-    anywhere = pl.BlockSpec(memory_space=pl.ANY)
+            count, width = 1, size - begin
+            shapes.append((rows, width))
+            starts.append(begin // width)
+            block = (rows // split, width)
+            in_specs.append(pl.BlockSpec(block, lambda k, r, p, n=number: (r, p[n])))
+            out_specs.append(pl.BlockSpec(block, lambda k, r, p: (r, 0)))
     arrays = [array for array, _, _ in requests]
     return pl.pallas_call(
-        lambda *refs: copy_kernel(plans, *refs),
-        in_specs=[pl.BlockSpec(memory_space=pltpu.SMEM)]
-        + [anywhere] * (len(arrays) + len(earlier)),
-        out_specs=[anywhere] * len(plans),
+        lambda *refs: copy_kernel(len(arrays), *refs),
+        grid_spec=pltpu.PrefetchScalarGridSpec(
+            num_scalar_prefetch=1,
+            grid=(count, split),
+            in_specs=in_specs + [pl.BlockSpec(memory_space=pl.ANY)] * len(earlier),
+            out_specs=out_specs,
+        ),
         out_shape=[jax.ShapeDtypeStruct(shape, BF16) for shape in shapes],
-        scratch_shapes=[pltpu.SemaphoreType.DMA((total,))],
         cost_estimate=NO_COST,
     )(jnp.stack([jnp.int32(start) for start in starts]), *arrays, *earlier)
 
@@ -527,7 +515,8 @@
     damp = jnp.where(expert == 0, damping[0], damping[1])[None]
     order = [member ^ other for other in member_order(bits)]
 
-    lead_factor = factor_old[:LEAD].astype(BF16).reshape(group, LEAD // group, width)
+    lead_factor = factor_old.reshape(-1, LEAD // group, width)
+    lead_factor = copied([(lead_factor, 0, group)], [])[0]
     lead_factor = share_of_first(lead_factor, member, group, bits)
 
     live = jnp.arange(tok_rows) < counts[0]

time: 725 us -> 412 us (0.57)
  Pallas kernels: 560 us -> 191 us
  waiting for transfers between devices: 65.4 us -> 124 us
    pallas_call x13 -> x14, Pallas kernels: 441 us -> 71.4 us  [copied(): pl.pallas_call(lambda *refs: copy_kernel(len(arrays), *refs), grid_spec=p...]
    ppermute x23, waiting for transfers between devices: 65.3 us -> 124 us  [swapped(): lax.ppermute(value, 'tok', [(source, source ^ mask) for source in range(s...]
  transfers between devices with their start and end apart: 31 -> 31, of which waited for: 4 -> 6; matrix products, arithmetic and copies ran while one was open for 4% -> 7% of each run, Pallas kernels for 75% -> 41%
where the time goes in v5:
time: 412 us; the launch traced here: 407 us
  Pallas kernels  191 us (46%)
  waiting for transfers between devices  124 us (30%)
  starting transfers between devices  24.3 us (6%)
  between operations  24 us (6%)
  local copies, waits for them, and re-layouts  23.7 us (6%)
  other arithmetic  12.7 us (3%)
  matrix products  7.16 us (2%)
    ppermute x23, waiting for transfers between devices, swapped(): lax.ppermute(value, 'tok', [(source, source ^ mask) for source in range(s...  124 us
    pallas_call x4, Pallas kernels, finish_rows(): pl.pallas_call(lambda *refs: finish_kernel(count, gram_steps, begin == 0,...  75 us
    pallas_call x14, Pallas kernels, copied(): pl.pallas_call(lambda *refs: copy_kernel(len(arrays), *refs), grid_spec=p...  71.4 us
    pallas_call x1, Pallas kernels, factor_lead(): pl.pallas_call(lambda *refs: factor_kernel(len(lead), *refs), out_shape=(...  28.9 us
    ppermute x23, starting transfers between devices, swapped(): lax.ppermute(value, 'tok', [(source, source ^ mask) for source in range(s...  16.1 us
    pallas_call x1, Pallas kernels, panel_columns(): pl.pallas_call(lambda *refs: panel_kernel(count, *refs), grid=(width // c...  15.6 us
    unnamed x63, local copies, waits for them, and re-layouts  13.7 us
  transfers between devices with their start and end apart: 31, of which 6 were waited for; matrix products, arithmetic and copies ran while one was open for 7% of the time, Pallas kernels for 41%

profile of v5, /device:TPU:2, one launch (start us, length us, event | category | flops | bytes accessed | tf_op | source)
XLA Modules:
  0.0 406.8 jit_solution(4584015367470632474)
XLA Ops:
  7.2 9.7 %shard_map.85 = bf16[4,128,1536]{2,1,0:T(8,128)(2,1)} custom-call(s32[1]{0:T(128)} %constant.90.clone.1.refs_0_, f32[12,128,1536]{2,1,0:T(8,128)} %bitcast.63), custom_call_target="tpu_custom_call" | custom-call | flops 1 | bytes 1 | tf_op jit(solution)/shard_map/pallas_call | solution.py:440
  44.9 21.5 %collective-permute-done.4.refs_11_ = bf16[320,1536]{1,0:T(8,128)(2,1)} collective-permute-done((bf16[320,1536]{1,0:T(8,128)(2,1)S(1)}, bf16[320,1536]{1,0:T(8,128)(2,1)}, u32[]{:S(2)}, u32[]{:S(2)}) %collective-permute-start.4) | collective-permute-done | bytes 983072 | tf_op jit(solution)/shard_map/ppermute | solution.py:405
  80.9 43.4 %collective-permute-done.5.refs_3_.refs_12_ = bf16[320,1536]{1,0:T(8,128)(2,1)} collective-permute-done((bf16[320,1536]{1,0:T(8,128)(2,1)}, bf16[320,1536]{1,0:T(8,128)(2,1)}, u32[]{:S(2)}, u32[]{:S(2)}) %collective-permute-start.5) | collective-permute-done | bytes 983072 | tf_op jit(solution)/shard_map/ppermute | solution.py:405
  124.3 4.7 %shard_map.89 = bf16[1,784,512]{2,1,0:T(8,128)(2,1)} custom-call(s32[1]{0:T(128)} %constant.90.clone.1.refs_0_, bf16[4,784,512]{2,1,0:T(8,128)(2,1)} %bitcast.65, bf16[448,1536]{1,0:T(8,128)(2,1)} %collective-permute-done.3.refs_2_.refs_8_, bf16[320,1536]{1,0:T(8,128)(2,1)} %collective-permute-done.5.refs_3_.refs_12_, ...), custom_call_target="tpu_custom_call" | custom-call | flops 1 | bytes 1 | tf_op jit(solution)/shard_map/pallas_call | solution.py:440
  130.6 16.1 %collective-permute-done.6.refs_4_.refs_2_.refs_3_ = bf16[784,512]{1,0:T(8,128)(2,1)S(1)} collective-permute-done((bf16[784,512]{1,0:T(8,128)(2,1)}, bf16[784,512]{1,0:T(8,128)(2,1)S(1)}, u32[]{:S(2)}, u32[]{:S(2)}) %collective-permute-start.6) | collective-permute-done | bytes 802848 | tf_op jit(solution)/shard_map/ppermute | solution.py:405
  147.6 5.7 %shard_map.92 = bf16[2,256,2048]{2,1,0:T(8,128)(2,1)} custom-call(s32[1]{0:T(128)} %constant.90.clone.1.refs_0_, bf16[6,256,2048]{2,1,0:T(8,128)(2,1)} %bitcast.64, bf16[784,512]{1,0:T(8,128)(2,1)} %copy-done.4), custom_call_target="tpu_custom_call" | custom-call | flops 1 | bytes 1 | tf_op jit(solution)/shard_map/pallas_call | solution.py:440
  155.2 8.2 %shard_map.95 = bf16[2,784,512]{2,1,0:T(8,128)(2,1)} custom-call(s32[1]{0:T(128)} %bitcast.28.refs_0_, bf16[4,784,512]{2,1,0:T(8,128)(2,1)} %bitcast.66, bf16[784,512]{1,0:T(8,128)(2,1)} %copy-done.4), custom_call_target="tpu_custom_call" | custom-call | flops 1 | bytes 1 | tf_op jit(solution)/shard_map/pallas_call | solution.py:440
  163.5 4.0 collective-permute-start.18
  176.9 28.9 %shard_map.90 = (f32[512,512]{1,0:T(8,128)S(1)}, f32[512,512]{1,0:T(8,128)S(1)}, f32[8,128]{1,0:T(8,128)S(1)}) custom-call(s32[7]{0:T(128)S(1)} %stack.54.refs_0_, f32[1]{0:T(128)} %bitcast.10.refs_1_, f32[512,512]{1,0:T(8,128)S(1)} %copy-done.7, bf16[784,512]{1,0:T(8,128)(2,1)S(1)} %bitcast.62, bf16[784,512]{1,0:T(8,128)(2,1)S(1)} %copy-done.5, ...), custom_call_target="tpu_custom_call" | custom-call | flops 1 | bytes 1 | tf_op jit(solution)/shard_map/pallas_call | solution.py:163
  215.3 5.5 %shard_map.93 = bf16[2,768,512]{2,1,0:T(8,128)(2,1)} custom-call(s32[1]{0:T(128)} %bitcast.28.refs_0_, bf16[4,768,512]{2,1,0:T(8,128)(2,1)} %bitcast.69, f32[512,512]{1,0:T(8,128)} %copy-done.2), custom_call_target="tpu_custom_call" | custom-call | flops 1 | bytes 1 | tf_op jit(solution)/shard_map/pallas_call | solution.py:440
  222.1 5.7 %shard_map.96 = (bf16[1,784,512]{2,1,0:T(8,128)(2,1)}, bf16[1,784,512]{2,1,0:T(8,128)(2,1)}) custom-call(s32[2]{0:T(128)} %pad_add_fusion.1.refs_0_, bf16[4,784,512]{2,1,0:T(8,128)(2,1)} %bitcast.67, bf16[2,784,512]{2,1,0:T(8,128)(2,1)} %collective-permute-done.18.refs_2_.refs_13_, bf16[784,512]{1,0:T(8,128)(2,1)} %copy-done.4), custom_call_target="tpu_custom_call" | custom-call | flops 1 | bytes 1 | tf_op jit(solution)/shard_map/pallas_call | solution.py:440
  228.3 27.3 %collective-permute-done.15.refs_2_.refs_12_ = bf16[2,768,512]{2,1,0:T(8,128)(2,1)S(1)} collective-permute-done((bf16[2,768,512]{2,1,0:T(8,128)(2,1)}, bf16[2,768,512]{2,1,0:T(8,128)(2,1)S(1)}, u32[]{:S(2)}, u32[]{:S(2)}) %collective-permute-start.15) | collective-permute-done | bytes 1572896 | tf_op jit(solution)/shard_map/ppermute | solution.py:405
  256.7 4.3 %shard_map.94 = (bf16[1,768,512]{2,1,0:T(8,128)(2,1)}, bf16[1,768,512]{2,1,0:T(8,128)(2,1)}) custom-call(s32[2]{0:T(128)} %pad_add_fusion.1.refs_0_, bf16[4,768,512]{2,1,0:T(8,128)(2,1)} %bitcast.70, bf16[2,768,512]{2,1,0:T(8,128)(2,1)} %copy-done.18, f32[512,512]{1,0:T(8,128)} %copy-done.2), custom_call_target="tpu_custom_call" | custom-call | flops 1 | bytes 1 | tf_op jit(solution)/shard_map/pallas_call | solution.py:440
  262.8 15.6 %shard_map.91 = (bf16[512,1536]{1,0:T(8,128)(2,1)}, bf16[2560,512]{1,0:T(8,128)(2,1)}, bf16[2560,1536]{1,0:T(8,128)(2,1)}) custom-call(s32[7]{0:T(128)} %copy-done.15, f32[8,128]{1,0:T(8,128)} %copy-done.14, f32[512,512]{1,0:T(8,128)} %copy-done.2, bf16[784,512]{1,0:T(8,128)(2,1)} %bitcast.60, bf16[784,512]{1,0:T(8,128)(2,1)} %copy-done.4, ...), custom_call_target="tpu_custom_call" | custom-call | flops 1 | bytes 1 | tf_op jit(solution)/shard_map/pallas_call | solution.py:204
  278.5 5.2 %shard_map.101 = bf16[2,768,256]{2,1,0:T(8,128)(2,1)} custom-call(s32[1]{0:T(128)} %bitcast.28.refs_0_, bf16[4,768,256]{2,1,0:T(8,128)(2,1)} %bitcast.72, bf16[512,1536]{1,0:T(8,128)(2,1)} %get-tuple-element.32.refs_5_.refs_2_.refs_3_), custom_call_target="tpu_custom_call" | custom-call | flops 1 | bytes 1 | tf_op jit(solution)/shard_map/pallas_call | solution.py:440
  285.3 6.0 %subtract_convert_fusion = (bf16[512,2048]{1,0:T(8,128)(2,1)}, bf16[512,2048]{1,0:T(8,128)(2,1)}) fusion(f32[512,512]{1,0:T(8,128)S(1)} %copy-done.3, bf16[512,2048]{1,0:T(8,128)(2,1)} %collective-permute-done.14, bf16[512,2048]{1,0:T(8,128)(2,1)} %select_select_fusion, pred[]{:T(512)S(6)} %eq.112), kind=kOutput, calls=%fused_computation | convolution fusion | flops 3226468352 | bytes 9437185 | tf_op jit(solution)/shard_map/dot_general | solution.py:570
  292.2 22.3 %shard_map.97 = (f32[1536,1536]{1,0:T(8,128)}, f32[1536,1536]{1,0:T(8,128)}, f32[1536,2048]{1,0:T(8,128)}, f32[8,128]{1,0:T(8,128)}) custom-call(s32[11]{0:T(128)} %stack.63.refs_0_, f32[1]{0:T(128)} %bitcast.10.refs_1_, f32[8,128]{1,0:T(8,128)} %copy-done.14, f32[1536,1536]{1,0:T(8,128)} %refs_3_.7, bf16[1536,2048]{1,0:T(8,128)(2,1)} %refs_4_.7, ...), custom_call_target="tpu_custom_call" | custom-call | flops 1 | bytes 1 | tf_op jit(solution)/shard_map/pallas_call | solution.py:373
  314.6 21.6 %shard_map.98 = (f32[1536,1536]{1,0:T(8,128)}, f32[1536,1536]{1,0:T(8,128)}, f32[1536,2048]{1,0:T(8,128)}, f32[8,128]{1,0:T(8,128)}) custom-call(s32[11]{0:T(128)} %stack.59.refs_0_, f32[1]{0:T(128)} %bitcast.10.refs_1_, f32[8,128]{1,0:T(8,128)} %copy-done.14, f32[1536,1536]{1,0:T(8,128)} %refs_3_.7, ...), custom_call_target="tpu_custom_call", output_to_operand_aliasing={{0}: (15, {}), {1}: (16, {}), {2}: (17, {})} | custom-call | flops 1 | bytes 1 | tf_op jit(solution)/shard_map/pallas_call | solution.py:373
  336.2 5.0 %shard_map.99 = bf16[2,768,256]{2,1,0:T(8,128)(2,1)} custom-call(s32[1]{0:T(128)} %bitcast.28.refs_0_, bf16[4,768,256]{2,1,0:T(8,128)(2,1)} %bitcast.76, f32[8,128]{1,0:T(8,128)} %get-tuple-element.43.refs_2_.refs_3_), custom_call_target="tpu_custom_call" | custom-call | flops 1 | bytes 1 | tf_op jit(solution)/shard_map/pallas_call | solution.py:440
  344.0 4.0 shard_map.102
  348.4 12.3 %collective-permute-done.21.refs_2_.refs_12_ = bf16[2,768,256]{2,1,0:T(8,128)(2,1)S(1)} collective-permute-done((bf16[2,768,256]{2,1,0:T(8,128)(2,1)}, bf16[2,768,256]{2,1,0:T(8,128)(2,1)S(1)}, u32[]{:S(2)}, u32[]{:S(2)}) %collective-permute-start.21) | collective-permute-done | bytes 786464 | tf_op jit(solution)/shard_map/ppermute | solution.py:405
  361.6 4.0 shard_map.100
  368.3 15.5 %shard_map.103 = (f32[1536,1536]{1,0:T(8,128)}, f32[1536,1536]{1,0:T(8,128)}, f32[1536,2048]{1,0:T(8,128)}, f32[8,128]{1,0:T(8,128)}) custom-call(s32[11]{0:T(128)} %stack.65.refs_0_, f32[1]{0:T(128)} %bitcast.10.refs_1_, f32[8,128]{1,0:T(8,128)} %copy-done.14, f32[1536,1536]{1,0:T(8,128)} %refs_3_.7, ...), custom_call_target="tpu_custom_call", output_to_operand_aliasing={{0}: (15, {}), {1}: (16, {}), {2}: (17, {})} | custom-call | flops 1 | bytes 1 | tf_op jit(solution)/shard_map/pallas_call | solution.py:373
  384.6 15.6 %shard_map.104 = (f32[1536,1536]{1,0:T(8,128)}, f32[1536,1536]{1,0:T(8,128)}, f32[1536,2048]{1,0:T(8,128)}, f32[8,128]{1,0:T(8,128)}) custom-call(s32[11]{0:T(128)} %stack.52.refs_0_, f32[1]{0:T(128)} %bitcast.10.refs_1_, f32[8,128]{1,0:T(8,128)} %copy-done.14, f32[1536,1536]{1,0:T(8,128)} %refs_3_.7, ...), custom_call_target="tpu_custom_call", output_to_operand_aliasing={{0}: (15, {}), {1}: (16, {}), {2}: (17, {})} | custom-call | flops 1 | bytes 1 | tf_op jit(solution)/shard_map/pallas_call | solution.py:373
  (171 shorter events, 70.7 us)
Async XLA Ops:
  7.2 117.1 %all-gather.9.cloned.1.call-start = ((), (), s32[]{:S(2)}) async-start(), calls=%async_computation | async-start | bytes 4014080 | tf_op jit(solution)/shard_map/all_gather | solution.py:554
  39.8 175.4 %all-gather.13.cloned.1.call-start = ((), (), s32[]{:S(2)}) async-start(), calls=%async_computation.2 | async-start | bytes 3932160 | tf_op jit(solution)/shard_map/all_gather | solution.py:554
  43.3 23.1 %collective-permute-start.4 = (bf16[320,1536]{1,0:T(8,128)(2,1)S(1)}, bf16[320,1536]{1,0:T(8,128)(2,1)}, u32[]{:S(2)}, u32[]{:S(2)}) collective-permute-start(bf16[320,1536]{1,0:T(8,128)(2,1)S(1)} %get-tuple-element.63), channel_id=1, source_target_pairs={{0,16},{4,20},{8,24},{12,28},{16,0},{20,4},{24,8},{28,12},{1,17},{... | collective-permute-start | bytes 2949128 | tf_op jit(solution)/shard_map/ppermute | solution.py:405
  72.5 206.0 %all-gather.15.cloned.1.call-start = ((), (), s32[]{:S(2)}) async-start(), calls=%async_computation.3 | async-start | bytes 1966080 | tf_op jit(solution)/shard_map/all_gather | solution.py:554
  72.6 51.7 %collective-permute-start.3 = (bf16[448,1536]{1,0:T(8,128)(2,1)S(1)}, bf16[448,1536]{1,0:T(8,128)(2,1)}, u32[]{:S(2)}, u32[]{:S(2)}) collective-permute-start(bf16[448,1536]{1,0:T(8,128)(2,1)S(1)} %pad_maximum_fusion.1.refs_7_), channel_id=1, source_target_pairs={{0,8},{4,12},{8,0},{12,4},{16,24},{20,28},{24,16},{28,20},{1,9},{5... | collective-permute-start | bytes 4128776 | tf_op jit(solution)/shard_map/ppermute | solution.py:405
  73.8 50.5 %collective-permute-start.5 = (bf16[320,1536]{1,0:T(8,128)(2,1)}, bf16[320,1536]{1,0:T(8,128)(2,1)}, u32[]{:S(2)}, u32[]{:S(2)}) collective-permute-start(bf16[320,1536]{1,0:T(8,128)(2,1)} %collective-permute-done.4.refs_11_), channel_id=1, source_target_pairs={{0,8},{4,12},{8,0},{12,4},{16,24},{20,28},{24,16},{28,20},{1,9},{5... | collective-permute-start | bytes 2949128 | tf_op jit(solution)/shard_map/ppermute | solution.py:405
  153.3 55.0 %collective-permute-start.13 = (bf16[512,2048]{1,0:T(8,128)(2,1)}, bf16[512,2048]{1,0:T(8,128)(2,1)}, u32[]{:S(2)}, u32[]{:S(2)}) collective-permute-start(bf16[512,2048]{1,0:T(8,128)(2,1)} %bitcast.79), channel_id=1, source_target_pairs={{0,8},{16,24},{1,9},{17,25},{2,10},{18,26},{3,11},{19,27}} | collective-permute-start | bytes 6291464 | tf_op jit(solution)/shard_map/ppermute | solution.py:488
  154.6 181.6 %all-gather.11.cloned.1.call-start = ((), (), s32[]{:S(2)}) async-start(), calls=%async_computation.1 | async-start | bytes 1966080 | tf_op jit(solution)/shard_map/all_gather | solution.py:554
  163.5 57.9 %collective-permute-start.18 = (bf16[2,784,512]{2,1,0:T(8,128)(2,1)}, bf16[2,784,512]{2,1,0:T(8,128)(2,1)}, u32[]{:S(2)}, u32[]{:S(2)}) collective-permute-start(bf16[2,784,512]{2,1,0:T(8,128)(2,1)} %shard_map.95), channel_id=1, source_target_pairs={{0,8},{4,12},{8,0},{12,4},{16,24},{20,28},{24,16},{28,20},{1,9},{5... | collective-permute-start | bytes 4816904 | tf_op jit(solution)/shard_map/ppermute | solution.py:405
  171.6 49.4 %collective-permute-start.11 = (bf16[320,1536]{1,0:T(8,128)(2,1)}, bf16[320,1536]{1,0:T(8,128)(2,1)}, u32[]{:S(2)}, u32[]{:S(2)}) collective-permute-start(bf16[320,1536]{1,0:T(8,128)(2,1)} %collective-permute-done.4.refs_11_), channel_id=1, source_target_pairs={{0,4},{4,0},{8,12},{12,8},{16,20},{20,16},{24,28},{28,24},{1,5},{5... | collective-permute-start | bytes 2949128 | tf_op jit(solution)/shard_map/ppermute | solution.py:405
  211.5 73.5 %collective-permute-start.14 = (bf16[512,2048]{1,0:T(8,128)(2,1)}, bf16[512,2048]{1,0:T(8,128)(2,1)}, u32[]{:S(2)}, u32[]{:S(2)}) collective-permute-start(bf16[512,2048]{1,0:T(8,128)(2,1)} %select_select_fusion), channel_id=1, source_target_pairs={{0,4},{8,12},{16,20},{24,28},{1,5},{9,13},{17,21},{25,29},{2,6},{1... | collective-permute-start | bytes 6291464 | tf_op jit(solution)/shard_map/ppermute | solution.py:488
  220.8 34.8 %collective-permute-start.15 = (bf16[2,768,512]{2,1,0:T(8,128)(2,1)}, bf16[2,768,512]{2,1,0:T(8,128)(2,1)S(1)}, u32[]{:S(2)}, u32[]{:S(2)}) collective-permute-start(bf16[2,768,512]{2,1,0:T(8,128)(2,1)} %shard_map.93), channel_id=1, source_target_pairs={{0,8},{4,12},{8,0},{12,4},{16,24},{20,28},{24,16},{28,20},{1,9},{5... | collective-permute-start | bytes 4718600 | tf_op jit(solution)/shard_map/ppermute | solution.py:405
  220.9 40.1 %collective-permute-start.10 = (bf16[448,1536]{1,0:T(8,128)(2,1)}, bf16[448,1536]{1,0:T(8,128)(2,1)}, u32[]{:S(2)}, u32[]{:S(2)}) collective-permute-start(bf16[448,1536]{1,0:T(8,128)(2,1)} %collective-permute-done.3.refs_2_.refs_8_), channel_id=1, source_target_pairs={{0,4},{4,0},{8,12},{12,8},{16,20},{20,16},{24,28},{28,24},{1,5},{5... | collective-permute-start | bytes 4128776 | tf_op jit(solution)/shard_map/ppermute | solution.py:405
  221.4 39.6 %collective-permute-start.12 = (bf16[320,1536]{1,0:T(8,128)(2,1)}, bf16[320,1536]{1,0:T(8,128)(2,1)}, u32[]{:S(2)}, u32[]{:S(2)}) collective-permute-start(bf16[320,1536]{1,0:T(8,128)(2,1)} %collective-permute-done.5.refs_3_.refs_12_), channel_id=1, source_target_pairs={{0,4},{4,0},{8,12},{12,8},{16,20},{20,16},{24,28},{28,24},{1,5},{5... | collective-permute-start | bytes 2949128 | tf_op jit(solution)/shard_map/ppermute | solution.py:405
  227.8 63.4 %collective-permute-start.19 = (bf16[1,784,512]{2,1,0:T(8,128)(2,1)}, bf16[1,784,512]{2,1,0:T(8,128)(2,1)S(1)}, u32[]{:S(2)}, u32[]{:S(2)}) collective-permute-start(bf16[1,784,512]{2,1,0:T(8,128)(2,1)} %get-tuple-element.38), channel_id=1, source_target_pairs={{0,4},{4,0},{8,12},{12,8},{16,20},{20,16},{24,28},{28,24},{1,5},{5... | collective-permute-start | bytes 2408456 | tf_op jit(solution)/shard_map/ppermute | solution.py:405
  255.6 35.7 %collective-permute-start.20 = (bf16[1,784,512]{2,1,0:T(8,128)(2,1)}, bf16[1,784,512]{2,1,0:T(8,128)(2,1)}, u32[]{:S(2)}, u32[]{:S(2)}) collective-permute-start(bf16[1,784,512]{2,1,0:T(8,128)(2,1)} %get-tuple-element.39), channel_id=1, source_target_pairs={{0,4},{4,0},{8,12},{12,8},{16,20},{20,16},{24,28},{28,24},{1,5},{5... | collective-permute-start | bytes 2408456 | tf_op jit(solution)/shard_map/ppermute | solution.py:405
  261.0 53.5 %collective-permute-start.16 = (bf16[1,768,512]{2,1,0:T(8,128)(2,1)}, bf16[1,768,512]{2,1,0:T(8,128)(2,1)}, u32[]{:S(2)}, u32[]{:S(2)}) collective-permute-start(bf16[1,768,512]{2,1,0:T(8,128)(2,1)} %get-tuple-element.35), channel_id=1, source_target_pairs={{0,4},{4,0},{8,12},{12,8},{16,20},{20,16},{24,28},{28,24},{1,5},{5... | collective-permute-start | bytes 2359304 | tf_op jit(solution)/shard_map/ppermute | solution.py:405
  261.0 53.5 %collective-permute-start.17 = (bf16[1,768,512]{2,1,0:T(8,128)(2,1)}, bf16[1,768,512]{2,1,0:T(8,128)(2,1)}, u32[]{:S(2)}, u32[]{:S(2)}) collective-permute-start(bf16[1,768,512]{2,1,0:T(8,128)(2,1)} %get-tuple-element.36), channel_id=1, source_target_pairs={{0,4},{4,0},{8,12},{12,8},{16,20},{20,16},{24,28},{28,24},{1,5},{5... | collective-permute-start | bytes 2359304 | tf_op jit(solution)/shard_map/ppermute | solution.py:405
  285.0 58.1 %collective-permute-start.24 = (bf16[2,768,256]{2,1,0:T(8,128)(2,1)}, bf16[2,768,256]{2,1,0:T(8,128)(2,1)S(1)}, u32[]{:S(2)}, u32[]{:S(2)}) collective-permute-start(bf16[2,768,256]{2,1,0:T(8,128)(2,1)} %shard_map.101), channel_id=1, source_target_pairs={{0,8},{4,12},{8,0},{12,4},{16,24},{20,28},{24,16},{28,20},{1,9},{5... | collective-permute-start | bytes 2359304 | tf_op jit(solution)/shard_map/ppermute | solution.py:405
  341.2 19.5 %collective-permute-start.21 = (bf16[2,768,256]{2,1,0:T(8,128)(2,1)}, bf16[2,768,256]{2,1,0:T(8,128)(2,1)S(1)}, u32[]{:S(2)}, u32[]{:S(2)}) collective-permute-start(bf16[2,768,256]{2,1,0:T(8,128)(2,1)} %shard_map.99), channel_id=1, source_target_pairs={{0,8},{4,12},{8,0},{12,4},{16,24},{20,28},{24,16},{28,20},{1,9},{5... | collective-permute-start | bytes 2359304 | tf_op jit(solution)/shard_map/ppermute | solution.py:405
  347.9 19.4 %collective-permute-start.25 = (bf16[1,768,256]{2,1,0:T(8,128)(2,1)}, bf16[1,768,256]{2,1,0:T(8,128)(2,1)S(1)}, u32[]{:S(2)}, u32[]{:S(2)}) collective-permute-start(bf16[1,768,256]{2,1,0:T(8,128)(2,1)} %get-tuple-element.46), channel_id=1, source_target_pairs={{0,4},{4,0},{8,12},{12,8},{16,20},{20,16},{24,28},{28,24},{1,5},{5... | collective-permute-start | bytes 1179656 | tf_op jit(solution)/shard_map/ppermute | solution.py:405
  347.9 19.4 %collective-permute-start.26 = (bf16[1,768,256]{2,1,0:T(8,128)(2,1)}, bf16[1,768,256]{2,1,0:T(8,128)(2,1)S(1)}, u32[]{:S(2)}, u32[]{:S(2)}) collective-permute-start(bf16[1,768,256]{2,1,0:T(8,128)(2,1)} %get-tuple-element.47), channel_id=1, source_target_pairs={{0,4},{4,0},{8,12},{12,8},{16,20},{20,16},{24,28},{28,24},{1,5},{5... | collective-permute-start | bytes 1179656 | tf_op jit(solution)/shard_map/ppermute | solution.py:405
  365.6 18.2 %collective-permute-start.22 = (bf16[1,768,256]{2,1,0:T(8,128)(2,1)}, bf16[1,768,256]{2,1,0:T(8,128)(2,1)S(1)}, u32[]{:S(2)}, u32[]{:S(2)}) collective-permute-start(bf16[1,768,256]{2,1,0:T(8,128)(2,1)} %get-tuple-element.44), channel_id=1, source_target_pairs={{0,4},{4,0},{8,12},{12,8},{16,20},{20,16},{24,28},{28,24},{1,5},{5... | collective-permute-start | bytes 1179656 | tf_op jit(solution)/shard_map/ppermute | solution.py:405
  365.6 18.2 %collective-permute-start.23 = (bf16[1,768,256]{2,1,0:T(8,128)(2,1)}, bf16[1,768,256]{2,1,0:T(8,128)(2,1)S(1)}, u32[]{:S(2)}, u32[]{:S(2)}) collective-permute-start(bf16[1,768,256]{2,1,0:T(8,128)(2,1)} %get-tuple-element.45), channel_id=1, source_target_pairs={{0,4},{4,0},{8,12},{12,8},{16,20},{20,16},{24,28},{28,24},{1,5},{5... | collective-permute-start | bytes 1179656 | tf_op jit(solution)/shard_map/ppermute | solution.py:405
  (38 other events, 251.2 us)
Sparse Core Ops, SparseCore 0:
  39.9 65.8 all-gather.8
  107.3 62.1 all-gather.12
  171.1 35.7 all-gather.14
  220.9 38.7 all-gather.10

commit v6 on v5

--- a/solution.py
+++ b/solution.py
@@ -12,6 +12,7 @@
 ROWS = 256
 COLS = 512
 PLACES = 3
+ANYWHERE = pl.BlockSpec(memory_space=pl.ANY)
 NO_COST = pl.CostEstimate(flops=1, bytes_accessed=1, transcendentals=0)
 DECAY = 0.8
 
@@ -23,6 +24,21 @@
 def dot_t(left, right, precision=None):
     return lax.dot_general(
         left, right, (((0,), (0,)), ((), ())), precision=precision, preferred_element_type=F32
+    )
+
+
+def split(value):
+    high = value.astype(BF16)
+    return high, (value - high.astype(F32)).astype(BF16)
+
+
+def dot_split(left, right, contract):
+    (left_high, left_low), (right_high, right_low) = split(left), split(right)
+    product = lambda a, b: lax.dot_general(
+        a, b, (contract, ((), ())), preferred_element_type=F32
+    )
+    return product(left_high, right_high) + (
+        product(left_high, right_low) + product(left_low, right_high)
     )
 
 
@@ -82,7 +98,7 @@
 
 def factor_kernel(count, places_ref, damp_ref, exact_ref, *refs):
     lead_refs = refs[:count]
-    upper_ref, inverse_ref, share_ref, work_ref = refs[-4:]
+    lower_ref, inverse_ref, share_ref, work_ref, upper_ref = refs[-5:]
     steps = LEAD // TILE
     side = LEAD // count
     marks = sum(lead[2 * CAP + side :, :].astype(F32) for lead in lead_refs)
@@ -154,21 +170,22 @@
         return carry
 
     lax.fori_loop(0, steps, tile_step, 0)
-
-
-def factor_lead(places, damp, exact, lead):
+    lower_ref[...] = upper_ref[...].T
+
+
+def factor_lead(places, damp, exact, lead, earlier):
     shape = jax.ShapeDtypeStruct((LEAD, LEAD), F32)
     vmem = pl.BlockSpec(memory_space=pltpu.VMEM)
     smem = pl.BlockSpec(memory_space=pltpu.SMEM)
     return pl.pallas_call(
         lambda *refs: factor_kernel(len(lead), *refs),
         out_shape=(shape, shape, jax.ShapeDtypeStruct((GROUP, TILE), F32)),
-        in_specs=[smem, smem] + [vmem] * (1 + len(lead)),
+        in_specs=[smem, smem] + [vmem] * (1 + len(lead)) + [ANYWHERE] * len(earlier),
         out_specs=(vmem, vmem, vmem),
-        scratch_shapes=[pltpu.VMEM((LEAD, LEAD), F32)],
+        scratch_shapes=[pltpu.VMEM((LEAD, LEAD), F32)] * 2,
         compiler_params=pltpu.CompilerParams(vmem_limit_bytes=32 * 1024 * 1024),
         cost_estimate=NO_COST,
-    )(places, damp, exact, *lead)
+    )(places, damp, exact, *lead, *earlier)
 
 
 def panel_kernel(count, places_ref, share_ref, inverse_ref, *refs):
@@ -189,9 +206,7 @@
 
     gram = dot_t(lead_ref[...], across_ref[...])
     beside = DECAY * near_ref[...] + share_ref[:1, :1] * gram
-    out_ref[...] = jnp.dot(
-        inverse_ref[...], beside, precision=HIGHEST, preferred_element_type=F32
-    ).astype(BF16)
+    out_ref[...] = dot_split(inverse_ref[...], beside, ((1,), (0,))).astype(BF16)
 
 
 def panel_columns(places, share, inverse, lead, own, other):
@@ -224,6 +239,34 @@
     )(places, share, inverse, *lead, *own, *other)
 
 
+def solve_kernel(flag_ref, inverse_ref, first_ref, second_ref, *refs):
+    high_ref, low_ref = refs[-2:]
+    values = jnp.where(flag_ref[0] == 1, first_ref[...], second_ref[...])
+    high, low = split(inverse_ref[...])
+    solved = jnp.dot(high, values, preferred_element_type=F32)
+    solved = solved + jnp.dot(low, values, preferred_element_type=F32)
+    high_ref[...], low_ref[...] = split(solved)
+
+
+def solve_lead(flag, inverse, first, second, earlier):
+    tiled = pl.BlockSpec((LEAD, ROWS), lambda j: (0, j))
+    return pl.pallas_call(
+        solve_kernel,
+        grid=(first.shape[1] // ROWS,),
+        out_shape=(jax.ShapeDtypeStruct(first.shape, BF16),) * 2,
+        in_specs=[
+            pl.BlockSpec(memory_space=pltpu.SMEM),
+            pl.BlockSpec((LEAD, LEAD), lambda j: (0, 0)),
+            tiled,
+            tiled,
+        ]
+        + [ANYWHERE] * len(earlier),
+        out_specs=(tiled, tiled),
+        compiler_params=pltpu.CompilerParams(vmem_limit_bytes=32 * 1024 * 1024),
+        cost_estimate=NO_COST,
+    )(flag, inverse, first, second, *earlier)
+
+
 def finish_kernel(
     count,
     gram_steps,
@@ -237,13 +280,12 @@
     panel_ref,
     inverse_ref,
     high_ref,
-    low_ref,
     lead_ref,
     across_ref,
     *refs,
 ):
     if first_chunk:
-        lower_ref, *refs = refs
+        lower_ref, low_ref, *refs = refs
     mine = refs[:count]
     outs = refs[count + unread :]
     running_ref, factored_ref, precond_ref, token_ref, mine_ref, rows_ref, first_ref = outs
@@ -271,13 +313,7 @@
         col = lax.broadcasted_iota(jnp.int32, (height, LEAD), 1)
         source = DECAY * source + share * gram
         source = source + jnp.where(row == col, damp, 0.0)
-        rows_ref[span, :] = lax.dot_general(
-            source,
-            inverse_ref[...],
-            (((1,), (1,)), ((), ())),
-            precision=HIGHEST,
-            preferred_element_type=F32,
-        )
+        rows_ref[span, :] = dot_split(source, inverse_ref[...], ((1,), (1,)))
 
     panel = rows_ref[span, :].astype(BF16)
 
@@ -305,9 +341,7 @@
                     def _():
                         factored_ref[...] = lower_ref[span, edge]
 
-    high, low = high_ref[...], low_ref[...]
-    product = jnp.dot(panel, high, preferred_element_type=F32)
-    product = product + jnp.dot(panel, low, preferred_element_type=F32)
+    product = jnp.dot(panel, high_ref[...], preferred_element_type=F32)
     precond_ref[...] = grad_ref[...].astype(F32) - product
 
     if first_chunk:
@@ -356,20 +390,19 @@
         pl.BlockSpec((LEAD, cols), lambda j, i, p: (0, gram_col(j))),
         lead_whole,
         pl.BlockSpec((LEAD, cols), lambda j, i, p: (0, j)),
-        pl.BlockSpec((LEAD, cols), lambda j, i, p: (0, j)),
         pl.BlockSpec((tall, LEAD), lambda j, i, p: (0, 0)),
         pl.BlockSpec((tall, cols), lambda j, i, p: (0, gram_col(j))),
     ]
-    operands = [damp, share, factor, grad, panel, inverse, high, low, lead, across]
+    operands = [damp, share, factor, grad, panel, inverse, high, lead, across]
     if begin == 0:
-        in_specs += [lead_whole]
-        operands += [lower]
+        in_specs += [lead_whole, pl.BlockSpec((LEAD, cols), lambda j, i, p: (0, j))]
+        operands += [lower, low]
     in_specs += [mine_spec(q) for q in range(count)]
     operands += mine
     aliases = {1 + len(operands) + k: k for k in range(len(results))}
     operands += [*results, *earlier]
     unread = len(results) + len(earlier)
-    in_specs += [pl.BlockSpec(memory_space=pl.ANY)] * unread
+    in_specs += [ANYWHERE] * unread
     return pl.pallas_call(
         lambda *refs: finish_kernel(count, gram_steps, begin == 0, unread, *refs),
         grid_spec=pltpu.PrefetchScalarGridSpec(
@@ -412,57 +445,75 @@
     return pieces
 
 
-def copy_kernel(count, starts_ref, *refs):
+def copy_kernel(count, places_ref, *refs):
     for source, out in zip(refs[:count], refs[-count:]):
         out[...] = source[...].astype(BF16)
 
 
 def copied(requests, earlier):
-    in_specs, out_specs, shapes, starts = [], [], [], []
-    for number, (array, begin, size) in enumerate(requests):
-        rows = array.shape[-2]
-        split = next(parts for parts in (4, 7, 1) if rows % (16 * parts) == 0)
-        if array.ndim == 3:
-            count, width = size, array.shape[2]
-            shapes.append((count, rows, width))
-            starts.append(begin)
-            block = (1, rows // split, width)
-            in_specs.append(pl.BlockSpec(block, lambda k, r, p, n=number: (p[n] + k, r, 0)))
-            out_specs.append(pl.BlockSpec(block, lambda k, r, p: (k, r, 0)))
-        else:
-            count, width = 1, size - begin
-            shapes.append((rows, width))
-            starts.append(begin // width)
-            block = (rows // split, width)
-            in_specs.append(pl.BlockSpec(block, lambda k, r, p, n=number: (r, p[n])))
-            out_specs.append(pl.BlockSpec(block, lambda k, r, p: (r, 0)))
+    in_specs, out_specs, shapes, places = [], [], [], []
+    for array, block, place in requests:
+        at = len(places)
+        places += place
+        shape = tuple(size for size in block if size is not None)
+        shapes.append(shape)
+        in_specs.append(
+            pl.BlockSpec(block, lambda i, p, a=at, n=len(block): tuple(p[a + k] for k in range(n)))
+        )
+        out_specs.append(pl.BlockSpec(shape, lambda i, p: (0, 0)))
     arrays = [array for array, _, _ in requests]
     return pl.pallas_call(
         lambda *refs: copy_kernel(len(arrays), *refs),
         grid_spec=pltpu.PrefetchScalarGridSpec(
             num_scalar_prefetch=1,
-            grid=(count, split),
-            in_specs=in_specs + [pl.BlockSpec(memory_space=pl.ANY)] * len(earlier),
+            grid=(1,),
+            in_specs=in_specs + [ANYWHERE] * len(earlier),
             out_specs=out_specs,
         ),
         out_shape=[jax.ShapeDtypeStruct(shape, BF16) for shape in shapes],
+        compiler_params=pltpu.CompilerParams(vmem_limit_bytes=32 * 1024 * 1024),
         cost_estimate=NO_COST,
-    )(jnp.stack([jnp.int32(start) for start in starts]), *arrays, *earlier)
-
-
-def exchange_members(blocks, member, bits, earlier):
-    views = [(blocks, 0)]
-    sent = []
-    count = blocks.shape[0]
+    )(jnp.stack([jnp.int32(place) for place in places]), *arrays, *earlier)
+
+
+def choose_kernel(flag_ref, first_ref, second_ref, *refs):
+    refs[-1][...] = jnp.where(flag_ref[0] == 1, first_ref[...], second_ref[...])
+
+
+def chosen(flag, first, second, earlier):
+    tiled = pl.BlockSpec((first.shape[0] // 2, first.shape[1]), lambda i: (i, 0))
+    return pl.pallas_call(
+        choose_kernel,
+        grid=(2,),
+        out_shape=jax.ShapeDtypeStruct(first.shape, first.dtype),
+        in_specs=[pl.BlockSpec(memory_space=pltpu.SMEM), tiled, tiled] + [ANYWHERE] * len(earlier),
+        out_specs=tiled,
+        compiler_params=pltpu.CompilerParams(vmem_limit_bytes=32 * 1024 * 1024),
+        cost_estimate=NO_COST,
+    )(flag, first, second, *earlier)
+
+
+def member_blocks(blocks, member, group, earlier):
+    _, rows, width = blocks.shape
+    return copied(
+        [(blocks, (None, rows, width), [member ^ other, 0, 0]) for other in range(1, group)],
+        earlier,
+    )
+
+
+def exchange_members(blocks, sent, bits, earlier):
+    held = [[blocks]] + [[part] for part in sent]
     for bit in reversed(range(bits)):
-        count = count // 2
-        mine = member >> bit & 1
-        sent = copied(
-            [(array, at + (1 - mine) * count, count) for array, at in views], earlier
-        )
-        kept = [(array, at + mine * count) for array, at in views]
-        views = kept + [(swapped(part, 1 << bit), 0) for part in sent]
-    return views
+        half = 1 << bit
+        for passed in held[half:]:
+            if earlier:
+                passed[1:] = [copied([(part, part.shape, [0, 0])], earlier)[0] for part in passed[1:]]
+        held = [
+            kept + [swapped(part, half) for part in passed]
+            for kept, passed in zip(held[:half], held[half:])
+        ]
+    first, *others = held[0]
+    return [first] + [part[None] for part in others]
 
 
 def member_order(bits):
@@ -481,21 +532,15 @@
     ]
 
 
-def from_first_member(value, member, group, bits, earlier):
+def share_of_first(lower, upper, member, group, bits):
+    arrived = None
     for bit in reversed(range(bits)):
-        if 1 << bit < group // 2:
-            value = after(value, earlier)
-        moved = lax.ppermute(value, "tok", down_pairs(bit, group))
-        value = jnp.where(member >> bit & 1 == 1, moved, value)
-    return value
-
-
-def share_of_first(blocks, member, group, bits):
-    for bit in reversed(range(bits)):
+        moved = lax.ppermute(upper, "tok", down_pairs(bit, group))
+        arrived = moved if arrived is None else arrived
+        blocks = jnp.where(member >> bit & 1 == 1, moved, lower)
         half = blocks.shape[0] // 2
-        moved = lax.ppermute(blocks[half:], "tok", down_pairs(bit, group))
-        blocks = jnp.where(member >> bit & 1 == 1, moved, blocks[:half])
-    return blocks[0]
+        lower, upper = blocks[:half], blocks[half:]
+    return blocks, arrived
 
 
 def count_rows(number, row, width):
@@ -515,9 +560,9 @@
     damp = jnp.where(expert == 0, damping[0], damping[1])[None]
     order = [member ^ other for other in member_order(bits)]
 
-    lead_factor = factor_old.reshape(-1, LEAD // group, width)
-    lead_factor = copied([(lead_factor, 0, group)], [])[0]
-    lead_factor = share_of_first(lead_factor, member, group, bits)
+    side = LEAD // 2
+    halves = [(factor_old, (side, width), [place, 0]) for place in range(2)]
+    lead_factor, arrived = share_of_first(*copied(halves, []), member, group, bits)
 
     live = jnp.arange(tok_rows) < counts[0]
     named = routes[:, 0]
@@ -544,43 +589,54 @@
     )
     incoming = swapped(after(packed[CAP:], front), group)
     outgoing = jnp.concatenate([packed[:CAP], lead_factor], 0)
+    quarter = jnp.concatenate([packed[:CAP], incoming, lead_factor], 0)
+
+    grad_cols = weight_grad.shape[1]
+    near = copied([(weight_grad, (LEAD, grad_cols), [0, 0])], [arrived])[0]
+    across_own = gather_members(outgoing, bits)
+    across_other = gather_members(incoming, bits)
+    for bit in reversed(range(bits)):
+        moved = lax.ppermute(near, "tok", down_pairs(bit, group))
+        flag = (member >> bit & 1)[None]
+        if bit:
+            near = chosen(flag, moved, near, [across_own[1]])
 
     ends = [end for end in (LEAD, 2 * LEAD, 2 * LEAD + ROWS) if end < width] + [width]
     chunks = list(zip([0, *ends], ends))
-    parts = [first_part]
-    quarter = jnp.concatenate([packed[:CAP], incoming, lead_factor], 0)
-    for begin, end in chunks[1:]:
-        parts += copied([(quarter, begin, end)], [parts[-1]])
+    rows = quarter.shape[0]
+    later = [
+        (quarter, (rows, end - begin), [0, begin // (end - begin)]) for begin, end in chunks[1:]
+    ]
+    parts = [first_part, *copied(later, [across_own[1]])]
     spread = [lax.all_gather(part, "fac") for part in parts]
-    across_own = gather_members(outgoing, bits)
-    across_other = gather_members(incoming, bits)
-    earlier = [across_own[1], across_other[1], *parts[1:]]
-    lead = gather_members(copied([(spread[0], 0, 1)], earlier)[0][0], bits)
-
-    places = [member, column, member * width]
-    assert len(places) == PLACES
-    slots = jnp.stack(places + order).astype(jnp.int32)
-    upper, inverse, share = factor_lead(slots, damp, factor_old[:LEAD, :LEAD], lead)
+    rows = first_part.shape[0]
+    lead = copied([(spread[0], (None, rows, LEAD), [0, 0, 0])], parts[1:])[0]
+    lead = gather_members(lead, bits)
+    sent = member_blocks(spread[0], member, group, [lead[1]])
+
+    slots = jnp.stack([member, column, member * width] + order).astype(jnp.int32)
+    lower, inverse, share = factor_lead(
+        slots, damp, factor_old[:LEAD, :LEAD], lead, sent[:1]
+    )
     panel, lead_stack, across_stack = panel_columns(
         slots, share, inverse, lead, across_own, across_other
     )
-    near_grad = weight_grad.reshape(-1, ROWS, weight_grad.shape[1])
-    near_grad = copied([(near_grad, 0, LEAD // ROWS)], [lead[1]])[0].reshape(LEAD, -1)
-    near_grad = from_first_member(near_grad, member, group, bits, inverse)
-    solved = jnp.dot(inverse, near_grad.astype(F32), precision=lax.Precision.HIGH)
-    high = solved.astype(BF16)
-    low = (solved - high.astype(F32)).astype(BF16)
-    lower = upper.T
-
-    results = ()
-    gates = [lead[1], inverse, panel]
-    for (begin, end), part in zip(chunks, spread):
-        views = exchange_members(part, member, bits, [gates.pop(0)])
-        places[2] = member * width + begin
-        slots = jnp.stack(places + order + [jnp.int32(at) for _, at in views])
+    token = panel
+    results = []
+    for number, (begin, _) in enumerate(chunks):
+        ahead = number + 1 < len(chunks)
+        gate = [token] if number else []
+        if ahead:
+            coming = member_blocks(spread[number + 1], member, group, [token])
+            gate = coming[:1] if number else []
+        pieces = exchange_members(spread[number], sent, bits, gate)
+        if number == 0:
+            high, low = solve_lead(flag, inverse, moved, near, coming[:1])
+        slots = [member, column, member * width + begin] + order + [member] + [0] * (group - 1)
+        assert len(slots) == PLACES + 2 * group
         *results, token = finish_rows(
             begin,
-            slots.astype(jnp.int32),
+            jnp.stack([jnp.int32(slot) for slot in slots]),
             damp,
             share,
             factor_old,
@@ -592,12 +648,11 @@
             low,
             lead_stack,
             across_stack,
-            [array for array, _ in views],
-            list(results),
-            [] if begin else spread[2:3],
+            pieces,
+            results,
+            coming[:1] if ahead else [],
         )
-        if begin:
-            gates.append(token)
+        sent = coming
     return tuple(results)
 
 

time: 412 us -> 338 us (0.82)
  Pallas kernels: 191 us -> 136 us
  waiting for transfers between devices: 124 us -> 107 us
  local copies, waits for them, and re-layouts: 23.7 us -> 37.5 us
  other arithmetic: 12.7 us -> 5.71 us
  matrix products: 7.16 us -> 1.18 us
    pallas_call x14 -> x11, Pallas kernels: 71.4 us -> 15.1 us  [copied(): pl.pallas_call(lambda *refs: copy_kernel(len(arrays), *refs), grid_spec=p...]
    unnamed x63 -> x81, local copies, waits for them, and re-layouts: 13.7 us -> 31.3 us
    ppermute x23 -> x27, waiting for transfers between devices: 124 us -> 106 us  [swapped(): lax.ppermute(value, 'tok', [(source, source ^ mask) for source in range(s...]
    pallas_call x0 -> x2, Pallas kernels: none -> 10.1 us  [the longest x1 6.88 us: solve_lead(): pl.pallas_call(solve_kernel, grid=(first.shape[1] // ROWS,), out_shape=(j...]
    pallas_call x4, Pallas kernels: 75 us -> 67 us  [finish_rows(): pl.pallas_call(lambda *refs: finish_kernel(count, gram_steps, begin == 0,...]
    dot_general x1 -> x0, matrix products: 5.98 us -> none  [local(): jnp.dot(inverse, near_grad.astype(F32), precision=lax.Precision.HIGH)]
    select_n x3 -> x2, other arithmetic: 5.99 us -> 0.14 us  [share_of_first(): blocks = jnp.where(member >> bit & 1 == 1, moved, lower)]
    ppermute x23 -> x27, starting transfers between devices: 16.1 us -> 18.6 us  [swapped(): lax.ppermute(value, 'tok', [(source, source ^ mask) for source in range(s...]
  transfers between devices with their start and end apart: 31 -> 35, of which waited for: 6 -> 9; matrix products, arithmetic and copies ran while one was open for 7% -> 4% of each run, Pallas kernels for 41% -> 36%
where the time goes in v6:
time: 338 us; the launch traced here: 336 us
  Pallas kernels  136 us (40%)
  waiting for transfers between devices  107 us (32%)
  local copies, waits for them, and re-layouts  37.5 us (11%)
  starting transfers between devices  26 us (8%)
  between operations  22.8 us (7%)
  other arithmetic  5.71 us (2%)
    ppermute x27, waiting for transfers between devices, swapped(): lax.ppermute(value, 'tok', [(source, source ^ mask) for source in range(s...  106 us
    pallas_call x4, Pallas kernels, finish_rows(): pl.pallas_call(lambda *refs: finish_kernel(count, gram_steps, begin == 0,...  67 us
    unnamed x81, local copies, waits for them, and re-layouts  31.3 us
    pallas_call x1, Pallas kernels, factor_lead(): pl.pallas_call(lambda *refs: factor_kernel(len(lead), *refs), out_shape=(...  30.5 us
    ppermute x27, starting transfers between devices, swapped(): lax.ppermute(value, 'tok', [(source, source ^ mask) for source in range(s...  18.6 us
    pallas_call x11, Pallas kernels, copied(): pl.pallas_call(lambda *refs: copy_kernel(len(arrays), *refs), grid_spec=p...  15.1 us
    pallas_call x1, Pallas kernels, panel_columns(): pl.pallas_call(lambda *refs: panel_kernel(count, *refs), grid=(width // c...  13.1 us
    pallas_call x1, Pallas kernels, solve_lead(): pl.pallas_call(solve_kernel, grid=(first.shape[1] // ROWS,), out_shape=(j...  6.88 us
  transfers between devices with their start and end apart: 35, of which 9 were waited for; matrix products, arithmetic and copies ran while one was open for 4% of the time, Pallas kernels for 36%

profile of v6, /device:TPU:2, one launch (start us, length us, event | category | flops | bytes accessed | tf_op | source)
XLA Modules:
  0.0 335.6 jit_solution(8894508944008303582)
XLA Ops:
  7.2 3.8 %copy-done.2 = f32[1536,1536]{1,0:T(8,128)S(1)} copy-done((f32[1536,1536]{1,0:T(8,128)S(1)}, f32[1536,1536]{1,0:T(8,128)}, u32[]{:S(2)}) %copy-start.2) | copy-done | bytes 9437208
  28.8 3.4 %collective-permute-done = bf16[336,512]{1,0:T(8,128)(2,1)S(1)} collective-permute-done((bf16[336,512]{1,0:T(8,128)(2,1)S(1)}, bf16[336,512]{1,0:T(8,128)(2,1)S(1)}, u32[]{:S(2)}, u32[]{:S(2)}) %collective-permute-start) | collective-permute-done | bytes 344096 | tf_op jit(solution)/shard_map/ppermute | solution.py:438
  39.3 21.9 %collective-permute-done.3.refs_11_ = bf16[320,1536]{1,0:T(8,128)(2,1)} collective-permute-done((bf16[320,1536]{1,0:T(8,128)(2,1)S(1)}, bf16[320,1536]{1,0:T(8,128)(2,1)}, u32[]{:S(2)}, u32[]{:S(2)}) %collective-permute-start.3) | collective-permute-done | bytes 983072 | tf_op jit(solution)/shard_map/ppermute | solution.py:438
  62.5 5.5 %collective-permute-done.4.refs_4_.refs_8_.refs_0_ = bf16[448,1536]{1,0:T(8,128)(2,1)S(1)} collective-permute-done((bf16[448,1536]{1,0:T(8,128)(2,1)S(1)}, bf16[448,1536]{1,0:T(8,128)(2,1)S(1)}, u32[]{:S(2)}, u32[]{:S(2)}) %collective-permute-start.4) | collective-permute-done | bytes 1376288 | tf_op jit(solution)/shard_map/ppermute | solution.py:438
  70.7 2.8 copy-done.3
  73.4 2.0 shard_map.91.second_ref
  76.8 4.1 %collective-permute-start.10 = (bf16[320,1536]{1,0:T(8,128)(2,1)}, bf16[320,1536]{1,0:T(8,128)(2,1)}, u32[]{:S(2)}, u32[]{:S(2)}) collective-permute-start(bf16[320,1536]{1,0:T(8,128)(2,1)} %collective-permute-done.3.refs_11_), channel_id=1, source_target_pairs={{0,8},{4,12},{8,0},{12,4},{16,24},{20,28},{24,16},{28,20},{1,9},{5... | collective-permute-start | bytes 2949128 | tf_op jit(solution)/shard_map/ppermute | solution.py:438
  81.4 41.8 %collective-permute-done.10.refs_12_ = bf16[320,1536]{1,0:T(8,128)(2,1)} collective-permute-done((bf16[320,1536]{1,0:T(8,128)(2,1)}, bf16[320,1536]{1,0:T(8,128)(2,1)}, u32[]{:S(2)}, u32[]{:S(2)}) %collective-permute-start.10) | collective-permute-done | bytes 983072 | tf_op jit(solution)/shard_map/ppermute | solution.py:438
  123.2 1.9 copy-done.4
  128.3 3.3 shard_map.92.second_ref
  131.6 3.3 collective-permute-start.14
  135.0 13.3 %collective-permute-done.5.refs_4_ = bf16[784,512]{1,0:T(8,128)(2,1)S(1)} collective-permute-done((bf16[784,512]{1,0:T(8,128)(2,1)}, bf16[784,512]{1,0:T(8,128)(2,1)S(1)}, u32[]{:S(2)}, u32[]{:S(2)}) %collective-permute-start.5) | collective-permute-done | bytes 802848 | tf_op jit(solution)/shard_map/ppermute | solution.py:438
  148.3 2.2 copy-done.5
  153.6 1.8 collective-permute-start.18
  155.7 18.6 %collective-permute-done.20 = bf16[784,512]{1,0:T(8,128)(2,1)} collective-permute-done((bf16[784,512]{1,0:T(8,128)(2,1)}, bf16[784,512]{1,0:T(8,128)(2,1)}, u32[]{:S(2)}, u32[]{:S(2)}) %collective-permute-start.20) | collective-permute-done | bytes 802848 | tf_op jit(solution)/shard_map/ppermute | solution.py:438
  178.7 30.5 %shard_map.89 = (f32[512,512]{1,0:T(8,128)S(1)}, f32[512,512]{1,0:T(8,128)S(1)}, f32[8,128]{1,0:T(8,128)S(1)}) custom-call(s32[7]{0:T(128)S(1)} %stack.42.refs_0_, f32[1]{0:T(128)} %bitcast.8.refs_1_, f32[512,512]{1,0:T(8,128)S(1)} %slice.54.refs_2_, bf16[784,512]{1,0:T(8,128)(2,1)} %shard_map.87.refs_3_, bf16[784,512]{1,0:T(8,128)(2,1)S(1)} %copy-done.15, ...), custom_call_target="tpu_custom_call" | custom-call | flops 1 | bytes 1 | tf_op jit(solution)/shard_map/pallas_call | solution.py:180
  211.8 13.1 %shard_map.90 = (bf16[512,1536]{1,0:T(8,128)(2,1)}, bf16[2560,512]{1,0:T(8,128)(2,1)}, bf16[2560,1536]{1,0:T(8,128)(2,1)}) custom-call(s32[7]{0:T(128)} %copy-done.26, f32[8,128]{1,0:T(8,128)} %copy-done.25, f32[512,512]{1,0:T(8,128)} %copy-done.8, bf16[784,512]{1,0:T(8,128)(2,1)} %shard_map.87.refs_3_, bf16[784,512]{1,0:T(8,128)(2,1)} %copy-done.14, ...), custom_call_target="tpu_custom_call" | custom-call | flops 1 | bytes 1 | tf_op jit(solution)/shard_map/pallas_call | solution.py:219
  224.9 1.9 copy-done.6
  228.2 1.9 shard_map.93
  231.4 6.9 %shard_map.94 = (bf16[512,2048]{1,0:T(8,128)(2,1)S(1)}, bf16[512,2048]{1,0:T(8,128)(2,1)S(1)}) custom-call(s32[1]{0:T(128)} %bitcast.19.flag_ref, f32[512,512]{1,0:T(8,128)S(1)} %copy-done.9, bf16[512,2048]{1,0:T(8,128)(2,1)} %collective-permute-done.14.first_ref, bf16[512,2048]{1,0:T(8,128)(2,1)} %shard_map.92.second_ref, ...), custom_call_target="tpu_custom_call" | custom-call | flops 1 | bytes 1 | tf_op jit(solution)/shard_map/pallas_call | solution.py:253
  242.7 20.9 %shard_map.95 = (f32[1536,1536]{1,0:T(8,128)}, f32[1536,1536]{1,0:T(8,128)}, f32[1536,2048]{1,0:T(8,128)}, f32[8,128]{1,0:T(8,128)}) custom-call(s32[11]{0:T(128)} %stack.48.refs_0_, f32[1]{0:T(128)} %bitcast.8.refs_1_, f32[8,128]{1,0:T(8,128)} %copy-done.25, f32[1536,1536]{1,0:T(8,128)} %refs_3_.7, bf16[1536,2048]{1,0:T(8,128)(2,1)} %refs_4_.7, ...), custom_call_target="tpu_custom_call" | custom-call | flops 1 | bytes 1 | tf_op jit(solution)/shard_map/pallas_call | solution.py:406
  271.1 18.9 %shard_map.98 = (f32[1536,1536]{1,0:T(8,128)}, f32[1536,1536]{1,0:T(8,128)}, f32[1536,2048]{1,0:T(8,128)}, f32[8,128]{1,0:T(8,128)}) custom-call(s32[11]{0:T(128)} %stack.47.refs_0_, f32[1]{0:T(128)} %bitcast.8.refs_1_, f32[8,128]{1,0:T(8,128)} %copy-done.25, f32[1536,1536]{1,0:T(8,128)} %refs_3_.7, ...), custom_call_target="tpu_custom_call", output_to_operand_aliasing={{0}: (14, {}), {1}: (15, {}), {2}: (16, {})} | custom-call | flops 1 | bytes 1 | tf_op jit(solution)/shard_map/pallas_call | solution.py:406
  297.2 13.5 %shard_map.101 = (f32[1536,1536]{1,0:T(8,128)}, f32[1536,1536]{1,0:T(8,128)}, f32[1536,2048]{1,0:T(8,128)}, f32[8,128]{1,0:T(8,128)}) custom-call(s32[11]{0:T(128)} %stack.50.refs_0_, f32[1]{0:T(128)} %bitcast.8.refs_1_, f32[8,128]{1,0:T(8,128)} %copy-done.25, f32[1536,1536]{1,0:T(8,128)} %refs_3_.7, ...), custom_call_target="tpu_custom_call", output_to_operand_aliasing={{0}: (14, {}), {1}: (15, {}), {2}: (16, {})} | custom-call | flops 1 | bytes 1 | tf_op jit(solution)/shard_map/pallas_call | solution.py:406
  315.4 13.6 %shard_map.103 = (f32[1536,1536]{1,0:T(8,128)}, f32[1536,1536]{1,0:T(8,128)}, f32[1536,2048]{1,0:T(8,128)}, f32[8,128]{1,0:T(8,128)}) custom-call(s32[11]{0:T(128)} %stack.40.refs_0_, f32[1]{0:T(128)} %bitcast.8.refs_1_, f32[8,128]{1,0:T(8,128)} %copy-done.25, f32[1536,1536]{1,0:T(8,128)} %refs_3_.7, ...), custom_call_target="tpu_custom_call", output_to_operand_aliasing={{0}: (14, {}), {1}: (15, {}), {2}: (16, {})} | custom-call | flops 1 | bytes 1 | tf_op jit(solution)/shard_map/pallas_call | solution.py:406
  (192 shorter events, 62.0 us)
Async XLA Ops:
  7.2 116.0 %all-gather.9.cloned.1.call-start = ((), (), s32[]{:S(2)}) async-start(), calls=%async_computation | async-start | bytes 4014080 | tf_op jit(solution)/shard_map/all_gather | solution.py:611
  33.4 191.5 %all-gather.11.cloned.1.call-start = ((), (), s32[]{:S(2)}) async-start(), calls=%async_computation.1 | async-start | bytes 3932160 | tf_op jit(solution)/shard_map/all_gather | solution.py:611
  37.0 31.0 %collective-permute-start.4 = (bf16[448,1536]{1,0:T(8,128)(2,1)S(1)}, bf16[448,1536]{1,0:T(8,128)(2,1)S(1)}, u32[]{:S(2)}, u32[]{:S(2)}) collective-permute-start(bf16[448,1536]{1,0:T(8,128)(2,1)S(1)} %pad_maximum_fusion.1.refs_7_), channel_id=1, source_target_pairs={{0,8},{4,12},{8,0},{12,4},{16,24},{20,28},{24,16},{28,20},{1,9},{5... | collective-permute-start | bytes 4128776 | tf_op jit(solution)/shard_map/ppermute | solution.py:438
  37.7 23.4 %collective-permute-start.3 = (bf16[320,1536]{1,0:T(8,128)(2,1)S(1)}, bf16[320,1536]{1,0:T(8,128)(2,1)}, u32[]{:S(2)}, u32[]{:S(2)}) collective-permute-start(bf16[320,1536]{1,0:T(8,128)(2,1)S(1)} %get-tuple-element.88), channel_id=1, source_target_pairs={{0,16},{4,20},{8,24},{12,28},{16,0},{20,4},{24,8},{28,12},{1,17},{... | collective-permute-start | bytes 2949128 | tf_op jit(solution)/shard_map/ppermute | solution.py:438
  70.6 193.1 %all-gather.15.cloned.1.call-start = ((), (), s32[]{:S(2)}) async-start(), calls=%async_computation.3 | async-start | bytes 1966080 | tf_op jit(solution)/shard_map/all_gather | solution.py:611
  75.4 52.3 %collective-permute-start.13 = (bf16[512,2048]{1,0:T(8,128)(2,1)}, bf16[512,2048]{1,0:T(8,128)(2,1)}, u32[]{:S(2)}, u32[]{:S(2)}) collective-permute-start(bf16[512,2048]{1,0:T(8,128)(2,1)} %shard_map.91.second_ref), channel_id=1, source_target_pairs={{0,8},{16,24},{1,9},{17,25},{2,10},{18,26},{3,11},{19,27}} | collective-permute-start | bytes 6291464 | tf_op jit(solution)/shard_map/ppermute | solution.py:599
  76.8 213.3 %all-gather.13.cloned.1.call-start = ((), (), s32[]{:S(2)}) async-start(), calls=%async_computation.2 | async-start | bytes 1966080 | tf_op jit(solution)/shard_map/all_gather | solution.py:611
  76.8 46.4 %collective-permute-start.10 = (bf16[320,1536]{1,0:T(8,128)(2,1)}, bf16[320,1536]{1,0:T(8,128)(2,1)}, u32[]{:S(2)}, u32[]{:S(2)}) collective-permute-start(bf16[320,1536]{1,0:T(8,128)(2,1)} %collective-permute-done.3.refs_11_), channel_id=1, source_target_pairs={{0,8},{4,12},{8,0},{12,4},{16,24},{20,28},{24,16},{28,20},{1,9},{5... | collective-permute-start | bytes 2949128 | tf_op jit(solution)/shard_map/ppermute | solution.py:438
  80.9 50.7 %collective-permute-start.11 = (bf16[320,1536]{1,0:T(8,128)(2,1)}, bf16[320,1536]{1,0:T(8,128)(2,1)}, u32[]{:S(2)}, u32[]{:S(2)}) collective-permute-start(bf16[320,1536]{1,0:T(8,128)(2,1)} %collective-permute-done.3.refs_11_), channel_id=1, source_target_pairs={{0,4},{4,0},{8,12},{12,8},{16,20},{20,16},{24,28},{28,24},{1,5},{5... | collective-permute-start | bytes 2949128 | tf_op jit(solution)/shard_map/ppermute | solution.py:438
  80.9 72.2 %collective-permute-start.8 = (bf16[448,1536]{1,0:T(8,128)(2,1)}, bf16[448,1536]{1,0:T(8,128)(2,1)}, u32[]{:S(2)}, u32[]{:S(2)}) collective-permute-start(bf16[448,1536]{1,0:T(8,128)(2,1)} %copy-done.33), channel_id=1, source_target_pairs={{0,4},{4,0},{8,12},{12,8},{16,20},{20,16},{24,28},{28,24},{1,5},{5... | collective-permute-start | bytes 4128776 | tf_op jit(solution)/shard_map/ppermute | solution.py:438
  123.2 30.1 %collective-permute-start.12 = (bf16[320,1536]{1,0:T(8,128)(2,1)}, bf16[320,1536]{1,0:T(8,128)(2,1)}, u32[]{:S(2)}, u32[]{:S(2)}) collective-permute-start(bf16[320,1536]{1,0:T(8,128)(2,1)} %collective-permute-done.10.refs_12_), channel_id=1, source_target_pairs={{0,4},{4,0},{8,12},{12,8},{16,20},{20,16},{24,28},{28,24},{1,5},{5... | collective-permute-start | bytes 2949128 | tf_op jit(solution)/shard_map/ppermute | solution.py:438
  127.8 20.5 %collective-permute-start.5 = (bf16[784,512]{1,0:T(8,128)(2,1)}, bf16[784,512]{1,0:T(8,128)(2,1)S(1)}, u32[]{:S(2)}, u32[]{:S(2)}) collective-permute-start(bf16[784,512]{1,0:T(8,128)(2,1)} %shard_map.87.refs_3_), channel_id=1, source_target_pairs={{0,8},{4,12},{8,0},{12,4},{16,24},{20,28},{24,16},{28,20},{1,9},{5... | collective-permute-start | bytes 2408456 | tf_op jit(solution)/shard_map/ppermute | solution.py:438
  127.8 84.0 %collective-permute-start.9 = (bf16[448,1536]{1,0:T(8,128)(2,1)S(1)}, bf16[448,1536]{1,0:T(8,128)(2,1)}, u32[]{:S(2)}, u32[]{:S(2)}) collective-permute-start(bf16[448,1536]{1,0:T(8,128)(2,1)S(1)} %collective-permute-done.4.refs_4_.refs_8_.refs_0_), channel_id=1, source_target_pairs={{0,4},{4,0},{8,12},{12,8},{16,20},{20,16},{24,28},{28,24},{1,5},{5... | collective-permute-start | bytes 4128776 | tf_op jit(solution)/shard_map/ppermute | solution.py:438
  131.6 99.4 %collective-permute-start.14 = (bf16[512,2048]{1,0:T(8,128)(2,1)}, bf16[512,2048]{1,0:T(8,128)(2,1)}, u32[]{:S(2)}, u32[]{:S(2)}) collective-permute-start(bf16[512,2048]{1,0:T(8,128)(2,1)} %shard_map.92.second_ref), channel_id=1, source_target_pairs={{0,4},{8,12},{16,20},{24,28},{1,5},{9,13},{17,21},{25,29},{2,6},{1... | collective-permute-start | bytes 6291464 | tf_op jit(solution)/shard_map/ppermute | solution.py:599
  153.3 21.0 %collective-permute-start.20 = (bf16[784,512]{1,0:T(8,128)(2,1)}, bf16[784,512]{1,0:T(8,128)(2,1)}, u32[]{:S(2)}, u32[]{:S(2)}) collective-permute-start(bf16[784,512]{1,0:T(8,128)(2,1)} %get-tuple-element.61), channel_id=1, source_target_pairs={{0,8},{4,12},{8,0},{12,4},{16,24},{20,28},{24,16},{28,20},{1,9},{5... | collective-permute-start | bytes 2408456 | tf_op jit(solution)/shard_map/ppermute | solution.py:438
  153.6 87.5 %collective-permute-start.18 = (bf16[784,512]{1,0:T(8,128)(2,1)}, bf16[784,512]{1,0:T(8,128)(2,1)}, u32[]{:S(2)}, u32[]{:S(2)}) collective-permute-start(bf16[784,512]{1,0:T(8,128)(2,1)} %copy-done.32), channel_id=1, source_target_pairs={{0,8},{4,12},{8,0},{12,4},{16,24},{20,28},{24,16},{28,20},{1,9},{5... | collective-permute-start | bytes 2408456 | tf_op jit(solution)/shard_map/ppermute | solution.py:438
  155.5 87.2 %collective-permute-start.19 = (bf16[784,512]{1,0:T(8,128)(2,1)S(1)}, bf16[784,512]{1,0:T(8,128)(2,1)}, u32[]{:S(2)}, u32[]{:S(2)}) collective-permute-start(bf16[784,512]{1,0:T(8,128)(2,1)S(1)} %get-tuple-element.48.refs_7_), channel_id=1, source_target_pairs={{0,4},{4,0},{8,12},{12,8},{16,20},{20,16},{24,28},{28,24},{1,5},{5... | collective-permute-start | bytes 2408456 | tf_op jit(solution)/shard_map/ppermute | solution.py:438
  174.3 68.4 %collective-permute-start.21 = (bf16[784,512]{1,0:T(8,128)(2,1)}, bf16[784,512]{1,0:T(8,128)(2,1)}, u32[]{:S(2)}, u32[]{:S(2)}) collective-permute-start(bf16[784,512]{1,0:T(8,128)(2,1)} %collective-permute-done.20), channel_id=1, source_target_pairs={{0,4},{4,0},{8,12},{12,8},{16,20},{20,16},{24,28},{28,24},{1,5},{5... | collective-permute-start | bytes 2408456 | tf_op jit(solution)/shard_map/ppermute | solution.py:438
  230.0 36.3 %collective-permute-start.17 = (bf16[768,512]{1,0:T(8,128)(2,1)}, bf16[768,512]{1,0:T(8,128)(2,1)}, u32[]{:S(2)}, u32[]{:S(2)}) collective-permute-start(bf16[768,512]{1,0:T(8,128)(2,1)} %get-tuple-element.57), channel_id=1, source_target_pairs={{0,8},{4,12},{8,0},{12,4},{16,24},{20,28},{24,16},{28,20},{1,9},{5... | collective-permute-start | bytes 2359304 | tf_op jit(solution)/shard_map/ppermute | solution.py:438
  231.0 40.1 %collective-permute-start.16 = (bf16[768,512]{1,0:T(8,128)(2,1)S(1)}, bf16[768,512]{1,0:T(8,128)(2,1)}, u32[]{:S(2)}, u32[]{:S(2)}) collective-permute-start(bf16[768,512]{1,0:T(8,128)(2,1)S(1)} %get-tuple-element.52.refs_0_.refs_16_), channel_id=1, source_target_pairs={{0,4},{4,0},{8,12},{12,8},{16,20},{20,16},{24,28},{28,24},{1,5},{5... | collective-permute-start | bytes 2359304 | tf_op jit(solution)/shard_map/ppermute | solution.py:438
  241.1 28.6 %collective-permute-start.15 = (bf16[768,512]{1,0:T(8,128)(2,1)}, bf16[768,512]{1,0:T(8,128)(2,1)}, u32[]{:S(2)}, u32[]{:S(2)}) collective-permute-start(bf16[768,512]{1,0:T(8,128)(2,1)} %get-tuple-element.56), channel_id=1, source_target_pairs={{0,8},{4,12},{8,0},{12,4},{16,24},{20,28},{24,16},{28,20},{1,9},{5... | collective-permute-start | bytes 2359304 | tf_op jit(solution)/shard_map/ppermute | solution.py:438
  268.2 25.4 %collective-permute-start.28 = (bf16[768,256]{1,0:T(8,128)(2,1)S(1)}, bf16[768,256]{1,0:T(8,128)(2,1)S(1)}, u32[]{:S(2)}, u32[]{:S(2)}) collective-permute-start(bf16[768,256]{1,0:T(8,128)(2,1)S(1)} %get-tuple-element.72), channel_id=1, source_target_pairs={{0,8},{4,12},{8,0},{12,4},{16,24},{20,28},{24,16},{28,20},{1,9},{5... | collective-permute-start | bytes 1179656 | tf_op jit(solution)/shard_map/ppermute | solution.py:438
  269.5 27.7 %collective-permute-start.27 = (bf16[768,256]{1,0:T(8,128)(2,1)S(1)}, bf16[768,256]{1,0:T(8,128)(2,1)}, u32[]{:S(2)}, u32[]{:S(2)}) collective-permute-start(bf16[768,256]{1,0:T(8,128)(2,1)S(1)} %get-tuple-element.63.refs_2_.refs_17_), channel_id=1, source_target_pairs={{0,4},{4,0},{8,12},{12,8},{16,20},{20,16},{24,28},{28,24},{1,5},{5... | collective-permute-start | bytes 1179656 | tf_op jit(solution)/shard_map/ppermute | solution.py:438
  269.7 26.0 %collective-permute-start.26 = (bf16[768,256]{1,0:T(8,128)(2,1)S(1)}, bf16[768,256]{1,0:T(8,128)(2,1)}, u32[]{:S(2)}, u32[]{:S(2)}) collective-permute-start(bf16[768,256]{1,0:T(8,128)(2,1)S(1)} %get-tuple-element.71), channel_id=1, source_target_pairs={{0,8},{4,12},{8,0},{12,4},{16,24},{20,28},{24,16},{28,20},{1,9},{5... | collective-permute-start | bytes 1179656 | tf_op jit(solution)/shard_map/ppermute | solution.py:438
  (51 other events, 387.9 us)
Sparse Core Ops, SparseCore 0:
  33.5 65.8 all-gather.8
  100.9 62.1 all-gather.10
  164.6 35.7 all-gather.14
  201.8 35.9 all-gather.12

commit v7 on v6

--- a/solution.py
+++ b/solution.py
@@ -12,6 +12,7 @@
 ROWS = 256
 COLS = 512
 PLACES = 3
+VMEM_BYTES = 60 * 1024 * 1024
 ANYWHERE = pl.BlockSpec(memory_space=pl.ANY)
 NO_COST = pl.CostEstimate(flops=1, bytes_accessed=1, transcendentals=0)
 DECAY = 0.8
@@ -183,7 +184,7 @@
         in_specs=[smem, smem] + [vmem] * (1 + len(lead)) + [ANYWHERE] * len(earlier),
         out_specs=(vmem, vmem, vmem),
         scratch_shapes=[pltpu.VMEM((LEAD, LEAD), F32)] * 2,
-        compiler_params=pltpu.CompilerParams(vmem_limit_bytes=32 * 1024 * 1024),
+        compiler_params=pltpu.CompilerParams(vmem_limit_bytes=VMEM_BYTES),
         cost_estimate=NO_COST,
     )(places, damp, exact, *lead, *earlier)
 
@@ -234,7 +235,7 @@
         + [tiled(CAP)] * count,
         out_specs=(tiled(LEAD), whole(tall), tiled(tall)),
         scratch_shapes=[pltpu.VMEM((LEAD, cols), F32)],
-        compiler_params=pltpu.CompilerParams(vmem_limit_bytes=56 * 1024 * 1024),
+        compiler_params=pltpu.CompilerParams(vmem_limit_bytes=VMEM_BYTES),
         cost_estimate=NO_COST,
     )(places, share, inverse, *lead, *own, *other)
 
@@ -262,7 +263,7 @@
         ]
         + [ANYWHERE] * len(earlier),
         out_specs=(tiled, tiled),
-        compiler_params=pltpu.CompilerParams(vmem_limit_bytes=32 * 1024 * 1024),
+        compiler_params=pltpu.CompilerParams(vmem_limit_bytes=VMEM_BYTES),
         cost_estimate=NO_COST,
     )(flag, inverse, first, second, *earlier)
 
@@ -423,14 +424,9 @@
             jax.ShapeDtypeStruct((GROUP, TILE), F32),
         ),
         input_output_aliases=aliases,
-        compiler_params=pltpu.CompilerParams(vmem_limit_bytes=56 * 1024 * 1024),
+        compiler_params=pltpu.CompilerParams(vmem_limit_bytes=VMEM_BYTES),
         cost_estimate=NO_COST,
     )(places, *operands)
-
-
-def after(value, earlier):
-    mark = earlier[(0,) * earlier.ndim]
-    return jnp.where(mark == mark, value, jnp.zeros_like(value))
 
 
 def swapped(value, mask):
@@ -471,7 +467,7 @@
             out_specs=out_specs,
         ),
         out_shape=[jax.ShapeDtypeStruct(shape, BF16) for shape in shapes],
-        compiler_params=pltpu.CompilerParams(vmem_limit_bytes=32 * 1024 * 1024),
+        compiler_params=pltpu.CompilerParams(vmem_limit_bytes=VMEM_BYTES),
         cost_estimate=NO_COST,
     )(jnp.stack([jnp.int32(place) for place in places]), *arrays, *earlier)
 
@@ -488,7 +484,7 @@
         out_shape=jax.ShapeDtypeStruct(first.shape, first.dtype),
         in_specs=[pl.BlockSpec(memory_space=pltpu.SMEM), tiled, tiled] + [ANYWHERE] * len(earlier),
         out_specs=tiled,
-        compiler_params=pltpu.CompilerParams(vmem_limit_bytes=32 * 1024 * 1024),
+        compiler_params=pltpu.CompilerParams(vmem_limit_bytes=VMEM_BYTES),
         cost_estimate=NO_COST,
     )(flag, first, second, *earlier)
 
@@ -506,8 +502,7 @@
     for bit in reversed(range(bits)):
         half = 1 << bit
         for passed in held[half:]:
-            if earlier:
-                passed[1:] = [copied([(part, part.shape, [0, 0])], earlier)[0] for part in passed[1:]]
+            passed[1:] = [copied([(part, part.shape, [0, 0])], earlier)[0] for part in passed[1:]]
         held = [
             kept + [swapped(part, half) for part in passed]
             for kept, passed in zip(held[:half], held[half:])
@@ -587,12 +582,12 @@
         ],
         0,
     )
-    incoming = swapped(after(packed[CAP:], front), group)
+    grad_cols = weight_grad.shape[1]
+    near = copied([(weight_grad, (LEAD, grad_cols), [0, 0])], [arrived])[0]
+    away_rows = copied([(packed, (CAP, width), [1, 0])], [front, near])[0]
+    incoming = swapped(away_rows, group)
     outgoing = jnp.concatenate([packed[:CAP], lead_factor], 0)
     quarter = jnp.concatenate([packed[:CAP], incoming, lead_factor], 0)
-
-    grad_cols = weight_grad.shape[1]
-    near = copied([(weight_grad, (LEAD, grad_cols), [0, 0])], [arrived])[0]
     across_own = gather_members(outgoing, bits)
     across_other = gather_members(incoming, bits)
     for bit in reversed(range(bits)):
@@ -625,11 +620,11 @@
     results = []
     for number, (begin, _) in enumerate(chunks):
         ahead = number + 1 < len(chunks)
-        gate = [token] if number else []
         if ahead:
             coming = member_blocks(spread[number + 1], member, group, [token])
-            gate = coming[:1] if number else []
-        pieces = exchange_members(spread[number], sent, bits, gate)
+        pieces = exchange_members(
+            spread[number], sent, bits, coming[:1] if ahead else [token]
+        )
         if number == 0:
             high, low = solve_lead(flag, inverse, moved, near, coming[:1])
         slots = [member, column, member * width + begin] + order + [member] + [0] * (group - 1)

time: 338 us -> 320 us (0.947)
  Pallas kernels: 136 us -> 165 us
  waiting for transfers between devices: 107 us -> 83 us
  local copies, waits for them, and re-layouts: 37.5 us -> 17.8 us
    ppermute x27, waiting for transfers between devices: 106 us -> 58 us  [swapped(): lax.ppermute(value, 'tok', [(source, source ^ mask) for source in range(s...]
    pallas_call x11 -> x13, Pallas kernels: 15.1 us -> 40.8 us  [copied(): pl.pallas_call(lambda *refs: copy_kernel(len(arrays), *refs), grid_spec=p...]
    all_gather x4, waiting for transfers between devices: 0.06 us -> 24.4 us  [local(): spread = [lax.all_gather(part, 'fac') for part in parts]]
    unnamed x81 -> x61, local copies, waits for them, and re-layouts: 31.3 us -> 7.67 us
  transfers between devices with their start and end apart: 35 -> 35, of which waited for: 9 -> 7; matrix products, arithmetic and copies ran while one was open for 4% -> 5% of each run, Pallas kernels for 36% -> 47%
where the time goes in v7:
time: 320 us; the launch traced here: 317 us
  Pallas kernels  165 us (52%)
  waiting for transfers between devices  83 us (26%)
  starting transfers between devices  23.4 us (7%)
  between operations  21.2 us (7%)
  local copies, waits for them, and re-layouts  17.8 us (6%)
  other arithmetic  5.48 us (2%)
    pallas_call x4, Pallas kernels, finish_rows(): pl.pallas_call(lambda *refs: finish_kernel(count, gram_steps, begin == 0,...  67.1 us
    ppermute x27, waiting for transfers between devices, swapped(): lax.ppermute(value, 'tok', [(source, source ^ mask) for source in range(s...  58 us
    pallas_call x13, Pallas kernels, copied(): pl.pallas_call(lambda *refs: copy_kernel(len(arrays), *refs), grid_spec=p...  40.8 us
    pallas_call x1, Pallas kernels, factor_lead(): pl.pallas_call(lambda *refs: factor_kernel(len(lead), *refs), out_shape=(...  32.1 us
    all_gather x4, waiting for transfers between devices, local(): spread = [lax.all_gather(part, 'fac') for part in parts]  24.4 us
    ppermute x27, starting transfers between devices, swapped(): lax.ppermute(value, 'tok', [(source, source ^ mask) for source in range(s...  16 us
    pallas_call x1, Pallas kernels, panel_columns(): pl.pallas_call(lambda *refs: panel_kernel(count, *refs), grid=(width // c...  13.1 us
    pallas_call x1, Pallas kernels, solve_lead(): pl.pallas_call(solve_kernel, grid=(first.shape[1] // ROWS,), out_shape=(j...  8.6 us
  transfers between devices with their start and end apart: 35, of which 7 were waited for; matrix products, arithmetic and copies ran while one was open for 5% of the time, Pallas kernels for 47%

profile of v7, /device:TPU:2, one launch (start us, length us, event | category | flops | bytes accessed | tf_op | source)
XLA Modules:
  0.0 317.0 jit_solution(14086647717221835312)
XLA Ops:
  7.2 3.9 %shard_map.85 = (bf16[256,1536]{1,0:T(8,128)(2,1)}, bf16[256,1536]{1,0:T(8,128)(2,1)}) custom-call(s32[4]{0:T(128)} %constant.94.clone.1.refs_0_, f32[1536,1536]{1,0:T(8,128)} %refs_3_.7, f32[1536,1536]{1,0:T(8,128)} %refs_3_.7), custom_call_target="tpu_custom_call" | custom-call | flops 1 | bytes 1 | tf_op jit(solution)/shard_map/pallas_call | solution.py:461
  26.7 2.9 collective-permute-done.refs_2_
  34.6 3.7 %shard_map.86.refs_3_.second_ref = bf16[512,2048]{1,0:T(8,128)(2,1)} custom-call(s32[2]{0:T(128)} %broadcast_3_refs_0_.2.refs_0_, bf16[1536,2048]{1,0:T(8,128)(2,1)} %refs_4_.7, bf16[256,1536]{1,0:T(8,128)(2,1)} %copy-done.8), custom_call_target="tpu_custom_call" | custom-call | flops 1 | bytes 1 | tf_op jit(solution)/shard_map/pallas_call | solution.py:461
  38.3 3.0 shard_map.87
  42.8 22.1 %collective-permute-done.3.refs_11_ = bf16[320,1536]{1,0:T(8,128)(2,1)S(1)} collective-permute-done((bf16[320,1536]{1,0:T(8,128)(2,1)}, bf16[320,1536]{1,0:T(8,128)(2,1)S(1)}, u32[]{:S(2)}, u32[]{:S(2)}) %collective-permute-start.3) | collective-permute-done | bytes 983072 | tf_op jit(solution)/shard_map/ppermute | solution.py:434
  67.7 3.2 %shard_map.88 = (bf16[768,512]{1,0:T(8,128)(2,1)}, bf16[768,256]{1,0:T(8,128)(2,1)}, bf16[768,256]{1,0:T(8,128)(2,1)}) custom-call(s32[6]{0:T(128)} %constant.95.clone.1.refs_0_, bf16[768,1536]{1,0:T(8,128)(2,1)} %pad_maximum_fusion.refs_1_.refs_2_.refs_3_, bf16[768,1536]{1,0:T(8,128)(2,1)} %pad_maximum_fusion.refs_1_.refs_2_.refs_3_, ...), custom_call_target="tpu_custom_call" | custom-call | flops 1 | bytes 1 | tf_op jit(solution)/shard_map/pallas_call | solution.py:461
  72.5 24.3 %all-gather.9.cloned.1.call-done = bf16[3136,512]{1,0:T(8,128)(2,1)} async-done(((bf16[784,512]{1,0:T(8,128)(2,1)}), bf16[3136,512]{1,0:T(8,128)(2,1)}) %all-gather.9.cloned.1.call-update) | async-done | bytes 3211280 | tf_op jit(solution)/shard_map/all_gather | solution.py:606
  97.3 2.9 shard_map.89.refs_3_
  102.2 19.0 %collective-permute-done.5.refs_4_ = bf16[784,512]{1,0:T(8,128)(2,1)S(1)} collective-permute-done((bf16[784,512]{1,0:T(8,128)(2,1)}, bf16[784,512]{1,0:T(8,128)(2,1)S(1)}, u32[]{:S(2)}, u32[]{:S(2)}) %collective-permute-start.5) | collective-permute-done | bytes 802848 | tf_op jit(solution)/shard_map/ppermute | solution.py:434
  121.7 3.3 %shard_map.93.second_ref = bf16[512,2048]{1,0:T(8,128)(2,1)} custom-call(s32[1]{0:T(128)} %bitcast.19.flag_ref, bf16[512,2048]{1,0:T(8,128)(2,1)} %collective-permute-done.13.first_ref, bf16[512,2048]{1,0:T(8,128)(2,1)} %shard_map.86.refs_3_.second_ref, bf16[448,1536]{1,0:T(8,128)(2,1)} %copy-done.2), custom_call_target="tpu_custom_call" | custom-call | flops 1 | bytes 1 | tf_op jit(solution)/shard_map/pallas_call | solution.py:481
  125.0 3.3 %collective-permute-start.14 = (bf16[512,2048]{1,0:T(8,128)(2,1)}, bf16[512,2048]{1,0:T(8,128)(2,1)}, u32[]{:S(2)}, u32[]{:S(2)}) collective-permute-start(bf16[512,2048]{1,0:T(8,128)(2,1)} %shard_map.93.second_ref), channel_id=1, source_target_pairs={{0,4},{8,12},{16,20},{24,28},{1,5},{9,13},{17,21},{25,29},{2,6},{1... | collective-permute-start | bytes 6291464 | tf_op jit(solution)/shard_map/ppermute | solution.py:594
  128.3 12.9 %collective-permute-done.10.refs_12_ = bf16[320,1536]{1,0:T(8,128)(2,1)} collective-permute-done((bf16[320,1536]{1,0:T(8,128)(2,1)S(1)}, bf16[320,1536]{1,0:T(8,128)(2,1)}, u32[]{:S(2)}, u32[]{:S(2)}) %collective-permute-start.10) | collective-permute-done | bytes 983072 | tf_op jit(solution)/shard_map/ppermute | solution.py:434
  142.3 3.8 %shard_map.90 = (bf16[784,512]{1,0:T(8,128)(2,1)}, bf16[784,512]{1,0:T(8,128)(2,1)}, bf16[784,512]{1,0:T(8,128)(2,1)}) custom-call(s32[9]{0:T(128)} %stack.45.refs_0_, bf16[4,784,512]{2,1,0:T(8,128)(2,1)} %bitcast.58, bf16[4,784,512]{2,1,0:T(8,128)(2,1)} %bitcast.59, bf16[4,784,512]{2,1,0:T(8,128)(2,1)} %bitcast.60, bf16[784,512]{1,0:T(8,128)(2,1)} %copy-done.4), custom_call_target="tpu_custom_call" | custom-call | flops 1 | bytes 1 | tf_op jit(solution)/shard_map/pallas_call | solution.py:461
  151.5 32.1 %shard_map.91 = (f32[512,512]{1,0:T(8,128)}, f32[512,512]{1,0:T(8,128)}, f32[8,128]{1,0:T(8,128)}) custom-call(s32[7]{0:T(128)} %stack.42.refs_0_, f32[1]{0:T(128)} %bitcast.8.refs_1_, f32[512,512]{1,0:T(8,128)} %slice.48.refs_2_, bf16[784,512]{1,0:T(8,128)(2,1)} %shard_map.89.refs_3_, bf16[784,512]{1,0:T(8,128)(2,1)} %copy-done.4, ...), custom_call_target="tpu_custom_call" | custom-call | flops 1 | bytes 1 | tf_op jit(solution)/shard_map/pallas_call | solution.py:181
  185.2 13.1 %shard_map.92 = (bf16[512,1536]{1,0:T(8,128)(2,1)}, bf16[2560,512]{1,0:T(8,128)(2,1)}, bf16[2560,1536]{1,0:T(8,128)(2,1)}) custom-call(s32[7]{0:T(128)} %stack.42.refs_0_, f32[8,128]{1,0:T(8,128)} %get-tuple-element.49.refs_1_.refs_2_, f32[512,512]{1,0:T(8,128)} %get-tuple-element.50.refs_2_.inverse_ref.refs_6_, bf16[784,512]{1,0:T(8,128)(2,1)} %shard_map.89.refs_3_, ...), custom_call_target="tpu_custom_call" | custom-call | flops 1 | bytes 1 | tf_op jit(solution)/shard_map/pallas_call | solution.py:220
  198.4 3.8 %shard_map.94 = (bf16[768,512]{1,0:T(8,128)(2,1)}, bf16[768,512]{1,0:T(8,128)(2,1)}, bf16[768,512]{1,0:T(8,128)(2,1)}) custom-call(s32[9]{0:T(128)} %stack.45.refs_0_, bf16[4,768,512]{2,1,0:T(8,128)(2,1)} %bitcast.62, bf16[4,768,512]{2,1,0:T(8,128)(2,1)} %bitcast.63, bf16[4,768,512]{2,1,0:T(8,128)(2,1)} %bitcast.64, ...), custom_call_target="tpu_custom_call" | custom-call | flops 1 | bytes 1 | tf_op jit(solution)/shard_map/pallas_call | solution.py:461
  202.2 2.9 shard_map.96
  206.4 8.6 %shard_map.95 = (bf16[512,2048]{1,0:T(8,128)(2,1)}, bf16[512,2048]{1,0:T(8,128)(2,1)}) custom-call(s32[1]{0:T(128)} %bitcast.18.flag_ref, f32[512,512]{1,0:T(8,128)} %get-tuple-element.50.refs_2_.inverse_ref.refs_6_, bf16[512,2048]{1,0:T(8,128)(2,1)} %collective-permute-done.14.first_ref, bf16[512,2048]{1,0:T(8,128)(2,1)} %shard_map.93.second_ref, ...), custom_call_target="tpu_custom_call" | custom-call | flops 1 | bytes 1 | tf_op jit(solution)/shard_map/pallas_call | solution.py:254
  217.4 21.0 %shard_map.97 = (f32[1536,1536]{1,0:T(8,128)}, f32[1536,1536]{1,0:T(8,128)}, f32[1536,2048]{1,0:T(8,128)}, f32[8,128]{1,0:T(8,128)}) custom-call(s32[11]{0:T(128)} %stack.48.refs_0_, f32[1]{0:T(128)} %bitcast.8.refs_1_, f32[8,128]{1,0:T(8,128)} %get-tuple-element.49.refs_1_.refs_2_, f32[1536,1536]{1,0:T(8,128)} %refs_3_.7, bf16[1536,2048]{1,0:T(8,128)(2,1)} %refs_4_.7, ...), custom_call_target="tpu_custom_call" | custom-call | flops 1 | bytes 1 | tf_op jit(solution)/shard_map/pallas_call | solution.py:407
  238.5 3.0 shard_map.98
  248.3 18.9 %shard_map.100 = (f32[1536,1536]{1,0:T(8,128)}, f32[1536,1536]{1,0:T(8,128)}, f32[1536,2048]{1,0:T(8,128)}, f32[8,128]{1,0:T(8,128)}) custom-call(s32[11]{0:T(128)} %stack.47.refs_0_, f32[1]{0:T(128)} %bitcast.8.refs_1_, f32[8,128]{1,0:T(8,128)} %get-tuple-element.49.refs_1_.refs_2_, ...), custom_call_target="tpu_custom_call", output_to_operand_aliasing={{0}: (14, {}), {1}: (15, {}), {2}: (16, {})} | custom-call | flops 1 | bytes 1 | tf_op jit(solution)/shard_map/pallas_call | solution.py:407
  267.3 3.0 shard_map.101
  277.3 13.6 %shard_map.103 = (f32[1536,1536]{1,0:T(8,128)}, f32[1536,1536]{1,0:T(8,128)}, f32[1536,2048]{1,0:T(8,128)}, f32[8,128]{1,0:T(8,128)}) custom-call(s32[11]{0:T(128)} %stack.50.refs_0_, f32[1]{0:T(128)} %bitcast.8.refs_1_, f32[8,128]{1,0:T(8,128)} %get-tuple-element.49.refs_1_.refs_2_, ...), custom_call_target="tpu_custom_call", output_to_operand_aliasing={{0}: (14, {}), {1}: (15, {}), {2}: (16, {})} | custom-call | flops 1 | bytes 1 | tf_op jit(solution)/shard_map/pallas_call | solution.py:407
  296.8 13.6 %shard_map.105 = (f32[1536,1536]{1,0:T(8,128)}, f32[1536,1536]{1,0:T(8,128)}, f32[1536,2048]{1,0:T(8,128)}, f32[8,128]{1,0:T(8,128)}) custom-call(s32[11]{0:T(128)} %stack.40.refs_0_, f32[1]{0:T(128)} %bitcast.8.refs_1_, f32[8,128]{1,0:T(8,128)} %get-tuple-element.49.refs_1_.refs_2_, ...), custom_call_target="tpu_custom_call", output_to_operand_aliasing={{0}: (14, {}), {1}: (15, {}), {2}: (16, {})} | custom-call | flops 1 | bytes 1 | tf_op jit(solution)/shard_map/pallas_call | solution.py:407
  (173 shorter events, 54.0 us)
Async XLA Ops:
  7.2 89.6 %all-gather.9.cloned.1.call-start = ((), (), s32[]{:S(2)}) async-start(), calls=%async_computation | async-start | bytes 4014080 | tf_op jit(solution)/shard_map/all_gather | solution.py:606
  30.8 167.6 %all-gather.11.cloned.1.call-start = ((), (), s32[]{:S(2)}) async-start(), calls=%async_computation.1 | async-start | bytes 3932160 | tf_op jit(solution)/shard_map/all_gather | solution.py:606
  33.3 33.3 %collective-permute-start.4 = (bf16[448,1536]{1,0:T(8,128)(2,1)}, bf16[448,1536]{1,0:T(8,128)(2,1)S(1)}, u32[]{:S(2)}, u32[]{:S(2)}) collective-permute-start(bf16[448,1536]{1,0:T(8,128)(2,1)} %pad_maximum_fusion.1.refs_7_), channel_id=1, source_target_pairs={{0,8},{4,12},{8,0},{12,4},{16,24},{20,28},{24,16},{28,20},{1,9},{5... | collective-permute-start | bytes 4128776 | tf_op jit(solution)/shard_map/ppermute | solution.py:434
  41.3 23.7 %collective-permute-start.3 = (bf16[320,1536]{1,0:T(8,128)(2,1)}, bf16[320,1536]{1,0:T(8,128)(2,1)S(1)}, u32[]{:S(2)}, u32[]{:S(2)}) collective-permute-start(bf16[320,1536]{1,0:T(8,128)(2,1)} %shard_map.87), channel_id=1, source_target_pairs={{0,16},{4,20},{8,24},{12,28},{16,0},{20,4},{24,8},{28,12},{1,17},{... | collective-permute-start | bytes 2949128 | tf_op jit(solution)/shard_map/ppermute | solution.py:434
  71.0 167.5 %all-gather.15.cloned.1.call-start = ((), (), s32[]{:S(2)}) async-start(), calls=%async_computation.3 | async-start | bytes 1966080 | tf_op jit(solution)/shard_map/all_gather | solution.py:606
  71.0 50.2 %collective-permute-start.13 = (bf16[512,2048]{1,0:T(8,128)(2,1)}, bf16[512,2048]{1,0:T(8,128)(2,1)}, u32[]{:S(2)}, u32[]{:S(2)}) collective-permute-start(bf16[512,2048]{1,0:T(8,128)(2,1)} %shard_map.86.refs_3_.second_ref), channel_id=1, source_target_pairs={{0,8},{16,24},{1,9},{17,25},{2,10},{18,26},{3,11},{19,27}} | collective-permute-start | bytes 6291464 | tf_op jit(solution)/shard_map/ppermute | solution.py:594
  72.3 194.9 %all-gather.13.cloned.1.call-start = ((), (), s32[]{:S(2)}) async-start(), calls=%async_computation.2 | async-start | bytes 1966080 | tf_op jit(solution)/shard_map/all_gather | solution.py:606
  72.4 52.6 %collective-permute-start.8 = (bf16[448,1536]{1,0:T(8,128)(2,1)}, bf16[448,1536]{1,0:T(8,128)(2,1)}, u32[]{:S(2)}, u32[]{:S(2)}) collective-permute-start(bf16[448,1536]{1,0:T(8,128)(2,1)} %pad_maximum_fusion.1.refs_7_), channel_id=1, source_target_pairs={{0,4},{4,0},{8,12},{12,8},{16,20},{20,16},{24,28},{28,24},{1,5},{5... | collective-permute-start | bytes 4128776 | tf_op jit(solution)/shard_map/ppermute | solution.py:434
  100.7 40.4 %collective-permute-start.10 = (bf16[320,1536]{1,0:T(8,128)(2,1)S(1)}, bf16[320,1536]{1,0:T(8,128)(2,1)}, u32[]{:S(2)}, u32[]{:S(2)}) collective-permute-start(bf16[320,1536]{1,0:T(8,128)(2,1)S(1)} %collective-permute-done.3.refs_11_), channel_id=1, source_target_pairs={{0,8},{4,12},{8,0},{12,4},{16,24},{20,28},{24,16},{28,20},{1,9},{5... | collective-permute-start | bytes 2949128 | tf_op jit(solution)/shard_map/ppermute | solution.py:434
  102.2 39.0 %collective-permute-start.6 = (bf16[784,512]{1,0:T(8,128)(2,1)}, bf16[784,512]{1,0:T(8,128)(2,1)}, u32[]{:S(2)}, u32[]{:S(2)}) collective-permute-start(bf16[784,512]{1,0:T(8,128)(2,1)} %shard_map.89.refs_3_), channel_id=1, source_target_pairs={{0,4},{4,0},{8,12},{12,8},{16,20},{20,16},{24,28},{28,24},{1,5},{5... | collective-permute-start | bytes 2408456 | tf_op jit(solution)/shard_map/ppermute | solution.py:434
  121.2 24.9 %collective-permute-start.7 = (bf16[784,512]{1,0:T(8,128)(2,1)S(1)}, bf16[784,512]{1,0:T(8,128)(2,1)}, u32[]{:S(2)}, u32[]{:S(2)}) collective-permute-start(bf16[784,512]{1,0:T(8,128)(2,1)S(1)} %collective-permute-done.5.refs_4_), channel_id=1, source_target_pairs={{0,4},{4,0},{8,12},{12,8},{16,20},{20,16},{24,28},{28,24},{1,5},{5... | collective-permute-start | bytes 2408456 | tf_op jit(solution)/shard_map/ppermute | solution.py:434
  121.2 64.0 %collective-permute-start.9 = (bf16[448,1536]{1,0:T(8,128)(2,1)S(1)}, bf16[448,1536]{1,0:T(8,128)(2,1)}, u32[]{:S(2)}, u32[]{:S(2)}) collective-permute-start(bf16[448,1536]{1,0:T(8,128)(2,1)S(1)} %copy-done.3), channel_id=1, source_target_pairs={{0,4},{4,0},{8,12},{12,8},{16,20},{20,16},{24,28},{28,24},{1,5},{5... | collective-permute-start | bytes 4128776 | tf_op jit(solution)/shard_map/ppermute | solution.py:434
  125.0 81.3 %collective-permute-start.14 = (bf16[512,2048]{1,0:T(8,128)(2,1)}, bf16[512,2048]{1,0:T(8,128)(2,1)}, u32[]{:S(2)}, u32[]{:S(2)}) collective-permute-start(bf16[512,2048]{1,0:T(8,128)(2,1)} %shard_map.93.second_ref), channel_id=1, source_target_pairs={{0,4},{8,12},{16,20},{24,28},{1,5},{9,13},{17,21},{25,29},{2,6},{1... | collective-permute-start | bytes 6291464 | tf_op jit(solution)/shard_map/ppermute | solution.py:594
  141.2 42.5 %collective-permute-start.11 = (bf16[320,1536]{1,0:T(8,128)(2,1)S(1)}, bf16[320,1536]{1,0:T(8,128)(2,1)}, u32[]{:S(2)}, u32[]{:S(2)}) collective-permute-start(bf16[320,1536]{1,0:T(8,128)(2,1)S(1)} %collective-permute-done.3.refs_11_), channel_id=1, source_target_pairs={{0,4},{4,0},{8,12},{12,8},{16,20},{20,16},{24,28},{28,24},{1,5},{5... | collective-permute-start | bytes 2949128 | tf_op jit(solution)/shard_map/ppermute | solution.py:434
  141.2 42.5 %collective-permute-start.12 = (bf16[320,1536]{1,0:T(8,128)(2,1)}, bf16[320,1536]{1,0:T(8,128)(2,1)}, u32[]{:S(2)}, u32[]{:S(2)}) collective-permute-start(bf16[320,1536]{1,0:T(8,128)(2,1)} %collective-permute-done.10.refs_12_), channel_id=1, source_target_pairs={{0,4},{4,0},{8,12},{12,8},{16,20},{20,16},{24,28},{28,24},{1,5},{5... | collective-permute-start | bytes 2949128 | tf_op jit(solution)/shard_map/ppermute | solution.py:434
  146.1 56.1 %collective-permute-start.20 = (bf16[784,512]{1,0:T(8,128)(2,1)}, bf16[784,512]{1,0:T(8,128)(2,1)}, u32[]{:S(2)}, u32[]{:S(2)}) collective-permute-start(bf16[784,512]{1,0:T(8,128)(2,1)} %get-tuple-element.61), channel_id=1, source_target_pairs={{0,8},{4,12},{8,0},{12,4},{16,24},{20,28},{24,16},{28,20},{1,9},{5... | collective-permute-start | bytes 2408456 | tf_op jit(solution)/shard_map/ppermute | solution.py:434
  183.6 32.9 %collective-permute-start.19 = (bf16[784,512]{1,0:T(8,128)(2,1)}, bf16[784,512]{1,0:T(8,128)(2,1)S(1)}, u32[]{:S(2)}, u32[]{:S(2)}) collective-permute-start(bf16[784,512]{1,0:T(8,128)(2,1)} %get-tuple-element.48.refs_7_), channel_id=1, source_target_pairs={{0,4},{4,0},{8,12},{12,8},{16,20},{20,16},{24,28},{28,24},{1,5},{5... | collective-permute-start | bytes 2408456 | tf_op jit(solution)/shard_map/ppermute | solution.py:434
  183.7 31.4 %collective-permute-start.18 = (bf16[784,512]{1,0:T(8,128)(2,1)}, bf16[784,512]{1,0:T(8,128)(2,1)S(1)}, u32[]{:S(2)}, u32[]{:S(2)}) collective-permute-start(bf16[784,512]{1,0:T(8,128)(2,1)} %get-tuple-element.60), channel_id=1, source_target_pairs={{0,8},{4,12},{8,0},{12,4},{16,24},{20,28},{24,16},{28,20},{1,9},{5... | collective-permute-start | bytes 2408456 | tf_op jit(solution)/shard_map/ppermute | solution.py:434
  205.2 36.2 %collective-permute-start.17 = (bf16[768,512]{1,0:T(8,128)(2,1)}, bf16[768,512]{1,0:T(8,128)(2,1)}, u32[]{:S(2)}, u32[]{:S(2)}) collective-permute-start(bf16[768,512]{1,0:T(8,128)(2,1)} %get-tuple-element.57), channel_id=1, source_target_pairs={{0,8},{4,12},{8,0},{12,4},{16,24},{20,28},{24,16},{28,20},{1,9},{5... | collective-permute-start | bytes 2359304 | tf_op jit(solution)/shard_map/ppermute | solution.py:434
  206.3 40.7 %collective-permute-start.16 = (bf16[768,512]{1,0:T(8,128)(2,1)S(1)}, bf16[768,512]{1,0:T(8,128)(2,1)S(1)}, u32[]{:S(2)}, u32[]{:S(2)}) collective-permute-start(bf16[768,512]{1,0:T(8,128)(2,1)S(1)} %copy-done.5), channel_id=1, source_target_pairs={{0,4},{4,0},{8,12},{12,8},{16,20},{20,16},{24,28},{28,24},{1,5},{5... | collective-permute-start | bytes 2359304 | tf_op jit(solution)/shard_map/ppermute | solution.py:434
  215.0 30.7 %collective-permute-start.15 = (bf16[768,512]{1,0:T(8,128)(2,1)}, bf16[768,512]{1,0:T(8,128)(2,1)}, u32[]{:S(2)}, u32[]{:S(2)}) collective-permute-start(bf16[768,512]{1,0:T(8,128)(2,1)} %get-tuple-element.56), channel_id=1, source_target_pairs={{0,8},{4,12},{8,0},{12,4},{16,24},{20,28},{24,16},{28,20},{1,9},{5... | collective-permute-start | bytes 2359304 | tf_op jit(solution)/shard_map/ppermute | solution.py:434
  244.4 25.8 %collective-permute-start.28 = (bf16[768,256]{1,0:T(8,128)(2,1)}, bf16[768,256]{1,0:T(8,128)(2,1)S(1)}, u32[]{:S(2)}, u32[]{:S(2)}) collective-permute-start(bf16[768,256]{1,0:T(8,128)(2,1)} %get-tuple-element.72), channel_id=1, source_target_pairs={{0,8},{4,12},{8,0},{12,4},{16,24},{20,28},{24,16},{28,20},{1,9},{5... | collective-permute-start | bytes 1179656 | tf_op jit(solution)/shard_map/ppermute | solution.py:434
  245.5 30.9 %collective-permute-start.27 = (bf16[768,256]{1,0:T(8,128)(2,1)}, bf16[768,256]{1,0:T(8,128)(2,1)S(1)}, u32[]{:S(2)}, u32[]{:S(2)}) collective-permute-start(bf16[768,256]{1,0:T(8,128)(2,1)} %get-tuple-element.63.refs_2_.refs_17_), channel_id=1, source_target_pairs={{0,4},{4,0},{8,12},{12,8},{16,20},{20,16},{24,28},{28,24},{1,5},{5... | collective-permute-start | bytes 1179656 | tf_op jit(solution)/shard_map/ppermute | solution.py:434
  245.8 29.3 %collective-permute-start.26 = (bf16[768,256]{1,0:T(8,128)(2,1)}, bf16[768,256]{1,0:T(8,128)(2,1)S(1)}, u32[]{:S(2)}, u32[]{:S(2)}) collective-permute-start(bf16[768,256]{1,0:T(8,128)(2,1)} %get-tuple-element.71), channel_id=1, source_target_pairs={{0,8},{4,12},{8,0},{12,4},{16,24},{20,28},{24,16},{28,20},{1,9},{5... | collective-permute-start | bytes 1179656 | tf_op jit(solution)/shard_map/ppermute | solution.py:434
  (41 other events, 347.6 us)
Sparse Core Ops, SparseCore 0:
  30.9 65.8 all-gather.8
  98.3 62.1 all-gather.10
  162.1 35.7 all-gather.14
  199.3 35.9 all-gather.12

commit v8 on v7

--- a/solution.py
+++ b/solution.py
@@ -241,37 +241,41 @@
 
 
 def solve_kernel(flag_ref, inverse_ref, first_ref, second_ref, *refs):
-    high_ref, low_ref = refs[-2:]
+    high_ref, low_ref, parts_ref = refs
+
+    @pl.when(pl.program_id(0) == 0)
+    def _():
+        parts_ref[0], parts_ref[1] = split(inverse_ref[...])
+
     values = jnp.where(flag_ref[0] == 1, first_ref[...], second_ref[...])
-    high, low = split(inverse_ref[...])
-    solved = jnp.dot(high, values, preferred_element_type=F32)
-    solved = solved + jnp.dot(low, values, preferred_element_type=F32)
+    solved = jnp.dot(parts_ref[0], values, preferred_element_type=F32)
+    solved = solved + jnp.dot(parts_ref[1], values, preferred_element_type=F32)
     high_ref[...], low_ref[...] = split(solved)
 
 
-def solve_lead(flag, inverse, first, second, earlier):
-    tiled = pl.BlockSpec((LEAD, ROWS), lambda j: (0, j))
+def solve_lead(flag, inverse, first, second):
+    tiled = pl.BlockSpec((LEAD, COLS), lambda j: (0, j))
     return pl.pallas_call(
         solve_kernel,
-        grid=(first.shape[1] // ROWS,),
+        grid=(first.shape[1] // COLS,),
         out_shape=(jax.ShapeDtypeStruct(first.shape, BF16),) * 2,
         in_specs=[
             pl.BlockSpec(memory_space=pltpu.SMEM),
             pl.BlockSpec((LEAD, LEAD), lambda j: (0, 0)),
             tiled,
             tiled,
-        ]
-        + [ANYWHERE] * len(earlier),
+        ],
         out_specs=(tiled, tiled),
+        scratch_shapes=[pltpu.VMEM((2, LEAD, LEAD), BF16)],
         compiler_params=pltpu.CompilerParams(vmem_limit_bytes=VMEM_BYTES),
         cost_estimate=NO_COST,
-    )(flag, inverse, first, second, *earlier)
+    )(flag, inverse, first, second)
 
 
 def finish_kernel(
     count,
     gram_steps,
-    first_chunk,
+    begin,
     unread,
     places_ref,
     damp_ref,
@@ -285,13 +289,14 @@
     across_ref,
     *refs,
 ):
+    first_chunk = begin == 0
     if first_chunk:
         lower_ref, low_ref, *refs = refs
     mine = refs[:count]
     outs = refs[count + unread :]
     running_ref, factored_ref, precond_ref, token_ref, mine_ref, rows_ref, first_ref = outs
     j, i = pl.program_id(0), pl.program_id(1)
-    member, column, base = places_ref[0], places_ref[1], places_ref[2]
+    member, column, base = places_ref[0], places_ref[1], places_ref[2] + begin
     share, damp = share_ref[:1, :1], damp_ref[0]
     height, cols = running_ref.shape
     depth = 2 * CAP
@@ -304,8 +309,8 @@
         token_ref[...] = jnp.zeros_like(token_ref)
         for q in range(count):
             mine_ref[span, q * depth : (q + 1) * depth] = mine[q][0, :depth, :].T
-            begin = pl.multiple_of(places_ref[PLACES + q] * side, side)
-            first_ref[pl.ds(begin, side), :] = mine[q][0, depth : depth + side, :].astype(F32)
+            place = pl.multiple_of(places_ref[PLACES + q] * side, side)
+            first_ref[pl.ds(place, side), :] = mine[q][0, depth : depth + side, :].astype(F32)
         source = first_ref[...].T
         if cols == LEAD:
             source = jnp.where(column == 0, factor_ref[...], source)
@@ -405,7 +410,7 @@
     unread = len(results) + len(earlier)
     in_specs += [ANYWHERE] * unread
     return pl.pallas_call(
-        lambda *refs: finish_kernel(count, gram_steps, begin == 0, unread, *refs),
+        lambda *refs: finish_kernel(count, gram_steps, begin, unread, *refs),
         grid_spec=pltpu.PrefetchScalarGridSpec(
             num_scalar_prefetch=1,
             grid=(steps, tiles),
@@ -489,26 +494,32 @@
     )(flag, first, second, *earlier)
 
 
-def member_blocks(blocks, member, group, earlier):
+def member_blocks(blocks, member, group):
     _, rows, width = blocks.shape
-    return copied(
-        [(blocks, (None, rows, width), [member ^ other, 0, 0]) for other in range(1, group)],
-        earlier,
-    )
-
-
-def exchange_members(blocks, sent, bits, earlier):
+    return [(blocks, (None, rows, width), [member ^ other, 0, 0]) for other in range(1, group)]
+
+
+def exchange_members(blocks, sent, bits, requests, earlier):
     held = [[blocks]] + [[part] for part in sent]
+    copies = None
     for bit in reversed(range(bits)):
         half = 1 << bit
-        for passed in held[half:]:
-            passed[1:] = [copied([(part, part.shape, [0, 0])], earlier)[0] for part in passed[1:]]
+        arrived = [(part, part.shape, [0, 0]) for passed in held[half:] for part in passed[1:]]
+        if arrived:
+            passing = copied(
+                requests + arrived if copies is None else arrived, earlier + held[0][1:]
+            )
+            if copies is None:
+                copies, passing = passing[: len(requests)], passing[len(requests) :]
+            for passed in held[half:]:
+                count = len(passed) - 1
+                passed[1:], passing = passing[:count], passing[count:]
         held = [
             kept + [swapped(part, half) for part in passed]
             for kept, passed in zip(held[:half], held[half:])
         ]
     first, *others = held[0]
-    return [first] + [part[None] for part in others]
+    return [first] + [part[None] for part in others], copies
 
 
 def member_order(bits):
@@ -528,14 +539,12 @@
 
 
 def share_of_first(lower, upper, member, group, bits):
-    arrived = None
     for bit in reversed(range(bits)):
         moved = lax.ppermute(upper, "tok", down_pairs(bit, group))
-        arrived = moved if arrived is None else arrived
         blocks = jnp.where(member >> bit & 1 == 1, moved, lower)
         half = blocks.shape[0] // 2
         lower, upper = blocks[:half], blocks[half:]
-    return blocks, arrived
+    return blocks
 
 
 def count_rows(number, row, width):
@@ -557,7 +566,7 @@
 
     side = LEAD // 2
     halves = [(factor_old, (side, width), [place, 0]) for place in range(2)]
-    lead_factor, arrived = share_of_first(*copied(halves, []), member, group, bits)
+    lead_factor = share_of_first(*copied(halves, []), member, group, bits)
 
     live = jnp.arange(tok_rows) < counts[0]
     named = routes[:, 0]
@@ -582,19 +591,12 @@
         ],
         0,
     )
-    grad_cols = weight_grad.shape[1]
-    near = copied([(weight_grad, (LEAD, grad_cols), [0, 0])], [arrived])[0]
-    away_rows = copied([(packed, (CAP, width), [1, 0])], [front, near])[0]
+    away_rows = copied([(packed, (CAP, width), [1, 0])], [front])[0]
     incoming = swapped(away_rows, group)
     outgoing = jnp.concatenate([packed[:CAP], lead_factor], 0)
     quarter = jnp.concatenate([packed[:CAP], incoming, lead_factor], 0)
     across_own = gather_members(outgoing, bits)
     across_other = gather_members(incoming, bits)
-    for bit in reversed(range(bits)):
-        moved = lax.ppermute(near, "tok", down_pairs(bit, group))
-        flag = (member >> bit & 1)[None]
-        if bit:
-            near = chosen(flag, moved, near, [across_own[1]])
 
     ends = [end for end in (LEAD, 2 * LEAD, 2 * LEAD + ROWS) if end < width] + [width]
     chunks = list(zip([0, *ends], ends))
@@ -605,11 +607,17 @@
     parts = [first_part, *copied(later, [across_own[1]])]
     spread = [lax.all_gather(part, "fac") for part in parts]
     rows = first_part.shape[0]
-    lead = copied([(spread[0], (None, rows, LEAD), [0, 0, 0])], parts[1:])[0]
+    earlier = [across_other[1], *parts[1:]]
+    lead = copied([(spread[0], (None, rows, LEAD), [0, 0, 0])], earlier)[0]
     lead = gather_members(lead, bits)
-    sent = member_blocks(spread[0], member, group, [lead[1]])
-
-    slots = jnp.stack([member, column, member * width] + order).astype(jnp.int32)
+    grad_cols = weight_grad.shape[1]
+    requests = member_blocks(spread[0], member, group)
+    requests += [(weight_grad, (LEAD, grad_cols), [0, 0])]
+    *sent, near = copied(requests, [lead[1]])
+
+    slots = [member, column, member * width] + order + [member] + [0] * (group - 1)
+    assert len(slots) == PLACES + 2 * group
+    slots = jnp.stack([jnp.int32(slot) for slot in slots])
     lower, inverse, share = factor_lead(
         slots, damp, factor_old[:LEAD, :LEAD], lead, sent[:1]
     )
@@ -619,19 +627,20 @@
     token = panel
     results = []
     for number, (begin, _) in enumerate(chunks):
-        ahead = number + 1 < len(chunks)
-        if ahead:
-            coming = member_blocks(spread[number + 1], member, group, [token])
-        pieces = exchange_members(
-            spread[number], sent, bits, coming[:1] if ahead else [token]
-        )
+        requests = []
+        if number + 1 < len(chunks):
+            requests = member_blocks(spread[number + 1], member, group)
+        pieces, sent = exchange_members(spread[number], sent, bits, requests, [token])
         if number == 0:
-            high, low = solve_lead(flag, inverse, moved, near, coming[:1])
-        slots = [member, column, member * width + begin] + order + [member] + [0] * (group - 1)
-        assert len(slots) == PLACES + 2 * group
+            for bit in reversed(range(bits)):
+                moved = lax.ppermute(near, "tok", down_pairs(bit, group))
+                flag = (member >> bit & 1)[None]
+                if bit:
+                    near = chosen(flag, moved, near, sent[:1])
+            high, low = solve_lead(flag, inverse, moved, near)
         *results, token = finish_rows(
             begin,
-            jnp.stack([jnp.int32(slot) for slot in slots]),
+            slots,
             damp,
             share,
             factor_old,
@@ -645,9 +654,8 @@
             across_stack,
             pieces,
             results,
-            coming[:1] if ahead else [],
+            sent[:1],
         )
-        sent = coming
     return tuple(results)
 
 

time: 320 us -> 318 us (level)
  Pallas kernels: 165 us -> 154 us
  waiting for transfers between devices: 83 us -> 87.6 us
  starting transfers between devices: 23.4 us -> 27.3 us
    ppermute x27, waiting for transfers between devices: 58 us -> 80.5 us  [swapped(): lax.ppermute(value, 'tok', [(source, source ^ mask) for source in range(s...]
    all_gather x4, waiting for transfers between devices: 24.4 us -> 6.22 us  [local(): spread = [lax.all_gather(part, 'fac') for part in parts]]
    pallas_call x13 -> x9, Pallas kernels: 40.8 us -> 31.4 us  [copied(): pl.pallas_call(lambda *refs: copy_kernel(len(arrays), *refs), grid_spec=p...]
    ppermute x27, starting transfers between devices: 16 us -> 20.4 us  [swapped(): lax.ppermute(value, 'tok', [(source, source ^ mask) for source in range(s...]
    unnamed x61 -> x63, local copies, waits for them, and re-layouts: 7.67 us -> 11.6 us
  transfers between devices with their start and end apart: 35 -> 35, of which waited for: 7 -> 14; matrix products, arithmetic and copies ran while one was open for 5% -> 4% of each run, Pallas kernels for 47% -> 43%
where the time goes in v8:
time: 318 us; the launch traced here: 316 us
  Pallas kernels  154 us (48%)
  waiting for transfers between devices  87.6 us (28%)
  starting transfers between devices  27.3 us (9%)
  between operations  20.9 us (7%)
  local copies, waits for them, and re-layouts  18.2 us (6%)
  other arithmetic  7.45 us (2%)
    ppermute x27, waiting for transfers between devices, swapped(): lax.ppermute(value, 'tok', [(source, source ^ mask) for source in range(s...  80.5 us
    pallas_call x4, Pallas kernels, finish_rows(): pl.pallas_call(lambda *refs: finish_kernel(count, gram_steps, begin, unre...  66.9 us
    pallas_call x1, Pallas kernels, factor_lead(): pl.pallas_call(lambda *refs: factor_kernel(len(lead), *refs), out_shape=(...  32.1 us
    pallas_call x9, Pallas kernels, copied(): pl.pallas_call(lambda *refs: copy_kernel(len(arrays), *refs), grid_spec=p...  31.4 us
    ppermute x27, starting transfers between devices, swapped(): lax.ppermute(value, 'tok', [(source, source ^ mask) for source in range(s...  20.4 us
    pallas_call x1, Pallas kernels, panel_columns(): pl.pallas_call(lambda *refs: panel_kernel(count, *refs), grid=(width // c...  13.1 us
    unnamed x63, local copies, waits for them, and re-layouts  11.6 us
    pallas_call x1, Pallas kernels, solve_lead(): pl.pallas_call(solve_kernel, grid=(first.shape[1] // COLS,), out_shape=(j...  6.85 us
  transfers between devices with their start and end apart: 35, of which 14 were waited for; matrix products, arithmetic and copies ran while one was open for 4% of the time, Pallas kernels for 43%

profile of v8, /device:TPU:2, one launch (start us, length us, event | category | flops | bytes accessed | tf_op | source)
XLA Modules:
  0.0 316.2 jit_solution(16055771598419494455)
XLA Ops:
  7.2 3.9 %shard_map.85 = (bf16[256,1536]{1,0:T(8,128)(2,1)}, bf16[256,1536]{1,0:T(8,128)(2,1)}) custom-call(s32[4]{0:T(128)} %constant.91.clone.1.refs_0_, f32[1536,1536]{1,0:T(8,128)} %refs_3_.7, f32[1536,1536]{1,0:T(8,128)} %refs_3_.7), custom_call_target="tpu_custom_call" | custom-call | flops 1 | bytes 1 | tf_op jit(solution)/shard_map/pallas_call | solution.py:466
  28.0 3.1 collective-permute-done.refs_2_
  35.0 2.9 shard_map.86
  39.4 22.0 %collective-permute-done.3.refs_11_ = bf16[320,1536]{1,0:T(8,128)(2,1)S(1)} collective-permute-done((bf16[320,1536]{1,0:T(8,128)(2,1)}, bf16[320,1536]{1,0:T(8,128)(2,1)S(1)}, u32[]{:S(2)}, u32[]{:S(2)}) %collective-permute-start.3) | collective-permute-done | bytes 983072 | tf_op jit(solution)/shard_map/ppermute | solution.py:439
  63.0 2.8 collective-permute-done.5.refs_4_.refs_8_
  66.9 3.3 %shard_map.87 = (bf16[768,512]{1,0:T(8,128)(2,1)}, bf16[768,256]{1,0:T(8,128)(2,1)}, bf16[768,256]{1,0:T(8,128)(2,1)}) custom-call(s32[6]{0:T(128)} %constant.93.clone.1.refs_0_, bf16[768,1536]{1,0:T(8,128)(2,1)} %pad_maximum_fusion.refs_1_.refs_2_.refs_3_, bf16[768,1536]{1,0:T(8,128)(2,1)} %pad_maximum_fusion.refs_1_.refs_2_.refs_3_, ...), custom_call_target="tpu_custom_call" | custom-call | flops 1 | bytes 1 | tf_op jit(solution)/shard_map/pallas_call | solution.py:466
  71.7 21.1 %collective-permute-done.4.refs_2_.refs_12_ = bf16[320,1536]{1,0:T(8,128)(2,1)S(1)} collective-permute-done((bf16[320,1536]{1,0:T(8,128)(2,1)S(1)}, bf16[320,1536]{1,0:T(8,128)(2,1)S(1)}, u32[]{:S(2)}, u32[]{:S(2)}) %collective-permute-start.4) | collective-permute-done | bytes 983072 | tf_op jit(solution)/shard_map/ppermute | solution.py:439
  92.8 6.2 %all-gather.9.cloned.1.call-done = bf16[3136,512]{1,0:T(8,128)(2,1)} async-done(((bf16[784,512]{1,0:T(8,128)(2,1)}), bf16[3136,512]{1,0:T(8,128)(2,1)}) %all-gather.9.cloned.1.call-update) | async-done | bytes 3211280 | tf_op jit(solution)/shard_map/all_gather | solution.py:608
  103.9 18.1 %collective-permute-done.6.refs_5_.refs_4_ = bf16[784,512]{1,0:T(8,128)(2,1)S(1)} collective-permute-done((bf16[784,512]{1,0:T(8,128)(2,1)}, bf16[784,512]{1,0:T(8,128)(2,1)S(1)}, u32[]{:S(2)}, u32[]{:S(2)}) %collective-permute-start.6) | collective-permute-done | bytes 802848 | tf_op jit(solution)/shard_map/ppermute | solution.py:439
  122.9 5.2 %shard_map.89 = (bf16[784,512]{1,0:T(8,128)(2,1)}, bf16[784,512]{1,0:T(8,128)(2,1)}, bf16[784,512]{1,0:T(8,128)(2,1)}, bf16[512,2048]{1,0:T(8,128)(2,1)}) custom-call(s32[11]{0:T(128)} %stack.57.refs_0_, bf16[4,784,512]{2,1,0:T(8,128)(2,1)} %bitcast.55, bf16[4,784,512]{2,1,0:T(8,128)(2,1)} %bitcast.56, bf16[4,784,512]{2,1,0:T(8,128)(2,1)} %bitcast.57, ...), custom_call_target="tpu_custom_call" | custom-call | flops 1 | bytes 1 | tf_op jit(solution)/shard_map/pallas_call | solution.py:466
  132.3 4.0 %collective-permute-start.14 = (bf16[784,512]{1,0:T(8,128)(2,1)}, bf16[784,512]{1,0:T(8,128)(2,1)}, u32[]{:S(2)}, u32[]{:S(2)}) collective-permute-start(bf16[784,512]{1,0:T(8,128)(2,1)} %get-tuple-element.57), channel_id=1, source_target_pairs={{0,8},{4,12},{8,0},{12,4},{16,24},{20,28},{24,16},{28,20},{1,9},{5... | collective-permute-start | bytes 2408456 | tf_op jit(solution)/shard_map/ppermute | solution.py:439
  143.9 32.1 %shard_map.90 = (f32[512,512]{1,0:T(8,128)}, f32[512,512]{1,0:T(8,128)}, f32[8,128]{1,0:T(8,128)}) custom-call(s32[11]{0:T(128)} %stack.26.refs_0_, f32[1]{0:T(128)} %bitcast.8.refs_1_, f32[512,512]{1,0:T(8,128)} %slice.48.refs_2_, bf16[784,512]{1,0:T(8,128)(2,1)} %shard_map.88.refs_3_, bf16[784,512]{1,0:T(8,128)(2,1)} %copy-done.3, ...), custom_call_target="tpu_custom_call" | custom-call | flops 1 | bytes 1 | tf_op jit(solution)/shard_map/pallas_call | solution.py:181
  176.9 13.1 %shard_map.91 = (bf16[512,1536]{1,0:T(8,128)(2,1)}, bf16[2560,512]{1,0:T(8,128)(2,1)}, bf16[2560,1536]{1,0:T(8,128)(2,1)}) custom-call(s32[11]{0:T(128)} %stack.26.refs_0_, f32[8,128]{1,0:T(8,128)} %get-tuple-element.53.refs_1_.refs_2_, f32[512,512]{1,0:T(8,128)} %get-tuple-element.54.refs_2_.inverse_ref.refs_6_, bf16[784,512]{1,0:T(8,128)(2,1)} %shard_map.88.refs_3_, ...), custom_call_target="tpu_custom_call" | custom-call | flops 1 | bytes 1 | tf_op jit(solution)/shard_map/pallas_call | solution.py:220
  191.6 4.2 %shard_map.92 = (bf16[768,512]{1,0:T(8,128)(2,1)}, bf16[768,512]{1,0:T(8,128)(2,1)}, bf16[768,512]{1,0:T(8,128)(2,1)}, bf16[784,512]{1,0:T(8,128)(2,1)}) custom-call(s32[11]{0:T(128)} %stack.57.refs_0_, bf16[4,768,512]{2,1,0:T(8,128)(2,1)} %bitcast.59, bf16[4,768,512]{2,1,0:T(8,128)(2,1)} %bitcast.60, bf16[4,768,512]{2,1,0:T(8,128)(2,1)} %bitcast.61, ...), custom_call_target="tpu_custom_call" | custom-call | flops 1 | bytes 1 | tf_op jit(solution)/shard_map/pallas_call | solution.py:466
  195.9 3.4 %shard_map.93.second_ref = bf16[512,2048]{1,0:T(8,128)(2,1)} custom-call(s32[1]{0:T(128)} %bitcast.18.flag_ref, bf16[512,2048]{1,0:T(8,128)(2,1)} %collective-permute-done.13.first_ref, bf16[512,2048]{1,0:T(8,128)(2,1)} %get-tuple-element.56.second_ref, bf16[768,512]{1,0:T(8,128)(2,1)} %get-tuple-element.59.refs_0_.refs_16_), custom_call_target="tpu_custom_call" | custom-call | flops 1 | bytes 1 | tf_op jit(solution)/shard_map/pallas_call | solution.py:486
  205.1 6.9 %shard_map.94 = (bf16[512,2048]{1,0:T(8,128)(2,1)}, bf16[512,2048]{1,0:T(8,128)(2,1)}) custom-call(s32[1]{0:T(128)} %bitcast.17.flag_ref, f32[512,512]{1,0:T(8,128)} %get-tuple-element.54.refs_2_.inverse_ref.refs_6_, bf16[512,2048]{1,0:T(8,128)(2,1)} %collective-permute-done.16.first_ref, bf16[512,2048]{1,0:T(8,128)(2,1)} %shard_map.93.second_ref), custom_call_target="tpu_custom_call" | custom-call | flops 1 | bytes 1 | tf_op jit(solution)/shard_map/pallas_call | solution.py:258
  213.2 20.8 %shard_map.95 = (f32[1536,1536]{1,0:T(8,128)}, f32[1536,1536]{1,0:T(8,128)}, f32[1536,2048]{1,0:T(8,128)}, f32[8,128]{1,0:T(8,128)}) custom-call(s32[11]{0:T(128)} %stack.26.refs_0_, f32[1]{0:T(128)} %bitcast.8.refs_1_, f32[8,128]{1,0:T(8,128)} %get-tuple-element.53.refs_1_.refs_2_, f32[1536,1536]{1,0:T(8,128)} %refs_3_.7, bf16[1536,2048]{1,0:T(8,128)(2,1)} %refs_4_.9, ...), custom_call_target="tpu_custom_call" | custom-call | flops 1 | bytes 1 | tf_op jit(solution)/shard_map/pallas_call | solution.py:412
  234.0 5.1 %collective-permute-done.20.refs_6_ = bf16[768,512]{1,0:T(8,128)(2,1)S(1)} collective-permute-done((bf16[768,512]{1,0:T(8,128)(2,1)}, bf16[768,512]{1,0:T(8,128)(2,1)S(1)}, u32[]{:S(2)}, u32[]{:S(2)}) %collective-permute-start.20) | collective-permute-done | bytes 786464 | tf_op jit(solution)/shard_map/ppermute | solution.py:439
  240.0 3.5 %shard_map.96 = (bf16[768,256]{1,0:T(8,128)(2,1)}, bf16[768,256]{1,0:T(8,128)(2,1)}, bf16[768,256]{1,0:T(8,128)(2,1)}, bf16[768,512]{1,0:T(8,128)(2,1)}) custom-call(s32[11]{0:T(128)} %stack.57.refs_0_, bf16[4,768,256]{2,1,0:T(8,128)(2,1)} %bitcast.63, bf16[4,768,256]{2,1,0:T(8,128)(2,1)} %bitcast.64, bf16[4,768,256]{2,1,0:T(8,128)(2,1)} %bitcast.65, ...), custom_call_target="tpu_custom_call" | custom-call | flops 1 | bytes 1 | tf_op jit(solution)/shard_map/pallas_call | solution.py:466
  246.9 18.9 %shard_map.97 = (f32[1536,1536]{1,0:T(8,128)}, f32[1536,1536]{1,0:T(8,128)}, f32[1536,2048]{1,0:T(8,128)}, f32[8,128]{1,0:T(8,128)}) custom-call(s32[11]{0:T(128)} %stack.26.refs_0_, f32[1]{0:T(128)} %bitcast.8.refs_1_, f32[8,128]{1,0:T(8,128)} %get-tuple-element.53.refs_1_.refs_2_, ...), custom_call_target="tpu_custom_call", output_to_operand_aliasing={{0}: (14, {}), {1}: (15, {}), {2}: (16, {})} | custom-call | flops 1 | bytes 1 | tf_op jit(solution)/shard_map/pallas_call | solution.py:412
  266.7 3.3 %shard_map.98 = (bf16[768,256]{1,0:T(8,128)(2,1)}, bf16[768,256]{1,0:T(8,128)(2,1)}, bf16[768,256]{1,0:T(8,128)(2,1)}, bf16[768,256]{1,0:T(8,128)(2,1)}) custom-call(s32[11]{0:T(128)} %stack.57.refs_0_, bf16[4,768,256]{2,1,0:T(8,128)(2,1)} %bitcast.67, bf16[4,768,256]{2,1,0:T(8,128)(2,1)} %bitcast.68, bf16[4,768,256]{2,1,0:T(8,128)(2,1)} %bitcast.69, ...), custom_call_target="tpu_custom_call" | custom-call | flops 1 | bytes 1 | tf_op jit(solution)/shard_map/pallas_call | solution.py:466
  273.1 13.5 %shard_map.99 = (f32[1536,1536]{1,0:T(8,128)}, f32[1536,1536]{1,0:T(8,128)}, f32[1536,2048]{1,0:T(8,128)}, f32[8,128]{1,0:T(8,128)}) custom-call(s32[11]{0:T(128)} %stack.26.refs_0_, f32[1]{0:T(128)} %bitcast.8.refs_1_, f32[8,128]{1,0:T(8,128)} %get-tuple-element.53.refs_1_.refs_2_, ...), custom_call_target="tpu_custom_call", output_to_operand_aliasing={{0}: (14, {}), {1}: (15, {}), {2}: (16, {})} | custom-call | flops 1 | bytes 1 | tf_op jit(solution)/shard_map/pallas_call | solution.py:412
  286.6 3.6 %collective-permute-done.27.refs_1_ = bf16[768,256]{1,0:T(8,128)(2,1)S(1)} collective-permute-done((bf16[768,256]{1,0:T(8,128)(2,1)}, bf16[768,256]{1,0:T(8,128)(2,1)S(1)}, u32[]{:S(2)}, u32[]{:S(2)}) %collective-permute-start.27) | collective-permute-done | bytes 393248 | tf_op jit(solution)/shard_map/ppermute | solution.py:439
  296.1 13.6 %shard_map.101 = (f32[1536,1536]{1,0:T(8,128)}, f32[1536,1536]{1,0:T(8,128)}, f32[1536,2048]{1,0:T(8,128)}, f32[8,128]{1,0:T(8,128)}) custom-call(s32[11]{0:T(128)} %stack.26.refs_0_, f32[1]{0:T(128)} %bitcast.8.refs_1_, f32[8,128]{1,0:T(8,128)} %get-tuple-element.53.refs_1_.refs_2_, ...), custom_call_target="tpu_custom_call", output_to_operand_aliasing={{0}: (14, {}), {1}: (15, {}), {2}: (16, {})} | custom-call | flops 1 | bytes 1 | tf_op jit(solution)/shard_map/pallas_call | solution.py:412
  (168 shorter events, 60.9 us)
Async XLA Ops:
  7.2 91.7 %all-gather.9.cloned.1.call-start = ((), (), s32[]{:S(2)}) async-start(), calls=%async_computation | async-start | bytes 4014080 | tf_op jit(solution)/shard_map/all_gather | solution.py:608
  32.9 157.1 %all-gather.11.cloned.1.call-start = ((), (), s32[]{:S(2)}) async-start(), calls=%async_computation.1 | async-start | bytes 3932160 | tf_op jit(solution)/shard_map/all_gather | solution.py:608
  34.2 31.5 %collective-permute-start.5 = (bf16[448,1536]{1,0:T(8,128)(2,1)}, bf16[448,1536]{1,0:T(8,128)(2,1)S(1)}, u32[]{:S(2)}, u32[]{:S(2)}) collective-permute-start(bf16[448,1536]{1,0:T(8,128)(2,1)} %pad_maximum_fusion.1.refs_7_), channel_id=1, source_target_pairs={{0,8},{4,12},{8,0},{12,4},{16,24},{20,28},{24,16},{28,20},{1,9},{5... | collective-permute-start | bytes 4128776 | tf_op jit(solution)/shard_map/ppermute | solution.py:439
  37.8 23.5 %collective-permute-start.3 = (bf16[320,1536]{1,0:T(8,128)(2,1)}, bf16[320,1536]{1,0:T(8,128)(2,1)S(1)}, u32[]{:S(2)}, u32[]{:S(2)}) collective-permute-start(bf16[320,1536]{1,0:T(8,128)(2,1)} %shard_map.86), channel_id=1, source_target_pairs={{0,16},{4,20},{8,24},{12,28},{16,0},{20,4},{24,8},{28,12},{1,17},{... | collective-permute-start | bytes 2949128 | tf_op jit(solution)/shard_map/ppermute | solution.py:439
  70.1 163.9 %all-gather.15.cloned.1.call-start = ((), (), s32[]{:S(2)}) async-start(), calls=%async_computation.3 | async-start | bytes 1966080 | tf_op jit(solution)/shard_map/all_gather | solution.py:608
  70.2 22.6 %collective-permute-start.4 = (bf16[320,1536]{1,0:T(8,128)(2,1)S(1)}, bf16[320,1536]{1,0:T(8,128)(2,1)S(1)}, u32[]{:S(2)}, u32[]{:S(2)}) collective-permute-start(bf16[320,1536]{1,0:T(8,128)(2,1)S(1)} %collective-permute-done.3.refs_11_), channel_id=1, source_target_pairs={{0,8},{4,12},{8,0},{12,4},{16,24},{20,28},{24,16},{28,20},{1,9},{5... | collective-permute-start | bytes 2949128 | tf_op jit(solution)/shard_map/ppermute | solution.py:439
  102.2 19.8 %collective-permute-start.6 = (bf16[784,512]{1,0:T(8,128)(2,1)}, bf16[784,512]{1,0:T(8,128)(2,1)S(1)}, u32[]{:S(2)}, u32[]{:S(2)}) collective-permute-start(bf16[784,512]{1,0:T(8,128)(2,1)} %shard_map.88.refs_3_), channel_id=1, source_target_pairs={{0,8},{4,12},{8,0},{12,4},{16,24},{20,28},{24,16},{28,20},{1,9},{5... | collective-permute-start | bytes 2408456 | tf_op jit(solution)/shard_map/ppermute | solution.py:439
  102.7 27.5 %collective-permute-start.9 = (bf16[448,1536]{1,0:T(8,128)(2,1)}, bf16[448,1536]{1,0:T(8,128)(2,1)}, u32[]{:S(2)}, u32[]{:S(2)}) collective-permute-start(bf16[448,1536]{1,0:T(8,128)(2,1)} %pad_maximum_fusion.1.refs_7_), channel_id=1, source_target_pairs={{0,4},{4,0},{8,12},{12,8},{16,20},{20,16},{24,28},{28,24},{1,5},{5... | collective-permute-start | bytes 4128776 | tf_op jit(solution)/shard_map/ppermute | solution.py:439
  102.7 27.4 %collective-permute-start.11 = (bf16[320,1536]{1,0:T(8,128)(2,1)S(1)}, bf16[320,1536]{1,0:T(8,128)(2,1)}, u32[]{:S(2)}, u32[]{:S(2)}) collective-permute-start(bf16[320,1536]{1,0:T(8,128)(2,1)S(1)} %collective-permute-done.3.refs_11_), channel_id=1, source_target_pairs={{0,4},{4,0},{8,12},{12,8},{16,20},{20,16},{24,28},{28,24},{1,5},{5... | collective-permute-start | bytes 2949128 | tf_op jit(solution)/shard_map/ppermute | solution.py:439
  128.0 67.8 %collective-permute-start.13 = (bf16[512,2048]{1,0:T(8,128)(2,1)}, bf16[512,2048]{1,0:T(8,128)(2,1)}, u32[]{:S(2)}, u32[]{:S(2)}) collective-permute-start(bf16[512,2048]{1,0:T(8,128)(2,1)} %get-tuple-element.56.second_ref), channel_id=1, source_target_pairs={{0,8},{16,24},{1,9},{17,25},{2,10},{18,26},{3,11},{19,27}} | collective-permute-start | bytes 6291464 | tf_op jit(solution)/shard_map/ppermute | solution.py:636
  129.5 136.3 %all-gather.13.cloned.1.call-start = ((), (), s32[]{:S(2)}) async-start(), calls=%async_computation.2 | async-start | bytes 1966080 | tf_op jit(solution)/shard_map/all_gather | solution.py:608
  130.1 45.8 %collective-permute-start.10 = (bf16[448,1536]{1,0:T(8,128)(2,1)}, bf16[448,1536]{1,0:T(8,128)(2,1)}, u32[]{:S(2)}, u32[]{:S(2)}) collective-permute-start(bf16[448,1536]{1,0:T(8,128)(2,1)} %copy-done.5), channel_id=1, source_target_pairs={{0,4},{4,0},{8,12},{12,8},{16,20},{20,16},{24,28},{28,24},{1,5},{5... | collective-permute-start | bytes 4128776 | tf_op jit(solution)/shard_map/ppermute | solution.py:439
  130.2 45.8 %collective-permute-start.12 = (bf16[320,1536]{1,0:T(8,128)(2,1)}, bf16[320,1536]{1,0:T(8,128)(2,1)S(1)}, u32[]{:S(2)}, u32[]{:S(2)}) collective-permute-start(bf16[320,1536]{1,0:T(8,128)(2,1)} %copy-done.7), channel_id=1, source_target_pairs={{0,4},{4,0},{8,12},{12,8},{16,20},{20,16},{24,28},{28,24},{1,5},{5... | collective-permute-start | bytes 2949128 | tf_op jit(solution)/shard_map/ppermute | solution.py:439
  132.3 57.8 %collective-permute-start.14 = (bf16[784,512]{1,0:T(8,128)(2,1)}, bf16[784,512]{1,0:T(8,128)(2,1)}, u32[]{:S(2)}, u32[]{:S(2)}) collective-permute-start(bf16[784,512]{1,0:T(8,128)(2,1)} %get-tuple-element.57), channel_id=1, source_target_pairs={{0,8},{4,12},{8,0},{12,4},{16,24},{20,28},{24,16},{28,20},{1,9},{5... | collective-permute-start | bytes 2408456 | tf_op jit(solution)/shard_map/ppermute | solution.py:439
  137.2 53.5 %collective-permute-start.15 = (bf16[784,512]{1,0:T(8,128)(2,1)}, bf16[784,512]{1,0:T(8,128)(2,1)S(1)}, u32[]{:S(2)}, u32[]{:S(2)}) collective-permute-start(bf16[784,512]{1,0:T(8,128)(2,1)} %get-tuple-element.58), channel_id=1, source_target_pairs={{0,8},{4,12},{8,0},{12,4},{16,24},{20,28},{24,16},{28,20},{1,9},{5... | collective-permute-start | bytes 2408456 | tf_op jit(solution)/shard_map/ppermute | solution.py:439
  202.6 31.5 %collective-permute-start.17 = (bf16[768,512]{1,0:T(8,128)(2,1)}, bf16[768,512]{1,0:T(8,128)(2,1)}, u32[]{:S(2)}, u32[]{:S(2)}) collective-permute-start(bf16[768,512]{1,0:T(8,128)(2,1)} %get-tuple-element.63), channel_id=1, source_target_pairs={{0,8},{4,12},{8,0},{12,4},{16,24},{20,28},{24,16},{28,20},{1,9},{5... | collective-permute-start | bytes 2359304 | tf_op jit(solution)/shard_map/ppermute | solution.py:439
  202.8 36.3 %collective-permute-start.20 = (bf16[768,512]{1,0:T(8,128)(2,1)}, bf16[768,512]{1,0:T(8,128)(2,1)S(1)}, u32[]{:S(2)}, u32[]{:S(2)}) collective-permute-start(bf16[768,512]{1,0:T(8,128)(2,1)} %get-tuple-element.68), channel_id=1, source_target_pairs={{0,8},{4,12},{8,0},{12,4},{16,24},{20,28},{24,16},{28,20},{1,9},{5... | collective-permute-start | bytes 2359304 | tf_op jit(solution)/shard_map/ppermute | solution.py:439
  204.7 40.8 %collective-permute-start.22 = (bf16[768,512]{1,0:T(8,128)(2,1)S(1)}, bf16[768,512]{1,0:T(8,128)(2,1)}, u32[]{:S(2)}, u32[]{:S(2)}) collective-permute-start(bf16[768,512]{1,0:T(8,128)(2,1)S(1)} %copy-done.12), channel_id=1, source_target_pairs={{0,4},{4,0},{8,12},{12,8},{16,20},{20,16},{24,28},{28,24},{1,5},{5... | collective-permute-start | bytes 2359304 | tf_op jit(solution)/shard_map/ppermute | solution.py:439
  243.5 22.3 %collective-permute-start.21 = (bf16[768,256]{1,0:T(8,128)(2,1)}, bf16[768,256]{1,0:T(8,128)(2,1)S(1)}, u32[]{:S(2)}, u32[]{:S(2)}) collective-permute-start(bf16[768,256]{1,0:T(8,128)(2,1)} %get-tuple-element.69), channel_id=1, source_target_pairs={{0,8},{4,12},{8,0},{12,4},{16,24},{20,28},{24,16},{28,20},{1,9},{5... | collective-permute-start | bytes 1179656 | tf_op jit(solution)/shard_map/ppermute | solution.py:439
  243.8 22.1 %collective-permute-start.24 = (bf16[768,256]{1,0:T(8,128)(2,1)}, bf16[768,256]{1,0:T(8,128)(2,1)S(1)}, u32[]{:S(2)}, u32[]{:S(2)}) collective-permute-start(bf16[768,256]{1,0:T(8,128)(2,1)} %get-tuple-element.76), channel_id=1, source_target_pairs={{0,8},{4,12},{8,0},{12,4},{16,24},{20,28},{24,16},{28,20},{1,9},{5... | collective-permute-start | bytes 1179656 | tf_op jit(solution)/shard_map/ppermute | solution.py:439
  245.5 26.7 %collective-permute-start.28 = (bf16[768,256]{1,0:T(8,128)(2,1)}, bf16[768,256]{1,0:T(8,128)(2,1)S(1)}, u32[]{:S(2)}, u32[]{:S(2)}) collective-permute-start(bf16[768,256]{1,0:T(8,128)(2,1)} %get-tuple-element.74.refs_17_), channel_id=1, source_target_pairs={{0,4},{4,0},{8,12},{12,8},{16,20},{20,16},{24,28},{28,24},{1,5},{5... | collective-permute-start | bytes 1179656 | tf_op jit(solution)/shard_map/ppermute | solution.py:439
  270.1 16.5 %collective-permute-start.25 = (bf16[768,256]{1,0:T(8,128)(2,1)}, bf16[768,256]{1,0:T(8,128)(2,1)S(1)}, u32[]{:S(2)}, u32[]{:S(2)}) collective-permute-start(bf16[768,256]{1,0:T(8,128)(2,1)} %get-tuple-element.77), channel_id=1, source_target_pairs={{0,8},{4,12},{8,0},{12,4},{16,24},{20,28},{24,16},{28,20},{1,9},{5... | collective-permute-start | bytes 1179656 | tf_op jit(solution)/shard_map/ppermute | solution.py:439
  270.4 19.7 %collective-permute-start.27 = (bf16[768,256]{1,0:T(8,128)(2,1)}, bf16[768,256]{1,0:T(8,128)(2,1)S(1)}, u32[]{:S(2)}, u32[]{:S(2)}) collective-permute-start(bf16[768,256]{1,0:T(8,128)(2,1)} %get-tuple-element.79), channel_id=1, source_target_pairs={{0,8},{4,12},{8,0},{12,4},{16,24},{20,28},{24,16},{28,20},{1,9},{5... | collective-permute-start | bytes 1179656 | tf_op jit(solution)/shard_map/ppermute | solution.py:439
  272.2 21.2 %collective-permute-start.26 = (bf16[768,256]{1,0:T(8,128)(2,1)}, bf16[768,256]{1,0:T(8,128)(2,1)S(1)}, u32[]{:S(2)}, u32[]{:S(2)}) collective-permute-start(bf16[768,256]{1,0:T(8,128)(2,1)} %get-tuple-element.78.refs_17_), channel_id=1, source_target_pairs={{0,4},{4,0},{8,12},{12,8},{16,20},{20,16},{24,28},{28,24},{1,5},{5... | collective-permute-start | bytes 1179656 | tf_op jit(solution)/shard_map/ppermute | solution.py:439
  (42 other events, 294.7 us)
Sparse Core Ops, SparseCore 0:
  33.1 65.8 all-gather.8
  100.5 62.1 all-gather.10
  164.2 35.7 all-gather.14
  202.1 35.9 all-gather.12

commit v9 on v8

--- a/solution.py
+++ b/solution.py
@@ -122,8 +122,6 @@
     work_ref[...] = (
         DECAY * work_ref[...] + share * gram + jnp.where(rows == cols, damp_ref[0], 0.0)
     )
-    upper_ref[...] = jnp.zeros_like(upper_ref)
-    inverse_ref[...] = jnp.zeros_like(inverse_ref)
     lanes = lax.broadcasted_iota(jnp.int32, (GROUP, TILE), 1)
     subs = lax.broadcasted_iota(jnp.int32, (GROUP, TILE), 0)
 
@@ -140,34 +138,19 @@
         inverse_tile = jnp.concatenate(
             [jnp.where(lanes <= subs + g * GROUP, part, 0.0) for g, part in enumerate(inverse)], 0
         )
-        band = jnp.dot(
-            inverse_tile,
-            work_ref[pl.ds(begin, TILE), :],
-            precision=HIGHEST,
-            preferred_element_type=F32,
-        )
+        band = dot_split(inverse_tile, work_ref[pl.ds(begin, TILE), :], ((1,), (0,)))
         work_ref[pl.ds(begin, TILE), :] = band
         work_ref[pl.ds(begin, TILE), pl.ds(begin, TILE)] = inverse_tile
+        band = work_ref[pl.ds(begin, TILE), :]
+        at = lax.broadcasted_iota(jnp.int32, (TILE, LEAD), 1)
+        right = jnp.where(at >= begin + TILE, band, 0.0)
+        inverse_ref[pl.ds(begin, TILE), :] = jnp.where(at < begin + TILE, band, 0.0)
+        upper_ref[pl.ds(begin, TILE), :] = right
         upper_ref[pl.ds(begin, TILE), pl.ds(begin, TILE)] = upper_tile
-        inverse_ref[pl.ds(begin, TILE), pl.ds(begin, TILE)] = inverse_tile
-        for other in range(steps):
-
-            @pl.when(other < k)
-            def _():
-                inverse_ref[pl.ds(begin, TILE), other * TILE : (other + 1) * TILE] = work_ref[
-                    pl.ds(begin, TILE), other * TILE : (other + 1) * TILE
-                ]
-
-            @pl.when(other > k)
-            def _():
-                span = slice(other * TILE, (other + 1) * TILE)
-                part = work_ref[pl.ds(begin, TILE), span]
-                upper_ref[pl.ds(begin, TILE), span] = part
-                work_ref[span, pl.ds(begin, TILE)] = jnp.zeros((TILE, TILE), F32)
-                work_ref[span, :] = work_ref[span, :] - dot_t(
-                    part, work_ref[pl.ds(begin, TILE), :], HIGHEST
-                )
-
+        down = lax.broadcasted_iota(jnp.int32, (LEAD, TILE), 0)
+        column = work_ref[:, pl.ds(begin, TILE)]
+        work_ref[:, pl.ds(begin, TILE)] = jnp.where(down >= begin + TILE, 0.0, column)
+        work_ref[...] = work_ref[...] - dot_split(right, band, ((0,), (0,)))
         return carry
 
     lax.fori_loop(0, steps, tile_step, 0)
@@ -180,8 +163,11 @@
     smem = pl.BlockSpec(memory_space=pltpu.SMEM)
     return pl.pallas_call(
         lambda *refs: factor_kernel(len(lead), *refs),
+        grid=(1,),
         out_shape=(shape, shape, jax.ShapeDtypeStruct((GROUP, TILE), F32)),
-        in_specs=[smem, smem] + [vmem] * (1 + len(lead)) + [ANYWHERE] * len(earlier),
+        in_specs=[smem, smem, pl.BlockSpec((LEAD, LEAD), lambda i: (0, 0))]
+        + [vmem] * len(lead)
+        + [ANYWHERE] * len(earlier),
         out_specs=(vmem, vmem, vmem),
         scratch_shapes=[pltpu.VMEM((LEAD, LEAD), F32)] * 2,
         compiler_params=pltpu.CompilerParams(vmem_limit_bytes=VMEM_BYTES),
@@ -189,16 +175,43 @@
     )(places, damp, exact, *lead, *earlier)
 
 
-def panel_kernel(count, places_ref, share_ref, inverse_ref, *refs):
-    lead, own, other = refs[:count], refs[count : 2 * count], refs[2 * count : 3 * count]
-    out_ref, lead_ref, across_ref, near_ref = refs[-4:]
-    side = LEAD // count
+def stack_kernel(count, places_ref, *refs):
+    own, other = refs[:count], refs[count : 2 * count]
+    stack_ref, near_ref = refs[-2:]
+    depth, side = 2 * CAP, LEAD // count
+    for q in range(count):
+        stack_ref[q * depth : q * depth + CAP, :] = own[q][:CAP, :]
+        stack_ref[q * depth + CAP : (q + 1) * depth, :] = other[q][...]
+        begin = pl.multiple_of(places_ref[PLACES + q] * side, side)
+        near_ref[pl.ds(begin, side), :] = own[q][CAP:, :]
+
+
+def stacked(places, own, other, earlier):
+    count = len(own)
+    rows, width = own[0].shape
+    cols = COLS if width % COLS == 0 else ROWS
+    tiled = lambda height: pl.BlockSpec((height, cols), lambda j: (0, j))
+    return pl.pallas_call(
+        lambda *refs: stack_kernel(count, *refs),
+        grid=(width // cols,),
+        out_shape=(
+            jax.ShapeDtypeStruct((2 * CAP * count, width), BF16),
+            jax.ShapeDtypeStruct((LEAD, width), BF16),
+        ),
+        in_specs=[pl.BlockSpec(memory_space=pltpu.SMEM)]
+        + [tiled(rows)] * count
+        + [tiled(CAP)] * count
+        + [ANYWHERE] * len(earlier),
+        out_specs=(tiled(2 * CAP * count), tiled(LEAD)),
+        compiler_params=pltpu.CompilerParams(vmem_limit_bytes=VMEM_BYTES),
+        cost_estimate=NO_COST,
+    )(places, *own, *other, *earlier)
+
+
+def panel_kernel(count, share_ref, inverse_ref, near_ref, across_ref, *refs):
+    lead = refs[:count]
+    out_ref, lead_ref = refs[-2:]
     depth = 2 * CAP
-    for q in range(count):
-        across_ref[q * depth : q * depth + CAP, :] = own[q][:CAP, :]
-        across_ref[q * depth + CAP : (q + 1) * depth, :] = other[q][...]
-        begin = pl.multiple_of(places_ref[PLACES + q] * side, side)
-        near_ref[pl.ds(begin, side), :] = own[q][CAP:, :].astype(F32)
 
     @pl.when(pl.program_id(0) == 0)
     def _():
@@ -206,15 +219,14 @@
             lead_ref[q * depth : (q + 1) * depth, :] = lead[q][:depth, :]
 
     gram = dot_t(lead_ref[...], across_ref[...])
-    beside = DECAY * near_ref[...] + share_ref[:1, :1] * gram
+    beside = DECAY * near_ref[...].astype(F32) + share_ref[:1, :1] * gram
     out_ref[...] = dot_split(inverse_ref[...], beside, ((1,), (0,))).astype(BF16)
 
 
-def panel_columns(places, share, inverse, lead, own, other):
+def panel_columns(share, inverse, near, lead, across, earlier):
     count = len(lead)
-    width = own[0].shape[1]
+    tall, width = across.shape
     cols = COLS if width % COLS == 0 else ROWS
-    tall = 2 * CAP * count
     whole = lambda height: pl.BlockSpec((height, LEAD), lambda j: (0, 0))
     tiled = lambda height: pl.BlockSpec((height, cols), lambda j: (0, j))
     return pl.pallas_call(
@@ -223,25 +235,23 @@
         out_shape=(
             jax.ShapeDtypeStruct((LEAD, width), BF16),
             jax.ShapeDtypeStruct((tall, LEAD), BF16),
-            jax.ShapeDtypeStruct((tall, width), BF16),
         ),
         in_specs=[
-            pl.BlockSpec(memory_space=pltpu.SMEM),
             pl.BlockSpec((GROUP, TILE), lambda j: (0, 0)),
             whole(LEAD),
+            tiled(LEAD),
+            tiled(tall),
         ]
         + [whole(lead[0].shape[0])] * count
-        + [tiled(own[0].shape[0])] * count
-        + [tiled(CAP)] * count,
-        out_specs=(tiled(LEAD), whole(tall), tiled(tall)),
-        scratch_shapes=[pltpu.VMEM((LEAD, cols), F32)],
+        + [ANYWHERE] * len(earlier),
+        out_specs=(tiled(LEAD), whole(tall)),
         compiler_params=pltpu.CompilerParams(vmem_limit_bytes=VMEM_BYTES),
         cost_estimate=NO_COST,
-    )(places, share, inverse, *lead, *own, *other)
+    )(share, inverse, near, across, *lead, *earlier)
 
 
 def solve_kernel(flag_ref, inverse_ref, first_ref, second_ref, *refs):
-    high_ref, low_ref, parts_ref = refs
+    high_ref, low_ref, parts_ref = refs[-3:]
 
     @pl.when(pl.program_id(0) == 0)
     def _():
@@ -253,7 +263,7 @@
     high_ref[...], low_ref[...] = split(solved)
 
 
-def solve_lead(flag, inverse, first, second):
+def solve_lead(flag, inverse, first, second, earlier):
     tiled = pl.BlockSpec((LEAD, COLS), lambda j: (0, j))
     return pl.pallas_call(
         solve_kernel,
@@ -264,12 +274,13 @@
             pl.BlockSpec((LEAD, LEAD), lambda j: (0, 0)),
             tiled,
             tiled,
-        ],
+        ]
+        + [ANYWHERE] * len(earlier),
         out_specs=(tiled, tiled),
         scratch_shapes=[pltpu.VMEM((2, LEAD, LEAD), BF16)],
         compiler_params=pltpu.CompilerParams(vmem_limit_bytes=VMEM_BYTES),
         cost_estimate=NO_COST,
-    )(flag, inverse, first, second)
+    )(flag, inverse, first, second, *earlier)
 
 
 def finish_kernel(
@@ -609,21 +620,21 @@
     rows = first_part.shape[0]
     earlier = [across_other[1], *parts[1:]]
     lead = copied([(spread[0], (None, rows, LEAD), [0, 0, 0])], earlier)[0]
+    slots = [member, column, member * width] + order + [member] + [0] * (group - 1)
+    assert len(slots) == PLACES + 2 * group
+    slots = jnp.stack([jnp.int32(slot) for slot in slots])
+    across, near_factor = stacked(slots, across_own, across_other, [lead])
     lead = gather_members(lead, bits)
     grad_cols = weight_grad.shape[1]
     requests = member_blocks(spread[0], member, group)
     requests += [(weight_grad, (LEAD, grad_cols), [0, 0])]
-    *sent, near = copied(requests, [lead[1]])
-
-    slots = [member, column, member * width] + order + [member] + [0] * (group - 1)
-    assert len(slots) == PLACES + 2 * group
-    slots = jnp.stack([jnp.int32(slot) for slot in slots])
-    lower, inverse, share = factor_lead(
-        slots, damp, factor_old[:LEAD, :LEAD], lead, sent[:1]
-    )
-    panel, lead_stack, across_stack = panel_columns(
-        slots, share, inverse, lead, across_own, across_other
-    )
+    *sent, near = copied(requests, [lead[1], across])
+
+    lower, inverse, share = factor_lead(slots, damp, factor_old, lead, sent[:1])
+    panel, lead_stack = panel_columns(
+        share, inverse, near_factor, lead, across, spread[1:2]
+    )
+
     token = panel
     results = []
     for number, (begin, _) in enumerate(chunks):
@@ -637,7 +648,7 @@
                 flag = (member >> bit & 1)[None]
                 if bit:
                     near = chosen(flag, moved, near, sent[:1])
-            high, low = solve_lead(flag, inverse, moved, near)
+            high, low = solve_lead(flag, inverse, moved, near, spread[2:3])
         *results, token = finish_rows(
             begin,
             slots,
@@ -651,7 +662,7 @@
             high,
             low,
             lead_stack,
-            across_stack,
+            across,
             pieces,
             results,
             sent[:1],

time: 318 us -> 318 us (level)
  Pallas kernels: 154 us -> 161 us
  local copies, waits for them, and re-layouts: 18.2 us -> 14.3 us
    pallas_call x1 -> x2, Pallas kernels: 32.1 us -> 40 us  [the longest x1 31.5 us: factor_lead(): pl.pallas_call(lambda *refs: factor_kernel(len(lead), *refs), grid=(1,),...]
    unnamed x63 -> x57, local copies, waits for them, and re-layouts: 11.6 us -> 10.8 us
  transfers between devices with their start and end apart: 35 -> 35, of which waited for: 14 -> 14; matrix products, arithmetic and copies ran while one was open for 4% -> 4% of each run, Pallas kernels for 43% -> 45%
where the time goes in v9:
time: 318 us; the launch traced here: 316 us
  Pallas kernels  161 us (51%)
  waiting for transfers between devices  86.5 us (27%)
  starting transfers between devices  24.6 us (8%)
  between operations  20.8 us (7%)
  local copies, waits for them, and re-layouts  14.3 us (4%)
  other arithmetic  7.51 us (2%)
    ppermute x27, waiting for transfers between devices, swapped(): lax.ppermute(value, 'tok', [(source, source ^ mask) for source in range(s...  78.8 us
    pallas_call x4, Pallas kernels, finish_rows(): pl.pallas_call(lambda *refs: finish_kernel(count, gram_steps, begin, unre...  66.8 us
    pallas_call x9, Pallas kernels, copied(): pl.pallas_call(lambda *refs: copy_kernel(len(arrays), *refs), grid_spec=p...  31.6 us
    pallas_call x1, Pallas kernels, factor_lead(): pl.pallas_call(lambda *refs: factor_kernel(len(lead), *refs), grid=(1,),...  31.5 us
    ppermute x27, starting transfers between devices, swapped(): lax.ppermute(value, 'tok', [(source, source ^ mask) for source in range(s...  17.9 us
    pallas_call x1, Pallas kernels, panel_columns(): pl.pallas_call(lambda *refs: panel_kernel(count, *refs), grid=(width // c...  12.1 us
    unnamed x57, local copies, waits for them, and re-layouts  10.8 us
    pallas_call x1, Pallas kernels, stacked(): pl.pallas_call(lambda *refs: stack_kernel(count, *refs), grid=(width // c...  8.45 us
  transfers between devices with their start and end apart: 35, of which 14 were waited for; matrix products, arithmetic and copies ran while one was open for 4% of the time, Pallas kernels for 45%

profile of v9, /device:TPU:2, one launch (start us, length us, event | category | flops | bytes accessed | tf_op | source)
XLA Modules:
  0.0 315.6 jit_solution(14515342701159852452)
XLA Ops:
  7.2 3.9 %shard_map.85 = (bf16[256,1536]{1,0:T(8,128)(2,1)}, bf16[256,1536]{1,0:T(8,128)(2,1)}) custom-call(s32[4]{0:T(128)} %constant.91.clone.1.refs_0_, f32[1536,1536]{1,0:T(8,128)} %refs_3_.7, f32[1536,1536]{1,0:T(8,128)} %refs_3_.7), custom_call_target="tpu_custom_call" | custom-call | flops 1 | bytes 1 | tf_op jit(solution)/shard_map/pallas_call | solution.py:477
  34.5 2.9 shard_map.86
  38.9 21.9 %collective-permute-done.3.refs_5_ = bf16[320,1536]{1,0:T(8,128)(2,1)S(1)} collective-permute-done((bf16[320,1536]{1,0:T(8,128)(2,1)}, bf16[320,1536]{1,0:T(8,128)(2,1)S(1)}, u32[]{:S(2)}, u32[]{:S(2)}) %collective-permute-start.3) | collective-permute-done | bytes 983072 | tf_op jit(solution)/shard_map/ppermute | solution.py:450
  66.5 3.3 %shard_map.87 = (bf16[768,512]{1,0:T(8,128)(2,1)}, bf16[768,256]{1,0:T(8,128)(2,1)}, bf16[768,256]{1,0:T(8,128)(2,1)}) custom-call(s32[6]{0:T(128)} %constant.93.clone.1.refs_0_, bf16[768,1536]{1,0:T(8,128)(2,1)} %pad_maximum_fusion.refs_1_.refs_2_.refs_3_, bf16[768,1536]{1,0:T(8,128)(2,1)} %pad_maximum_fusion.refs_1_.refs_2_.refs_3_, ...), custom_call_target="tpu_custom_call" | custom-call | flops 1 | bytes 1 | tf_op jit(solution)/shard_map/pallas_call | solution.py:477
  71.7 20.5 %collective-permute-done.4.refs_2_.refs_6_ = bf16[320,1536]{1,0:T(8,128)(2,1)S(1)} collective-permute-done((bf16[320,1536]{1,0:T(8,128)(2,1)S(1)}, bf16[320,1536]{1,0:T(8,128)(2,1)S(1)}, u32[]{:S(2)}, u32[]{:S(2)}) %collective-permute-start.4) | collective-permute-done | bytes 983072 | tf_op jit(solution)/shard_map/ppermute | solution.py:450
  92.2 6.2 %all-gather.9.cloned.1.call-done = bf16[3136,512]{1,0:T(8,128)(2,1)} async-done(((bf16[784,512]{1,0:T(8,128)(2,1)}), bf16[3136,512]{1,0:T(8,128)(2,1)}) %all-gather.9.cloned.1.call-update) | async-done | bytes 3211280 | tf_op jit(solution)/shard_map/all_gather | solution.py:619
  103.6 8.5 %shard_map.89 = (bf16[2560,1536]{1,0:T(8,128)(2,1)}, bf16[512,1536]{1,0:T(8,128)(2,1)}) custom-call(s32[11]{0:T(128)} %stack.26.refs_0_, bf16[448,1536]{1,0:T(8,128)(2,1)} %pad_maximum_fusion.1.refs_1_, bf16[448,1536]{1,0:T(8,128)(2,1)} %copy-done.5, bf16[448,1536]{1,0:T(8,128)(2,1)} %collective-permute-done.9.refs_3_, ...), custom_call_target="tpu_custom_call" | custom-call | flops 1 | bytes 1 | tf_op jit(solution)/shard_map/pallas_call | solution.py:194
  112.1 9.4 %collective-permute-done.6.refs_5_.refs_4_ = bf16[784,512]{1,0:T(8,128)(2,1)S(1)} collective-permute-done((bf16[784,512]{1,0:T(8,128)(2,1)}, bf16[784,512]{1,0:T(8,128)(2,1)S(1)}, u32[]{:S(2)}, u32[]{:S(2)}) %collective-permute-start.6) | collective-permute-done | bytes 802848 | tf_op jit(solution)/shard_map/ppermute | solution.py:450
  122.4 5.3 %shard_map.90 = (bf16[784,512]{1,0:T(8,128)(2,1)}, bf16[784,512]{1,0:T(8,128)(2,1)}, bf16[784,512]{1,0:T(8,128)(2,1)}, bf16[512,2048]{1,0:T(8,128)(2,1)}) custom-call(s32[11]{0:T(128)} %stack.57.refs_0_, bf16[4,784,512]{2,1,0:T(8,128)(2,1)} %bitcast.55, bf16[4,784,512]{2,1,0:T(8,128)(2,1)} %bitcast.56, bf16[4,784,512]{2,1,0:T(8,128)(2,1)} %bitcast.57, ...), custom_call_target="tpu_custom_call" | custom-call | flops 1 | bytes 1 | tf_op jit(solution)/shard_map/pallas_call | solution.py:477
  129.6 4.0 %collective-permute-start.14 = (bf16[784,512]{1,0:T(8,128)(2,1)}, bf16[784,512]{1,0:T(8,128)(2,1)}, u32[]{:S(2)}, u32[]{:S(2)}) collective-permute-start(bf16[784,512]{1,0:T(8,128)(2,1)} %get-tuple-element.60), channel_id=1, source_target_pairs={{0,8},{4,12},{8,0},{12,4},{16,24},{20,28},{24,16},{28,20},{1,9},{5... | collective-permute-start | bytes 2408456 | tf_op jit(solution)/shard_map/ppermute | solution.py:450
  136.2 31.5 %shard_map.91 = (f32[512,512]{1,0:T(8,128)}, f32[512,512]{1,0:T(8,128)}, f32[8,128]{1,0:T(8,128)}) custom-call(s32[11]{0:T(128)} %stack.26.refs_0_, f32[1]{0:T(128)} %bitcast.8.refs_1_, f32[1536,1536]{1,0:T(8,128)} %refs_3_.7, bf16[784,512]{1,0:T(8,128)(2,1)} %shard_map.88.refs_9_.refs_3_.refs_4_, bf16[784,512]{1,0:T(8,128)(2,1)} %copy-done.3, ...), custom_call_target="tpu_custom_call" | custom-call | flops 1 | bytes 1 | tf_op jit(solution)/shard_map/pallas_call | solution.py:164
  167.8 12.1 %shard_map.92 = (bf16[512,1536]{1,0:T(8,128)(2,1)}, bf16[2560,512]{1,0:T(8,128)(2,1)}) custom-call(f32[8,128]{1,0:T(8,128)} %get-tuple-element.55.refs_0_.refs_2_, f32[512,512]{1,0:T(8,128)} %get-tuple-element.56.refs_1_.inverse_ref.refs_6_, bf16[512,1536]{1,0:T(8,128)(2,1)} %get-tuple-element.57.refs_2_, ...), custom_call_target="tpu_custom_call" | custom-call | flops 1 | bytes 1 | tf_op jit(solution)/shard_map/pallas_call | solution.py:232
  181.7 8.5 %collective-permute-done.15.refs_6_ = bf16[784,512]{1,0:T(8,128)(2,1)S(1)} collective-permute-done((bf16[784,512]{1,0:T(8,128)(2,1)}, bf16[784,512]{1,0:T(8,128)(2,1)S(1)}, u32[]{:S(2)}, u32[]{:S(2)}) %collective-permute-start.15) | collective-permute-done | bytes 802848 | tf_op jit(solution)/shard_map/ppermute | solution.py:450
  191.1 4.2 %shard_map.93 = (bf16[768,512]{1,0:T(8,128)(2,1)}, bf16[768,512]{1,0:T(8,128)(2,1)}, bf16[768,512]{1,0:T(8,128)(2,1)}, bf16[784,512]{1,0:T(8,128)(2,1)}) custom-call(s32[11]{0:T(128)} %stack.57.refs_0_, bf16[4,768,512]{2,1,0:T(8,128)(2,1)} %bitcast.60, bf16[4,768,512]{2,1,0:T(8,128)(2,1)} %bitcast.61, bf16[4,768,512]{2,1,0:T(8,128)(2,1)} %bitcast.62, ...), custom_call_target="tpu_custom_call" | custom-call | flops 1 | bytes 1 | tf_op jit(solution)/shard_map/pallas_call | solution.py:477
  195.4 3.3 %shard_map.94.second_ref = bf16[512,2048]{1,0:T(8,128)(2,1)} custom-call(s32[1]{0:T(128)} %bitcast.19.flag_ref, bf16[512,2048]{1,0:T(8,128)(2,1)} %collective-permute-done.13.first_ref, bf16[512,2048]{1,0:T(8,128)(2,1)} %get-tuple-element.59.second_ref, bf16[768,512]{1,0:T(8,128)(2,1)} %get-tuple-element.62.refs_0_.refs_16_), custom_call_target="tpu_custom_call" | custom-call | flops 1 | bytes 1 | tf_op jit(solution)/shard_map/pallas_call | solution.py:497
  204.5 6.8 %shard_map.95 = (bf16[512,2048]{1,0:T(8,128)(2,1)}, bf16[512,2048]{1,0:T(8,128)(2,1)}) custom-call(s32[1]{0:T(128)} %bitcast.18.flag_ref, f32[512,512]{1,0:T(8,128)} %get-tuple-element.56.refs_1_.inverse_ref.refs_6_, bf16[512,2048]{1,0:T(8,128)(2,1)} %collective-permute-done.16.first_ref, bf16[512,2048]{1,0:T(8,128)(2,1)} %shard_map.94.second_ref, ...), custom_call_target="tpu_custom_call" | custom-call | flops 1 | bytes 1 | tf_op jit(solution)/shard_map/pallas_call | solution.py:268
  212.5 20.8 %shard_map.96 = (f32[1536,1536]{1,0:T(8,128)}, f32[1536,1536]{1,0:T(8,128)}, f32[1536,2048]{1,0:T(8,128)}, f32[8,128]{1,0:T(8,128)}) custom-call(s32[11]{0:T(128)} %stack.26.refs_0_, f32[1]{0:T(128)} %bitcast.8.refs_1_, f32[8,128]{1,0:T(8,128)} %get-tuple-element.55.refs_0_.refs_2_, f32[1536,1536]{1,0:T(8,128)} %refs_3_.7, bf16[1536,2048]{1,0:T(8,128)(2,1)} %refs_4_.9, ...), custom_call_target="tpu_custom_call" | custom-call | flops 1 | bytes 1 | tf_op jit(solution)/shard_map/pallas_call | solution.py:423
  233.4 5.2 %collective-permute-done.20.refs_6_ = bf16[768,512]{1,0:T(8,128)(2,1)S(1)} collective-permute-done((bf16[768,512]{1,0:T(8,128)(2,1)}, bf16[768,512]{1,0:T(8,128)(2,1)S(1)}, u32[]{:S(2)}, u32[]{:S(2)}) %collective-permute-start.20) | collective-permute-done | bytes 786464 | tf_op jit(solution)/shard_map/ppermute | solution.py:450
  239.4 3.5 %shard_map.97 = (bf16[768,256]{1,0:T(8,128)(2,1)}, bf16[768,256]{1,0:T(8,128)(2,1)}, bf16[768,256]{1,0:T(8,128)(2,1)}, bf16[768,512]{1,0:T(8,128)(2,1)}) custom-call(s32[11]{0:T(128)} %stack.57.refs_0_, bf16[4,768,256]{2,1,0:T(8,128)(2,1)} %bitcast.65, bf16[4,768,256]{2,1,0:T(8,128)(2,1)} %bitcast.66, bf16[4,768,256]{2,1,0:T(8,128)(2,1)} %bitcast.67, ...), custom_call_target="tpu_custom_call" | custom-call | flops 1 | bytes 1 | tf_op jit(solution)/shard_map/pallas_call | solution.py:477
  246.3 18.9 %shard_map.98 = (f32[1536,1536]{1,0:T(8,128)}, f32[1536,1536]{1,0:T(8,128)}, f32[1536,2048]{1,0:T(8,128)}, f32[8,128]{1,0:T(8,128)}) custom-call(s32[11]{0:T(128)} %stack.26.refs_0_, f32[1]{0:T(128)} %bitcast.8.refs_1_, f32[8,128]{1,0:T(8,128)} %get-tuple-element.55.refs_0_.refs_2_, ...), custom_call_target="tpu_custom_call", output_to_operand_aliasing={{0}: (14, {}), {1}: (15, {}), {2}: (16, {})} | custom-call | flops 1 | bytes 1 | tf_op jit(solution)/shard_map/pallas_call | solution.py:423
  266.1 3.2 %shard_map.99 = (bf16[768,256]{1,0:T(8,128)(2,1)}, bf16[768,256]{1,0:T(8,128)(2,1)}, bf16[768,256]{1,0:T(8,128)(2,1)}, bf16[768,256]{1,0:T(8,128)(2,1)}) custom-call(s32[11]{0:T(128)} %stack.57.refs_0_, bf16[4,768,256]{2,1,0:T(8,128)(2,1)} %bitcast.69, bf16[4,768,256]{2,1,0:T(8,128)(2,1)} %bitcast.70, bf16[4,768,256]{2,1,0:T(8,128)(2,1)} %bitcast.71, ...), custom_call_target="tpu_custom_call" | custom-call | flops 1 | bytes 1 | tf_op jit(solution)/shard_map/pallas_call | solution.py:477
  272.5 13.5 %shard_map.100 = (f32[1536,1536]{1,0:T(8,128)}, f32[1536,1536]{1,0:T(8,128)}, f32[1536,2048]{1,0:T(8,128)}, f32[8,128]{1,0:T(8,128)}) custom-call(s32[11]{0:T(128)} %stack.26.refs_0_, f32[1]{0:T(128)} %bitcast.8.refs_1_, f32[8,128]{1,0:T(8,128)} %get-tuple-element.55.refs_0_.refs_2_, ...), custom_call_target="tpu_custom_call", output_to_operand_aliasing={{0}: (14, {}), {1}: (15, {}), {2}: (16, {})} | custom-call | flops 1 | bytes 1 | tf_op jit(solution)/shard_map/pallas_call | solution.py:423
  286.0 3.5 %collective-permute-done.27.refs_1_ = bf16[768,256]{1,0:T(8,128)(2,1)S(1)} collective-permute-done((bf16[768,256]{1,0:T(8,128)(2,1)}, bf16[768,256]{1,0:T(8,128)(2,1)S(1)}, u32[]{:S(2)}, u32[]{:S(2)}) %collective-permute-start.27) | collective-permute-done | bytes 393248 | tf_op jit(solution)/shard_map/ppermute | solution.py:450
  295.4 13.6 %shard_map.102 = (f32[1536,1536]{1,0:T(8,128)}, f32[1536,1536]{1,0:T(8,128)}, f32[1536,2048]{1,0:T(8,128)}, f32[8,128]{1,0:T(8,128)}) custom-call(s32[11]{0:T(128)} %stack.26.refs_0_, f32[1]{0:T(128)} %bitcast.8.refs_1_, f32[8,128]{1,0:T(8,128)} %get-tuple-element.55.refs_0_.refs_2_, ...), custom_call_target="tpu_custom_call", output_to_operand_aliasing={{0}: (14, {}), {1}: (15, {}), {2}: (16, {})} | custom-call | flops 1 | bytes 1 | tf_op jit(solution)/shard_map/pallas_call | solution.py:423
  (162 shorter events, 60.2 us)
Async XLA Ops:
  7.2 91.2 %all-gather.9.cloned.1.call-start = ((), (), s32[]{:S(2)}) async-start(), calls=%async_computation | async-start | bytes 4014080 | tf_op jit(solution)/shard_map/all_gather | solution.py:619
  11.1 14.2 %collective-permute-start.1 = (bf16[256,1536]{1,0:T(8,128)(2,1)}, bf16[256,1536]{1,0:T(8,128)(2,1)}, u32[]{:S(2)}, u32[]{:S(2)}) collective-permute-start(bf16[256,1536]{1,0:T(8,128)(2,1)} %get-tuple-element.48), channel_id=1, source_target_pairs={{0,8},{16,24},{1,9},{17,25},{2,10},{18,26},{3,11},{19,27}} | collective-permute-start | bytes 2359304 | tf_op jit(solution)/shard_map/ppermute | solution.py:554
  32.4 135.3 %all-gather.11.cloned.1.call-start = ((), (), s32[]{:S(2)}) async-start(), calls=%async_computation.1 | async-start | bytes 3932160 | tf_op jit(solution)/shard_map/all_gather | solution.py:619
  33.7 31.6 %collective-permute-start.5 = (bf16[448,1536]{1,0:T(8,128)(2,1)}, bf16[448,1536]{1,0:T(8,128)(2,1)S(1)}, u32[]{:S(2)}, u32[]{:S(2)}) collective-permute-start(bf16[448,1536]{1,0:T(8,128)(2,1)} %pad_maximum_fusion.1.refs_1_), channel_id=1, source_target_pairs={{0,8},{4,12},{8,0},{12,4},{16,24},{20,28},{24,16},{28,20},{1,9},{5... | collective-permute-start | bytes 4128776 | tf_op jit(solution)/shard_map/ppermute | solution.py:450
  37.3 23.4 %collective-permute-start.3 = (bf16[320,1536]{1,0:T(8,128)(2,1)}, bf16[320,1536]{1,0:T(8,128)(2,1)S(1)}, u32[]{:S(2)}, u32[]{:S(2)}) collective-permute-start(bf16[320,1536]{1,0:T(8,128)(2,1)} %shard_map.86), channel_id=1, source_target_pairs={{0,16},{4,20},{8,24},{12,28},{16,0},{20,4},{24,8},{28,12},{1,17},{... | collective-permute-start | bytes 2949128 | tf_op jit(solution)/shard_map/ppermute | solution.py:450
  69.8 134.6 %all-gather.13.cloned.1.call-start = ((), (), s32[]{:S(2)}) async-start(), calls=%async_computation.2 | async-start | bytes 1966080 | tf_op jit(solution)/shard_map/all_gather | solution.py:619
  69.9 22.3 %collective-permute-start.4 = (bf16[320,1536]{1,0:T(8,128)(2,1)S(1)}, bf16[320,1536]{1,0:T(8,128)(2,1)S(1)}, u32[]{:S(2)}, u32[]{:S(2)}) collective-permute-start(bf16[320,1536]{1,0:T(8,128)(2,1)S(1)} %copy-done.7), channel_id=1, source_target_pairs={{0,8},{4,12},{8,0},{12,4},{16,24},{20,28},{24,16},{28,20},{1,9},{5... | collective-permute-start | bytes 2949128 | tf_op jit(solution)/shard_map/ppermute | solution.py:450
  71.2 32.4 %collective-permute-start.9 = (bf16[448,1536]{1,0:T(8,128)(2,1)}, bf16[448,1536]{1,0:T(8,128)(2,1)}, u32[]{:S(2)}, u32[]{:S(2)}) collective-permute-start(bf16[448,1536]{1,0:T(8,128)(2,1)} %pad_maximum_fusion.1.refs_1_), channel_id=1, source_target_pairs={{0,4},{4,0},{8,12},{12,8},{16,20},{20,16},{24,28},{28,24},{1,5},{5... | collective-permute-start | bytes 4128776 | tf_op jit(solution)/shard_map/ppermute | solution.py:450
  71.2 32.4 %collective-permute-start.10 = (bf16[448,1536]{1,0:T(8,128)(2,1)}, bf16[448,1536]{1,0:T(8,128)(2,1)}, u32[]{:S(2)}, u32[]{:S(2)}) collective-permute-start(bf16[448,1536]{1,0:T(8,128)(2,1)} %copy-done.5), channel_id=1, source_target_pairs={{0,4},{4,0},{8,12},{12,8},{16,20},{20,16},{24,28},{28,24},{1,5},{5... | collective-permute-start | bytes 4128776 | tf_op jit(solution)/shard_map/ppermute | solution.py:450
  71.7 31.9 %collective-permute-start.11 = (bf16[320,1536]{1,0:T(8,128)(2,1)S(1)}, bf16[320,1536]{1,0:T(8,128)(2,1)}, u32[]{:S(2)}, u32[]{:S(2)}) collective-permute-start(bf16[320,1536]{1,0:T(8,128)(2,1)S(1)} %copy-done.7), channel_id=1, source_target_pairs={{0,4},{4,0},{8,12},{12,8},{16,20},{20,16},{24,28},{28,24},{1,5},{5... | collective-permute-start | bytes 2949128 | tf_op jit(solution)/shard_map/ppermute | solution.py:450
  101.7 19.8 %collective-permute-start.6 = (bf16[784,512]{1,0:T(8,128)(2,1)}, bf16[784,512]{1,0:T(8,128)(2,1)S(1)}, u32[]{:S(2)}, u32[]{:S(2)}) collective-permute-start(bf16[784,512]{1,0:T(8,128)(2,1)} %shard_map.88.refs_9_.refs_3_.refs_4_), channel_id=1, source_target_pairs={{0,8},{4,12},{8,0},{12,4},{16,24},{20,28},{24,16},{28,20},{1,9},{5... | collective-permute-start | bytes 2408456 | tf_op jit(solution)/shard_map/ppermute | solution.py:450
  127.7 67.7 %collective-permute-start.13 = (bf16[512,2048]{1,0:T(8,128)(2,1)}, bf16[512,2048]{1,0:T(8,128)(2,1)}, u32[]{:S(2)}, u32[]{:S(2)}) collective-permute-start(bf16[512,2048]{1,0:T(8,128)(2,1)} %get-tuple-element.59.second_ref), channel_id=1, source_target_pairs={{0,8},{16,24},{1,9},{17,25},{2,10},{18,26},{3,11},{19,27}} | collective-permute-start | bytes 6291464 | tf_op jit(solution)/shard_map/ppermute | solution.py:647
  129.0 136.2 %all-gather.15.cloned.1.call-start = ((), (), s32[]{:S(2)}) async-start(), calls=%async_computation.3 | async-start | bytes 1966080 | tf_op jit(solution)/shard_map/all_gather | solution.py:619
  129.6 52.1 %collective-permute-start.14 = (bf16[784,512]{1,0:T(8,128)(2,1)}, bf16[784,512]{1,0:T(8,128)(2,1)}, u32[]{:S(2)}, u32[]{:S(2)}) collective-permute-start(bf16[784,512]{1,0:T(8,128)(2,1)} %get-tuple-element.60), channel_id=1, source_target_pairs={{0,8},{4,12},{8,0},{12,4},{16,24},{20,28},{24,16},{28,20},{1,9},{5... | collective-permute-start | bytes 2408456 | tf_op jit(solution)/shard_map/ppermute | solution.py:450
  133.6 56.6 %collective-permute-start.15 = (bf16[784,512]{1,0:T(8,128)(2,1)}, bf16[784,512]{1,0:T(8,128)(2,1)S(1)}, u32[]{:S(2)}, u32[]{:S(2)}) collective-permute-start(bf16[784,512]{1,0:T(8,128)(2,1)} %get-tuple-element.61), channel_id=1, source_target_pairs={{0,8},{4,12},{8,0},{12,4},{16,24},{20,28},{24,16},{28,20},{1,9},{5... | collective-permute-start | bytes 2408456 | tf_op jit(solution)/shard_map/ppermute | solution.py:450
  202.0 31.4 %collective-permute-start.17 = (bf16[768,512]{1,0:T(8,128)(2,1)}, bf16[768,512]{1,0:T(8,128)(2,1)}, u32[]{:S(2)}, u32[]{:S(2)}) collective-permute-start(bf16[768,512]{1,0:T(8,128)(2,1)} %get-tuple-element.65), channel_id=1, source_target_pairs={{0,8},{4,12},{8,0},{12,4},{16,24},{20,28},{24,16},{28,20},{1,9},{5... | collective-permute-start | bytes 2359304 | tf_op jit(solution)/shard_map/ppermute | solution.py:450
  202.0 36.6 %collective-permute-start.20 = (bf16[768,512]{1,0:T(8,128)(2,1)}, bf16[768,512]{1,0:T(8,128)(2,1)S(1)}, u32[]{:S(2)}, u32[]{:S(2)}) collective-permute-start(bf16[768,512]{1,0:T(8,128)(2,1)} %get-tuple-element.70), channel_id=1, source_target_pairs={{0,8},{4,12},{8,0},{12,4},{16,24},{20,28},{24,16},{28,20},{1,9},{5... | collective-permute-start | bytes 2359304 | tf_op jit(solution)/shard_map/ppermute | solution.py:450
  204.1 40.9 %collective-permute-start.22 = (bf16[768,512]{1,0:T(8,128)(2,1)S(1)}, bf16[768,512]{1,0:T(8,128)(2,1)}, u32[]{:S(2)}, u32[]{:S(2)}) collective-permute-start(bf16[768,512]{1,0:T(8,128)(2,1)S(1)} %copy-done.12), channel_id=1, source_target_pairs={{0,4},{4,0},{8,12},{12,8},{16,20},{20,16},{24,28},{28,24},{1,5},{5... | collective-permute-start | bytes 2359304 | tf_op jit(solution)/shard_map/ppermute | solution.py:450
  242.9 22.3 %collective-permute-start.21 = (bf16[768,256]{1,0:T(8,128)(2,1)}, bf16[768,256]{1,0:T(8,128)(2,1)S(1)}, u32[]{:S(2)}, u32[]{:S(2)}) collective-permute-start(bf16[768,256]{1,0:T(8,128)(2,1)} %get-tuple-element.71), channel_id=1, source_target_pairs={{0,8},{4,12},{8,0},{12,4},{16,24},{20,28},{24,16},{28,20},{1,9},{5... | collective-permute-start | bytes 1179656 | tf_op jit(solution)/shard_map/ppermute | solution.py:450
  243.2 22.1 %collective-permute-start.24 = (bf16[768,256]{1,0:T(8,128)(2,1)}, bf16[768,256]{1,0:T(8,128)(2,1)S(1)}, u32[]{:S(2)}, u32[]{:S(2)}) collective-permute-start(bf16[768,256]{1,0:T(8,128)(2,1)} %get-tuple-element.78), channel_id=1, source_target_pairs={{0,8},{4,12},{8,0},{12,4},{16,24},{20,28},{24,16},{28,20},{1,9},{5... | collective-permute-start | bytes 1179656 | tf_op jit(solution)/shard_map/ppermute | solution.py:450
  244.9 26.6 %collective-permute-start.28 = (bf16[768,256]{1,0:T(8,128)(2,1)}, bf16[768,256]{1,0:T(8,128)(2,1)S(1)}, u32[]{:S(2)}, u32[]{:S(2)}) collective-permute-start(bf16[768,256]{1,0:T(8,128)(2,1)} %get-tuple-element.76.refs_17_), channel_id=1, source_target_pairs={{0,4},{4,0},{8,12},{12,8},{16,20},{20,16},{24,28},{28,24},{1,5},{5... | collective-permute-start | bytes 1179656 | tf_op jit(solution)/shard_map/ppermute | solution.py:450
  269.5 16.5 %collective-permute-start.25 = (bf16[768,256]{1,0:T(8,128)(2,1)}, bf16[768,256]{1,0:T(8,128)(2,1)S(1)}, u32[]{:S(2)}, u32[]{:S(2)}) collective-permute-start(bf16[768,256]{1,0:T(8,128)(2,1)} %get-tuple-element.79), channel_id=1, source_target_pairs={{0,8},{4,12},{8,0},{12,4},{16,24},{20,28},{24,16},{28,20},{1,9},{5... | collective-permute-start | bytes 1179656 | tf_op jit(solution)/shard_map/ppermute | solution.py:450
  269.8 19.7 %collective-permute-start.27 = (bf16[768,256]{1,0:T(8,128)(2,1)}, bf16[768,256]{1,0:T(8,128)(2,1)S(1)}, u32[]{:S(2)}, u32[]{:S(2)}) collective-permute-start(bf16[768,256]{1,0:T(8,128)(2,1)} %get-tuple-element.81), channel_id=1, source_target_pairs={{0,8},{4,12},{8,0},{12,4},{16,24},{20,28},{24,16},{28,20},{1,9},{5... | collective-permute-start | bytes 1179656 | tf_op jit(solution)/shard_map/ppermute | solution.py:450
  271.6 21.2 %collective-permute-start.26 = (bf16[768,256]{1,0:T(8,128)(2,1)}, bf16[768,256]{1,0:T(8,128)(2,1)S(1)}, u32[]{:S(2)}, u32[]{:S(2)}) collective-permute-start(bf16[768,256]{1,0:T(8,128)(2,1)} %get-tuple-element.80.refs_17_), channel_id=1, source_target_pairs={{0,4},{4,0},{8,12},{12,8},{16,20},{20,16},{24,28},{28,24},{1,5},{5... | collective-permute-start | bytes 1179656 | tf_op jit(solution)/shard_map/ppermute | solution.py:450
  (39 other events, 181.5 us)
Sparse Core Ops, SparseCore 0:
  32.6 65.8 all-gather.8
  100.0 62.1 all-gather.10
  163.7 35.7 all-gather.12
  201.5 35.9 all-gather.14

commit v10 on v9

--- a/solution.py
+++ b/solution.py
@@ -64,6 +64,9 @@
             [splat(first[t], base + u) if u >= t else None for u in range(GROUP)]
             for t in range(GROUP)
         ]
+        coming = rows[step + 1] if step + 1 < TILE // GROUP else block
+        factors = [splat(coming, base + u) for u in range(GROUP)]
+        coming = jnp.where(inside, 0.0, coming)
         scale = [None] * GROUP
         for t in range(GROUP):
             scale[t] = lax.rsqrt(pivot[t][t])
@@ -74,16 +77,21 @@
                     pivot[u][w] = pivot[u][w] - pivot[t][u] * pivot[t][w]
             first[t] = first[t] * scale[t]
             second[t] = second[t] * scale[t]
+            factors[t] = factors[t] * scale[t]
+            coming = coming - factors[t] * second[t]
             for u in range(t + 1, GROUP):
                 first[u] = first[u] - pivot[t][u] * first[t]
                 second[u] = second[u] - pivot[t][u] * second[t]
+                factors[u] = factors[u] - pivot[t][u] * factors[t]
         solved = [None] * GROUP
         for t in reversed(range(GROUP)):
             value = second[t]
             for u in range(t + 1, GROUP):
                 value = value - pivot[t][u] * solved[u]
             solved[t] = value * scale[t]
-        for later in range(step + 1, TILE // GROUP):
+        if step + 1 < TILE // GROUP:
+            rows[step + 1] = coming
+        for later in range(step + 2, TILE // GROUP):
             value = jnp.where(inside, 0.0, rows[later])
             for t in range(GROUP):
                 value = value - splat(rows[later], base + t) * solved[t]
@@ -577,7 +585,11 @@
 
     side = LEAD // 2
     halves = [(factor_old, (side, width), [place, 0]) for place in range(2)]
-    lead_factor = share_of_first(*copied(halves, []), member, group, bits)
+    halves = copied(halves, [])
+    lead_factor = share_of_first(*halves, member, group, bits)
+
+    near = copied([(weight_grad, (LEAD, weight_grad.shape[1]), [0, 0])], halves[:1])[0]
+    moved = lax.ppermute(near, "tok", down_pairs(bits - 1, group))
 
     live = jnp.arange(tok_rows) < counts[0]
     named = routes[:, 0]
@@ -602,7 +614,7 @@
         ],
         0,
     )
-    away_rows = copied([(packed, (CAP, width), [1, 0])], [front])[0]
+    away_rows = copied([(packed, (CAP, width), [1, 0])], [front, moved])[0]
     incoming = swapped(away_rows, group)
     outgoing = jnp.concatenate([packed[:CAP], lead_factor], 0)
     quarter = jnp.concatenate([packed[:CAP], incoming, lead_factor], 0)
@@ -625,10 +637,12 @@
     slots = jnp.stack([jnp.int32(slot) for slot in slots])
     across, near_factor = stacked(slots, across_own, across_other, [lead])
     lead = gather_members(lead, bits)
-    grad_cols = weight_grad.shape[1]
-    requests = member_blocks(spread[0], member, group)
-    requests += [(weight_grad, (LEAD, grad_cols), [0, 0])]
-    *sent, near = copied(requests, [lead[1], across])
+    flag = (member >> (bits - 1) & 1)[None]
+    for bit in reversed(range(bits - 1)):
+        near = chosen(flag, moved, near, [across])
+        moved = lax.ppermute(near, "tok", down_pairs(bit, group))
+        flag = (member >> bit & 1)[None]
+    sent = copied(member_blocks(spread[0], member, group), [lead[1], near])
 
     lower, inverse, share = factor_lead(slots, damp, factor_old, lead, sent[:1])
     panel, lead_stack = panel_columns(
@@ -643,11 +657,6 @@
             requests = member_blocks(spread[number + 1], member, group)
         pieces, sent = exchange_members(spread[number], sent, bits, requests, [token])
         if number == 0:
-            for bit in reversed(range(bits)):
-                moved = lax.ppermute(near, "tok", down_pairs(bit, group))
-                flag = (member >> bit & 1)[None]
-                if bit:
-                    near = chosen(flag, moved, near, sent[:1])
             high, low = solve_lead(flag, inverse, moved, near, spread[2:3])
         *results, token = finish_rows(
             begin,

time: 318 us -> 316 us (level)
    ppermute x0 -> x1, waiting for transfers between devices: none -> 37.7 us  [local(): moved = lax.ppermute(near, 'tok', down_pairs(bits - 1, group))]
    ppermute x27, waiting for transfers between devices: 78.8 us -> 41.5 us  [swapped(): lax.ppermute(value, 'tok', [(source, source ^ mask) for source in range(s...]
    pallas_call x1, Pallas kernels: 31.5 us -> 27.5 us  [factor_lead(): pl.pallas_call(lambda *refs: factor_kernel(len(lead), *refs), grid=(1,),...]
    pallas_call x9 -> x10, Pallas kernels: 31.6 us -> 33.9 us  [copied(): pl.pallas_call(lambda *refs: copy_kernel(len(arrays), *refs), grid_spec=p...]
    unnamed x57 -> x55, local copies, waits for them, and re-layouts: 10.8 us -> 10.1 us
  transfers between devices with their start and end apart: 35 -> 35, of which waited for: 14 -> 11; matrix products, arithmetic and copies ran while one was open for 4% -> 4% of each run, Pallas kernels for 45% -> 45%
where the time goes in v10:
time: 316 us; the launch traced here: 314 us
  Pallas kernels  159 us (50%)
  waiting for transfers between devices  87.6 us (28%)
  starting transfers between devices  23.2 us (7%)
  between operations  21.2 us (7%)
  local copies, waits for them, and re-layouts  16.3 us (5%)
  other arithmetic  5.54 us (2%)
    pallas_call x4, Pallas kernels, finish_rows(): pl.pallas_call(lambda *refs: finish_kernel(count, gram_steps, begin, unre...  67 us
    ppermute x27, waiting for transfers between devices, swapped(): lax.ppermute(value, 'tok', [(source, source ^ mask) for source in range(s...  41.5 us
    ppermute x1, waiting for transfers between devices, local(): moved = lax.ppermute(near, 'tok', down_pairs(bits - 1, group))  37.7 us
    pallas_call x10, Pallas kernels, copied(): pl.pallas_call(lambda *refs: copy_kernel(len(arrays), *refs), grid_spec=p...  33.9 us
    pallas_call x1, Pallas kernels, factor_lead(): pl.pallas_call(lambda *refs: factor_kernel(len(lead), *refs), grid=(1,),...  27.5 us
    ppermute x27, starting transfers between devices, swapped(): lax.ppermute(value, 'tok', [(source, source ^ mask) for source in range(s...  15.8 us
    pallas_call x1, Pallas kernels, panel_columns(): pl.pallas_call(lambda *refs: panel_kernel(count, *refs), grid=(width // c...  11.8 us
    unnamed x55, local copies, waits for them, and re-layouts  10.1 us
  transfers between devices with their start and end apart: 35, of which 11 were waited for; matrix products, arithmetic and copies ran while one was open for 4% of the time, Pallas kernels for 45%

profile of v10, /device:TPU:2, one launch (start us, length us, event | category | flops | bytes accessed | tf_op | source)
XLA Modules:
  0.0 313.9 jit_solution(15549244437489346030)
XLA Ops:
  7.2 3.9 %shard_map.85 = (bf16[256,1536]{1,0:T(8,128)(2,1)}, bf16[256,1536]{1,0:T(8,128)(2,1)}) custom-call(s32[4]{0:T(128)} %constant.91.clone.1.refs_0_, f32[1536,1536]{1,0:T(8,128)} %refs_3_.7, f32[1536,1536]{1,0:T(8,128)} %refs_3_.7), custom_call_target="tpu_custom_call" | custom-call | flops 1 | bytes 1 | tf_op jit(solution)/shard_map/pallas_call | solution.py:485
  26.7 3.2 %collective-permute-done.refs_2_ = bf16[336,512]{1,0:T(8,128)(2,1)S(1)} collective-permute-done((bf16[336,512]{1,0:T(8,128)(2,1)S(1)}, bf16[336,512]{1,0:T(8,128)(2,1)S(1)}, u32[]{:S(2)}, u32[]{:S(2)}) %collective-permute-start) | collective-permute-done | bytes 344096 | tf_op jit(solution)/shard_map/ppermute | solution.py:458
  31.7 3.7 %shard_map.86.second_ref = bf16[512,2048]{1,0:T(8,128)(2,1)} custom-call(s32[2]{0:T(128)} %broadcast_5_refs_0_.2.refs_0_, bf16[1536,2048]{1,0:T(8,128)(2,1)} %refs_4_.7, bf16[256,1536]{1,0:T(8,128)(2,1)} %get-tuple-element.48.refs_2_), custom_call_target="tpu_custom_call" | custom-call | flops 1 | bytes 1 | tf_op jit(solution)/shard_map/pallas_call | solution.py:485
  42.0 37.7 %collective-permute-done.3.refs_3_.first_ref = bf16[512,2048]{1,0:T(8,128)(2,1)S(1)} collective-permute-done((bf16[512,2048]{1,0:T(8,128)(2,1)}, bf16[512,2048]{1,0:T(8,128)(2,1)S(1)}, u32[]{:S(2)}, u32[]{:S(2)}) %collective-permute-start.3) | collective-permute-done | bytes 2097184 | tf_op jit(solution)/shard_map/ppermute | solution.py:592
  85.5 12.7 %collective-permute-done.4.refs_5_ = bf16[320,1536]{1,0:T(8,128)(2,1)S(1)} collective-permute-done((bf16[320,1536]{1,0:T(8,128)(2,1)}, bf16[320,1536]{1,0:T(8,128)(2,1)S(1)}, u32[]{:S(2)}, u32[]{:S(2)}) %collective-permute-start.4) | collective-permute-done | bytes 983072 | tf_op jit(solution)/shard_map/ppermute | solution.py:458
  102.7 3.2 %shard_map.88 = (bf16[768,512]{1,0:T(8,128)(2,1)}, bf16[768,256]{1,0:T(8,128)(2,1)}, bf16[768,256]{1,0:T(8,128)(2,1)}) custom-call(s32[6]{0:T(128)} %constant.93.clone.1.refs_0_, bf16[768,1536]{1,0:T(8,128)(2,1)} %pad_maximum_fusion.refs_1_.refs_2_.refs_3_, bf16[768,1536]{1,0:T(8,128)(2,1)} %pad_maximum_fusion.refs_1_.refs_2_.refs_3_, ...), custom_call_target="tpu_custom_call" | custom-call | flops 1 | bytes 1 | tf_op jit(solution)/shard_map/pallas_call | solution.py:485
  107.4 12.8 %collective-permute-done.5.refs_2_.refs_6_ = bf16[320,1536]{1,0:T(8,128)(2,1)S(1)} collective-permute-done((bf16[320,1536]{1,0:T(8,128)(2,1)S(1)}, bf16[320,1536]{1,0:T(8,128)(2,1)S(1)}, u32[]{:S(2)}, u32[]{:S(2)}) %collective-permute-start.5) | collective-permute-done | bytes 983072 | tf_op jit(solution)/shard_map/ppermute | solution.py:458
  124.7 8.5 %shard_map.90 = (bf16[2560,1536]{1,0:T(8,128)(2,1)}, bf16[512,1536]{1,0:T(8,128)(2,1)}) custom-call(s32[11]{0:T(128)} %stack.56.refs_0_, bf16[448,1536]{1,0:T(8,128)(2,1)} %pad_maximum_fusion.1.refs_1_, bf16[448,1536]{1,0:T(8,128)(2,1)} %collective-permute-done.6.refs_4_.refs_2_, bf16[448,1536]{1,0:T(8,128)(2,1)} %collective-permute-done.10.refs_3_, ...), custom_call_target="tpu_custom_call" | custom-call | flops 1 | bytes 1 | tf_op jit(solution)/shard_map/pallas_call | solution.py:202
  133.2 3.4 %shard_map.91.refs_5_.second_ref = bf16[512,2048]{1,0:T(8,128)(2,1)} custom-call(s32[1]{0:T(128)} %bitcast.17.flag_ref, bf16[512,2048]{1,0:T(8,128)(2,1)} %copy-done.3, bf16[512,2048]{1,0:T(8,128)(2,1)} %shard_map.86.second_ref, bf16[2560,1536]{1,0:T(8,128)(2,1)} %get-tuple-element.52.refs_0_.refs_3_.refs_9_), custom_call_target="tpu_custom_call" | custom-call | flops 1 | bytes 1 | tf_op jit(solution)/shard_map/pallas_call | solution.py:505
  136.6 3.4 %collective-permute-start.14 = (bf16[512,2048]{1,0:T(8,128)(2,1)}, bf16[512,2048]{1,0:T(8,128)(2,1)}, u32[]{:S(2)}, u32[]{:S(2)}) collective-permute-start(bf16[512,2048]{1,0:T(8,128)(2,1)} %shard_map.91.refs_5_.second_ref), channel_id=1, source_target_pairs={{0,4},{8,12},{16,20},{24,28},{1,5},{9,13},{17,21},{25,29},{2,6},{1... | collective-permute-start | bytes 6291464 | tf_op jit(solution)/shard_map/ppermute | solution.py:643
  140.0 4.2 %collective-permute-done.7.refs_4_.refs_5_ = bf16[784,512]{1,0:T(8,128)(2,1)S(1)} collective-permute-done((bf16[784,512]{1,0:T(8,128)(2,1)}, bf16[784,512]{1,0:T(8,128)(2,1)S(1)}, u32[]{:S(2)}, u32[]{:S(2)}) %collective-permute-start.7) | collective-permute-done | bytes 802848 | tf_op jit(solution)/shard_map/ppermute | solution.py:458
  145.1 3.9 %shard_map.92 = (bf16[784,512]{1,0:T(8,128)(2,1)}, bf16[784,512]{1,0:T(8,128)(2,1)}, bf16[784,512]{1,0:T(8,128)(2,1)}) custom-call(s32[9]{0:T(128)} %stack.59.refs_0_, bf16[4,784,512]{2,1,0:T(8,128)(2,1)} %bitcast.55, bf16[4,784,512]{2,1,0:T(8,128)(2,1)} %bitcast.56, bf16[4,784,512]{2,1,0:T(8,128)(2,1)} %bitcast.57, bf16[784,512]{1,0:T(8,128)(2,1)} %copy-done.4, ...), custom_call_target="tpu_custom_call" | custom-call | flops 1 | bytes 1 | tf_op jit(solution)/shard_map/pallas_call | solution.py:485
  153.8 27.5 %shard_map.93 = (f32[512,512]{1,0:T(8,128)}, f32[512,512]{1,0:T(8,128)}, f32[8,128]{1,0:T(8,128)}) custom-call(s32[11]{0:T(128)} %stack.56.refs_0_, f32[1]{0:T(128)} %bitcast.8.refs_1_, f32[1536,1536]{1,0:T(8,128)} %refs_3_.7, bf16[784,512]{1,0:T(8,128)(2,1)} %shard_map.89.refs_9_.refs_3_.refs_4_, bf16[784,512]{1,0:T(8,128)(2,1)} %copy-done.4, ...), custom_call_target="tpu_custom_call" | custom-call | flops 1 | bytes 1 | tf_op jit(solution)/shard_map/pallas_call | solution.py:172
  181.4 11.8 %shard_map.94 = (bf16[512,1536]{1,0:T(8,128)(2,1)}, bf16[2560,512]{1,0:T(8,128)(2,1)}) custom-call(f32[8,128]{1,0:T(8,128)} %get-tuple-element.54.refs_0_.refs_2_, f32[512,512]{1,0:T(8,128)} %get-tuple-element.55.refs_1_.inverse_ref.refs_6_, bf16[512,1536]{1,0:T(8,128)(2,1)} %get-tuple-element.56.refs_2_, ...), custom_call_target="tpu_custom_call" | custom-call | flops 1 | bytes 1 | tf_op jit(solution)/shard_map/pallas_call | solution.py:240
  194.1 4.2 %shard_map.96 = (bf16[768,512]{1,0:T(8,128)(2,1)}, bf16[768,512]{1,0:T(8,128)(2,1)}, bf16[768,512]{1,0:T(8,128)(2,1)}, bf16[784,512]{1,0:T(8,128)(2,1)}) custom-call(s32[11]{0:T(128)} %stack.60.refs_0_, bf16[4,768,512]{2,1,0:T(8,128)(2,1)} %bitcast.60, bf16[4,768,512]{2,1,0:T(8,128)(2,1)} %bitcast.61, bf16[4,768,512]{2,1,0:T(8,128)(2,1)} %bitcast.62, ...), custom_call_target="tpu_custom_call" | custom-call | flops 1 | bytes 1 | tf_op jit(solution)/shard_map/pallas_call | solution.py:485
  200.8 7.0 %all-gather.13.cloned.1.call-done = bf16[3072,256]{1,0:T(8,128)(2,1)} async-done(((bf16[768,256]{1,0:T(8,128)(2,1)}), bf16[3072,256]{1,0:T(8,128)(2,1)}) %all-gather.13.cloned.1.call-update) | async-done | bytes 1572880 | tf_op jit(solution)/shard_map/all_gather | solution.py:631
  207.8 6.8 %shard_map.95 = (bf16[512,2048]{1,0:T(8,128)(2,1)}, bf16[512,2048]{1,0:T(8,128)(2,1)}) custom-call(s32[1]{0:T(128)} %bitcast.19.flag_ref, f32[512,512]{1,0:T(8,128)} %get-tuple-element.55.refs_1_.inverse_ref.refs_6_, bf16[512,2048]{1,0:T(8,128)(2,1)} %collective-permute-done.14.first_ref, bf16[512,2048]{1,0:T(8,128)(2,1)} %shard_map.91.refs_5_.second_ref, ...), custom_call_target="tpu_custom_call" | custom-call | flops 1 | bytes 1 | tf_op jit(solution)/shard_map/pallas_call | solution.py:276
  215.8 20.8 %shard_map.97 = (f32[1536,1536]{1,0:T(8,128)}, f32[1536,1536]{1,0:T(8,128)}, f32[1536,2048]{1,0:T(8,128)}, f32[8,128]{1,0:T(8,128)}) custom-call(s32[11]{0:T(128)} %stack.56.refs_0_, f32[1]{0:T(128)} %bitcast.8.refs_1_, f32[8,128]{1,0:T(8,128)} %get-tuple-element.54.refs_0_.refs_2_, f32[1536,1536]{1,0:T(8,128)} %refs_3_.7, bf16[1536,2048]{1,0:T(8,128)(2,1)} %refs_4_.7, ...), custom_call_target="tpu_custom_call" | custom-call | flops 1 | bytes 1 | tf_op jit(solution)/shard_map/pallas_call | solution.py:431
  237.5 3.5 %shard_map.98 = (bf16[768,256]{1,0:T(8,128)(2,1)}, bf16[768,256]{1,0:T(8,128)(2,1)}, bf16[768,256]{1,0:T(8,128)(2,1)}, bf16[768,512]{1,0:T(8,128)(2,1)}) custom-call(s32[11]{0:T(128)} %stack.60.refs_0_, bf16[4,768,256]{2,1,0:T(8,128)(2,1)} %bitcast.65, bf16[4,768,256]{2,1,0:T(8,128)(2,1)} %bitcast.66, bf16[4,768,256]{2,1,0:T(8,128)(2,1)} %bitcast.67, ...), custom_call_target="tpu_custom_call" | custom-call | flops 1 | bytes 1 | tf_op jit(solution)/shard_map/pallas_call | solution.py:485
  244.4 19.1 %shard_map.99 = (f32[1536,1536]{1,0:T(8,128)}, f32[1536,1536]{1,0:T(8,128)}, f32[1536,2048]{1,0:T(8,128)}, f32[8,128]{1,0:T(8,128)}) custom-call(s32[11]{0:T(128)} %stack.56.refs_0_, f32[1]{0:T(128)} %bitcast.8.refs_1_, f32[8,128]{1,0:T(8,128)} %get-tuple-element.54.refs_0_.refs_2_, ...), custom_call_target="tpu_custom_call", output_to_operand_aliasing={{0}: (14, {}), {1}: (15, {}), {2}: (16, {})} | custom-call | flops 1 | bytes 1 | tf_op jit(solution)/shard_map/pallas_call | solution.py:431
  264.4 3.2 %shard_map.100 = (bf16[768,256]{1,0:T(8,128)(2,1)}, bf16[768,256]{1,0:T(8,128)(2,1)}, bf16[768,256]{1,0:T(8,128)(2,1)}, bf16[768,256]{1,0:T(8,128)(2,1)}) custom-call(s32[11]{0:T(128)} %stack.60.refs_0_, bf16[4,768,256]{2,1,0:T(8,128)(2,1)} %bitcast.69, bf16[4,768,256]{2,1,0:T(8,128)(2,1)} %bitcast.70, bf16[4,768,256]{2,1,0:T(8,128)(2,1)} %bitcast.71, ...), custom_call_target="tpu_custom_call" | custom-call | flops 1 | bytes 1 | tf_op jit(solution)/shard_map/pallas_call | solution.py:485
  270.9 13.5 %shard_map.101 = (f32[1536,1536]{1,0:T(8,128)}, f32[1536,1536]{1,0:T(8,128)}, f32[1536,2048]{1,0:T(8,128)}, f32[8,128]{1,0:T(8,128)}) custom-call(s32[11]{0:T(128)} %stack.56.refs_0_, f32[1]{0:T(128)} %bitcast.8.refs_1_, f32[8,128]{1,0:T(8,128)} %get-tuple-element.54.refs_0_.refs_2_, ...), custom_call_target="tpu_custom_call", output_to_operand_aliasing={{0}: (14, {}), {1}: (15, {}), {2}: (16, {})} | custom-call | flops 1 | bytes 1 | tf_op jit(solution)/shard_map/pallas_call | solution.py:431
  284.5 3.4 %collective-permute-done.27.refs_1_ = bf16[768,256]{1,0:T(8,128)(2,1)S(1)} collective-permute-done((bf16[768,256]{1,0:T(8,128)(2,1)}, bf16[768,256]{1,0:T(8,128)(2,1)S(1)}, u32[]{:S(2)}, u32[]{:S(2)}) %collective-permute-start.27) | collective-permute-done | bytes 393248 | tf_op jit(solution)/shard_map/ppermute | solution.py:458
  293.7 13.6 %shard_map.103 = (f32[1536,1536]{1,0:T(8,128)}, f32[1536,1536]{1,0:T(8,128)}, f32[1536,2048]{1,0:T(8,128)}, f32[8,128]{1,0:T(8,128)}) custom-call(s32[11]{0:T(128)} %stack.56.refs_0_, f32[1]{0:T(128)} %bitcast.8.refs_1_, f32[8,128]{1,0:T(8,128)} %get-tuple-element.54.refs_0_.refs_2_, ...), custom_call_target="tpu_custom_call", output_to_operand_aliasing={{0}: (14, {}), {1}: (15, {}), {2}: (16, {})} | custom-call | flops 1 | bytes 1 | tf_op jit(solution)/shard_map/pallas_call | solution.py:431
  (162 shorter events, 57.6 us)
Async XLA Ops:
  7.2 113.0 %all-gather.9.cloned.1.call-start = ((), (), s32[]{:S(2)}) async-start(), calls=%async_computation | async-start | bytes 4014080 | tf_op jit(solution)/shard_map/all_gather | solution.py:631
  31.1 150.3 %all-gather.11.cloned.1.call-start = ((), (), s32[]{:S(2)}) async-start(), calls=%async_computation.1 | async-start | bytes 3932160 | tf_op jit(solution)/shard_map/all_gather | solution.py:631
  35.4 44.3 %collective-permute-start.3 = (bf16[512,2048]{1,0:T(8,128)(2,1)}, bf16[512,2048]{1,0:T(8,128)(2,1)S(1)}, u32[]{:S(2)}, u32[]{:S(2)}) collective-permute-start(bf16[512,2048]{1,0:T(8,128)(2,1)} %shard_map.86.second_ref), channel_id=1, source_target_pairs={{0,8},{16,24},{1,9},{17,25},{2,10},{18,26},{3,11},{19,27}} | collective-permute-start | bytes 6291464 | tf_op jit(solution)/shard_map/ppermute | solution.py:592
  39.1 63.6 %collective-permute-start.6 = (bf16[448,1536]{1,0:T(8,128)(2,1)}, bf16[448,1536]{1,0:T(8,128)(2,1)}, u32[]{:S(2)}, u32[]{:S(2)}) collective-permute-start(bf16[448,1536]{1,0:T(8,128)(2,1)} %pad_maximum_fusion.1.refs_1_), channel_id=1, source_target_pairs={{0,8},{4,12},{8,0},{12,4},{16,24},{20,28},{24,16},{28,20},{1,9},{5... | collective-permute-start | bytes 4128776 | tf_op jit(solution)/shard_map/ppermute | solution.py:458
  106.0 101.9 %all-gather.13.cloned.1.call-start = ((), (), s32[]{:S(2)}) async-start(), calls=%async_computation.2 | async-start | bytes 1966080 | tf_op jit(solution)/shard_map/all_gather | solution.py:631
  106.7 156.8 %all-gather.15.cloned.1.call-start = ((), (), s32[]{:S(2)}) async-start(), calls=%async_computation.3 | async-start | bytes 1966080 | tf_op jit(solution)/shard_map/all_gather | solution.py:631
  106.8 18.0 %collective-permute-start.10 = (bf16[448,1536]{1,0:T(8,128)(2,1)}, bf16[448,1536]{1,0:T(8,128)(2,1)}, u32[]{:S(2)}, u32[]{:S(2)}) collective-permute-start(bf16[448,1536]{1,0:T(8,128)(2,1)} %pad_maximum_fusion.1.refs_1_), channel_id=1, source_target_pairs={{0,4},{4,0},{8,12},{12,8},{16,20},{20,16},{24,28},{28,24},{1,5},{5... | collective-permute-start | bytes 4128776 | tf_op jit(solution)/shard_map/ppermute | solution.py:458
  106.8 17.9 %collective-permute-start.11 = (bf16[448,1536]{1,0:T(8,128)(2,1)}, bf16[448,1536]{1,0:T(8,128)(2,1)}, u32[]{:S(2)}, u32[]{:S(2)}) collective-permute-start(bf16[448,1536]{1,0:T(8,128)(2,1)} %collective-permute-done.6.refs_4_.refs_2_), channel_id=1, source_target_pairs={{0,4},{4,0},{8,12},{12,8},{16,20},{20,16},{24,28},{28,24},{1,5},{5... | collective-permute-start | bytes 4128776 | tf_op jit(solution)/shard_map/ppermute | solution.py:458
  107.3 17.4 %collective-permute-start.12 = (bf16[320,1536]{1,0:T(8,128)(2,1)S(1)}, bf16[320,1536]{1,0:T(8,128)(2,1)}, u32[]{:S(2)}, u32[]{:S(2)}) collective-permute-start(bf16[320,1536]{1,0:T(8,128)(2,1)S(1)} %collective-permute-done.4.refs_5_), channel_id=1, source_target_pairs={{0,4},{4,0},{8,12},{12,8},{16,20},{20,16},{24,28},{28,24},{1,5},{5... | collective-permute-start | bytes 2949128 | tf_op jit(solution)/shard_map/ppermute | solution.py:458
  124.0 20.2 %collective-permute-start.7 = (bf16[784,512]{1,0:T(8,128)(2,1)}, bf16[784,512]{1,0:T(8,128)(2,1)S(1)}, u32[]{:S(2)}, u32[]{:S(2)}) collective-permute-start(bf16[784,512]{1,0:T(8,128)(2,1)} %shard_map.89.refs_9_.refs_3_.refs_4_), channel_id=1, source_target_pairs={{0,8},{4,12},{8,0},{12,4},{16,24},{20,28},{24,16},{28,20},{1,9},{5... | collective-permute-start | bytes 2408456 | tf_op jit(solution)/shard_map/ppermute | solution.py:458
  136.6 64.2 %collective-permute-start.14 = (bf16[512,2048]{1,0:T(8,128)(2,1)}, bf16[512,2048]{1,0:T(8,128)(2,1)}, u32[]{:S(2)}, u32[]{:S(2)}) collective-permute-start(bf16[512,2048]{1,0:T(8,128)(2,1)} %shard_map.91.refs_5_.second_ref), channel_id=1, source_target_pairs={{0,4},{8,12},{16,20},{24,28},{1,5},{9,13},{17,21},{25,29},{2,6},{1... | collective-permute-start | bytes 6291464 | tf_op jit(solution)/shard_map/ppermute | solution.py:643
  149.0 44.1 %collective-permute-start.15 = (bf16[784,512]{1,0:T(8,128)(2,1)}, bf16[784,512]{1,0:T(8,128)(2,1)}, u32[]{:S(2)}, u32[]{:S(2)}) collective-permute-start(bf16[784,512]{1,0:T(8,128)(2,1)} %get-tuple-element.60), channel_id=1, source_target_pairs={{0,8},{4,12},{8,0},{12,4},{16,24},{20,28},{24,16},{28,20},{1,9},{5... | collective-permute-start | bytes 2408456 | tf_op jit(solution)/shard_map/ppermute | solution.py:458
  149.3 43.9 %collective-permute-start.16 = (bf16[784,512]{1,0:T(8,128)(2,1)}, bf16[784,512]{1,0:T(8,128)(2,1)S(1)}, u32[]{:S(2)}, u32[]{:S(2)}) collective-permute-start(bf16[784,512]{1,0:T(8,128)(2,1)} %get-tuple-element.61), channel_id=1, source_target_pairs={{0,8},{4,12},{8,0},{12,4},{16,24},{20,28},{24,16},{28,20},{1,9},{5... | collective-permute-start | bytes 2408456 | tf_op jit(solution)/shard_map/ppermute | solution.py:458
  153.7 60.9 %collective-permute-start.18 = (bf16[784,512]{1,0:T(8,128)(2,1)}, bf16[784,512]{1,0:T(8,128)(2,1)S(1)}, u32[]{:S(2)}, u32[]{:S(2)}) collective-permute-start(bf16[784,512]{1,0:T(8,128)(2,1)} %get-tuple-element.53.refs_7_), channel_id=1, source_target_pairs={{0,4},{4,0},{8,12},{12,8},{16,20},{20,16},{24,28},{28,24},{1,5},{5... | collective-permute-start | bytes 2408456 | tf_op jit(solution)/shard_map/ppermute | solution.py:458
  198.3 16.3 %collective-permute-start.19 = (bf16[784,512]{1,0:T(8,128)(2,1)}, bf16[784,512]{1,0:T(8,128)(2,1)S(1)}, u32[]{:S(2)}, u32[]{:S(2)}) collective-permute-start(bf16[784,512]{1,0:T(8,128)(2,1)} %get-tuple-element.65), channel_id=1, source_target_pairs={{0,4},{4,0},{8,12},{12,8},{16,20},{20,16},{24,28},{28,24},{1,5},{5... | collective-permute-start | bytes 2408456 | tf_op jit(solution)/shard_map/ppermute | solution.py:458
  198.8 37.8 %collective-permute-start.17 = (bf16[768,512]{1,0:T(8,128)(2,1)}, bf16[768,512]{1,0:T(8,128)(2,1)}, u32[]{:S(2)}, u32[]{:S(2)}) collective-permute-start(bf16[768,512]{1,0:T(8,128)(2,1)} %get-tuple-element.62), channel_id=1, source_target_pairs={{0,8},{4,12},{8,0},{12,4},{16,24},{20,28},{24,16},{28,20},{1,9},{5... | collective-permute-start | bytes 2359304 | tf_op jit(solution)/shard_map/ppermute | solution.py:458
  199.1 37.5 %collective-permute-start.20 = (bf16[768,512]{1,0:T(8,128)(2,1)}, bf16[768,512]{1,0:T(8,128)(2,1)S(1)}, u32[]{:S(2)}, u32[]{:S(2)}) collective-permute-start(bf16[768,512]{1,0:T(8,128)(2,1)} %get-tuple-element.68), channel_id=1, source_target_pairs={{0,8},{4,12},{8,0},{12,4},{16,24},{20,28},{24,16},{28,20},{1,9},{5... | collective-permute-start | bytes 2359304 | tf_op jit(solution)/shard_map/ppermute | solution.py:458
  200.8 42.2 %collective-permute-start.22 = (bf16[768,512]{1,0:T(8,128)(2,1)}, bf16[768,512]{1,0:T(8,128)(2,1)S(1)}, u32[]{:S(2)}, u32[]{:S(2)}) collective-permute-start(bf16[768,512]{1,0:T(8,128)(2,1)} %get-tuple-element.66.refs_16_), channel_id=1, source_target_pairs={{0,4},{4,0},{8,12},{12,8},{16,20},{20,16},{24,28},{28,24},{1,5},{5... | collective-permute-start | bytes 2359304 | tf_op jit(solution)/shard_map/ppermute | solution.py:458
  241.0 22.5 %collective-permute-start.21 = (bf16[768,256]{1,0:T(8,128)(2,1)}, bf16[768,256]{1,0:T(8,128)(2,1)S(1)}, u32[]{:S(2)}, u32[]{:S(2)}) collective-permute-start(bf16[768,256]{1,0:T(8,128)(2,1)} %get-tuple-element.69), channel_id=1, source_target_pairs={{0,8},{4,12},{8,0},{12,4},{16,24},{20,28},{24,16},{28,20},{1,9},{5... | collective-permute-start | bytes 1179656 | tf_op jit(solution)/shard_map/ppermute | solution.py:458
  241.7 21.8 %collective-permute-start.24 = (bf16[768,256]{1,0:T(8,128)(2,1)}, bf16[768,256]{1,0:T(8,128)(2,1)S(1)}, u32[]{:S(2)}, u32[]{:S(2)}) collective-permute-start(bf16[768,256]{1,0:T(8,128)(2,1)} %get-tuple-element.76), channel_id=1, source_target_pairs={{0,8},{4,12},{8,0},{12,4},{16,24},{20,28},{24,16},{28,20},{1,9},{5... | collective-permute-start | bytes 1179656 | tf_op jit(solution)/shard_map/ppermute | solution.py:458
  243.0 27.0 %collective-permute-start.28 = (bf16[768,256]{1,0:T(8,128)(2,1)}, bf16[768,256]{1,0:T(8,128)(2,1)S(1)}, u32[]{:S(2)}, u32[]{:S(2)}) collective-permute-start(bf16[768,256]{1,0:T(8,128)(2,1)} %get-tuple-element.74.refs_17_), channel_id=1, source_target_pairs={{0,4},{4,0},{8,12},{12,8},{16,20},{20,16},{24,28},{28,24},{1,5},{5... | collective-permute-start | bytes 1179656 | tf_op jit(solution)/shard_map/ppermute | solution.py:458
  268.0 16.4 %collective-permute-start.25 = (bf16[768,256]{1,0:T(8,128)(2,1)}, bf16[768,256]{1,0:T(8,128)(2,1)S(1)}, u32[]{:S(2)}, u32[]{:S(2)}) collective-permute-start(bf16[768,256]{1,0:T(8,128)(2,1)} %get-tuple-element.77), channel_id=1, source_target_pairs={{0,8},{4,12},{8,0},{12,4},{16,24},{20,28},{24,16},{28,20},{1,9},{5... | collective-permute-start | bytes 1179656 | tf_op jit(solution)/shard_map/ppermute | solution.py:458
  268.7 19.1 %collective-permute-start.27 = (bf16[768,256]{1,0:T(8,128)(2,1)}, bf16[768,256]{1,0:T(8,128)(2,1)S(1)}, u32[]{:S(2)}, u32[]{:S(2)}) collective-permute-start(bf16[768,256]{1,0:T(8,128)(2,1)} %get-tuple-element.79), channel_id=1, source_target_pairs={{0,8},{4,12},{8,0},{12,4},{16,24},{20,28},{24,16},{28,20},{1,9},{5... | collective-permute-start | bytes 1179656 | tf_op jit(solution)/shard_map/ppermute | solution.py:458
  270.0 21.0 %collective-permute-start.26 = (bf16[768,256]{1,0:T(8,128)(2,1)}, bf16[768,256]{1,0:T(8,128)(2,1)S(1)}, u32[]{:S(2)}, u32[]{:S(2)}) collective-permute-start(bf16[768,256]{1,0:T(8,128)(2,1)} %get-tuple-element.78.refs_17_), channel_id=1, source_target_pairs={{0,4},{4,0},{8,12},{12,8},{16,20},{20,16},{24,28},{28,24},{1,5},{5... | collective-permute-start | bytes 1179656 | tf_op jit(solution)/shard_map/ppermute | solution.py:458
  (38 other events, 173.2 us)
Sparse Core Ops, SparseCore 0:
  31.2 65.7 all-gather.8
  106.1 64.3 all-gather.10
  172.1 35.7 all-gather.12
  209.3 35.9 all-gather.14

commit v11 on v10

--- a/solution.py
+++ b/solution.py
@@ -293,135 +293,105 @@
 
 def finish_kernel(
     count,
-    gram_steps,
     begin,
     unread,
     places_ref,
     damp_ref,
     share_ref,
     factor_ref,
-    grad_ref,
     panel_ref,
     inverse_ref,
-    high_ref,
     lead_ref,
     across_ref,
     *refs,
 ):
     first_chunk = begin == 0
     if first_chunk:
-        lower_ref, low_ref, *refs = refs
+        lower_ref, *refs = refs
     mine = refs[:count]
-    outs = refs[count + unread :]
-    running_ref, factored_ref, precond_ref, token_ref, mine_ref, rows_ref, first_ref = outs
-    j, i = pl.program_id(0), pl.program_id(1)
+    running_ref, factored_ref, panels_ref, token_ref, mine_ref, rows_ref, first_ref = refs[
+        count + unread :
+    ]
+    j = pl.program_id(0)
     member, column, base = places_ref[0], places_ref[1], places_ref[2] + begin
     share, damp = share_ref[:1, :1], damp_ref[0]
     height, cols = running_ref.shape
     depth = 2 * CAP
     side = LEAD // count
-    span = pl.ds(pl.multiple_of(i * height, height), height)
     head = (member == 0) & first_chunk
 
     @pl.when(j == 0)
     def _():
         token_ref[...] = jnp.zeros_like(token_ref)
         for q in range(count):
-            mine_ref[span, q * depth : (q + 1) * depth] = mine[q][0, :depth, :].T
+            mine_ref[:, q * depth : (q + 1) * depth] = mine[q][0, :depth, :].T
             place = pl.multiple_of(places_ref[PLACES + q] * side, side)
             first_ref[pl.ds(place, side), :] = mine[q][0, depth : depth + side, :].astype(F32)
         source = first_ref[...].T
         if cols == LEAD:
             source = jnp.where(column == 0, factor_ref[...], source)
-        gram = jnp.dot(mine_ref[span, :], lead_ref[...], preferred_element_type=F32)
-        row = base + i * height + lax.broadcasted_iota(jnp.int32, (height, LEAD), 0)
+        gram = jnp.dot(mine_ref[...], lead_ref[...], preferred_element_type=F32)
+        row = base + lax.broadcasted_iota(jnp.int32, (height, LEAD), 0)
         col = lax.broadcasted_iota(jnp.int32, (height, LEAD), 1)
         source = DECAY * source + share * gram
         source = source + jnp.where(row == col, damp, 0.0)
-        rows_ref[span, :] = dot_split(source, inverse_ref[...], ((1,), (1,)))
-
-    panel = rows_ref[span, :].astype(BF16)
-
-    @pl.when(j < gram_steps)
-    def _():
-        gram = jnp.dot(mine_ref[span, :], across_ref[...], preferred_element_type=F32)
-        running = DECAY * factor_ref[...] + share * gram
-        running_ref[...] = running
-        row = base + i * height + lax.broadcasted_iota(jnp.int32, (height, cols), 0)
-        col = (column * gram_steps + j) * cols + lax.broadcasted_iota(jnp.int32, (height, cols), 1)
-        matrix = running + jnp.where(row == col, damp, 0.0)
-        factored = matrix - jnp.dot(panel, panel_ref[...], preferred_element_type=F32)
-        factored_ref[...] = jnp.where(head, 0.0, factored)
-
-        for part in range(LEAD // cols):
-            edge = slice(part * cols, (part + 1) * cols)
-
-            @pl.when((column == 0) & (j == part))
-            def _():
-                factored_ref[...] = rows_ref[span, edge]
-
-                if first_chunk:
-
-                    @pl.when(head)
-                    def _():
-                        factored_ref[...] = lower_ref[span, edge]
-
-    product = jnp.dot(panel, high_ref[...], preferred_element_type=F32)
-    precond_ref[...] = grad_ref[...].astype(F32) - product
-
-    if first_chunk:
-
-        @pl.when(head)
+        rows_ref[...] = dot_split(source, inverse_ref[...], ((1,), (1,)))
+        panels_ref[...] = rows_ref[...].astype(BF16)
+
+    gram = jnp.dot(mine_ref[...], across_ref[...], preferred_element_type=F32)
+    running = DECAY * factor_ref[...] + share * gram
+    running_ref[...] = running
+    row = base + lax.broadcasted_iota(jnp.int32, (height, cols), 0)
+    col = (column * pl.num_programs(0) + j) * cols
+    col = col + lax.broadcasted_iota(jnp.int32, (height, cols), 1)
+    matrix = running + jnp.where(row == col, damp, 0.0)
+    factored = matrix - jnp.dot(panels_ref[...], panel_ref[...], preferred_element_type=F32)
+    factored_ref[...] = jnp.where(head, 0.0, factored)
+
+    for part in range(LEAD // cols):
+        edge = slice(part * cols, (part + 1) * cols)
+
+        @pl.when((column == 0) & (j == part))
         def _():
-            precond_ref[...] = high_ref[span, :].astype(F32) + low_ref[span, :].astype(F32)
+            factored_ref[...] = rows_ref[:, edge]
+
+            if first_chunk:
+
+                @pl.when(head)
+                def _():
+                    factored_ref[...] = lower_ref[:, edge]
 
 
 def finish_rows(
-    begin, places, damp, share, factor, grad, panel, inverse, lower, high, low,
-    lead, across, mine, results, earlier,
+    begin, places, damp, share, factor, panel, inverse, lower, lead, across, mine, results, earlier
 ):
     count = len(mine)
-    deep, rows = mine[0].shape[1:]
-    width, grad_cols = factor.shape[0], grad.shape[1]
-    tall = lead.shape[0]
-    height = min(rows, COLS)
-    tiles = rows // height
+    deep, height = mine[0].shape[1:]
+    width, tall = factor.shape[0], lead.shape[0]
     start = begin // height
     cols = COLS if width % COLS == 0 else ROWS
-    gram_steps, steps = width // cols, grad_cols // cols
-    assert steps >= gram_steps and rows % height == 0 and begin % height == 0
+    assert begin % height == 0
 
     def mine_spec(q):
-        return pl.BlockSpec(
-            (1, deep, height),
-            lambda j, i, p: (p[PLACES + count + q], 0, jnp.where(j == 0, i, tiles - 1)),
-        )
-
-    def gram_col(j):
-        return jnp.minimum(j, gram_steps - 1)
-
-    def gram_tile(j, i, p):
-        return (start + jnp.where(j < gram_steps, i, tiles - 1), gram_col(j))
-
-    grad_spec = pl.BlockSpec((height, cols), lambda j, i, p: (start + i, j))
-    factor_spec = pl.BlockSpec((height, cols), gram_tile)
-    lead_whole = pl.BlockSpec((LEAD, LEAD), lambda j, i, p: (0, 0))
-    small = pl.BlockSpec((GROUP, TILE), lambda j, i, p: (0, 0))
+        return pl.BlockSpec((1, deep, height), lambda j, p: (p[PLACES + count + q], 0, 0))
+
+    factor_spec = pl.BlockSpec((height, cols), lambda j, p: (start, j))
+    rows_spec = pl.BlockSpec((height, LEAD), lambda j, p: (start, 0))
+    lead_whole = pl.BlockSpec((LEAD, LEAD), lambda j, p: (0, 0))
+    small = pl.BlockSpec((GROUP, TILE), lambda j, p: (0, 0))
     in_specs = [
         pl.BlockSpec(memory_space=pltpu.SMEM),
         small,
         factor_spec,
-        grad_spec,
-        pl.BlockSpec((LEAD, cols), lambda j, i, p: (0, gram_col(j))),
+        pl.BlockSpec((LEAD, cols), lambda j, p: (0, j)),
         lead_whole,
-        pl.BlockSpec((LEAD, cols), lambda j, i, p: (0, j)),
-        pl.BlockSpec((tall, LEAD), lambda j, i, p: (0, 0)),
-        pl.BlockSpec((tall, cols), lambda j, i, p: (0, gram_col(j))),
+        pl.BlockSpec((tall, LEAD), lambda j, p: (0, 0)),
+        pl.BlockSpec((tall, cols), lambda j, p: (0, j)),
     ]
-    operands = [damp, share, factor, grad, panel, inverse, high, lead, across]
+    operands = [damp, share, factor, panel, inverse, lead, across]
     if begin == 0:
-        in_specs += [lead_whole, pl.BlockSpec((LEAD, cols), lambda j, i, p: (0, j))]
-        operands += [lower, low]
+        in_specs += [lead_whole]
+        operands += [lower]
     in_specs += [mine_spec(q) for q in range(count)]
     operands += mine
     aliases = {1 + len(operands) + k: k for k in range(len(results))}
@@ -429,28 +399,65 @@
     unread = len(results) + len(earlier)
     in_specs += [ANYWHERE] * unread
     return pl.pallas_call(
-        lambda *refs: finish_kernel(count, gram_steps, begin, unread, *refs),
+        lambda *refs: finish_kernel(count, begin, unread, *refs),
         grid_spec=pltpu.PrefetchScalarGridSpec(
             num_scalar_prefetch=1,
-            grid=(steps, tiles),
+            grid=(width // cols,),
             in_specs=in_specs,
-            out_specs=(factor_spec, factor_spec, grad_spec, small),
+            out_specs=(factor_spec, factor_spec, rows_spec, small),
             scratch_shapes=[
-                pltpu.VMEM((rows, tall), BF16),
-                pltpu.VMEM((rows, LEAD), F32),
+                pltpu.VMEM((height, tall), BF16),
+                pltpu.VMEM((height, LEAD), F32),
                 pltpu.VMEM((LEAD, height), F32),
             ],
         ),
         out_shape=(
             jax.ShapeDtypeStruct(factor.shape, F32),
             jax.ShapeDtypeStruct(factor.shape, F32),
-            jax.ShapeDtypeStruct(grad.shape, F32),
+            jax.ShapeDtypeStruct((width, LEAD), BF16),
             jax.ShapeDtypeStruct((GROUP, TILE), F32),
         ),
         input_output_aliases=aliases,
         compiler_params=pltpu.CompilerParams(vmem_limit_bytes=VMEM_BYTES),
         cost_estimate=NO_COST,
     )(places, *operands)
+
+
+def precond_kernel(first, places_ref, grad_ref, panels_ref, high_ref, low_ref, *refs):
+    out_ref = refs[-1]
+    product = jnp.dot(panels_ref[...], high_ref[...], preferred_element_type=F32)
+    out_ref[...] = grad_ref[...].astype(F32) - product
+    if first:
+
+        @pl.when((places_ref[0] == 0) & (pl.program_id(1) == 0))
+        def _():
+            out_ref[...] = high_ref[...].astype(F32) + low_ref[...].astype(F32)
+
+
+def precond_rows(begin, end, places, grad, panels, high, low, results):
+    height = min(LEAD, end - begin)
+    start = begin // height
+    cols = COLS
+    rows_spec = pl.BlockSpec((height, cols), lambda j, i: (start + i, j))
+    tiled = pl.BlockSpec((LEAD, cols), lambda j, i: (0, j))
+    low_spec = tiled if begin == 0 else ANYWHERE
+    return pl.pallas_call(
+        lambda *refs: precond_kernel(begin == 0, *refs),
+        grid=(grad.shape[1] // cols, (end - begin) // height),
+        out_shape=jax.ShapeDtypeStruct(grad.shape, F32),
+        in_specs=[
+            pl.BlockSpec(memory_space=pltpu.SMEM),
+            rows_spec,
+            pl.BlockSpec((height, LEAD), lambda j, i: (start + i, 0)),
+            tiled,
+            low_spec,
+        ]
+        + [ANYWHERE] * len(results),
+        out_specs=rows_spec,
+        input_output_aliases={5: 0} if results else {},
+        compiler_params=pltpu.CompilerParams(vmem_limit_bytes=VMEM_BYTES),
+        cost_estimate=NO_COST,
+    )(places, grad, panels, high, low, *results)
 
 
 def swapped(value, mask):
@@ -518,25 +525,33 @@
     return [(blocks, (None, rows, width), [member ^ other, 0, 0]) for other in range(1, group)]
 
 
-def exchange_members(blocks, sent, bits, requests, earlier):
+def first_hop(blocks, sent, bits):
     held = [[blocks]] + [[part] for part in sent]
+    return hop(held, bits - 1)
+
+
+def hop(held, bit):
+    half = 1 << bit
+    return [
+        kept + [swapped(part, half) for part in passed]
+        for kept, passed in zip(held[:half], held[half:])
+    ]
+
+
+def exchange_members(held, bits, requests, earlier):
     copies = None
-    for bit in reversed(range(bits)):
+    for bit in reversed(range(bits - 1)):
         half = 1 << bit
         arrived = [(part, part.shape, [0, 0]) for passed in held[half:] for part in passed[1:]]
         if arrived:
-            passing = copied(
-                requests + arrived if copies is None else arrived, earlier + held[0][1:]
-            )
+            asked = requests + arrived if copies is None else arrived
+            passing = list(copied(asked, earlier + held[0][1:]))
             if copies is None:
                 copies, passing = passing[: len(requests)], passing[len(requests) :]
             for passed in held[half:]:
                 count = len(passed) - 1
                 passed[1:], passing = passing[:count], passing[count:]
-        held = [
-            kept + [swapped(part, half) for part in passed]
-            for kept, passed in zip(held[:half], held[half:])
-        ]
+        held = hop(held, bit)
     first, *others = held[0]
     return [first] + [part[None] for part in others], copies
 
@@ -587,9 +602,6 @@
     halves = [(factor_old, (side, width), [place, 0]) for place in range(2)]
     halves = copied(halves, [])
     lead_factor = share_of_first(*halves, member, group, bits)
-
-    near = copied([(weight_grad, (LEAD, weight_grad.shape[1]), [0, 0])], halves[:1])[0]
-    moved = lax.ppermute(near, "tok", down_pairs(bits - 1, group))
 
     live = jnp.arange(tok_rows) < counts[0]
     named = routes[:, 0]
@@ -614,7 +626,7 @@
         ],
         0,
     )
-    away_rows = copied([(packed, (CAP, width), [1, 0])], [front, moved])[0]
+    away_rows = copied([(packed, (CAP, width), [1, 0])], [front])[0]
     incoming = swapped(away_rows, group)
     outgoing = jnp.concatenate([packed[:CAP], lead_factor], 0)
     quarter = jnp.concatenate([packed[:CAP], incoming, lead_factor], 0)
@@ -631,52 +643,60 @@
     spread = [lax.all_gather(part, "fac") for part in parts]
     rows = first_part.shape[0]
     earlier = [across_other[1], *parts[1:]]
-    lead = copied([(spread[0], (None, rows, LEAD), [0, 0, 0])], earlier)[0]
+    requests = [(spread[0], (None, rows, LEAD), [0, 0, 0])]
+    lead = copied(requests, earlier)[0]
     slots = [member, column, member * width] + order + [member] + [0] * (group - 1)
     assert len(slots) == PLACES + 2 * group
     slots = jnp.stack([jnp.int32(slot) for slot in slots])
     across, near_factor = stacked(slots, across_own, across_other, [lead])
     lead = gather_members(lead, bits)
-    flag = (member >> (bits - 1) & 1)[None]
-    for bit in reversed(range(bits - 1)):
-        near = chosen(flag, moved, near, [across])
-        moved = lax.ppermute(near, "tok", down_pairs(bit, group))
-        flag = (member >> bit & 1)[None]
-    sent = copied(member_blocks(spread[0], member, group), [lead[1], near])
-
-    lower, inverse, share = factor_lead(slots, damp, factor_old, lead, sent[:1])
+    sent = copied(member_blocks(spread[0], member, group), [lead[1], across])
+    held = first_hop(spread[0], sent, bits)
+    near = copied([(weight_grad, (LEAD, weight_grad.shape[1]), [0, 0])], sent[:1])[0]
+    lower, inverse, share = factor_lead(slots, damp, factor_old, lead, [near])
     panel, lead_stack = panel_columns(
         share, inverse, near_factor, lead, across, spread[1:2]
     )
 
     token = panel
-    results = []
+    results, precond = [], []
+    cut = LEAD * max(1, (width - 1) // LEAD)
     for number, (begin, _) in enumerate(chunks):
         requests = []
         if number + 1 < len(chunks):
             requests = member_blocks(spread[number + 1], member, group)
-        pieces, sent = exchange_members(spread[number], sent, bits, requests, [token])
+        if number:
+            held = first_hop(spread[number], sent, bits)
+        pieces, sent = exchange_members(held, bits, requests, [token])
+        gates = sent[:1]
         if number == 0:
-            high, low = solve_lead(flag, inverse, moved, near, spread[2:3])
+            for bit in reversed(range(bits)):
+                moved = lax.ppermute(near, "tok", down_pairs(bit, group))
+                flag = (member >> bit & 1)[None]
+                if bit:
+                    near = chosen(flag, moved, near, gates)
+            high, low = solve_lead(flag, inverse, moved, near, [])
+            gates = gates + [high]
+        if number + 1 == len(chunks):
+            precond = [precond_rows(0, cut, slots, weight_grad, results[2], high, low, [])]
         *results, token = finish_rows(
             begin,
             slots,
             damp,
             share,
             factor_old,
-            weight_grad,
             panel,
             inverse,
             lower,
-            high,
-            low,
             lead_stack,
             across,
             pieces,
             results,
-            sent[:1],
+            gates + precond,
         )
-    return tuple(results)
+    running, factored, panels = results
+    precond = precond_rows(cut, width, slots, weight_grad, panels, high, low, precond)
+    return (running, factored, precond)
 
 
 def solution(mesh):

time: 316 us -> 332 us (1.051)
  Pallas kernels: 159 us -> 166 us
  waiting for transfers between devices: 87.6 us -> 93.9 us
    ppermute x27, waiting for transfers between devices: 41.5 us -> 88.2 us  [swapped(): lax.ppermute(value, 'tok', [(source, source ^ mask) for source in range(s...]
    ppermute x1 -> x0, waiting for transfers between devices: 37.7 us -> none  [local(): moved = lax.ppermute(near, 'tok', down_pairs(bits - 1, group))]
    pallas_call x4 -> x6, Pallas kernels: 67 us -> 73.9 us  [the longest x4 56.4 us: finish_rows(): pl.pallas_call(lambda *refs: finish_kernel(count, begin, unread, *refs),...]
    unnamed x55 -> x61, local copies, waits for them, and re-layouts: 10.1 us -> 9.59 us
  transfers between devices with their start and end apart: 35 -> 35, of which waited for: 11 -> 14; matrix products, arithmetic and copies ran while one was open for 4% -> 4% of each run, Pallas kernels for 45% -> 44%
where the time goes in v11:
time: 332 us; the launch traced here: 329 us
  Pallas kernels  166 us (50%)
  waiting for transfers between devices  93.9 us (28%)
  starting transfers between devices  25 us (8%)
  between operations  21.2 us (6%)
  local copies, waits for them, and re-layouts  14.5 us (4%)
  other arithmetic  7.35 us (2%)
    ppermute x27, waiting for transfers between devices, swapped(): lax.ppermute(value, 'tok', [(source, source ^ mask) for source in range(s...  88.2 us
    pallas_call x4, Pallas kernels, finish_rows(): pl.pallas_call(lambda *refs: finish_kernel(count, begin, unread, *refs),...  56.4 us
    pallas_call x10, Pallas kernels, copied(): pl.pallas_call(lambda *refs: copy_kernel(len(arrays), *refs), grid_spec=p...  33.9 us
    pallas_call x1, Pallas kernels, factor_lead(): pl.pallas_call(lambda *refs: factor_kernel(len(lead), *refs), grid=(1,),...  27.5 us
    ppermute x27, starting transfers between devices, swapped(): lax.ppermute(value, 'tok', [(source, source ^ mask) for source in range(s...  18.3 us
    pallas_call x2, Pallas kernels, precond_rows(): pl.pallas_call(lambda *refs: precond_kernel(begin == 0, *refs), grid=(gra...  17.5 us
    pallas_call x1, Pallas kernels, panel_columns(): pl.pallas_call(lambda *refs: panel_kernel(count, *refs), grid=(width // c...  11.9 us
    unnamed x61, local copies, waits for them, and re-layouts  9.59 us
  transfers between devices with their start and end apart: 35, of which 14 were waited for; matrix products, arithmetic and copies ran while one was open for 4% of the time, Pallas kernels for 44%

profile of v11, /device:TPU:2, one launch (start us, length us, event | category | flops | bytes accessed | tf_op | source)
XLA Modules:
  0.0 328.9 jit_solution(17999372305390656255)
XLA Ops:
  7.2 3.9 %shard_map.85 = (bf16[256,1536]{1,0:T(8,128)(2,1)}, bf16[256,1536]{1,0:T(8,128)(2,1)}) custom-call(s32[4]{0:T(128)} %constant.91.clone.1.refs_0_, f32[1536,1536]{1,0:T(8,128)} %refs_3_.7, f32[1536,1536]{1,0:T(8,128)} %refs_3_.7), custom_call_target="tpu_custom_call" | custom-call | flops 1 | bytes 1 | tf_op jit(solution)/shard_map/pallas_call | solution.py:492
  39.1 22.5 %collective-permute-done.3.refs_5_ = bf16[320,1536]{1,0:T(8,128)(2,1)S(1)} collective-permute-done((bf16[320,1536]{1,0:T(8,128)(2,1)}, bf16[320,1536]{1,0:T(8,128)(2,1)S(1)}, u32[]{:S(2)}, u32[]{:S(2)}) %collective-permute-start.3) | collective-permute-done | bytes 983072 | tf_op jit(solution)/shard_map/ppermute | solution.py:465
  72.5 21.1 %collective-permute-done.4.refs_2_.refs_6_ = bf16[320,1536]{1,0:T(8,128)(2,1)S(1)} collective-permute-done((bf16[320,1536]{1,0:T(8,128)(2,1)S(1)}, bf16[320,1536]{1,0:T(8,128)(2,1)S(1)}, u32[]{:S(2)}, u32[]{:S(2)}) %collective-permute-start.4) | collective-permute-done | bytes 983072 | tf_op jit(solution)/shard_map/ppermute | solution.py:465
  93.6 5.0 %all-gather.9.cloned.1.call-done = bf16[3136,512]{1,0:T(8,128)(2,1)} async-done(((bf16[784,512]{1,0:T(8,128)(2,1)}), bf16[3136,512]{1,0:T(8,128)(2,1)}) %all-gather.9.cloned.1.call-update) | async-done | bytes 3211280 | tf_op jit(solution)/shard_map/all_gather | solution.py:643
  103.7 8.4 %shard_map.89 = (bf16[2560,1536]{1,0:T(8,128)(2,1)}, bf16[512,1536]{1,0:T(8,128)(2,1)}) custom-call(s32[11]{0:T(128)} %stack.56.refs_0_, bf16[448,1536]{1,0:T(8,128)(2,1)} %pad_maximum_fusion.1.refs_1_, bf16[448,1536]{1,0:T(8,128)(2,1)} %copy-done.6, bf16[448,1536]{1,0:T(8,128)(2,1)} %collective-permute-done.9.refs_3_, ...), custom_call_target="tpu_custom_call" | custom-call | flops 1 | bytes 1 | tf_op jit(solution)/shard_map/pallas_call | solution.py:202
  112.2 9.5 %collective-permute-done.6.refs_4_.refs_5_ = bf16[784,512]{1,0:T(8,128)(2,1)S(1)} collective-permute-done((bf16[784,512]{1,0:T(8,128)(2,1)}, bf16[784,512]{1,0:T(8,128)(2,1)S(1)}, u32[]{:S(2)}, u32[]{:S(2)}) %collective-permute-start.6) | collective-permute-done | bytes 802848 | tf_op jit(solution)/shard_map/ppermute | solution.py:465
  122.6 3.8 %shard_map.90 = (bf16[784,512]{1,0:T(8,128)(2,1)}, bf16[784,512]{1,0:T(8,128)(2,1)}, bf16[784,512]{1,0:T(8,128)(2,1)}) custom-call(s32[9]{0:T(128)} %stack.59.refs_0_, bf16[4,784,512]{2,1,0:T(8,128)(2,1)} %bitcast.55, bf16[4,784,512]{2,1,0:T(8,128)(2,1)} %bitcast.56, bf16[4,784,512]{2,1,0:T(8,128)(2,1)} %bitcast.57, bf16[784,512]{1,0:T(8,128)(2,1)} %copy-done.3, ...), custom_call_target="tpu_custom_call" | custom-call | flops 1 | bytes 1 | tf_op jit(solution)/shard_map/pallas_call | solution.py:492
  126.4 3.8 %shard_map.91.refs_7_.second_ref = bf16[512,2048]{1,0:T(8,128)(2,1)} custom-call(s32[2]{0:T(128)} %copy-done.26, bf16[1536,2048]{1,0:T(8,128)(2,1)} %refs_1_.7, bf16[784,512]{1,0:T(8,128)(2,1)} %get-tuple-element.53.refs_2_), custom_call_target="tpu_custom_call" | custom-call | flops 1 | bytes 1 | tf_op jit(solution)/shard_map/pallas_call | solution.py:492
  132.2 4.0 %collective-permute-start.13 = (bf16[784,512]{1,0:T(8,128)(2,1)}, bf16[784,512]{1,0:T(8,128)(2,1)}, u32[]{:S(2)}, u32[]{:S(2)}) collective-permute-start(bf16[784,512]{1,0:T(8,128)(2,1)} %get-tuple-element.59), channel_id=1, source_target_pairs={{0,8},{4,12},{8,0},{12,4},{16,24},{20,28},{24,16},{28,20},{1,9},{5... | collective-permute-start | bytes 2408456 | tf_op jit(solution)/shard_map/ppermute | solution.py:465
  139.6 27.5 %shard_map.92 = (f32[512,512]{1,0:T(8,128)}, f32[512,512]{1,0:T(8,128)}, f32[8,128]{1,0:T(8,128)}) custom-call(s32[11]{0:T(128)} %stack.56.refs_0_, f32[1]{0:T(128)} %bitcast.8.refs_1_, f32[1536,1536]{1,0:T(8,128)} %refs_3_.7, bf16[784,512]{1,0:T(8,128)(2,1)} %shard_map.88.refs_9_.refs_3_.refs_4_, bf16[784,512]{1,0:T(8,128)(2,1)} %copy-done.3, ...), custom_call_target="tpu_custom_call" | custom-call | flops 1 | bytes 1 | tf_op jit(solution)/shard_map/pallas_call | solution.py:172
  167.1 11.9 %shard_map.93 = (bf16[512,1536]{1,0:T(8,128)(2,1)}, bf16[2560,512]{1,0:T(8,128)(2,1)}) custom-call(f32[8,128]{1,0:T(8,128)} %get-tuple-element.54.refs_0_.refs_2_, f32[512,512]{1,0:T(8,128)} %get-tuple-element.55.refs_1_.inverse_ref.refs_5_, bf16[512,1536]{1,0:T(8,128)(2,1)} %get-tuple-element.56.refs_2_, ...), custom_call_target="tpu_custom_call" | custom-call | flops 1 | bytes 1 | tf_op jit(solution)/shard_map/pallas_call | solution.py:240
  179.0 5.2 %collective-permute-done.13.refs_4_ = bf16[784,512]{1,0:T(8,128)(2,1)} collective-permute-done((bf16[784,512]{1,0:T(8,128)(2,1)}, bf16[784,512]{1,0:T(8,128)(2,1)}, u32[]{:S(2)}, u32[]{:S(2)}) %collective-permute-start.13) | collective-permute-done | bytes 802848 | tf_op jit(solution)/shard_map/ppermute | solution.py:465
  184.3 8.6 %collective-permute-done.14.refs_6_ = bf16[784,512]{1,0:T(8,128)(2,1)} collective-permute-done((bf16[784,512]{1,0:T(8,128)(2,1)}, bf16[784,512]{1,0:T(8,128)(2,1)}, u32[]{:S(2)}, u32[]{:S(2)}) %collective-permute-start.14) | collective-permute-done | bytes 802848 | tf_op jit(solution)/shard_map/ppermute | solution.py:465
  192.9 4.2 %shard_map.94 = (bf16[768,512]{1,0:T(8,128)(2,1)}, bf16[768,512]{1,0:T(8,128)(2,1)}, bf16[768,512]{1,0:T(8,128)(2,1)}, bf16[784,512]{1,0:T(8,128)(2,1)}) custom-call(s32[11]{0:T(128)} %stack.60.refs_0_, bf16[4,768,512]{2,1,0:T(8,128)(2,1)} %bitcast.60, bf16[4,768,512]{2,1,0:T(8,128)(2,1)} %bitcast.61, bf16[4,768,512]{2,1,0:T(8,128)(2,1)} %bitcast.62, ...), custom_call_target="tpu_custom_call" | custom-call | flops 1 | bytes 1 | tf_op jit(solution)/shard_map/pallas_call | solution.py:492
  206.2 6.8 %shard_map.96 = (bf16[512,2048]{1,0:T(8,128)(2,1)}, bf16[512,2048]{1,0:T(8,128)(2,1)}) custom-call(s32[1]{0:T(128)} %bitcast.23.flag_ref, f32[512,512]{1,0:T(8,128)} %get-tuple-element.55.refs_1_.inverse_ref.refs_5_, bf16[512,2048]{1,0:T(8,128)(2,1)} %collective-permute-done.19.first_ref, bf16[512,2048]{1,0:T(8,128)(2,1)} %shard_map.95.second_ref), custom_call_target="tpu_custom_call" | custom-call | flops 1 | bytes 1 | tf_op jit(solution)/shard_map/pallas_call | solution.py:276
  213.9 16.7 %shard_map.97 = (f32[1536,1536]{1,0:T(8,128)}, f32[1536,1536]{1,0:T(8,128)}, bf16[1536,512]{1,0:T(8,128)(2,1)}, f32[8,128]{1,0:T(8,128)}) custom-call(s32[11]{0:T(128)} %stack.56.refs_0_, f32[1]{0:T(128)} %bitcast.8.refs_1_, f32[8,128]{1,0:T(8,128)} %get-tuple-element.54.refs_0_.refs_2_, f32[1536,1536]{1,0:T(8,128)} %refs_3_.7, ...), custom_call_target="tpu_custom_call" | custom-call | flops 1 | bytes 1 | tf_op jit(solution)/shard_map/pallas_call | solution.py:401
  230.7 9.7 %collective-permute-done.20.refs_6_ = bf16[768,512]{1,0:T(8,128)(2,1)S(1)} collective-permute-done((bf16[768,512]{1,0:T(8,128)(2,1)}, bf16[768,512]{1,0:T(8,128)(2,1)S(1)}, u32[]{:S(2)}, u32[]{:S(2)}) %collective-permute-start.20) | collective-permute-done | bytes 786464 | tf_op jit(solution)/shard_map/ppermute | solution.py:465
  241.2 3.5 %shard_map.98 = (bf16[768,256]{1,0:T(8,128)(2,1)}, bf16[768,256]{1,0:T(8,128)(2,1)}, bf16[768,256]{1,0:T(8,128)(2,1)}, bf16[768,512]{1,0:T(8,128)(2,1)}) custom-call(s32[11]{0:T(128)} %stack.60.refs_0_, bf16[4,768,256]{2,1,0:T(8,128)(2,1)} %bitcast.64, bf16[4,768,256]{2,1,0:T(8,128)(2,1)} %bitcast.65, bf16[4,768,256]{2,1,0:T(8,128)(2,1)} %bitcast.66, ...), custom_call_target="tpu_custom_call" | custom-call | flops 1 | bytes 1 | tf_op jit(solution)/shard_map/pallas_call | solution.py:492
  248.1 16.2 %shard_map.99 = (f32[1536,1536]{1,0:T(8,128)}, f32[1536,1536]{1,0:T(8,128)}, bf16[1536,512]{1,0:T(8,128)(2,1)}, f32[8,128]{1,0:T(8,128)}) custom-call(s32[11]{0:T(128)} %stack.56.refs_0_, f32[1]{0:T(128)} %bitcast.8.refs_1_, f32[8,128]{1,0:T(8,128)} %get-tuple-element.54.refs_0_.refs_2_, ...), custom_call_target="tpu_custom_call", output_to_operand_aliasing={{0}: (12, {}), {1}: (13, {}), {2}: (14, {})} | custom-call | flops 1 | bytes 1 | tf_op jit(solution)/shard_map/pallas_call | solution.py:401
  271.8 11.8 %shard_map.101 = (f32[1536,1536]{1,0:T(8,128)}, f32[1536,1536]{1,0:T(8,128)}, bf16[1536,512]{1,0:T(8,128)(2,1)}, f32[8,128]{1,0:T(8,128)}) custom-call(s32[11]{0:T(128)} %stack.56.refs_0_, f32[1]{0:T(128)} %bitcast.8.refs_1_, f32[8,128]{1,0:T(8,128)} %get-tuple-element.54.refs_0_.refs_2_, ...), custom_call_target="tpu_custom_call", output_to_operand_aliasing={{0}: (12, {}), {1}: (13, {}), {2}: (14, {})} | custom-call | flops 1 | bytes 1 | tf_op jit(solution)/shard_map/pallas_call | solution.py:401
  283.6 5.4 %collective-permute-done.27.refs_1_ = bf16[768,256]{1,0:T(8,128)(2,1)S(1)} collective-permute-done((bf16[768,256]{1,0:T(8,128)(2,1)}, bf16[768,256]{1,0:T(8,128)(2,1)S(1)}, u32[]{:S(2)}, u32[]{:S(2)}) %collective-permute-start.27) | collective-permute-done | bytes 393248 | tf_op jit(solution)/shard_map/ppermute | solution.py:465
  292.2 11.7 %shard_map.103.refs_15_.refs_5_ = f32[1536,2048]{1,0:T(8,128)} custom-call(s32[11]{0:T(128)} %stack.56.refs_0_, bf16[1536,2048]{1,0:T(8,128)(2,1)} %refs_1_.7, bf16[1536,512]{1,0:T(8,128)(2,1)} %get-tuple-element.86.refs_2_.refs_14_, bf16[512,2048]{1,0:T(8,128)(2,1)} %get-tuple-element.65.refs_14_.refs_3_, bf16[512,2048]{1,0:T(8,128)(2,1)} %get-tuple-element.87.refs_4_), custom_call_target="tpu_custom_call" | custom-call | flops 1 | bytes 1 | tf_op jit(solution)/shard_map/pallas_call | solution.py:444
  304.8 11.7 %shard_map.104 = (f32[1536,1536]{1,0:T(8,128)}, f32[1536,1536]{1,0:T(8,128)}, bf16[1536,512]{1,0:T(8,128)(2,1)}, f32[8,128]{1,0:T(8,128)}) custom-call(s32[11]{0:T(128)} %stack.56.refs_0_, f32[1]{0:T(128)} %bitcast.8.refs_1_, f32[8,128]{1,0:T(8,128)} %get-tuple-element.54.refs_0_.refs_2_, ...), custom_call_target="tpu_custom_call", output_to_operand_aliasing={{0}: (12, {}), {1}: (13, {}), {2}: (14, {})} | custom-call | flops 1 | bytes 1 | tf_op jit(solution)/shard_map/pallas_call | solution.py:401
  316.6 5.8 %shard_map.105 = f32[1536,2048]{1,0:T(8,128)} custom-call(s32[11]{0:T(128)} %stack.56.refs_0_, bf16[1536,2048]{1,0:T(8,128)(2,1)} %refs_1_.7, bf16[1536,512]{1,0:T(8,128)(2,1)} %get-tuple-element.90.refs_2_, bf16[512,2048]{1,0:T(8,128)(2,1)} %get-tuple-element.65.refs_14_.refs_3_, ...), custom_call_target="tpu_custom_call", output_to_operand_aliasing={{}: (5, {})} | custom-call | flops 1 | bytes 1 | tf_op jit(solution)/shard_map/pallas_call | solution.py:444
  (170 shorter events, 68.9 us)
Async XLA Ops:
  7.2 91.4 %all-gather.9.cloned.1.call-start = ((), (), s32[]{:S(2)}) async-start(), calls=%async_computation | async-start | bytes 4014080 | tf_op jit(solution)/shard_map/all_gather | solution.py:643
  11.1 14.2 %collective-permute-start.1 = (bf16[256,1536]{1,0:T(8,128)(2,1)}, bf16[256,1536]{1,0:T(8,128)(2,1)}, u32[]{:S(2)}, u32[]{:S(2)}) collective-permute-start(bf16[256,1536]{1,0:T(8,128)(2,1)} %get-tuple-element.47), channel_id=1, source_target_pairs={{0,8},{16,24},{1,9},{17,25},{2,10},{18,26},{3,11},{19,27}} | collective-permute-start | bytes 2359304 | tf_op jit(solution)/shard_map/ppermute | solution.py:577
  32.6 134.5 %all-gather.11.cloned.1.call-start = ((), (), s32[]{:S(2)}) async-start(), calls=%async_computation.1 | async-start | bytes 3932160 | tf_op jit(solution)/shard_map/all_gather | solution.py:643
  34.0 31.7 %collective-permute-start.5 = (bf16[448,1536]{1,0:T(8,128)(2,1)}, bf16[448,1536]{1,0:T(8,128)(2,1)S(1)}, u32[]{:S(2)}, u32[]{:S(2)}) collective-permute-start(bf16[448,1536]{1,0:T(8,128)(2,1)} %pad_maximum_fusion.1.refs_1_), channel_id=1, source_target_pairs={{0,8},{4,12},{8,0},{12,4},{16,24},{20,28},{24,16},{28,20},{1,9},{5... | collective-permute-start | bytes 4128776 | tf_op jit(solution)/shard_map/ppermute | solution.py:465
  37.6 23.9 %collective-permute-start.3 = (bf16[320,1536]{1,0:T(8,128)(2,1)}, bf16[320,1536]{1,0:T(8,128)(2,1)S(1)}, u32[]{:S(2)}, u32[]{:S(2)}) collective-permute-start(bf16[320,1536]{1,0:T(8,128)(2,1)} %shard_map.86), channel_id=1, source_target_pairs={{0,16},{4,20},{8,24},{12,28},{16,0},{20,4},{24,8},{28,12},{1,17},{... | collective-permute-start | bytes 2949128 | tf_op jit(solution)/shard_map/ppermute | solution.py:465
  70.1 160.5 %all-gather.15.cloned.1.call-start = ((), (), s32[]{:S(2)}) async-start(), calls=%async_computation.3 | async-start | bytes 1966080 | tf_op jit(solution)/shard_map/all_gather | solution.py:643
  70.2 23.4 %collective-permute-start.4 = (bf16[320,1536]{1,0:T(8,128)(2,1)S(1)}, bf16[320,1536]{1,0:T(8,128)(2,1)S(1)}, u32[]{:S(2)}, u32[]{:S(2)}) collective-permute-start(bf16[320,1536]{1,0:T(8,128)(2,1)S(1)} %copy-done.8), channel_id=1, source_target_pairs={{0,8},{4,12},{8,0},{12,4},{16,24},{20,28},{24,16},{28,20},{1,9},{5... | collective-permute-start | bytes 2949128 | tf_op jit(solution)/shard_map/ppermute | solution.py:465
  72.0 31.7 %collective-permute-start.9 = (bf16[448,1536]{1,0:T(8,128)(2,1)}, bf16[448,1536]{1,0:T(8,128)(2,1)}, u32[]{:S(2)}, u32[]{:S(2)}) collective-permute-start(bf16[448,1536]{1,0:T(8,128)(2,1)} %pad_maximum_fusion.1.refs_1_), channel_id=1, source_target_pairs={{0,4},{4,0},{8,12},{12,8},{16,20},{20,16},{24,28},{28,24},{1,5},{5... | collective-permute-start | bytes 4128776 | tf_op jit(solution)/shard_map/ppermute | solution.py:465
  72.0 31.7 %collective-permute-start.10 = (bf16[448,1536]{1,0:T(8,128)(2,1)}, bf16[448,1536]{1,0:T(8,128)(2,1)}, u32[]{:S(2)}, u32[]{:S(2)}) collective-permute-start(bf16[448,1536]{1,0:T(8,128)(2,1)} %copy-done.6), channel_id=1, source_target_pairs={{0,4},{4,0},{8,12},{12,8},{16,20},{20,16},{24,28},{28,24},{1,5},{5... | collective-permute-start | bytes 4128776 | tf_op jit(solution)/shard_map/ppermute | solution.py:465
  72.5 31.2 %collective-permute-start.11 = (bf16[320,1536]{1,0:T(8,128)(2,1)S(1)}, bf16[320,1536]{1,0:T(8,128)(2,1)}, u32[]{:S(2)}, u32[]{:S(2)}) collective-permute-start(bf16[320,1536]{1,0:T(8,128)(2,1)S(1)} %copy-done.8), channel_id=1, source_target_pairs={{0,4},{4,0},{8,12},{12,8},{16,20},{20,16},{24,28},{28,24},{1,5},{5... | collective-permute-start | bytes 2949128 | tf_op jit(solution)/shard_map/ppermute | solution.py:465
  101.9 19.8 %collective-permute-start.6 = (bf16[784,512]{1,0:T(8,128)(2,1)}, bf16[784,512]{1,0:T(8,128)(2,1)S(1)}, u32[]{:S(2)}, u32[]{:S(2)}) collective-permute-start(bf16[784,512]{1,0:T(8,128)(2,1)} %shard_map.88.refs_9_.refs_3_.refs_4_), channel_id=1, source_target_pairs={{0,8},{4,12},{8,0},{12,4},{16,24},{20,28},{24,16},{28,20},{1,9},{5... | collective-permute-start | bytes 2408456 | tf_op jit(solution)/shard_map/ppermute | solution.py:465
  130.2 66.8 %collective-permute-start.18 = (bf16[512,2048]{1,0:T(8,128)(2,1)}, bf16[512,2048]{1,0:T(8,128)(2,1)}, u32[]{:S(2)}, u32[]{:S(2)}) collective-permute-start(bf16[512,2048]{1,0:T(8,128)(2,1)} %shard_map.91.refs_7_.second_ref), channel_id=1, source_target_pairs={{0,8},{16,24},{1,9},{17,25},{2,10},{18,26},{3,11},{19,27}} | collective-permute-start | bytes 6291464 | tf_op jit(solution)/shard_map/ppermute | solution.py:674
  131.5 132.8 %all-gather.13.cloned.1.call-start = ((), (), s32[]{:S(2)}) async-start(), calls=%async_computation.2 | async-start | bytes 1966080 | tf_op jit(solution)/shard_map/all_gather | solution.py:643
  132.2 52.1 %collective-permute-start.13 = (bf16[784,512]{1,0:T(8,128)(2,1)}, bf16[784,512]{1,0:T(8,128)(2,1)}, u32[]{:S(2)}, u32[]{:S(2)}) collective-permute-start(bf16[784,512]{1,0:T(8,128)(2,1)} %get-tuple-element.59), channel_id=1, source_target_pairs={{0,8},{4,12},{8,0},{12,4},{16,24},{20,28},{24,16},{28,20},{1,9},{5... | collective-permute-start | bytes 2408456 | tf_op jit(solution)/shard_map/ppermute | solution.py:465
  136.2 56.7 %collective-permute-start.14 = (bf16[784,512]{1,0:T(8,128)(2,1)}, bf16[784,512]{1,0:T(8,128)(2,1)}, u32[]{:S(2)}, u32[]{:S(2)}) collective-permute-start(bf16[784,512]{1,0:T(8,128)(2,1)} %get-tuple-element.60), channel_id=1, source_target_pairs={{0,8},{4,12},{8,0},{12,4},{16,24},{20,28},{24,16},{28,20},{1,9},{5... | collective-permute-start | bytes 2408456 | tf_op jit(solution)/shard_map/ppermute | solution.py:465
  203.7 26.9 %collective-permute-start.15 = (bf16[768,512]{1,0:T(8,128)(2,1)}, bf16[768,512]{1,0:T(8,128)(2,1)}, u32[]{:S(2)}, u32[]{:S(2)}) collective-permute-start(bf16[768,512]{1,0:T(8,128)(2,1)} %get-tuple-element.61), channel_id=1, source_target_pairs={{0,8},{4,12},{8,0},{12,4},{16,24},{20,28},{24,16},{28,20},{1,9},{5... | collective-permute-start | bytes 2359304 | tf_op jit(solution)/shard_map/ppermute | solution.py:465
  203.7 36.6 %collective-permute-start.20 = (bf16[768,512]{1,0:T(8,128)(2,1)}, bf16[768,512]{1,0:T(8,128)(2,1)S(1)}, u32[]{:S(2)}, u32[]{:S(2)}) collective-permute-start(bf16[768,512]{1,0:T(8,128)(2,1)} %get-tuple-element.67), channel_id=1, source_target_pairs={{0,8},{4,12},{8,0},{12,4},{16,24},{20,28},{24,16},{28,20},{1,9},{5... | collective-permute-start | bytes 2359304 | tf_op jit(solution)/shard_map/ppermute | solution.py:465
  205.9 40.9 %collective-permute-start.22 = (bf16[768,512]{1,0:T(8,128)(2,1)S(1)}, bf16[768,512]{1,0:T(8,128)(2,1)}, u32[]{:S(2)}, u32[]{:S(2)}) collective-permute-start(bf16[768,512]{1,0:T(8,128)(2,1)S(1)} %copy-done.11), channel_id=1, source_target_pairs={{0,4},{4,0},{8,12},{12,8},{16,20},{20,16},{24,28},{28,24},{1,5},{5... | collective-permute-start | bytes 2359304 | tf_op jit(solution)/shard_map/ppermute | solution.py:465
  244.7 19.7 %collective-permute-start.21 = (bf16[768,256]{1,0:T(8,128)(2,1)}, bf16[768,256]{1,0:T(8,128)(2,1)S(1)}, u32[]{:S(2)}, u32[]{:S(2)}) collective-permute-start(bf16[768,256]{1,0:T(8,128)(2,1)} %get-tuple-element.68), channel_id=1, source_target_pairs={{0,8},{4,12},{8,0},{12,4},{16,24},{20,28},{24,16},{28,20},{1,9},{5... | collective-permute-start | bytes 1179656 | tf_op jit(solution)/shard_map/ppermute | solution.py:465
  245.0 19.9 %collective-permute-start.24 = (bf16[768,256]{1,0:T(8,128)(2,1)}, bf16[768,256]{1,0:T(8,128)(2,1)S(1)}, u32[]{:S(2)}, u32[]{:S(2)}) collective-permute-start(bf16[768,256]{1,0:T(8,128)(2,1)} %get-tuple-element.75), channel_id=1, source_target_pairs={{0,8},{4,12},{8,0},{12,4},{16,24},{20,28},{24,16},{28,20},{1,9},{5... | collective-permute-start | bytes 1179656 | tf_op jit(solution)/shard_map/ppermute | solution.py:465
  246.7 24.2 %collective-permute-start.28 = (bf16[768,256]{1,0:T(8,128)(2,1)}, bf16[768,256]{1,0:T(8,128)(2,1)S(1)}, u32[]{:S(2)}, u32[]{:S(2)}) collective-permute-start(bf16[768,256]{1,0:T(8,128)(2,1)} %get-tuple-element.73.refs_15_), channel_id=1, source_target_pairs={{0,4},{4,0},{8,12},{12,8},{16,20},{20,16},{24,28},{28,24},{1,5},{5... | collective-permute-start | bytes 1179656 | tf_op jit(solution)/shard_map/ppermute | solution.py:465
  268.9 14.7 %collective-permute-start.25 = (bf16[768,256]{1,0:T(8,128)(2,1)}, bf16[768,256]{1,0:T(8,128)(2,1)S(1)}, u32[]{:S(2)}, u32[]{:S(2)}) collective-permute-start(bf16[768,256]{1,0:T(8,128)(2,1)} %get-tuple-element.76), channel_id=1, source_target_pairs={{0,8},{4,12},{8,0},{12,4},{16,24},{20,28},{24,16},{28,20},{1,9},{5... | collective-permute-start | bytes 1179656 | tf_op jit(solution)/shard_map/ppermute | solution.py:465
  269.1 19.9 %collective-permute-start.27 = (bf16[768,256]{1,0:T(8,128)(2,1)}, bf16[768,256]{1,0:T(8,128)(2,1)S(1)}, u32[]{:S(2)}, u32[]{:S(2)}) collective-permute-start(bf16[768,256]{1,0:T(8,128)(2,1)} %get-tuple-element.78), channel_id=1, source_target_pairs={{0,8},{4,12},{8,0},{12,4},{16,24},{20,28},{24,16},{28,20},{1,9},{5... | collective-permute-start | bytes 1179656 | tf_op jit(solution)/shard_map/ppermute | solution.py:465
  270.9 33.0 %collective-permute-start.26 = (bf16[768,256]{1,0:T(8,128)(2,1)}, bf16[768,256]{1,0:T(8,128)(2,1)S(1)}, u32[]{:S(2)}, u32[]{:S(2)}) collective-permute-start(bf16[768,256]{1,0:T(8,128)(2,1)} %get-tuple-element.77.refs_15_), channel_id=1, source_target_pairs={{0,4},{4,0},{8,12},{12,8},{16,20},{20,16},{24,28},{28,24},{1,5},{5... | collective-permute-start | bytes 1179656 | tf_op jit(solution)/shard_map/ppermute | solution.py:465
  (41 other events, 206.9 us)
Sparse Core Ops, SparseCore 0:
  32.8 65.8 all-gather.8
  100.2 62.1 all-gather.10
  163.9 35.7 all-gather.14
  203.3 35.8 all-gather.12

commit v12 on v10

--- a/solution.py
+++ b/solution.py
@@ -614,14 +614,14 @@
         ],
         0,
     )
-    away_rows = copied([(packed, (CAP, width), [1, 0])], [front, moved])[0]
+    away_rows = copied([(packed, (CAP, width), [1, 0])], [front])[0]
     incoming = swapped(away_rows, group)
     outgoing = jnp.concatenate([packed[:CAP], lead_factor], 0)
     quarter = jnp.concatenate([packed[:CAP], incoming, lead_factor], 0)
     across_own = gather_members(outgoing, bits)
     across_other = gather_members(incoming, bits)
 
-    ends = [end for end in (LEAD, 2 * LEAD, 2 * LEAD + ROWS) if end < width] + [width]
+    ends = [*range(LEAD, width, LEAD), width]
     chunks = list(zip([0, *ends], ends))
     rows = quarter.shape[0]
     later = [
@@ -630,7 +630,7 @@
     parts = [first_part, *copied(later, [across_own[1]])]
     spread = [lax.all_gather(part, "fac") for part in parts]
     rows = first_part.shape[0]
-    earlier = [across_other[1], *parts[1:]]
+    earlier = [across_other[1], moved, *parts[1:]]
     lead = copied([(spread[0], (None, rows, LEAD), [0, 0, 0])], earlier)[0]
     slots = [member, column, member * width] + order + [member] + [0] * (group - 1)
     assert len(slots) == PLACES + 2 * group
@@ -657,7 +657,7 @@
             requests = member_blocks(spread[number + 1], member, group)
         pieces, sent = exchange_members(spread[number], sent, bits, requests, [token])
         if number == 0:
-            high, low = solve_lead(flag, inverse, moved, near, spread[2:3])
+            high, low = solve_lead(flag, inverse, moved, near, [])
         *results, token = finish_rows(
             begin,
             slots,

time: 316 us -> 313 us (level)
  Pallas kernels: 159 us -> 148 us
  waiting for transfers between devices: 87.6 us -> 98 us
  local copies, waits for them, and re-layouts: 16.3 us -> 12.7 us
    ppermute x27 -> x23, waiting for transfers between devices: 41.5 us -> 96.7 us  [swapped(): lax.ppermute(value, 'tok', [(source, source ^ mask) for source in range(s...]
    ppermute x1, waiting for transfers between devices: 37.7 us -> 0.01 us  [local(): moved = lax.ppermute(near, 'tok', down_pairs(bits - 1, group))]
    pallas_call x4 -> x3, Pallas kernels: 67 us -> 58.9 us  [finish_rows(): pl.pallas_call(lambda *refs: finish_kernel(count, gram_steps, begin, unre...]
    all_gather x4 -> x3, waiting for transfers between devices: 7.05 us -> 0.04 us  [local(): spread = [lax.all_gather(part, 'fac') for part in parts]]
    unnamed x55 -> x51, local copies, waits for them, and re-layouts: 10.1 us -> 7.28 us
    pallas_call x10 -> x9, Pallas kernels: 33.9 us -> 31.9 us  [copied(): pl.pallas_call(lambda *refs: copy_kernel(len(arrays), *refs), grid_spec=p...]
    ppermute x27 -> x23, starting transfers between devices: 15.8 us -> 14.9 us  [swapped(): lax.ppermute(value, 'tok', [(source, source ^ mask) for source in range(s...]
  transfers between devices with their start and end apart: 35 -> 30, of which waited for: 11 -> 10; matrix products, arithmetic and copies ran while one was open for 4% -> 4% of each run, Pallas kernels for 45% -> 40%
where the time goes in v12:
time: 313 us; the launch traced here: 311 us
  Pallas kernels  148 us (47%)
  waiting for transfers between devices  98 us (31%)
  starting transfers between devices  22.6 us (7%)
  between operations  21.1 us (7%)
  local copies, waits for them, and re-layouts  12.7 us (4%)
  other arithmetic  7.38 us (2%)
    ppermute x23, waiting for transfers between devices, swapped(): lax.ppermute(value, 'tok', [(source, source ^ mask) for source in range(s...  96.7 us
    pallas_call x3, Pallas kernels, finish_rows(): pl.pallas_call(lambda *refs: finish_kernel(count, gram_steps, begin, unre...  58.9 us
    pallas_call x9, Pallas kernels, copied(): pl.pallas_call(lambda *refs: copy_kernel(len(arrays), *refs), grid_spec=p...  31.9 us
    pallas_call x1, Pallas kernels, factor_lead(): pl.pallas_call(lambda *refs: factor_kernel(len(lead), *refs), grid=(1,),...  27.5 us
    ppermute x23, starting transfers between devices, swapped(): lax.ppermute(value, 'tok', [(source, source ^ mask) for source in range(s...  14.9 us
    pallas_call x1, Pallas kernels, panel_columns(): pl.pallas_call(lambda *refs: panel_kernel(count, *refs), grid=(width // c...  11.8 us
    pallas_call x1, Pallas kernels, stacked(): pl.pallas_call(lambda *refs: stack_kernel(count, *refs), grid=(width // c...  8.28 us
    unnamed x51, local copies, waits for them, and re-layouts  7.28 us
  transfers between devices with their start and end apart: 30, of which 10 were waited for; matrix products, arithmetic and copies ran while one was open for 4% of the time, Pallas kernels for 40%

profile of v12, /device:TPU:2, one launch (start us, length us, event | category | flops | bytes accessed | tf_op | source)
XLA Modules:
  0.0 311.4 jit_solution(11444566628482903311)
XLA Ops:
  7.2 3.9 %shard_map.85 = (bf16[256,1536]{1,0:T(8,128)(2,1)}, bf16[256,1536]{1,0:T(8,128)(2,1)}) custom-call(s32[4]{0:T(128)} %constant.91.clone.1.refs_0_, f32[1536,1536]{1,0:T(8,128)} %refs_3_.5, f32[1536,1536]{1,0:T(8,128)} %refs_3_.5), custom_call_target="tpu_custom_call" | custom-call | flops 1 | bytes 1 | tf_op jit(solution)/shard_map/pallas_call | solution.py:485
  28.0 3.1 %collective-permute-done.refs_2_ = bf16[336,512]{1,0:T(8,128)(2,1)S(1)} collective-permute-done((bf16[336,512]{1,0:T(8,128)(2,1)}, bf16[336,512]{1,0:T(8,128)(2,1)S(1)}, u32[]{:S(2)}, u32[]{:S(2)}) %collective-permute-start) | collective-permute-done | bytes 344096 | tf_op jit(solution)/shard_map/ppermute | solution.py:458
  34.9 2.9 shard_map.86
  39.3 21.1 %collective-permute-done.3.refs_5_ = bf16[320,1536]{1,0:T(8,128)(2,1)S(1)} collective-permute-done((bf16[320,1536]{1,0:T(8,128)(2,1)}, bf16[320,1536]{1,0:T(8,128)(2,1)S(1)}, u32[]{:S(2)}, u32[]{:S(2)}) %collective-permute-start.3) | collective-permute-done | bytes 983072 | tf_op jit(solution)/shard_map/ppermute | solution.py:458
  62.2 3.6 %collective-permute-done.6.refs_3_.refs_2_ = bf16[448,1536]{1,0:T(8,128)(2,1)S(1)} collective-permute-done((bf16[448,1536]{1,0:T(8,128)(2,1)}, bf16[448,1536]{1,0:T(8,128)(2,1)S(1)}, u32[]{:S(2)}, u32[]{:S(2)}) %collective-permute-start.6) | collective-permute-done | bytes 1376288 | tf_op jit(solution)/shard_map/ppermute | solution.py:458
  66.9 3.3 %shard_map.88 = (bf16[768,512]{1,0:T(8,128)(2,1)}, bf16[768,512]{1,0:T(8,128)(2,1)}) custom-call(s32[4]{0:T(128)} %constant.93.clone.1.refs_0_, bf16[768,1536]{1,0:T(8,128)(2,1)} %pad_maximum_fusion.refs_1_.refs_2_, bf16[768,1536]{1,0:T(8,128)(2,1)} %pad_maximum_fusion.refs_1_.refs_2_, bf16[448,1536]{1,0:T(8,128)(2,1)} %copy-done.5), custom_call_target="tpu_custom_call" | custom-call | flops 1 | bytes 1 | tf_op jit(solution)/shard_map/pallas_call | solution.py:485
  71.4 3.8 %shard_map.87.second_ref = bf16[512,2048]{1,0:T(8,128)(2,1)} custom-call(s32[2]{0:T(128)} %broadcast_5_refs_0_.2.refs_0_, bf16[1536,2048]{1,0:T(8,128)(2,1)} %refs_4_.5, bf16[256,1536]{1,0:T(8,128)(2,1)} %get-tuple-element.39.refs_2_), custom_call_target="tpu_custom_call" | custom-call | flops 1 | bytes 1 | tf_op jit(solution)/shard_map/pallas_call | solution.py:485
  76.6 4.0 %collective-permute-start.4 = (bf16[320,1536]{1,0:T(8,128)(2,1)S(1)}, bf16[320,1536]{1,0:T(8,128)(2,1)}, u32[]{:S(2)}, u32[]{:S(2)}) collective-permute-start(bf16[320,1536]{1,0:T(8,128)(2,1)S(1)} %copy-done.8), channel_id=1, source_target_pairs={{0,8},{4,12},{8,0},{12,4},{16,24},{20,28},{24,16},{28,20},{1,9},{5... | collective-permute-start | bytes 2949128 | tf_op jit(solution)/shard_map/ppermute | solution.py:458
  81.0 40.9 %collective-permute-done.4.refs_2_.refs_6_ = bf16[320,1536]{1,0:T(8,128)(2,1)} collective-permute-done((bf16[320,1536]{1,0:T(8,128)(2,1)S(1)}, bf16[320,1536]{1,0:T(8,128)(2,1)}, u32[]{:S(2)}, u32[]{:S(2)}) %collective-permute-start.4) | collective-permute-done | bytes 983072 | tf_op jit(solution)/shard_map/ppermute | solution.py:458
  126.0 8.3 %shard_map.90 = (bf16[2560,1536]{1,0:T(8,128)(2,1)}, bf16[512,1536]{1,0:T(8,128)(2,1)}) custom-call(s32[11]{0:T(128)} %stack.52.refs_0_, bf16[448,1536]{1,0:T(8,128)(2,1)} %pad_maximum_fusion.1.refs_1_, bf16[448,1536]{1,0:T(8,128)(2,1)} %copy-done.5, bf16[448,1536]{1,0:T(8,128)(2,1)} %collective-permute-done.10.refs_3_, ...), custom_call_target="tpu_custom_call" | custom-call | flops 1 | bytes 1 | tf_op jit(solution)/shard_map/pallas_call | solution.py:202
  134.3 3.4 %shard_map.91.refs_5_.second_ref = bf16[512,2048]{1,0:T(8,128)(2,1)} custom-call(s32[1]{0:T(128)} %bitcast.17.flag_ref, bf16[512,2048]{1,0:T(8,128)(2,1)} %collective-permute-done.5.refs_3_.first_ref, bf16[512,2048]{1,0:T(8,128)(2,1)} %shard_map.87.second_ref, bf16[2560,1536]{1,0:T(8,128)(2,1)} %get-tuple-element.42.refs_0_.refs_3_.refs_9_), custom_call_target="tpu_custom_call" | custom-call | flops 1 | bytes 1 | tf_op jit(solution)/shard_map/pallas_call | solution.py:505
  137.6 3.7 %collective-permute-start.14 = (bf16[512,2048]{1,0:T(8,128)(2,1)}, bf16[512,2048]{1,0:T(8,128)(2,1)}, u32[]{:S(2)}, u32[]{:S(2)}) collective-permute-start(bf16[512,2048]{1,0:T(8,128)(2,1)} %shard_map.91.refs_5_.second_ref), channel_id=1, source_target_pairs={{0,4},{8,12},{16,20},{24,28},{1,5},{9,13},{17,21},{25,29},{2,6},{1... | collective-permute-start | bytes 6291464 | tf_op jit(solution)/shard_map/ppermute | solution.py:643
  141.3 4.5 %collective-permute-done.7.refs_4_.refs_5_ = bf16[784,512]{1,0:T(8,128)(2,1)S(1)} collective-permute-done((bf16[784,512]{1,0:T(8,128)(2,1)}, bf16[784,512]{1,0:T(8,128)(2,1)S(1)}, u32[]{:S(2)}, u32[]{:S(2)}) %collective-permute-start.7) | collective-permute-done | bytes 802848 | tf_op jit(solution)/shard_map/ppermute | solution.py:458
  146.7 3.9 %shard_map.92 = (bf16[784,512]{1,0:T(8,128)(2,1)}, bf16[784,512]{1,0:T(8,128)(2,1)}, bf16[784,512]{1,0:T(8,128)(2,1)}) custom-call(s32[9]{0:T(128)} %stack.55.refs_0_, bf16[4,784,512]{2,1,0:T(8,128)(2,1)} %bitcast.51, bf16[4,784,512]{2,1,0:T(8,128)(2,1)} %bitcast.52, bf16[4,784,512]{2,1,0:T(8,128)(2,1)} %bitcast.53, bf16[784,512]{1,0:T(8,128)(2,1)} %copy-done.3, ...), custom_call_target="tpu_custom_call" | custom-call | flops 1 | bytes 1 | tf_op jit(solution)/shard_map/pallas_call | solution.py:485
  155.2 27.5 %shard_map.93 = (f32[512,512]{1,0:T(8,128)}, f32[512,512]{1,0:T(8,128)}, f32[8,128]{1,0:T(8,128)}) custom-call(s32[11]{0:T(128)} %stack.52.refs_0_, f32[1]{0:T(128)} %bitcast.8.refs_1_, f32[1536,1536]{1,0:T(8,128)} %refs_3_.5, bf16[784,512]{1,0:T(8,128)(2,1)} %shard_map.89.refs_9_.refs_3_.refs_4_, bf16[784,512]{1,0:T(8,128)(2,1)} %copy-done.3, ...), custom_call_target="tpu_custom_call" | custom-call | flops 1 | bytes 1 | tf_op jit(solution)/shard_map/pallas_call | solution.py:172
  182.7 11.8 %shard_map.94 = (bf16[512,1536]{1,0:T(8,128)(2,1)}, bf16[2560,512]{1,0:T(8,128)(2,1)}) custom-call(f32[8,128]{1,0:T(8,128)} %get-tuple-element.44.refs_0_.refs_2_, f32[512,512]{1,0:T(8,128)} %get-tuple-element.45.refs_1_.inverse_ref.refs_6_, bf16[512,1536]{1,0:T(8,128)(2,1)} %get-tuple-element.46.refs_2_, ...), custom_call_target="tpu_custom_call" | custom-call | flops 1 | bytes 1 | tf_op jit(solution)/shard_map/pallas_call | solution.py:240
  195.4 4.2 %shard_map.96 = (bf16[768,512]{1,0:T(8,128)(2,1)}, bf16[768,512]{1,0:T(8,128)(2,1)}, bf16[768,512]{1,0:T(8,128)(2,1)}, bf16[784,512]{1,0:T(8,128)(2,1)}) custom-call(s32[11]{0:T(128)} %stack.56.refs_0_, bf16[4,768,512]{2,1,0:T(8,128)(2,1)} %bitcast.56, bf16[4,768,512]{2,1,0:T(8,128)(2,1)} %bitcast.57, bf16[4,768,512]{2,1,0:T(8,128)(2,1)} %bitcast.58, ...), custom_call_target="tpu_custom_call" | custom-call | flops 1 | bytes 1 | tf_op jit(solution)/shard_map/pallas_call | solution.py:485
  202.2 6.8 %shard_map.95 = (bf16[512,2048]{1,0:T(8,128)(2,1)}, bf16[512,2048]{1,0:T(8,128)(2,1)}) custom-call(s32[1]{0:T(128)} %bitcast.19.flag_ref, f32[512,512]{1,0:T(8,128)} %get-tuple-element.45.refs_1_.inverse_ref.refs_6_, bf16[512,2048]{1,0:T(8,128)(2,1)} %collective-permute-done.14.first_ref, bf16[512,2048]{1,0:T(8,128)(2,1)} %shard_map.91.refs_5_.second_ref), custom_call_target="tpu_custom_call" | custom-call | flops 1 | bytes 1 | tf_op jit(solution)/shard_map/pallas_call | solution.py:276
  210.0 20.7 %shard_map.97 = (f32[1536,1536]{1,0:T(8,128)}, f32[1536,1536]{1,0:T(8,128)}, f32[1536,2048]{1,0:T(8,128)}, f32[8,128]{1,0:T(8,128)}) custom-call(s32[11]{0:T(128)} %stack.52.refs_0_, f32[1]{0:T(128)} %bitcast.8.refs_1_, f32[8,128]{1,0:T(8,128)} %get-tuple-element.44.refs_0_.refs_2_, f32[1536,1536]{1,0:T(8,128)} %refs_3_.5, bf16[1536,2048]{1,0:T(8,128)(2,1)} %refs_4_.5, ...), custom_call_target="tpu_custom_call" | custom-call | flops 1 | bytes 1 | tf_op jit(solution)/shard_map/pallas_call | solution.py:431
  230.7 6.0 %collective-permute-done.20.refs_6_ = bf16[768,512]{1,0:T(8,128)(2,1)S(1)} collective-permute-done((bf16[768,512]{1,0:T(8,128)(2,1)}, bf16[768,512]{1,0:T(8,128)(2,1)S(1)}, u32[]{:S(2)}, u32[]{:S(2)}) %collective-permute-start.20) | collective-permute-done | bytes 786464 | tf_op jit(solution)/shard_map/ppermute | solution.py:458
  237.6 4.2 %shard_map.98 = (bf16[768,512]{1,0:T(8,128)(2,1)}, bf16[768,512]{1,0:T(8,128)(2,1)}, bf16[768,512]{1,0:T(8,128)(2,1)}, bf16[768,512]{1,0:T(8,128)(2,1)}) custom-call(s32[11]{0:T(128)} %stack.56.refs_0_, bf16[4,768,512]{2,1,0:T(8,128)(2,1)} %bitcast.60, bf16[4,768,512]{2,1,0:T(8,128)(2,1)} %bitcast.61, bf16[4,768,512]{2,1,0:T(8,128)(2,1)} %bitcast.62, ...), custom_call_target="tpu_custom_call" | custom-call | flops 1 | bytes 1 | tf_op jit(solution)/shard_map/pallas_call | solution.py:485
  245.2 19.1 %shard_map.99 = (f32[1536,1536]{1,0:T(8,128)}, f32[1536,1536]{1,0:T(8,128)}, f32[1536,2048]{1,0:T(8,128)}, f32[8,128]{1,0:T(8,128)}) custom-call(s32[11]{0:T(128)} %stack.52.refs_0_, f32[1]{0:T(128)} %bitcast.8.refs_1_, f32[8,128]{1,0:T(8,128)} %get-tuple-element.44.refs_0_.refs_2_, ...), custom_call_target="tpu_custom_call", output_to_operand_aliasing={{0}: (14, {}), {1}: (15, {}), {2}: (16, {})} | custom-call | flops 1 | bytes 1 | tf_op jit(solution)/shard_map/pallas_call | solution.py:431
  264.3 14.5 %collective-permute-done.23.refs_1_ = bf16[768,512]{1,0:T(8,128)(2,1)S(1)} collective-permute-done((bf16[768,512]{1,0:T(8,128)(2,1)}, bf16[768,512]{1,0:T(8,128)(2,1)S(1)}, u32[]{:S(2)}, u32[]{:S(2)}) %collective-permute-start.23) | collective-permute-done | bytes 786464 | tf_op jit(solution)/shard_map/ppermute | solution.py:458
  285.8 19.0 %shard_map.101 = (f32[1536,1536]{1,0:T(8,128)}, f32[1536,1536]{1,0:T(8,128)}, f32[1536,2048]{1,0:T(8,128)}, f32[8,128]{1,0:T(8,128)}) custom-call(s32[11]{0:T(128)} %stack.52.refs_0_, f32[1]{0:T(128)} %bitcast.8.refs_1_, f32[8,128]{1,0:T(8,128)} %get-tuple-element.44.refs_0_.refs_2_, ...), custom_call_target="tpu_custom_call", output_to_operand_aliasing={{0}: (14, {}), {1}: (15, {}), {2}: (16, {})} | custom-call | flops 1 | bytes 1 | tf_op jit(solution)/shard_map/pallas_call | solution.py:431
  (145 shorter events, 46.1 us)
Async XLA Ops:
  7.2 114.7 %all-gather.7.cloned.1.call-start = ((), (), s32[]{:S(2)}) async-start(), calls=%async_computation | async-start | bytes 4014080 | tf_op jit(solution)/shard_map/all_gather | solution.py:631
  11.1 14.2 %collective-permute-start.1 = (bf16[256,1536]{1,0:T(8,128)(2,1)}, bf16[256,1536]{1,0:T(8,128)(2,1)}, u32[]{:S(2)}, u32[]{:S(2)}) collective-permute-start(bf16[256,1536]{1,0:T(8,128)(2,1)} %get-tuple-element.38), channel_id=1, source_target_pairs={{0,8},{16,24},{1,9},{17,25},{2,10},{18,26},{3,11},{19,27}} | collective-permute-start | bytes 2359304 | tf_op jit(solution)/shard_map/ppermute | solution.py:562
  20.8 10.3 %collective-permute-start = (bf16[336,512]{1,0:T(8,128)(2,1)}, bf16[336,512]{1,0:T(8,128)(2,1)S(1)}, u32[]{:S(2)}, u32[]{:S(2)}) collective-permute-start(bf16[336,512]{1,0:T(8,128)(2,1)} %pad_maximum_fusion.3), channel_id=1, source_target_pairs={{0,16},{4,20},{8,24},{12,28},{16,0},{20,4},{24,8},{28,12},{1,17},{... | collective-permute-start | bytes 1032200 | tf_op jit(solution)/shard_map/ppermute | solution.py:458
  32.9 149.8 %all-gather.9.cloned.1.call-start = ((), (), s32[]{:S(2)}) async-start(), calls=%async_computation.1 | async-start | bytes 3932160 | tf_op jit(solution)/shard_map/all_gather | solution.py:631
  34.2 31.6 %collective-permute-start.6 = (bf16[448,1536]{1,0:T(8,128)(2,1)}, bf16[448,1536]{1,0:T(8,128)(2,1)S(1)}, u32[]{:S(2)}, u32[]{:S(2)}) collective-permute-start(bf16[448,1536]{1,0:T(8,128)(2,1)} %pad_maximum_fusion.1.refs_1_), channel_id=1, source_target_pairs={{0,8},{4,12},{8,0},{12,4},{16,24},{20,28},{24,16},{28,20},{1,9},{5... | collective-permute-start | bytes 4128776 | tf_op jit(solution)/shard_map/ppermute | solution.py:458
  37.8 22.6 %collective-permute-start.3 = (bf16[320,1536]{1,0:T(8,128)(2,1)}, bf16[320,1536]{1,0:T(8,128)(2,1)S(1)}, u32[]{:S(2)}, u32[]{:S(2)}) collective-permute-start(bf16[320,1536]{1,0:T(8,128)(2,1)} %shard_map.86), channel_id=1, source_target_pairs={{0,16},{4,20},{8,24},{12,28},{16,0},{20,4},{24,8},{28,12},{1,17},{... | collective-permute-start | bytes 2949128 | tf_op jit(solution)/shard_map/ppermute | solution.py:458
  70.2 160.5 %all-gather.11.cloned.1.call-start = ((), (), s32[]{:S(2)}) async-start(), calls=%async_computation.2 | async-start | bytes 3932160 | tf_op jit(solution)/shard_map/all_gather | solution.py:631
  75.3 46.7 %collective-permute-start.5 = (bf16[512,2048]{1,0:T(8,128)(2,1)}, bf16[512,2048]{1,0:T(8,128)(2,1)}, u32[]{:S(2)}, u32[]{:S(2)}) collective-permute-start(bf16[512,2048]{1,0:T(8,128)(2,1)} %shard_map.87.second_ref), channel_id=1, source_target_pairs={{0,8},{16,24},{1,9},{17,25},{2,10},{18,26},{3,11},{19,27}} | collective-permute-start | bytes 6291464 | tf_op jit(solution)/shard_map/ppermute | solution.py:592
  76.6 45.4 %collective-permute-start.4 = (bf16[320,1536]{1,0:T(8,128)(2,1)S(1)}, bf16[320,1536]{1,0:T(8,128)(2,1)}, u32[]{:S(2)}, u32[]{:S(2)}) collective-permute-start(bf16[320,1536]{1,0:T(8,128)(2,1)S(1)} %copy-done.8), channel_id=1, source_target_pairs={{0,8},{4,12},{8,0},{12,4},{16,24},{20,28},{24,16},{28,20},{1,9},{5... | collective-permute-start | bytes 2949128 | tf_op jit(solution)/shard_map/ppermute | solution.py:458
  80.5 45.4 %collective-permute-start.10 = (bf16[448,1536]{1,0:T(8,128)(2,1)}, bf16[448,1536]{1,0:T(8,128)(2,1)}, u32[]{:S(2)}, u32[]{:S(2)}) collective-permute-start(bf16[448,1536]{1,0:T(8,128)(2,1)} %pad_maximum_fusion.1.refs_1_), channel_id=1, source_target_pairs={{0,4},{4,0},{8,12},{12,8},{16,20},{20,16},{24,28},{28,24},{1,5},{5... | collective-permute-start | bytes 4128776 | tf_op jit(solution)/shard_map/ppermute | solution.py:458
  80.5 45.5 %collective-permute-start.11 = (bf16[448,1536]{1,0:T(8,128)(2,1)S(1)}, bf16[448,1536]{1,0:T(8,128)(2,1)}, u32[]{:S(2)}, u32[]{:S(2)}) collective-permute-start(bf16[448,1536]{1,0:T(8,128)(2,1)S(1)} %copy-done.6), channel_id=1, source_target_pairs={{0,4},{4,0},{8,12},{12,8},{16,20},{20,16},{24,28},{28,24},{1,5},{5... | collective-permute-start | bytes 4128776 | tf_op jit(solution)/shard_map/ppermute | solution.py:458
  81.0 44.9 %collective-permute-start.12 = (bf16[320,1536]{1,0:T(8,128)(2,1)S(1)}, bf16[320,1536]{1,0:T(8,128)(2,1)}, u32[]{:S(2)}, u32[]{:S(2)}) collective-permute-start(bf16[320,1536]{1,0:T(8,128)(2,1)S(1)} %copy-done.8), channel_id=1, source_target_pairs={{0,4},{4,0},{8,12},{12,8},{16,20},{20,16},{24,28},{28,24},{1,5},{5... | collective-permute-start | bytes 2949128 | tf_op jit(solution)/shard_map/ppermute | solution.py:458
  125.3 20.5 %collective-permute-start.7 = (bf16[784,512]{1,0:T(8,128)(2,1)}, bf16[784,512]{1,0:T(8,128)(2,1)S(1)}, u32[]{:S(2)}, u32[]{:S(2)}) collective-permute-start(bf16[784,512]{1,0:T(8,128)(2,1)} %shard_map.89.refs_9_.refs_3_.refs_4_), channel_id=1, source_target_pairs={{0,8},{4,12},{8,0},{12,4},{16,24},{20,28},{24,16},{28,20},{1,9},{5... | collective-permute-start | bytes 2408456 | tf_op jit(solution)/shard_map/ppermute | solution.py:458
  137.6 64.6 %collective-permute-start.14 = (bf16[512,2048]{1,0:T(8,128)(2,1)}, bf16[512,2048]{1,0:T(8,128)(2,1)}, u32[]{:S(2)}, u32[]{:S(2)}) collective-permute-start(bf16[512,2048]{1,0:T(8,128)(2,1)} %shard_map.91.refs_5_.second_ref), channel_id=1, source_target_pairs={{0,4},{8,12},{16,20},{24,28},{1,5},{9,13},{17,21},{25,29},{2,6},{1... | collective-permute-start | bytes 6291464 | tf_op jit(solution)/shard_map/ppermute | solution.py:643
  141.3 13.8 %collective-permute-start.8 = (bf16[784,512]{1,0:T(8,128)(2,1)S(1)}, bf16[784,512]{1,0:T(8,128)(2,1)}, u32[]{:S(2)}, u32[]{:S(2)}) collective-permute-start(bf16[784,512]{1,0:T(8,128)(2,1)S(1)} %copy-done.2), channel_id=1, source_target_pairs={{0,4},{4,0},{8,12},{12,8},{16,20},{20,16},{24,28},{28,24},{1,5},{5... | collective-permute-start | bytes 2408456 | tf_op jit(solution)/shard_map/ppermute | solution.py:458
  150.6 43.9 %collective-permute-start.15 = (bf16[784,512]{1,0:T(8,128)(2,1)}, bf16[784,512]{1,0:T(8,128)(2,1)}, u32[]{:S(2)}, u32[]{:S(2)}) collective-permute-start(bf16[784,512]{1,0:T(8,128)(2,1)} %get-tuple-element.50), channel_id=1, source_target_pairs={{0,8},{4,12},{8,0},{12,4},{16,24},{20,28},{24,16},{28,20},{1,9},{5... | collective-permute-start | bytes 2408456 | tf_op jit(solution)/shard_map/ppermute | solution.py:458
  150.9 43.6 %collective-permute-start.16 = (bf16[784,512]{1,0:T(8,128)(2,1)}, bf16[784,512]{1,0:T(8,128)(2,1)S(1)}, u32[]{:S(2)}, u32[]{:S(2)}) collective-permute-start(bf16[784,512]{1,0:T(8,128)(2,1)} %get-tuple-element.51), channel_id=1, source_target_pairs={{0,8},{4,12},{8,0},{12,4},{16,24},{20,28},{24,16},{28,20},{1,9},{5... | collective-permute-start | bytes 2408456 | tf_op jit(solution)/shard_map/ppermute | solution.py:458
  155.1 53.9 %collective-permute-start.18 = (bf16[784,512]{1,0:T(8,128)(2,1)}, bf16[784,512]{1,0:T(8,128)(2,1)}, u32[]{:S(2)}, u32[]{:S(2)}) collective-permute-start(bf16[784,512]{1,0:T(8,128)(2,1)} %get-tuple-element.43.refs_7_), channel_id=1, source_target_pairs={{0,4},{4,0},{8,12},{12,8},{16,20},{20,16},{24,28},{28,24},{1,5},{5... | collective-permute-start | bytes 2408456 | tf_op jit(solution)/shard_map/ppermute | solution.py:458
  200.2 30.5 %collective-permute-start.17 = (bf16[768,512]{1,0:T(8,128)(2,1)}, bf16[768,512]{1,0:T(8,128)(2,1)S(1)}, u32[]{:S(2)}, u32[]{:S(2)}) collective-permute-start(bf16[768,512]{1,0:T(8,128)(2,1)} %get-tuple-element.52), channel_id=1, source_target_pairs={{0,8},{4,12},{8,0},{12,4},{16,24},{20,28},{24,16},{28,20},{1,9},{5... | collective-permute-start | bytes 2359304 | tf_op jit(solution)/shard_map/ppermute | solution.py:458
  200.5 36.2 %collective-permute-start.20 = (bf16[768,512]{1,0:T(8,128)(2,1)}, bf16[768,512]{1,0:T(8,128)(2,1)S(1)}, u32[]{:S(2)}, u32[]{:S(2)}) collective-permute-start(bf16[768,512]{1,0:T(8,128)(2,1)} %get-tuple-element.58), channel_id=1, source_target_pairs={{0,8},{4,12},{8,0},{12,4},{16,24},{20,28},{24,16},{28,20},{1,9},{5... | collective-permute-start | bytes 2359304 | tf_op jit(solution)/shard_map/ppermute | solution.py:458
  202.2 41.6 %collective-permute-start.24 = (bf16[768,512]{1,0:T(8,128)(2,1)}, bf16[768,512]{1,0:T(8,128)(2,1)S(1)}, u32[]{:S(2)}, u32[]{:S(2)}) collective-permute-start(bf16[768,512]{1,0:T(8,128)(2,1)} %get-tuple-element.56.refs_16_), channel_id=1, source_target_pairs={{0,4},{4,0},{8,12},{12,8},{16,20},{20,16},{24,28},{28,24},{1,5},{5... | collective-permute-start | bytes 2359304 | tf_op jit(solution)/shard_map/ppermute | solution.py:458
  241.8 22.5 %collective-permute-start.21 = (bf16[768,512]{1,0:T(8,128)(2,1)}, bf16[768,512]{1,0:T(8,128)(2,1)S(1)}, u32[]{:S(2)}, u32[]{:S(2)}) collective-permute-start(bf16[768,512]{1,0:T(8,128)(2,1)} %get-tuple-element.59), channel_id=1, source_target_pairs={{0,8},{4,12},{8,0},{12,4},{16,24},{20,28},{24,16},{28,20},{1,9},{5... | collective-permute-start | bytes 2359304 | tf_op jit(solution)/shard_map/ppermute | solution.py:458
  242.1 36.7 %collective-permute-start.23 = (bf16[768,512]{1,0:T(8,128)(2,1)}, bf16[768,512]{1,0:T(8,128)(2,1)S(1)}, u32[]{:S(2)}, u32[]{:S(2)}) collective-permute-start(bf16[768,512]{1,0:T(8,128)(2,1)} %get-tuple-element.61), channel_id=1, source_target_pairs={{0,8},{4,12},{8,0},{12,4},{16,24},{20,28},{24,16},{28,20},{1,9},{5... | collective-permute-start | bytes 2359304 | tf_op jit(solution)/shard_map/ppermute | solution.py:458
  243.8 38.6 %collective-permute-start.22 = (bf16[768,512]{1,0:T(8,128)(2,1)}, bf16[768,512]{1,0:T(8,128)(2,1)S(1)}, u32[]{:S(2)}, u32[]{:S(2)}) collective-permute-start(bf16[768,512]{1,0:T(8,128)(2,1)} %get-tuple-element.60.refs_17_), channel_id=1, source_target_pairs={{0,4},{4,0},{8,12},{12,8},{16,20},{20,16},{24,28},{28,24},{1,5},{5... | collective-permute-start | bytes 2359304 | tf_op jit(solution)/shard_map/ppermute | solution.py:458
  (31 other events, 159.6 us)
Sparse Core Ops, SparseCore 0:
  33.0 65.8 all-gather.6
  100.5 62.1 all-gather.8
  164.2 62.1 all-gather.10

commit v13 on v12

--- a/solution.py
+++ b/solution.py
@@ -588,9 +588,6 @@
     halves = copied(halves, [])
     lead_factor = share_of_first(*halves, member, group, bits)
 
-    near = copied([(weight_grad, (LEAD, weight_grad.shape[1]), [0, 0])], halves[:1])[0]
-    moved = lax.ppermute(near, "tok", down_pairs(bits - 1, group))
-
     live = jnp.arange(tok_rows) < counts[0]
     named = routes[:, 0]
     own = live & (named == expert)
@@ -630,21 +627,24 @@
     parts = [first_part, *copied(later, [across_own[1]])]
     spread = [lax.all_gather(part, "fac") for part in parts]
     rows = first_part.shape[0]
-    earlier = [across_other[1], moved, *parts[1:]]
+    earlier = [across_other[1], *parts[1:]]
     lead = copied([(spread[0], (None, rows, LEAD), [0, 0, 0])], earlier)[0]
     slots = [member, column, member * width] + order + [member] + [0] * (group - 1)
     assert len(slots) == PLACES + 2 * group
     slots = jnp.stack([jnp.int32(slot) for slot in slots])
     across, near_factor = stacked(slots, across_own, across_other, [lead])
     lead = gather_members(lead, bits)
+    sent = copied(member_blocks(spread[0], member, group), [lead[1], across])
+
+    near = copied([(weight_grad, (LEAD, weight_grad.shape[1]), [0, 0])], [across_other[1]])[0]
+    moved = lax.ppermute(near, "tok", down_pairs(bits - 1, group))
     flag = (member >> (bits - 1) & 1)[None]
     for bit in reversed(range(bits - 1)):
-        near = chosen(flag, moved, near, [across])
+        near = chosen(flag, moved, near, sent[:1])
         moved = lax.ppermute(near, "tok", down_pairs(bit, group))
         flag = (member >> bit & 1)[None]
-    sent = copied(member_blocks(spread[0], member, group), [lead[1], near])
-
-    lower, inverse, share = factor_lead(slots, damp, factor_old, lead, sent[:1])
+
+    lower, inverse, share = factor_lead(slots, damp, factor_old, lead, [near])
     panel, lead_stack = panel_columns(
         share, inverse, near_factor, lead, across, spread[1:2]
     )

time: 313 us -> 317 us (1.013)
    unnamed x51 -> x49, local copies, waits for them, and re-layouts: 7.28 us -> 8.5 us
where the time goes in v13:
time: 317 us; the launch traced here: 315 us
  Pallas kernels  148 us (47%)
  waiting for transfers between devices  97.9 us (31%)
  starting transfers between devices  24.5 us (8%)
  between operations  21.4 us (7%)
  local copies, waits for them, and re-layouts  14 us (4%)
  other arithmetic  7.37 us (2%)
    ppermute x23, waiting for transfers between devices, swapped(): lax.ppermute(value, 'tok', [(source, source ^ mask) for source in range(s...  97.7 us
    pallas_call x3, Pallas kernels, finish_rows(): pl.pallas_call(lambda *refs: finish_kernel(count, gram_steps, begin, unre...  58.9 us
    pallas_call x9, Pallas kernels, copied(): pl.pallas_call(lambda *refs: copy_kernel(len(arrays), *refs), grid_spec=p...  31.7 us
    pallas_call x1, Pallas kernels, factor_lead(): pl.pallas_call(lambda *refs: factor_kernel(len(lead), *refs), grid=(1,),...  27.5 us
    ppermute x23, starting transfers between devices, swapped(): lax.ppermute(value, 'tok', [(source, source ^ mask) for source in range(s...  17.6 us
    pallas_call x1, Pallas kernels, panel_columns(): pl.pallas_call(lambda *refs: panel_kernel(count, *refs), grid=(width // c...  11.8 us
    unnamed x49, local copies, waits for them, and re-layouts  8.5 us
    pallas_call x1, Pallas kernels, stacked(): pl.pallas_call(lambda *refs: stack_kernel(count, *refs), grid=(width // c...  8.24 us
  transfers between devices with their start and end apart: 30, of which 10 were waited for; matrix products, arithmetic and copies ran while one was open for 4% of the time, Pallas kernels for 40%

profile of v13, /device:TPU:2, one launch (start us, length us, event | category | flops | bytes accessed | tf_op | source)
XLA Modules:
  0.0 314.8 jit_solution(10829777013824774927)
XLA Ops:
  7.2 3.9 %shard_map.85 = (bf16[256,1536]{1,0:T(8,128)(2,1)}, bf16[256,1536]{1,0:T(8,128)(2,1)}) custom-call(s32[4]{0:T(128)} %constant.91.clone.1.refs_0_, f32[1536,1536]{1,0:T(8,128)} %refs_3_.5, f32[1536,1536]{1,0:T(8,128)} %refs_3_.5), custom_call_target="tpu_custom_call" | custom-call | flops 1 | bytes 1 | tf_op jit(solution)/shard_map/pallas_call | solution.py:485
  28.3 3.1 collective-permute-done.refs_2_
  35.3 2.9 shard_map.86
  39.7 22.3 %collective-permute-done.3.refs_5_ = bf16[320,1536]{1,0:T(8,128)(2,1)S(1)} collective-permute-done((bf16[320,1536]{1,0:T(8,128)(2,1)}, bf16[320,1536]{1,0:T(8,128)(2,1)S(1)}, u32[]{:S(2)}, u32[]{:S(2)}) %collective-permute-start.3) | collective-permute-done | bytes 983072 | tf_op jit(solution)/shard_map/ppermute | solution.py:458
  66.2 3.3 %shard_map.87 = (bf16[768,512]{1,0:T(8,128)(2,1)}, bf16[768,512]{1,0:T(8,128)(2,1)}) custom-call(s32[4]{0:T(128)} %constant.93.clone.1.refs_0_, bf16[768,1536]{1,0:T(8,128)(2,1)} %pad_maximum_fusion.refs_1_.refs_2_, bf16[768,1536]{1,0:T(8,128)(2,1)} %pad_maximum_fusion.refs_1_.refs_2_, bf16[448,1536]{1,0:T(8,128)(2,1)} %collective-permute-done.5.refs_3_.refs_2_), custom_call_target="tpu_custom_call" | custom-call | flops 1 | bytes 1 | tf_op jit(solution)/shard_map/pallas_call | solution.py:485
  71.3 21.3 %collective-permute-done.4.refs_2_.refs_6_ = bf16[320,1536]{1,0:T(8,128)(2,1)S(1)} collective-permute-done((bf16[320,1536]{1,0:T(8,128)(2,1)S(1)}, bf16[320,1536]{1,0:T(8,128)(2,1)S(1)}, u32[]{:S(2)}, u32[]{:S(2)}) %collective-permute-start.4) | collective-permute-done | bytes 983072 | tf_op jit(solution)/shard_map/ppermute | solution.py:458
  93.6 3.7 %shard_map.89.second_ref = bf16[512,2048]{1,0:T(8,128)(2,1)} custom-call(s32[2]{0:T(128)} %broadcast_4_refs_0_.2.refs_0_, bf16[1536,2048]{1,0:T(8,128)(2,1)} %refs_4_.5, bf16[320,1536]{1,0:T(8,128)(2,1)} %copy-done.3), custom_call_target="tpu_custom_call" | custom-call | flops 1 | bytes 1 | tf_op jit(solution)/shard_map/pallas_call | solution.py:485
  100.2 2.9 shard_map.88.refs_9_.refs_3_.refs_4_
  103.1 3.9 %collective-permute-start.6 = (bf16[784,512]{1,0:T(8,128)(2,1)}, bf16[784,512]{1,0:T(8,128)(2,1)S(1)}, u32[]{:S(2)}, u32[]{:S(2)}) collective-permute-start(bf16[784,512]{1,0:T(8,128)(2,1)} %shard_map.88.refs_9_.refs_3_.refs_4_), channel_id=1, source_target_pairs={{0,8},{4,12},{8,0},{12,4},{16,24},{20,28},{24,16},{28,20},{1,9},{5... | collective-permute-start | bytes 2408456 | tf_op jit(solution)/shard_map/ppermute | solution.py:458
  109.4 8.2 %shard_map.90 = (bf16[2560,1536]{1,0:T(8,128)(2,1)}, bf16[512,1536]{1,0:T(8,128)(2,1)}) custom-call(s32[11]{0:T(128)} %stack.52.refs_0_, bf16[448,1536]{1,0:T(8,128)(2,1)} %pad_maximum_fusion.1.refs_1_, bf16[448,1536]{1,0:T(8,128)(2,1)} %collective-permute-done.5.refs_3_.refs_2_, bf16[448,1536]{1,0:T(8,128)(2,1)} %copy-done.11, ...), custom_call_target="tpu_custom_call" | custom-call | flops 1 | bytes 1 | tf_op jit(solution)/shard_map/pallas_call | solution.py:202
  117.6 25.0 %collective-permute-done.6.refs_4_.refs_5_ = bf16[784,512]{1,0:T(8,128)(2,1)S(1)} collective-permute-done((bf16[784,512]{1,0:T(8,128)(2,1)}, bf16[784,512]{1,0:T(8,128)(2,1)S(1)}, u32[]{:S(2)}, u32[]{:S(2)}) %collective-permute-start.6) | collective-permute-done | bytes 802848 | tf_op jit(solution)/shard_map/ppermute | solution.py:458
  143.6 3.8 %shard_map.91 = (bf16[784,512]{1,0:T(8,128)(2,1)}, bf16[784,512]{1,0:T(8,128)(2,1)}, bf16[784,512]{1,0:T(8,128)(2,1)}) custom-call(s32[9]{0:T(128)} %stack.55.refs_0_, bf16[4,784,512]{2,1,0:T(8,128)(2,1)} %bitcast.51, bf16[4,784,512]{2,1,0:T(8,128)(2,1)} %bitcast.52, bf16[4,784,512]{2,1,0:T(8,128)(2,1)} %bitcast.53, bf16[784,512]{1,0:T(8,128)(2,1)} %copy-done.4, ...), custom_call_target="tpu_custom_call" | custom-call | flops 1 | bytes 1 | tf_op jit(solution)/shard_map/pallas_call | solution.py:485
  147.4 3.4 %shard_map.92.refs_7_.second_ref = bf16[512,2048]{1,0:T(8,128)(2,1)} custom-call(s32[1]{0:T(128)} %bitcast.17.flag_ref, bf16[512,2048]{1,0:T(8,128)(2,1)} %collective-permute-done.9.first_ref, bf16[512,2048]{1,0:T(8,128)(2,1)} %shard_map.89.second_ref, bf16[784,512]{1,0:T(8,128)(2,1)} %get-tuple-element.43.refs_0_), custom_call_target="tpu_custom_call" | custom-call | flops 1 | bytes 1 | tf_op jit(solution)/shard_map/pallas_call | solution.py:505
  158.6 27.5 %shard_map.93 = (f32[512,512]{1,0:T(8,128)}, f32[512,512]{1,0:T(8,128)}, f32[8,128]{1,0:T(8,128)}) custom-call(s32[11]{0:T(128)} %stack.52.refs_0_, f32[1]{0:T(128)} %bitcast.8.refs_1_, f32[1536,1536]{1,0:T(8,128)} %refs_3_.5, bf16[784,512]{1,0:T(8,128)(2,1)} %shard_map.88.refs_9_.refs_3_.refs_4_, bf16[784,512]{1,0:T(8,128)(2,1)} %copy-done.4, ...), custom_call_target="tpu_custom_call" | custom-call | flops 1 | bytes 1 | tf_op jit(solution)/shard_map/pallas_call | solution.py:172
  186.1 11.8 %shard_map.94 = (bf16[512,1536]{1,0:T(8,128)(2,1)}, bf16[2560,512]{1,0:T(8,128)(2,1)}) custom-call(f32[8,128]{1,0:T(8,128)} %get-tuple-element.44.refs_0_.refs_2_, f32[512,512]{1,0:T(8,128)} %get-tuple-element.45.refs_1_.inverse_ref.refs_6_, bf16[512,1536]{1,0:T(8,128)(2,1)} %get-tuple-element.46.refs_2_, ...), custom_call_target="tpu_custom_call" | custom-call | flops 1 | bytes 1 | tf_op jit(solution)/shard_map/pallas_call | solution.py:240
  198.8 4.2 %shard_map.96 = (bf16[768,512]{1,0:T(8,128)(2,1)}, bf16[768,512]{1,0:T(8,128)(2,1)}, bf16[768,512]{1,0:T(8,128)(2,1)}, bf16[784,512]{1,0:T(8,128)(2,1)}) custom-call(s32[11]{0:T(128)} %stack.56.refs_0_, bf16[4,768,512]{2,1,0:T(8,128)(2,1)} %bitcast.56, bf16[4,768,512]{2,1,0:T(8,128)(2,1)} %bitcast.57, bf16[4,768,512]{2,1,0:T(8,128)(2,1)} %bitcast.58, ...), custom_call_target="tpu_custom_call" | custom-call | flops 1 | bytes 1 | tf_op jit(solution)/shard_map/pallas_call | solution.py:485
  205.5 6.9 %shard_map.95 = (bf16[512,2048]{1,0:T(8,128)(2,1)}, bf16[512,2048]{1,0:T(8,128)(2,1)}) custom-call(s32[1]{0:T(128)} %bitcast.19.flag_ref, f32[512,512]{1,0:T(8,128)} %get-tuple-element.45.refs_1_.inverse_ref.refs_6_, bf16[512,2048]{1,0:T(8,128)(2,1)} %collective-permute-done.14.first_ref, bf16[512,2048]{1,0:T(8,128)(2,1)} %shard_map.92.refs_7_.second_ref), custom_call_target="tpu_custom_call" | custom-call | flops 1 | bytes 1 | tf_op jit(solution)/shard_map/pallas_call | solution.py:276
  213.3 20.7 %shard_map.97 = (f32[1536,1536]{1,0:T(8,128)}, f32[1536,1536]{1,0:T(8,128)}, f32[1536,2048]{1,0:T(8,128)}, f32[8,128]{1,0:T(8,128)}) custom-call(s32[11]{0:T(128)} %stack.52.refs_0_, f32[1]{0:T(128)} %bitcast.8.refs_1_, f32[8,128]{1,0:T(8,128)} %get-tuple-element.44.refs_0_.refs_2_, f32[1536,1536]{1,0:T(8,128)} %refs_3_.5, bf16[1536,2048]{1,0:T(8,128)(2,1)} %refs_4_.5, ...), custom_call_target="tpu_custom_call" | custom-call | flops 1 | bytes 1 | tf_op jit(solution)/shard_map/pallas_call | solution.py:431
  234.1 6.0 %collective-permute-done.20.refs_6_ = bf16[768,512]{1,0:T(8,128)(2,1)S(1)} collective-permute-done((bf16[768,512]{1,0:T(8,128)(2,1)}, bf16[768,512]{1,0:T(8,128)(2,1)S(1)}, u32[]{:S(2)}, u32[]{:S(2)}) %collective-permute-start.20) | collective-permute-done | bytes 786464 | tf_op jit(solution)/shard_map/ppermute | solution.py:458
  240.9 4.3 %shard_map.98 = (bf16[768,512]{1,0:T(8,128)(2,1)}, bf16[768,512]{1,0:T(8,128)(2,1)}, bf16[768,512]{1,0:T(8,128)(2,1)}, bf16[768,512]{1,0:T(8,128)(2,1)}) custom-call(s32[11]{0:T(128)} %stack.56.refs_0_, bf16[4,768,512]{2,1,0:T(8,128)(2,1)} %bitcast.60, bf16[4,768,512]{2,1,0:T(8,128)(2,1)} %bitcast.61, bf16[4,768,512]{2,1,0:T(8,128)(2,1)} %bitcast.62, ...), custom_call_target="tpu_custom_call" | custom-call | flops 1 | bytes 1 | tf_op jit(solution)/shard_map/pallas_call | solution.py:485
  248.5 19.1 %shard_map.99 = (f32[1536,1536]{1,0:T(8,128)}, f32[1536,1536]{1,0:T(8,128)}, f32[1536,2048]{1,0:T(8,128)}, f32[8,128]{1,0:T(8,128)}) custom-call(s32[11]{0:T(128)} %stack.52.refs_0_, f32[1]{0:T(128)} %bitcast.8.refs_1_, f32[8,128]{1,0:T(8,128)} %get-tuple-element.44.refs_0_.refs_2_, ...), custom_call_target="tpu_custom_call", output_to_operand_aliasing={{0}: (14, {}), {1}: (15, {}), {2}: (16, {})} | custom-call | flops 1 | bytes 1 | tf_op jit(solution)/shard_map/pallas_call | solution.py:431
  267.7 14.5 %collective-permute-done.23.refs_1_ = bf16[768,512]{1,0:T(8,128)(2,1)S(1)} collective-permute-done((bf16[768,512]{1,0:T(8,128)(2,1)}, bf16[768,512]{1,0:T(8,128)(2,1)S(1)}, u32[]{:S(2)}, u32[]{:S(2)}) %collective-permute-start.23) | collective-permute-done | bytes 786464 | tf_op jit(solution)/shard_map/ppermute | solution.py:458
  283.0 2.7 shard_map.100
  289.2 19.0 %shard_map.101 = (f32[1536,1536]{1,0:T(8,128)}, f32[1536,1536]{1,0:T(8,128)}, f32[1536,2048]{1,0:T(8,128)}, f32[8,128]{1,0:T(8,128)}) custom-call(s32[11]{0:T(128)} %stack.52.refs_0_, f32[1]{0:T(128)} %bitcast.8.refs_1_, f32[8,128]{1,0:T(8,128)} %get-tuple-element.44.refs_0_.refs_2_, ...), custom_call_target="tpu_custom_call", output_to_operand_aliasing={{0}: (14, {}), {1}: (15, {}), {2}: (16, {})} | custom-call | flops 1 | bytes 1 | tf_op jit(solution)/shard_map/pallas_call | solution.py:431
  (143 shorter events, 49.0 us)
Async XLA Ops:
  7.2 92.5 %all-gather.7.cloned.1.call-start = ((), (), s32[]{:S(2)}) async-start(), calls=%async_computation | async-start | bytes 4014080 | tf_op jit(solution)/shard_map/all_gather | solution.py:628
  11.1 14.2 %collective-permute-start.1 = (bf16[256,1536]{1,0:T(8,128)(2,1)}, bf16[256,1536]{1,0:T(8,128)(2,1)}, u32[]{:S(2)}, u32[]{:S(2)}) collective-permute-start(bf16[256,1536]{1,0:T(8,128)(2,1)} %get-tuple-element.38), channel_id=1, source_target_pairs={{0,8},{16,24},{1,9},{17,25},{2,10},{18,26},{3,11},{19,27}} | collective-permute-start | bytes 2359304 | tf_op jit(solution)/shard_map/ppermute | solution.py:562
  21.2 10.3 %collective-permute-start = (bf16[336,512]{1,0:T(8,128)(2,1)}, bf16[336,512]{1,0:T(8,128)(2,1)S(1)}, u32[]{:S(2)}, u32[]{:S(2)}) collective-permute-start(bf16[336,512]{1,0:T(8,128)(2,1)} %pad_maximum_fusion.3), channel_id=1, source_target_pairs={{0,16},{4,20},{8,24},{12,28},{16,0},{20,4},{24,8},{28,12},{1,17},{... | collective-permute-start | bytes 1032200 | tf_op jit(solution)/shard_map/ppermute | solution.py:458
  33.3 152.8 %all-gather.9.cloned.1.call-start = ((), (), s32[]{:S(2)}) async-start(), calls=%async_computation.1 | async-start | bytes 3932160 | tf_op jit(solution)/shard_map/all_gather | solution.py:628
  34.6 31.7 %collective-permute-start.5 = (bf16[448,1536]{1,0:T(8,128)(2,1)}, bf16[448,1536]{1,0:T(8,128)(2,1)}, u32[]{:S(2)}, u32[]{:S(2)}) collective-permute-start(bf16[448,1536]{1,0:T(8,128)(2,1)} %pad_maximum_fusion.1.refs_1_), channel_id=1, source_target_pairs={{0,8},{4,12},{8,0},{12,4},{16,24},{20,28},{24,16},{28,20},{1,9},{5... | collective-permute-start | bytes 4128776 | tf_op jit(solution)/shard_map/ppermute | solution.py:458
  38.2 23.8 %collective-permute-start.3 = (bf16[320,1536]{1,0:T(8,128)(2,1)}, bf16[320,1536]{1,0:T(8,128)(2,1)S(1)}, u32[]{:S(2)}, u32[]{:S(2)}) collective-permute-start(bf16[320,1536]{1,0:T(8,128)(2,1)} %shard_map.86), channel_id=1, source_target_pairs={{0,16},{4,20},{8,24},{12,28},{16,0},{20,4},{24,8},{28,12},{1,17},{... | collective-permute-start | bytes 2949128 | tf_op jit(solution)/shard_map/ppermute | solution.py:458
  69.6 164.5 %all-gather.11.cloned.1.call-start = ((), (), s32[]{:S(2)}) async-start(), calls=%async_computation.2 | async-start | bytes 3932160 | tf_op jit(solution)/shard_map/all_gather | solution.py:628
  69.6 23.0 %collective-permute-start.4 = (bf16[320,1536]{1,0:T(8,128)(2,1)S(1)}, bf16[320,1536]{1,0:T(8,128)(2,1)S(1)}, u32[]{:S(2)}, u32[]{:S(2)}) collective-permute-start(bf16[320,1536]{1,0:T(8,128)(2,1)S(1)} %collective-permute-done.3.refs_5_), channel_id=1, source_target_pairs={{0,8},{4,12},{8,0},{12,4},{16,24},{20,28},{24,16},{28,20},{1,9},{5... | collective-permute-start | bytes 2949128 | tf_op jit(solution)/shard_map/ppermute | solution.py:458
  97.3 50.1 %collective-permute-start.9 = (bf16[512,2048]{1,0:T(8,128)(2,1)}, bf16[512,2048]{1,0:T(8,128)(2,1)}, u32[]{:S(2)}, u32[]{:S(2)}) collective-permute-start(bf16[512,2048]{1,0:T(8,128)(2,1)} %shard_map.89.second_ref), channel_id=1, source_target_pairs={{0,8},{16,24},{1,9},{17,25},{2,10},{18,26},{3,11},{19,27}} | collective-permute-start | bytes 6291464 | tf_op jit(solution)/shard_map/ppermute | solution.py:640
  98.7 9.6 %collective-permute-start.10 = (bf16[448,1536]{1,0:T(8,128)(2,1)}, bf16[448,1536]{1,0:T(8,128)(2,1)S(1)}, u32[]{:S(2)}, u32[]{:S(2)}) collective-permute-start(bf16[448,1536]{1,0:T(8,128)(2,1)} %pad_maximum_fusion.1.refs_1_), channel_id=1, source_target_pairs={{0,4},{4,0},{8,12},{12,8},{16,20},{20,16},{24,28},{28,24},{1,5},{5... | collective-permute-start | bytes 4128776 | tf_op jit(solution)/shard_map/ppermute | solution.py:458
  99.2 9.1 %collective-permute-start.11 = (bf16[448,1536]{1,0:T(8,128)(2,1)}, bf16[448,1536]{1,0:T(8,128)(2,1)}, u32[]{:S(2)}, u32[]{:S(2)}) collective-permute-start(bf16[448,1536]{1,0:T(8,128)(2,1)} %collective-permute-done.5.refs_3_.refs_2_), channel_id=1, source_target_pairs={{0,4},{4,0},{8,12},{12,8},{16,20},{20,16},{24,28},{28,24},{1,5},{5... | collective-permute-start | bytes 4128776 | tf_op jit(solution)/shard_map/ppermute | solution.py:458
  99.3 9.0 %collective-permute-start.13 = (bf16[320,1536]{1,0:T(8,128)(2,1)}, bf16[320,1536]{1,0:T(8,128)(2,1)}, u32[]{:S(2)}, u32[]{:S(2)}) collective-permute-start(bf16[320,1536]{1,0:T(8,128)(2,1)} %copy-done.3), channel_id=1, source_target_pairs={{0,4},{4,0},{8,12},{12,8},{16,20},{20,16},{24,28},{28,24},{1,5},{5... | collective-permute-start | bytes 2949128 | tf_op jit(solution)/shard_map/ppermute | solution.py:458
  103.1 39.6 %collective-permute-start.6 = (bf16[784,512]{1,0:T(8,128)(2,1)}, bf16[784,512]{1,0:T(8,128)(2,1)S(1)}, u32[]{:S(2)}, u32[]{:S(2)}) collective-permute-start(bf16[784,512]{1,0:T(8,128)(2,1)} %shard_map.88.refs_9_.refs_3_.refs_4_), channel_id=1, source_target_pairs={{0,8},{4,12},{8,0},{12,4},{16,24},{20,28},{24,16},{28,20},{1,9},{5... | collective-permute-start | bytes 2408456 | tf_op jit(solution)/shard_map/ppermute | solution.py:458
  150.8 54.7 %collective-permute-start.14 = (bf16[512,2048]{1,0:T(8,128)(2,1)}, bf16[512,2048]{1,0:T(8,128)(2,1)}, u32[]{:S(2)}, u32[]{:S(2)}) collective-permute-start(bf16[512,2048]{1,0:T(8,128)(2,1)} %shard_map.92.refs_7_.second_ref), channel_id=1, source_target_pairs={{0,4},{8,12},{16,20},{24,28},{1,5},{9,13},{17,21},{25,29},{2,6},{1... | collective-permute-start | bytes 6291464 | tf_op jit(solution)/shard_map/ppermute | solution.py:644
  154.0 43.9 %collective-permute-start.15 = (bf16[784,512]{1,0:T(8,128)(2,1)}, bf16[784,512]{1,0:T(8,128)(2,1)}, u32[]{:S(2)}, u32[]{:S(2)}) collective-permute-start(bf16[784,512]{1,0:T(8,128)(2,1)} %get-tuple-element.50), channel_id=1, source_target_pairs={{0,8},{4,12},{8,0},{12,4},{16,24},{20,28},{24,16},{28,20},{1,9},{5... | collective-permute-start | bytes 2408456 | tf_op jit(solution)/shard_map/ppermute | solution.py:458
  154.0 43.9 %collective-permute-start.16 = (bf16[784,512]{1,0:T(8,128)(2,1)}, bf16[784,512]{1,0:T(8,128)(2,1)S(1)}, u32[]{:S(2)}, u32[]{:S(2)}) collective-permute-start(bf16[784,512]{1,0:T(8,128)(2,1)} %get-tuple-element.51), channel_id=1, source_target_pairs={{0,8},{4,12},{8,0},{12,4},{16,24},{20,28},{24,16},{28,20},{1,9},{5... | collective-permute-start | bytes 2408456 | tf_op jit(solution)/shard_map/ppermute | solution.py:458
  158.5 53.9 %collective-permute-start.18 = (bf16[784,512]{1,0:T(8,128)(2,1)}, bf16[784,512]{1,0:T(8,128)(2,1)}, u32[]{:S(2)}, u32[]{:S(2)}) collective-permute-start(bf16[784,512]{1,0:T(8,128)(2,1)} %get-tuple-element.43.refs_0_), channel_id=1, source_target_pairs={{0,4},{4,0},{8,12},{12,8},{16,20},{20,16},{24,28},{28,24},{1,5},{5... | collective-permute-start | bytes 2408456 | tf_op jit(solution)/shard_map/ppermute | solution.py:458
  203.0 9.4 %collective-permute-start.19 = (bf16[784,512]{1,0:T(8,128)(2,1)}, bf16[784,512]{1,0:T(8,128)(2,1)S(1)}, u32[]{:S(2)}, u32[]{:S(2)}) collective-permute-start(bf16[784,512]{1,0:T(8,128)(2,1)} %get-tuple-element.55), channel_id=1, source_target_pairs={{0,4},{4,0},{8,12},{12,8},{16,20},{20,16},{24,28},{28,24},{1,5},{5... | collective-permute-start | bytes 2408456 | tf_op jit(solution)/shard_map/ppermute | solution.py:458
  203.5 30.6 %collective-permute-start.17 = (bf16[768,512]{1,0:T(8,128)(2,1)}, bf16[768,512]{1,0:T(8,128)(2,1)S(1)}, u32[]{:S(2)}, u32[]{:S(2)}) collective-permute-start(bf16[768,512]{1,0:T(8,128)(2,1)} %get-tuple-element.52), channel_id=1, source_target_pairs={{0,8},{4,12},{8,0},{12,4},{16,24},{20,28},{24,16},{28,20},{1,9},{5... | collective-permute-start | bytes 2359304 | tf_op jit(solution)/shard_map/ppermute | solution.py:458
  203.5 36.5 %collective-permute-start.20 = (bf16[768,512]{1,0:T(8,128)(2,1)}, bf16[768,512]{1,0:T(8,128)(2,1)S(1)}, u32[]{:S(2)}, u32[]{:S(2)}) collective-permute-start(bf16[768,512]{1,0:T(8,128)(2,1)} %get-tuple-element.58), channel_id=1, source_target_pairs={{0,8},{4,12},{8,0},{12,4},{16,24},{20,28},{24,16},{28,20},{1,9},{5... | collective-permute-start | bytes 2359304 | tf_op jit(solution)/shard_map/ppermute | solution.py:458
  205.5 41.7 %collective-permute-start.24 = (bf16[768,512]{1,0:T(8,128)(2,1)}, bf16[768,512]{1,0:T(8,128)(2,1)S(1)}, u32[]{:S(2)}, u32[]{:S(2)}) collective-permute-start(bf16[768,512]{1,0:T(8,128)(2,1)} %get-tuple-element.56.refs_16_), channel_id=1, source_target_pairs={{0,4},{4,0},{8,12},{12,8},{16,20},{20,16},{24,28},{28,24},{1,5},{5... | collective-permute-start | bytes 2359304 | tf_op jit(solution)/shard_map/ppermute | solution.py:458
  245.2 22.5 %collective-permute-start.21 = (bf16[768,512]{1,0:T(8,128)(2,1)}, bf16[768,512]{1,0:T(8,128)(2,1)S(1)}, u32[]{:S(2)}, u32[]{:S(2)}) collective-permute-start(bf16[768,512]{1,0:T(8,128)(2,1)} %get-tuple-element.59), channel_id=1, source_target_pairs={{0,8},{4,12},{8,0},{12,4},{16,24},{20,28},{24,16},{28,20},{1,9},{5... | collective-permute-start | bytes 2359304 | tf_op jit(solution)/shard_map/ppermute | solution.py:458
  245.4 36.7 %collective-permute-start.23 = (bf16[768,512]{1,0:T(8,128)(2,1)}, bf16[768,512]{1,0:T(8,128)(2,1)S(1)}, u32[]{:S(2)}, u32[]{:S(2)}) collective-permute-start(bf16[768,512]{1,0:T(8,128)(2,1)} %get-tuple-element.61), channel_id=1, source_target_pairs={{0,8},{4,12},{8,0},{12,4},{16,24},{20,28},{24,16},{28,20},{1,9},{5... | collective-permute-start | bytes 2359304 | tf_op jit(solution)/shard_map/ppermute | solution.py:458
  247.2 38.6 %collective-permute-start.22 = (bf16[768,512]{1,0:T(8,128)(2,1)}, bf16[768,512]{1,0:T(8,128)(2,1)S(1)}, u32[]{:S(2)}, u32[]{:S(2)}) collective-permute-start(bf16[768,512]{1,0:T(8,128)(2,1)} %get-tuple-element.60.refs_17_), channel_id=1, source_target_pairs={{0,4},{4,0},{8,12},{12,8},{16,20},{20,16},{24,28},{28,24},{1,5},{5... | collective-permute-start | bytes 2359304 | tf_op jit(solution)/shard_map/ppermute | solution.py:458
  (30 other events, 179.6 us)
Sparse Core Ops, SparseCore 0:
  33.4 65.8 all-gather.6
  100.8 62.1 all-gather.8
  164.5 62.1 all-gather.10
